TPU v7x, 256 devices: a whole 4x4x8 slice. The times are simulated.
256 devices in a mesh: dp: 32 (over x, z), expert: 8 (over y, core).
Axes of the slice: x: 4, y: 4, z: 8, core: 2. Of those that a mesh axis runs over, the one named last changes fastest.
Arguments:
- tokens: bfloat16 [3072, 3072], P(('dp', 'expert')), may hold values from -6 to 6
- cotangent: bfloat16 [3072, 3072], P(('dp', 'expert')), may hold values from -6 to 6
- routes: int32 [3072, 2], P(('dp', 'expert')), may hold values from 0 to 7, all different within a row; in each aligned block of 12 rows (0 to 11, 12 to 23, ...) at most 4 rows name the same one
- example_ids: int32 [32, 96], P('dp', 'expert'), may hold values from 0 to 5, never falling along the last dimension, each value on 1 to 32 neighbouring positions
- w_gate: bfloat16 [8, 3072, 8192], P('expert', None, 'dp'), may hold values from -0.109375 to 0.109375
- w_up: bfloat16 [8, 3072, 8192], P('expert', None, 'dp'), may hold values from -0.109375 to 0.109375
- w_down: bfloat16 [8, 8192, 3072], P('expert', 'dp'), may hold values from -0.0625 to 0.0625
Outputs:
- mixed: bfloat16 [3072, 3072], P(('dp', 'expert'))
- example_norms: float32 [32, 6], P('dp')
- grad_gate: bfloat16 [8, 3072, 8192], P('expert', None, 'dp')
- grad_up: bfloat16 [8, 3072, 8192], P('expert', None, 'dp')
- grad_down: bfloat16 [8, 8192, 3072], P('expert', 'dp')
Inputs may be any that keep to these rules, and one draw needn't show every extreme that they name: `routes`: among the tokens of one device each expert is named at most 4 times, and exactly 4 times by some expert. `example_ids`: along a row example numbers never fall and every example has at least one token.
All inputs are finite; a program needn't handle non-finite values.
Results may differ from a plain program's by a relative error of at most 0.0059.
Values may be sent and summed in bfloat16 or wider, within the bound.
No kernel may reach another device: no remote copies, remote signals or barrier semaphores. Data moves between devices by JAX's collectives and lax.ppermute only.
A program may use at most 128 MiB of HBM per device.

v0:
```python
import math

import jax
import jax.numpy as jnp
from jax import lax
from jax.experimental import pallas as pl
from jax.experimental.pallas import tpu as pltpu
from jax.sharding import Mesh, PartitionSpec as P

D = 3072
FF = 8192
CAP = 4
EX_ROW = 6
NX, NZ, NE = 4, 8, 8
BLOCKS = NX * NZ
SLOTS = NE * CAP
ROWS = BLOCKS * SLOTS
HID = FF // BLOCKS
SIZE = {"x": NX, "z": NZ}
ORDER = {"x": (0, -1, 1, 2), "z": (0, -1, 1, -2, 2, -3, 3, 4)}
GAMMA = 0.01
RADIUS = math.sqrt(3.0 * D * FF * NE / (BLOCKS * EX_ROW))
EXPERT = ("y", "c")
BF = jnp.bfloat16
F32 = jnp.float32
MIB = 1 << 20
LANES = 128
TILE = NZ * SLOTS
MID = SLOTS // 2
COLS = 512
LEFT = D // 2


def shift(a, axis, step):
    n = SIZE[axis]
    return lax.ppermute(a, axis, [(i, (i + step) % n) for i in range(n)])


def ring_gather(a, axis):
    half = SIZE[axis] // 2
    mid = a.shape[-2] // 2
    pieces = [a]
    up = down = a
    for _ in range(1, half):
        up, down = shift(up, axis, 1), shift(down, axis, -1)
        pieces += [up, down]
    return pieces + [shift(up[..., :mid, :], axis, 1), shift(down[..., mid:, :], axis, -1)]


def line_of(pieces):
    return jnp.stack(pieces[:-2] + [jnp.concatenate(pieces[-2:], axis=-2)], axis=0)


def plus(a, b):
    return (a.astype(F32) + b.astype(F32)).astype(BF)


def ring_sum(parts, axis, hook):
    half = SIZE[axis] // 2
    place = ORDER[axis].index

    def get(k):
        return parts[place(k)]

    far = get(half)
    mid = far.shape[0] // 2
    up, down = shift(far[:mid], axis, 1), shift(far[mid:], axis, -1)
    own_up, own_down = get(half - 1), get(1 - half)
    up = jnp.concatenate([plus(up, own_up[:mid]), own_up[mid:]], axis=0)
    down = jnp.concatenate([own_down[:mid], plus(down, own_down[mid:])], axis=0)
    for k in range(half - 1, 0, -1):
        up, down = hook(half - k, (up, down))
        up, down = shift(up, axis, 1), shift(down, axis, -1)
        if k > 1:
            up, down = plus(up, get(k - 1)), plus(down, get(1 - k))
    up, down = hook(half, (up, down))
    return (up.astype(F32) + down.astype(F32) + get(0).astype(F32)).astype(BF)


def direct_sum(parts, axis):
    total = parts[0].astype(F32)
    for place, k in enumerate(ORDER[axis]):
        if k:
            total = total + shift(parts[place], axis, k).astype(F32)
    return total.astype(BF)


def spread(a, axes, n):
    return lax.all_to_all(jnp.broadcast_to(a[None], (n,) + a.shape), axes, 0, 0, tiled=True)


def dot(a, b, dims):
    return lax.dot_general(a, b, (dims, ((), ())), preferred_element_type=F32)


def forward_kernel(where_ref, *refs):
    a_refs, refs = refs[: NZ + 1], refs[NZ + 1 :]
    b_refs, refs = refs[: NX + 1], refs[NX + 1 :]
    wg_ref, wu_ref, wd_ref, x_out, gate_ref, up_ref, hidden_ref, left_ref, right_ref, rows_ref, in_sems, out_sems = refs
    step = pl.program_id(0)
    quarter = MID // 2
    arrivals = []
    for i in range(NX):
        moves = [(a_refs[j].at[i], rows_ref.at[i, j, pl.ds(0, MID)]) for j in range(NZ - 1)]
        moves += [(a_refs[NZ - 1 + h].at[i], rows_ref.at[i, NZ - 1, pl.ds(h * quarter, quarter)]) for h in range(2)]
        if i < NX - 1:
            moves += [(b_refs[i], rows_ref.at[i, :, pl.ds(MID, MID)])]
        else:
            moves += [(b_refs[i + h], rows_ref.at[i, :, pl.ds(MID + h * quarter, quarter)]) for h in range(2)]
        arrivals.append([pltpu.make_async_copy(s, d, in_sems.at[i, n]) for n, (s, d) in enumerate(moves)])
    leaving = [pltpu.make_async_copy(rows_ref.at[i], x_out.at[i], out_sems.at[i]) for i in range(NX)]

    @pl.when(step == 0)
    def _():
        for group in arrivals:
            for copy in group:
                copy.start()

    for i in range(NX):

        @pl.when(step == i)
        def _():
            for copy in arrivals[i]:
                copy.wait()
            leaving[i].start()

    x = rows_ref[step].reshape(TILE, D)
    gate = dot(x, wg_ref[0], ((1,), (0,)))
    up = dot(x, wu_ref[0], ((1,), (0,)))
    hidden = (gate * jax.nn.sigmoid(gate) * up).astype(BF)
    gate_ref[...] = gate
    up_ref[...] = up
    hidden_ref[...] = hidden
    out = dot(hidden, wd_ref[0, :, :LEFT], ((1,), (0,))).astype(BF)
    left_ref[...] = out.reshape(NZ, 1, SLOTS, LEFT)
    out = dot(hidden, wd_ref[0, :, LEFT:], ((1,), (0,))).astype(BF)
    for j in range(NZ):
        right_ref[0, where_ref[NX + j]] = out[j * SLOTS : (j + 1) * SLOTS]

    @pl.when(step == NX - 1)
    def _():
        for copy in leaving:
            copy.wait()


def forward(where, a_pieces, b_pieces, w_gate, w_up, w_down):
    outside = pl.BlockSpec(memory_space=pltpu.HBM)

    def whole(a):
        return pl.BlockSpec(a.shape, lambda i, where: (0, 0, 0), pipeline_mode=pl.Buffered(1))

    def tall(n):
        return pl.BlockSpec((TILE, n), lambda i, where: (i, 0))

    return pl.pallas_call(
        forward_kernel,
        grid_spec=pltpu.PrefetchScalarGridSpec(
            num_scalar_prefetch=1,
            grid=(NX,),
            in_specs=[outside] * (NZ + NX + 2) + [whole(w_gate), whole(w_up), whole(w_down)],
            out_specs=[
                outside,
                tall(HID),
                tall(HID),
                tall(HID),
                pl.BlockSpec((NZ, 1, SLOTS, LEFT), lambda i, where: (0, i, 0, 0)),
                pl.BlockSpec((1, NZ, SLOTS, D - LEFT), lambda i, where: (where[i], 0, 0, 0)),
            ],
            scratch_shapes=[
                pltpu.VMEM((NX, NZ, SLOTS, D), BF),
                pltpu.SemaphoreType.DMA((NX, NZ + 3)),
                pltpu.SemaphoreType.DMA((NX,)),
            ],
        ),
        out_shape=[
            jax.ShapeDtypeStruct((NX, NZ, SLOTS, D), BF),
            jax.ShapeDtypeStruct((ROWS, HID), F32),
            jax.ShapeDtypeStruct((ROWS, HID), F32),
            jax.ShapeDtypeStruct((ROWS, HID), BF),
            jax.ShapeDtypeStruct((NZ, NX, SLOTS, LEFT), BF),
            jax.ShapeDtypeStruct((NX, NZ, SLOTS, D - LEFT), BF),
        ],
        compiler_params=pltpu.CompilerParams(vmem_limit_bytes=40 * MIB),
        cost_estimate=pl.CostEstimate(flops=6 * ROWS * D * HID, bytes_accessed=20 * MIB, transcendentals=ROWS * HID),
        name="forward",
    )(where, *a_pieces, *b_pieces, w_gate, w_up, w_down)


def backward_kernel(where_ref, y_ref, id_ref, x_ref, wd_ref, gate_ref, up_ref, hidden_ref, dg_ref, du_ref, spot_ref, sum_ref, y_rows):
    i = pl.program_id(0)
    at_x = where_ref[i]
    spots = []
    for j in range(NZ):
        at_z = where_ref[NX + j]
        y_rows[j] = y_ref[at_z]
        block_id = id_ref[at_z].astype(F32)
        start = ((at_x * NZ + at_z) * 8).astype(F32)
        spots.append(jnp.where(block_id >= 0.0, block_id + start, -1.0))
    spot = jnp.concatenate(spots, axis=0)
    spot_ref[...] = spot[:, :1]
    y = y_rows[...].reshape(TILE, D)
    x = x_ref[0].reshape(TILE, D)
    back = dot(y, wd_ref[0], ((1,), (1,)))
    gate, up, hidden = gate_ref[...], up_ref[...], hidden_ref[...]
    sig = jax.nn.sigmoid(gate)
    d_gate = (back * up * sig * (1.0 + gate * (1.0 - sig))).astype(BF)
    d_up = (back * (gate * sig)).astype(BF)
    dg_ref[...] = d_gate
    du_ref[...] = d_up
    last = ((1,), (1,))
    pair = dot(x, x, last) * (dot(d_gate, d_gate, last) + dot(d_up, d_up, last))
    pair = pair + dot(y, y, last) * dot(hidden, hidden, last)
    same = (spot[:, :1] == spot.T[:1, :]) & (spot[:, :1] >= 0.0)
    row_sums = jnp.sum(jnp.where(same, pair, 0.0), axis=1, keepdims=True)
    lane = lax.broadcasted_iota(jnp.int32, (TILE, LANES), 1).astype(F32)

    @pl.when(i == 0)
    def _():
        sum_ref[...] = jnp.zeros_like(sum_ref)

    for half in range(2):
        hot = spot == lane + half * LANES
        sum_ref[half : half + 1, :] += jnp.sum(jnp.where(hot, row_sums, 0.0), axis=0, keepdims=True)


def backward(where, wide_y, x, w_down, gate, up, hidden):
    def tall(n):
        return pl.BlockSpec((TILE, n), lambda i, where: (i, 0))

    rows = pl.BlockSpec((1, NZ, SLOTS, D), lambda i, where: (i, 0, 0, 0))
    return pl.pallas_call(
        backward_kernel,
        grid_spec=pltpu.PrefetchScalarGridSpec(
            num_scalar_prefetch=1,
            grid=(NX,),
            in_specs=[
                pl.BlockSpec((NZ, SLOTS, D), lambda i, where: (where[i], 0, 0)),
                pl.BlockSpec((NZ, SLOTS, LANES), lambda i, where: (where[i], 0, D // LANES)),
                rows,
                pl.BlockSpec(w_down.shape, lambda i, where: (0, 0, 0), pipeline_mode=pl.Buffered(1)),
                tall(HID),
                tall(HID),
                tall(HID),
            ],
            out_specs=[tall(HID), tall(HID), tall(1), pl.BlockSpec((2, LANES), lambda i, where: (0, 0))],
            scratch_shapes=[pltpu.VMEM((NZ, SLOTS, D), BF)],
        ),
        out_shape=[
            jax.ShapeDtypeStruct((ROWS, HID), BF),
            jax.ShapeDtypeStruct((ROWS, HID), BF),
            jax.ShapeDtypeStruct((ROWS, 1), F32),
            jax.ShapeDtypeStruct((2, LANES), F32),
        ],
        compiler_params=pltpu.CompilerParams(vmem_limit_bytes=40 * MIB),
        cost_estimate=pl.CostEstimate(flops=5 * ROWS * D * HID, bytes_accessed=20 * MIB, transcendentals=ROWS * HID),
        name="backward",
    )(where, wide_y, wide_y, x, w_down, gate, up, hidden)


def grads_kernel(
    where_ref, x_ref, y_ref, hidden_ref, dg_ref, du_ref, spot_ref, factor_ref, gg_ref, gu_ref, gd_ref, scaled, turned, moved, by_row
):
    @pl.when(pl.program_id(0) == 0)
    def _():
        spot = spot_ref[...]
        lane = lax.broadcasted_iota(jnp.int32, (ROWS, LANES), 1).astype(F32)
        factor = jnp.zeros((ROWS, 1), F32)
        for half in range(2):
            chosen = jnp.where(spot == lane + half * LANES, factor_ref[half : half + 1, :], 0.0)
            factor = factor + jnp.sum(chosen, axis=1, keepdims=True)
        scaled[:, :HID] = (factor * dg_ref[...].astype(F32)).astype(BF)
        scaled[:, HID:] = (factor * du_ref[...].astype(F32)).astype(BF)
        for i in range(NX):
            for j in range(NZ):
                block = where_ref[i] * NZ + where_ref[NX + j]
                first = (i * NZ + j) * SLOTS
                moved[block] = hidden_ref[first : first + SLOTS]
                by_row[block] = factor[first : first + SLOTS]
        turned[...] = moved[...].reshape(ROWS, HID).T

    x = x_ref[...].reshape(ROWS, COLS)
    both = dot(x, scaled[...], ((0,), (0,))).astype(BF)
    gg_ref[0] = both[:, :HID]
    gu_ref[0] = both[:, HID:]
    cot = (by_row[...] * y_ref[...].astype(F32)).astype(BF).reshape(ROWS, COLS)
    gd_ref[0] = dot(turned[...], cot, ((1,), (0,))).astype(BF)


def gradients(where, x, wide_y, hidden, d_gate, d_up, spot, factors):
    def whole(a):
        return pl.BlockSpec(a.shape, lambda i, where: (0, 0), pipeline_mode=pl.Buffered(1))

    return pl.pallas_call(
        grads_kernel,
        grid_spec=pltpu.PrefetchScalarGridSpec(
            num_scalar_prefetch=1,
            grid=(D // COLS,),
            in_specs=[
                pl.BlockSpec((NX, NZ, SLOTS, COLS), lambda i, where: (0, 0, 0, i)),
                pl.BlockSpec((BLOCKS, SLOTS, COLS), lambda i, where: (0, 0, i)),
                whole(hidden),
                whole(d_gate),
                whole(d_up),
                whole(spot),
                whole(factors),
            ],
            out_specs=[
                pl.BlockSpec((1, COLS, HID), lambda i, where: (0, i, 0)),
                pl.BlockSpec((1, COLS, HID), lambda i, where: (0, i, 0)),
                pl.BlockSpec((1, HID, COLS), lambda i, where: (0, 0, i)),
            ],
            scratch_shapes=[
                pltpu.VMEM((ROWS, 2 * HID), BF),
                pltpu.VMEM((HID, ROWS), BF),
                pltpu.VMEM((BLOCKS, SLOTS, HID), BF),
                pltpu.VMEM((BLOCKS, SLOTS, 1), F32),
            ],
        ),
        out_shape=[
            jax.ShapeDtypeStruct((1, D, HID), BF),
            jax.ShapeDtypeStruct((1, D, HID), BF),
            jax.ShapeDtypeStruct((1, HID, D), BF),
        ],
        compiler_params=pltpu.CompilerParams(vmem_limit_bytes=40 * MIB),
        cost_estimate=pl.CostEstimate(flops=6 * ROWS * D * HID, bytes_accessed=18 * MIB, transcendentals=0),
        name="gradients",
    )(where, x, wide_y, hidden, d_gate, d_up, spot, factors)


def on_device(tokens, cotangent, routes, example_ids, w_gate, w_up, w_down):
    ix, iz = lax.axis_index("x"), lax.axis_index("z")
    where = jnp.concatenate([(ix + jnp.array(ORDER["x"])) % NX, (iz + jnp.array(ORDER["z"])) % NZ]).astype(jnp.int32)
    tok_count, width = tokens.shape
    flat_routes = routes.reshape(-1)
    owner_hot = (flat_routes[:, None] == jnp.arange(NE)[None, :]).astype(jnp.int32)
    before = jnp.cumsum(owner_hot, axis=0) - owner_hot
    slot_of = flat_routes * CAP + jnp.sum(before * owner_hot, axis=1)
    placed = (jnp.arange(SLOTS)[:, None] == slot_of[None, :]).astype(jnp.int32)
    placed = jnp.sum(placed.reshape(SLOTS, tok_count, 2), axis=2)
    placed_bf = placed.astype(BF)
    filled = jnp.sum(placed, axis=1) > 0
    send_ids = jnp.where(filled, jnp.sum(placed * example_ids.reshape(-1)[None, :], axis=1), -1)
    send_x = jnp.dot(placed_bf, tokens, preferred_element_type=F32).astype(BF)
    send_dy = jnp.dot(placed_bf, cotangent, preferred_element_type=F32).astype(BF)
    id_cols = jnp.broadcast_to(send_ids.astype(BF)[:, None], (SLOTS, LANES))
    send = jnp.concatenate(
        [
            jnp.concatenate([send_x, id_cols], axis=1).reshape(NE, CAP, width + LANES),
            jnp.concatenate([send_dy, id_cols], axis=1).reshape(NE, CAP, width + LANES),
        ],
        axis=1,
    )
    got = lax.all_to_all(send, EXPERT, split_axis=0, concat_axis=0, tiled=True)
    local_x = got[:, :CAP, :width].reshape(SLOTS, width)
    local_dy = got[:, CAP:].reshape(SLOTS, width + LANES)
    wide_y = lax.all_gather(local_dy, ("x", "z"), axis=0)
    line_x = line_of(ring_gather(local_x[:MID], "x"))
    line_z = line_of(ring_gather(local_x[MID:], "z"))
    a_pieces = ring_gather(line_x, "z")
    b_pieces = ring_gather(line_z, "x")
    x, gate, up_part, hidden, left, right = forward(where, a_pieces, b_pieces, w_gate, w_up, w_down)
    right, wide_y = lax.optimization_barrier((right, wide_y))
    right_line = lax.psum_scatter(right.reshape(ROWS, D - LEFT), "x", scatter_dimension=0, tiled=True)
    kept = {}

    def hook(step, pair):
        if step == 1:
            kept["back"] = backward(where, wide_y, x, w_down, gate, up_part, hidden)
            pair, kept["sum"] = lax.optimization_barrier((pair, kept["back"][3]))
        elif step == 2:
            total = jnp.sum(spread(kept["sum"], ("x", "z"), BLOCKS).reshape(BLOCKS, 2, LANES), axis=0)
            pair, kept["sum"] = lax.optimization_barrier((pair, total))
        elif step == 3:
            total = jnp.sum(spread(kept["sum"], EXPERT, NE).reshape(NE, 2, LANES), axis=0)
            pair, norms, line = lax.optimization_barrier((pair, jnp.sqrt(total), right_line.astype(F32)))
            kept["norms"], kept["line"] = norms, line
        else:
            d_gate, d_up, spot, _ = kept["back"]
            factors = RADIUS / (kept["norms"] + GAMMA)
            grads = gradients(where, x, wide_y, hidden, d_gate, d_up, spot, factors)
            pair, kept["grads"] = lax.optimization_barrier((pair, grads))
        return pair

    left_line = ring_sum(left, "z", hook)
    right_out = lax.psum_scatter(kept["line"], "z", scatter_dimension=0, tiled=True).astype(BF)
    left_out = direct_sum(left_line, "x")
    own_out = jnp.concatenate([left_out, right_out], axis=1)
    returned = lax.all_to_all(own_out.reshape(NE, CAP, width), EXPERT, split_axis=0, concat_axis=0, tiled=True)
    mixed = jnp.dot(placed_bf.T, returned.reshape(SLOTS, width), preferred_element_type=F32).astype(BF)
    norms = kept["norms"]
    own_norms = lax.dynamic_slice(norms.reshape(BLOCKS, 8), (ix * NZ + iz, 0), (1, EX_ROW))
    return (mixed, own_norms, *kept["grads"])


def solution(mesh):
    mesh = Mesh(mesh.devices.reshape(NX, NZ, 4, 2), ("x", "z", "y", "c"))
    data, every = ("x", "z"), ("x", "z", "y", "c")
    return jax.shard_map(
        on_device,
        mesh=mesh,
        in_specs=(
            P(every, None),
            P(every, None),
            P(every, None),
            P(data, EXPERT),
            P(EXPERT, None, data),
            P(EXPERT, None, data),
            P(EXPERT, data, None),
        ),
        out_specs=(
            P(every, None),
            P(data, None),
            P(EXPERT, None, data),
            P(EXPERT, None, data),
            P(EXPERT, data, None),
        ),
        check_vma=False,
    )
```

profile of v0, /device:TPU:1, one launch (start us, length us, event | category | flops | bytes accessed | tf_op | source)
XLA Modules:
  0.0 264.8 jit_solution(13254750426336730670)
XLA Ops:
  10.4 1.1 convolution_convert_fusion
  12.0 14.0 %all_to_all.20 = bf16[8,8,3200]{2,1,0:T(8,128)(2,1)S(1)} all-to-all(bf16[8,8,3200]{2,1,0:T(8,128)(2,1)S(1)} %pad_maximum_fusion), channel_id=1, replica_groups=mesh['x'=4,'z'=8,'y'=4,'c'=2] {'y','c'}, dimensions={0} | all-to-all | bytes 819200 | tf_op jit(solution)/shard_map/all_to_all | solution.py:353
  27.1 2.6 collective-permute-start.1
  29.7 1.7 collective-permute-start.12
  31.4 4.0 %collective-permute-start.13 = (bf16[16,3072]{1,0:T(8,128)(2,1)S(1)}, bf16[16,3072]{1,0:T(8,128)(2,1)S(1)}, u32[]{:S(2)}, u32[]{:S(2)}) collective-permute-start(bf16[16,3072]{1,0:T(8,128)(2,1)S(1)} %slice.117), channel_id=1, source_target_pairs={{0,56},{8,0},{16,8},{24,16},{32,24},{40,32},{48,40},{56,48},{1,57}... | collective-permute-start | bytes 294920 | tf_op jit(solution)/shard_map/ppermute | solution.py:36
  36.2 2.8 %collective-permute-start.3 = (bf16[8,3072]{1,0:T(8,128)(2,1)S(1)}, bf16[8,3072]{1,0:T(8,128)(2,1)S(1)}, u32[]{:S(2)}, u32[]{:S(2)}) collective-permute-start(bf16[8,3072]{1,0:T(8,128)(2,1)S(1)} %slice.144), channel_id=1, source_target_pairs={{0,192},{64,0},{128,64},{192,128},{1,193},{65,1},{129,65},{193,129... | collective-permute-start | bytes 147464 | tf_op jit(solution)/shard_map/ppermute | solution.py:36
  39.1 2.7 %collective-permute-start.15 = (bf16[16,3072]{1,0:T(8,128)(2,1)S(1)}, bf16[16,3072]{1,0:T(8,128)(2,1)S(1)}, u32[]{:S(2)}, u32[]{:S(2)}) collective-permute-start(bf16[16,3072]{1,0:T(8,128)(2,1)S(1)} %collective-permute-done.13), channel_id=1, source_target_pairs={{0,56},{8,0},{16,8},{24,16},{32,24},{40,32},{48,40},{56,48},{1,57}... | collective-permute-start | bytes 294920 | tf_op jit(solution)/shard_map/ppermute | solution.py:36
  43.3 2.7 %collective-permute-start.5 = (bf16[4,16,3072]{2,1,0:T(8,128)(2,1)S(1)}, bf16[4,16,3072]{2,1,0:T(8,128)(2,1)S(1)}, u32[]{:S(2)}, u32[]{:S(2)}) collective-permute-start(bf16[4,16,3072]{2,1,0:T(8,128)(2,1)S(1)} %pad_maximum_fusion.1.refs_0_), channel_id=1, source_target_pairs={{0,56},{8,0},{16,8},{24,16},{32,24},{40,32},{48,40},{56,48},{1,57}... | collective-permute-start | bytes 1179656 | tf_op jit(solution)/shard_map/ppermute | solution.py:36
  46.7 2.7 %collective-permute-start.17 = (bf16[16,3072]{1,0:T(8,128)(2,1)S(1)}, bf16[16,3072]{1,0:T(8,128)(2,1)S(1)}, u32[]{:S(2)}, u32[]{:S(2)}) collective-permute-start(bf16[16,3072]{1,0:T(8,128)(2,1)S(1)} %collective-permute-done.15), channel_id=1, source_target_pairs={{0,56},{8,0},{16,8},{24,16},{32,24},{40,32},{48,40},{56,48},{1,57}... | collective-permute-start | bytes 294920 | tf_op jit(solution)/shard_map/ppermute | solution.py:36
  50.7 6.0 %collective-permute-done.17 = bf16[16,3072]{1,0:T(8,128)(2,1)S(1)} collective-permute-done((bf16[16,3072]{1,0:T(8,128)(2,1)S(1)}, bf16[16,3072]{1,0:T(8,128)(2,1)S(1)}, u32[]{:S(2)}, u32[]{:S(2)}) %collective-permute-start.17) | collective-permute-done | bytes 98336 | tf_op jit(solution)/shard_map/ppermute | solution.py:36
  56.6 3.5 %collective-permute-start.19 = (bf16[8,3072]{1,0:T(8,128)(2,1)S(1)}, bf16[8,3072]{1,0:T(8,128)(2,1)S(1)}, u32[]{:S(2)}, u32[]{:S(2)}) collective-permute-start(bf16[8,3072]{1,0:T(8,128)(2,1)S(1)} %slice.149), channel_id=1, source_target_pairs={{0,56},{8,0},{16,8},{24,16},{32,24},{40,32},{48,40},{56,48},{1,57}... | collective-permute-start | bytes 147464 | tf_op jit(solution)/shard_map/ppermute | solution.py:36
  62.3 2.6 collective-permute-done.18
  65.5 4.2 %collective-permute-start.21 = (bf16[8,16,3072]{2,1,0:T(8,128)(2,1)}, bf16[8,16,3072]{2,1,0:T(8,128)(2,1)S(1)}, u32[]{:S(2)}, u32[]{:S(2)}) collective-permute-start(bf16[8,16,3072]{2,1,0:T(8,128)(2,1)} %fusion.10.refs_9_), channel_id=1, source_target_pairs={{0,192},{64,0},{128,64},{192,128},{1,193},{65,1},{129,65},{193,129... | collective-permute-start | bytes 2359304 | tf_op jit(solution)/shard_map/ppermute | solution.py:36
  70.5 2.7 %collective-permute-start.7 = (bf16[4,16,3072]{2,1,0:T(8,128)(2,1)S(1)}, bf16[4,16,3072]{2,1,0:T(8,128)(2,1)}, u32[]{:S(2)}, u32[]{:S(2)}) collective-permute-start(bf16[4,16,3072]{2,1,0:T(8,128)(2,1)S(1)} %collective-permute-done.5.refs_2_), channel_id=1, source_target_pairs={{0,56},{8,0},{16,8},{24,16},{32,24},{40,32},{48,40},{56,48},{1,57}... | collective-permute-start | bytes 1179656 | tf_op jit(solution)/shard_map/ppermute | solution.py:36
  73.9 3.9 %collective-permute-done.6.refs_3_ = bf16[4,16,3072]{2,1,0:T(8,128)(2,1)} collective-permute-done((bf16[4,16,3072]{2,1,0:T(8,128)(2,1)S(1)}, bf16[4,16,3072]{2,1,0:T(8,128)(2,1)}, u32[]{:S(2)}, u32[]{:S(2)}) %collective-permute-start.6) | collective-permute-done | bytes 393248 | tf_op jit(solution)/shard_map/ppermute | solution.py:36
  77.9 3.4 %collective-permute-start.9 = (bf16[4,16,3072]{2,1,0:T(8,128)(2,1)}, bf16[4,16,3072]{2,1,0:T(8,128)(2,1)}, u32[]{:S(2)}, u32[]{:S(2)}) collective-permute-start(bf16[4,16,3072]{2,1,0:T(8,128)(2,1)} %collective-permute-done.7.refs_4_), channel_id=1, source_target_pairs={{0,56},{8,0},{16,8},{24,16},{32,24},{40,32},{48,40},{56,48},{1,57}... | collective-permute-start | bytes 1179656 | tf_op jit(solution)/shard_map/ppermute | solution.py:36
  81.8 0.8 slice.150
  82.7 0.8 slice.151
  83.5 2.9 %collective-permute-start.23 = (bf16[8,8,3072]{2,1,0:T(8,128)(2,1)}, bf16[8,8,3072]{2,1,0:T(8,128)(2,1)}, u32[]{:S(2)}, u32[]{:S(2)}) collective-permute-start(bf16[8,8,3072]{2,1,0:T(8,128)(2,1)} %slice.151), channel_id=1, source_target_pairs={{0,192},{64,0},{128,64},{192,128},{1,193},{65,1},{129,65},{193,129... | collective-permute-start | bytes 1179656 | tf_op jit(solution)/shard_map/ppermute | solution.py:36
  86.5 9.0 %collective-permute-done.8.refs_5_ = bf16[4,16,3072]{2,1,0:T(8,128)(2,1)} collective-permute-done((bf16[4,16,3072]{2,1,0:T(8,128)(2,1)}, bf16[4,16,3072]{2,1,0:T(8,128)(2,1)}, u32[]{:S(2)}, u32[]{:S(2)}) %collective-permute-start.8) | collective-permute-done | bytes 393248 | tf_op jit(solution)/shard_map/ppermute | solution.py:36
  95.5 0.9 slice.145
  96.6 0.9 slice.146
  97.5 2.7 %collective-permute-start.11 = (bf16[4,8,3072]{2,1,0:T(8,128)(2,1)S(1)}, bf16[4,8,3072]{2,1,0:T(8,128)(2,1)S(1)}, u32[]{:S(2)}, u32[]{:S(2)}) collective-permute-start(bf16[4,8,3072]{2,1,0:T(8,128)(2,1)S(1)} %slice.146), channel_id=1, source_target_pairs={{0,56},{8,0},{16,8},{24,16},{32,24},{40,32},{48,40},{56,48},{1,57}... | collective-permute-start | bytes 589832 | tf_op jit(solution)/shard_map/ppermute | solution.py:36
  100.3 3.4 %collective-permute-done.22.refs_12_ = bf16[8,8,3072]{2,1,0:T(8,128)(2,1)} collective-permute-done((bf16[8,8,3072]{2,1,0:T(8,128)(2,1)}, bf16[8,8,3072]{2,1,0:T(8,128)(2,1)}, u32[]{:S(2)}, u32[]{:S(2)}) %collective-permute-start.22) | collective-permute-done | bytes 393248 | tf_op jit(solution)/shard_map/ppermute | solution.py:36
  104.1 2.2 collective-permute-done.10.refs_7_
  106.3 2.4 collective-permute-done.11.refs_8_
  108.7 1.0 copy-done.7
  109.7 1.1 copy-done.9
  110.9 1.2 copy-done.11
  112.0 1.4 copy-done.12
  113.5 1.4 copy-done.13
  114.9 1.0 copy-done.21
  115.9 1.0 copy-done.23
  116.9 11.0 %forward.1 = (bf16[4,8,32,3072]{3,2,1,0:T(8,128)(2,1)}, f32[1024,256]{1,0:T(8,128)S(1)}, f32[1024,256]{1,0:T(8,128)S(1)}, bf16[1024,256]{1,0:T(8,128)(2,1)S(1)},...) custom-call(s32[12]{0:T(128)S(1)} %pad_add_fusion.where_ref, bf16[4,16,3072]{2,1,0:T(8,128)(2,1)S(1)} %copy-done.7, ...), custom_call_target="tpu_custom_call" | custom-call | flops 4831838208 | bytes 20971520 | tf_op jit(solution)/shard_map/forward/pallas_call | solution.py:155
  128.0 1.0 copy-done.4
  128.9 1.7 all-gather.2.cloned.1.call-done.y_ref.id_ref
  130.7 1.4 slice_bitcast_fusion.1
  132.0 3.4 %collective-permute-start.25 = (bf16[2,32,1536]{2,1,0:T(8,128)(2,1)S(1)}, bf16[2,32,1536]{2,1,0:T(8,128)(2,1)S(1)}, u32[]{:S(2)}, u32[]{:S(2)}) collective-permute-start(bf16[2,32,1536]{2,1,0:T(8,128)(2,1)S(1)} %get-tuple-element.72), channel_id=1, source_target_pairs={{0,56},{8,0},{16,8},{24,16},{32,24},{40,32},{48,40},{56,48},{1,57}... | collective-permute-start | bytes 589832 | tf_op jit(solution)/shard_map/ppermute | solution.py:36
  135.4 2.7 %collective-permute-done.25 = bf16[2,32,1536]{2,1,0:T(8,128)(2,1)S(1)} collective-permute-done((bf16[2,32,1536]{2,1,0:T(8,128)(2,1)S(1)}, bf16[2,32,1536]{2,1,0:T(8,128)(2,1)S(1)}, u32[]{:S(2)}, u32[]{:S(2)}) %collective-permute-start.25) | collective-permute-done | bytes 196640 | tf_op jit(solution)/shard_map/ppermute | solution.py:36
  138.1 3.1 %collective-permute-done.24 = bf16[2,32,1536]{2,1,0:T(8,128)(2,1)S(1)} collective-permute-done((bf16[2,32,1536]{2,1,0:T(8,128)(2,1)S(1)}, bf16[2,32,1536]{2,1,0:T(8,128)(2,1)S(1)}, u32[]{:S(2)}, u32[]{:S(2)}) %collective-permute-start.24) | collective-permute-done | bytes 196640 | tf_op jit(solution)/shard_map/ppermute | solution.py:36
  141.2 1.2 fusion.5
  142.3 1.0 pad_maximum_fusion.2
  143.3 2.8 %copy-done.1 = bf16[4,8,32,3072]{3,2,1,0:T(8,128)(2,1)S(1)} copy-done((bf16[4,8,32,3072]{3,2,1,0:T(8,128)(2,1)S(1)}, bf16[4,8,32,3072]{3,2,1,0:T(8,128)(2,1)}, u32[]{:S(2)}) %copy-start.1) | copy-done | bytes 6291480
  146.1 9.0 %backward.1 = (bf16[1024,256]{1,0:T(8,128)(2,1)S(1)}, bf16[1024,256]{1,0:T(8,128)(2,1)S(1)}, f32[1024,1]{1,0:T(8,128)S(1)}, f32[2,128]{1,0:T(2,128)S(1)}) custom-call(s32[12]{0:T(128)S(1)} %pad_add_fusion.where_ref, bf16[32,32,3200]{2,1,0:T(8,128)(2,1)} %all-gather.2.cloned.1.call-done.y_ref.id_ref, ...), custom_call_target="tpu_custom_call" | custom-call | flops 4026531840 | bytes 20971520 | tf_op jit(solution)/shard_map/backward/pallas_call | solution.py:231
  157.5 1.5 collective-permute-start.26
  159.0 16.9 %all_to_all.21 = f32[32,2,128]{2,1,0:T(2,128)S(1)} all-to-all(f32[32,2,128]{2,1,0:T(2,128)S(1)} %broadcast_in_dim.12), channel_id=1, replica_groups=mesh['x'=4,'z'=8,'y'=4,'c'=2] {'x','z'}, dimensions={0} | all-to-all | bytes 65536 | tf_op jit(solution)/shard_map/all_to_all | solution.py:89
  175.9 1.4 fusion.3
  177.6 1.3 collective-permute-start.28
  178.8 26.3 %all_to_all.22 = f32[8,2,128]{2,1,0:T(2,128)S(1)} all-to-all(f32[8,2,128]{2,1,0:T(2,128)S(1)} %broadcast_in_dim.13), channel_id=1, replica_groups=mesh['x'=4,'z'=8,'y'=4,'c'=2] {'y','c'}, dimensions={0} | all-to-all | bytes 16384 | tf_op jit(solution)/shard_map/all_to_all | solution.py:89
  205.2 1.5 fusion.1
  206.7 2.5 convert_element_type.167
  209.6 2.3 collective-permute-start.31
  212.0 2.8 %copy-done.2 = bf16[4,8,32,3072]{3,2,1,0:T(8,128)(2,1)S(1)} copy-done((bf16[4,8,32,3072]{3,2,1,0:T(8,128)(2,1)S(1)}, bf16[4,8,32,3072]{3,2,1,0:T(8,128)(2,1)}, u32[]{:S(2)}) %copy-start.2) | copy-done | bytes 6291480
  214.8 10.4 %gradients.1 = (bf16[1,3072,256]{2,1,0:T(8,128)(2,1)}, bf16[1,3072,256]{2,1,0:T(8,128)(2,1)}, bf16[1,256,3072]{2,1,0:T(8,128)(2,1)}) custom-call(s32[12]{0:T(128)S(1)} %pad_add_fusion.where_ref, bf16[4,8,32,3072]{3,2,1,0:T(8,128)(2,1)S(1)} %copy-done.2, bf16[32,32,3200]{2,1,0:T(8,128)(2,1)} %all-gather.2.cloned.1.call-done.y_ref.id_ref, ...), custom_call_target="tpu_custom_call" | custom-call | flops 4831838208 | bytes 18874368 | tf_op jit(solution)/shard_map/gradients/pallas_call | solution.py:293
  225.2 1.2 fusion
  226.4 1.1 collective-permute-start.34
  228.0 2.2 collective-permute-start.32
  230.2 1.4 collective-permute-done.34
  231.5 1.6 collective-permute-done.33
  233.2 8.6 %reduce-scatter.5.cloned.1.call-done = f32[32,1536]{1,0:T(8,128)} async-done(((f32[256,1536]{1,0:T(8,128)}), f32[32,1536]{1,0:T(8,128)}) %reduce-scatter.5.cloned.1.call-update) | async-done | bytes 196624 | tf_op jit(solution)/shard_map/reduce_scatter | solution.py:385
  241.8 0.9 convert_element_type.179
  243.5 8.0 %all-to-all-start.3 = ((bf16[8,4,3072]{2,1,0:T(4,128)(2,1)}), bf16[8,4,3072]{2,1,0:T(4,128)(2,1)S(1)}, u32[]{:S(2)}, u32[]{:S(2)}) async-start(bf16[8,4,3072]{2,1,0:T(4,128)(2,1)} %reshape.86), calls=%async_computation.5 | async-start | bytes 393216 | tf_op jit(solution)/shard_map/all_to_all | solution.py:388
  252.1 5.3 %all-to-all-done.3 = bf16[8,4,3072]{2,1,0:T(4,128)(2,1)S(1)} async-done(((bf16[8,4,3072]{2,1,0:T(4,128)(2,1)}), bf16[8,4,3072]{2,1,0:T(4,128)(2,1)S(1)}, u32[]{:S(2)}, u32[]{:S(2)}) %all-to-all-start.3) | async-done | bytes 196640 | tf_op jit(solution)/shard_map/all_to_all | solution.py:388
  257.5 0.8 convolution_convert_fusion.2
  (144 shorter events, 19.9 us)
Async XLA Ops:
  7.2 3.0 %copy-start = (bf16[12,3072]{1,0:T(8,128)(2,1)S(1)}, bf16[12,3072]{1,0:T(8,128)(2,1)}, u32[]{:S(2)}) copy-start(bf16[12,3072]{1,0:T(8,128)(2,1)} %param.9) | copy-start | bytes 221188
  7.2 123.4 %all-gather.2.cloned.1.call-start = ((), (), s32[]{:S(2)}) async-start(), calls=%async_computation.6 | async-start | bytes 6758400 | tf_op jit(solution)/shard_map/all_gather | solution.py:356
  26.1 60.3 %copy-start.25 = (s32[8]{0:T(128)S(1)}, s32[8]{0:T(128)}, u32[]{:S(2)}) copy-start(s32[8]{0:T(128)} %constant.61.clone) | copy-start | bytes 100
  26.9 179.8 %reduce-scatter.3.cloned.1.call-start = ((), (), s32[]{:S(2)}) async-start(), calls=%async_computation.7 | async-start | bytes 3932160 | tf_op jit(solution)/shard_map/reduce_scatter | solution.py:363
  27.0 73.2 %copy-start.24 = (s32[4]{0:T(128)S(1)}, s32[4]{0:T(128)}, u32[]{:S(2)}) copy-start(s32[4]{0:T(128)} %constant.60.clone) | copy-start | bytes 52
  27.1 81.7 %copy-start.3 = (bf16[1,256,3072]{2,1,0:T(8,128)(2,1)S(1)}, bf16[1,256,3072]{2,1,0:T(8,128)(2,1)}, u32[]{:S(2)}) copy-start(bf16[1,256,3072]{2,1,0:T(8,128)(2,1)} %wd_ref.1) | copy-start | bytes 4718596
  27.1 9.0 %collective-permute-start.1 = (bf16[16,3072]{1,0:T(8,128)(2,1)S(1)}, bf16[16,3072]{1,0:T(8,128)(2,1)S(1)}, u32[]{:S(2)}, u32[]{:S(2)}) collective-permute-start(bf16[16,3072]{1,0:T(8,128)(2,1)S(1)} %slice.111), channel_id=1, source_target_pairs={{0,192},{64,0},{128,64},{192,128},{1,193},{65,1},{129,65},{193,129... | collective-permute-start | bytes 294920 | tf_op jit(solution)/shard_map/ppermute | solution.py:36
  29.7 9.3 %collective-permute-start = (bf16[16,3072]{1,0:T(8,128)(2,1)S(1)}, bf16[16,3072]{1,0:T(8,128)(2,1)S(1)}, u32[]{:S(2)}, u32[]{:S(2)}) collective-permute-start(bf16[16,3072]{1,0:T(8,128)(2,1)S(1)} %slice.111), channel_id=1, source_target_pairs={{0,64},{64,128},{128,192},{192,0},{1,65},{65,129},{129,193},{193,1... | collective-permute-start | bytes 294920 | tf_op jit(solution)/shard_map/ppermute | solution.py:36
  29.7 9.3 %collective-permute-start.12 = (bf16[16,3072]{1,0:T(8,128)(2,1)S(1)}, bf16[16,3072]{1,0:T(8,128)(2,1)S(1)}, u32[]{:S(2)}, u32[]{:S(2)}) collective-permute-start(bf16[16,3072]{1,0:T(8,128)(2,1)S(1)} %slice.117), channel_id=1, source_target_pairs={{0,8},{8,16},{16,24},{24,32},{32,40},{40,48},{48,56},{56,0},{1,9},... | collective-permute-start | bytes 294920 | tf_op jit(solution)/shard_map/ppermute | solution.py:36
  31.4 7.7 %collective-permute-start.13 = (bf16[16,3072]{1,0:T(8,128)(2,1)S(1)}, bf16[16,3072]{1,0:T(8,128)(2,1)S(1)}, u32[]{:S(2)}, u32[]{:S(2)}) collective-permute-start(bf16[16,3072]{1,0:T(8,128)(2,1)S(1)} %slice.117), channel_id=1, source_target_pairs={{0,56},{8,0},{16,8},{24,16},{32,24},{40,32},{48,40},{56,48},{1,57}... | collective-permute-start | bytes 294920 | tf_op jit(solution)/shard_map/ppermute | solution.py:36
  36.2 6.9 %collective-permute-start.3 = (bf16[8,3072]{1,0:T(8,128)(2,1)S(1)}, bf16[8,3072]{1,0:T(8,128)(2,1)S(1)}, u32[]{:S(2)}, u32[]{:S(2)}) collective-permute-start(bf16[8,3072]{1,0:T(8,128)(2,1)S(1)} %slice.144), channel_id=1, source_target_pairs={{0,192},{64,0},{128,64},{192,128},{1,193},{65,1},{129,65},{193,129... | collective-permute-start | bytes 147464 | tf_op jit(solution)/shard_map/ppermute | solution.py:36
  38.9 4.2 %collective-permute-start.2 = (bf16[8,3072]{1,0:T(8,128)(2,1)S(1)}, bf16[8,3072]{1,0:T(8,128)(2,1)S(1)}, u32[]{:S(2)}, u32[]{:S(2)}) collective-permute-start(bf16[8,3072]{1,0:T(8,128)(2,1)S(1)} %slice.143), channel_id=1, source_target_pairs={{0,64},{64,128},{128,192},{192,0},{1,65},{65,129},{129,193},{193,1... | collective-permute-start | bytes 147464 | tf_op jit(solution)/shard_map/ppermute | solution.py:36
  39.0 7.7 %collective-permute-start.14 = (bf16[16,3072]{1,0:T(8,128)(2,1)S(1)}, bf16[16,3072]{1,0:T(8,128)(2,1)S(1)}, u32[]{:S(2)}, u32[]{:S(2)}) collective-permute-start(bf16[16,3072]{1,0:T(8,128)(2,1)S(1)} %collective-permute-done.12), channel_id=1, source_target_pairs={{0,8},{8,16},{16,24},{24,32},{32,40},{40,48},{48,56},{56,0},{1,9},... | collective-permute-start | bytes 294920 | tf_op jit(solution)/shard_map/ppermute | solution.py:36
  39.1 7.6 %collective-permute-start.15 = (bf16[16,3072]{1,0:T(8,128)(2,1)S(1)}, bf16[16,3072]{1,0:T(8,128)(2,1)S(1)}, u32[]{:S(2)}, u32[]{:S(2)}) collective-permute-start(bf16[16,3072]{1,0:T(8,128)(2,1)S(1)} %collective-permute-done.13), channel_id=1, source_target_pairs={{0,56},{8,0},{16,8},{24,16},{32,24},{40,32},{48,40},{56,48},{1,57}... | collective-permute-start | bytes 294920 | tf_op jit(solution)/shard_map/ppermute | solution.py:36
  43.2 26.5 %collective-permute-start.4 = (bf16[4,16,3072]{2,1,0:T(8,128)(2,1)S(1)}, bf16[4,16,3072]{2,1,0:T(8,128)(2,1)S(1)}, u32[]{:S(2)}, u32[]{:S(2)}) collective-permute-start(bf16[4,16,3072]{2,1,0:T(8,128)(2,1)S(1)} %pad_maximum_fusion.1.refs_0_), channel_id=1, source_target_pairs={{0,8},{8,16},{16,24},{24,32},{32,40},{40,48},{48,56},{56,0},{1,9},... | collective-permute-start | bytes 1179656 | tf_op jit(solution)/shard_map/ppermute | solution.py:36
  43.3 27.2 %collective-permute-start.5 = (bf16[4,16,3072]{2,1,0:T(8,128)(2,1)S(1)}, bf16[4,16,3072]{2,1,0:T(8,128)(2,1)S(1)}, u32[]{:S(2)}, u32[]{:S(2)}) collective-permute-start(bf16[4,16,3072]{2,1,0:T(8,128)(2,1)S(1)} %pad_maximum_fusion.1.refs_0_), channel_id=1, source_target_pairs={{0,56},{8,0},{16,8},{24,16},{32,24},{40,32},{48,40},{56,48},{1,57}... | collective-permute-start | bytes 1179656 | tf_op jit(solution)/shard_map/ppermute | solution.py:36
  46.7 13.5 %collective-permute-start.16 = (bf16[16,3072]{1,0:T(8,128)(2,1)S(1)}, bf16[16,3072]{1,0:T(8,128)(2,1)S(1)}, u32[]{:S(2)}, u32[]{:S(2)}) collective-permute-start(bf16[16,3072]{1,0:T(8,128)(2,1)S(1)} %collective-permute-done.14), channel_id=1, source_target_pairs={{0,8},{8,16},{16,24},{24,32},{32,40},{40,48},{48,56},{56,0},{1,9},... | collective-permute-start | bytes 294920 | tf_op jit(solution)/shard_map/ppermute | solution.py:36
  46.7 9.9 %collective-permute-start.17 = (bf16[16,3072]{1,0:T(8,128)(2,1)S(1)}, bf16[16,3072]{1,0:T(8,128)(2,1)S(1)}, u32[]{:S(2)}, u32[]{:S(2)}) collective-permute-start(bf16[16,3072]{1,0:T(8,128)(2,1)S(1)} %collective-permute-done.15), channel_id=1, source_target_pairs={{0,56},{8,0},{16,8},{24,16},{32,24},{40,32},{48,40},{56,48},{1,57}... | collective-permute-start | bytes 294920 | tf_op jit(solution)/shard_map/ppermute | solution.py:36
  56.6 5.6 %collective-permute-start.19 = (bf16[8,3072]{1,0:T(8,128)(2,1)S(1)}, bf16[8,3072]{1,0:T(8,128)(2,1)S(1)}, u32[]{:S(2)}, u32[]{:S(2)}) collective-permute-start(bf16[8,3072]{1,0:T(8,128)(2,1)S(1)} %slice.149), channel_id=1, source_target_pairs={{0,56},{8,0},{16,8},{24,16},{32,24},{40,32},{48,40},{56,48},{1,57}... | collective-permute-start | bytes 147464 | tf_op jit(solution)/shard_map/ppermute | solution.py:36
  60.2 4.7 %collective-permute-start.18 = (bf16[8,3072]{1,0:T(8,128)(2,1)S(1)}, bf16[8,3072]{1,0:T(8,128)(2,1)S(1)}, u32[]{:S(2)}, u32[]{:S(2)}) collective-permute-start(bf16[8,3072]{1,0:T(8,128)(2,1)S(1)} %slice.148), channel_id=1, source_target_pairs={{0,8},{8,16},{16,24},{24,32},{32,40},{40,48},{48,56},{56,0},{1,9},... | collective-permute-start | bytes 147464 | tf_op jit(solution)/shard_map/ppermute | solution.py:36
  65.5 16.3 %collective-permute-start.20 = (bf16[8,16,3072]{2,1,0:T(8,128)(2,1)}, bf16[8,16,3072]{2,1,0:T(8,128)(2,1)S(1)}, u32[]{:S(2)}, u32[]{:S(2)}) collective-permute-start(bf16[8,16,3072]{2,1,0:T(8,128)(2,1)} %fusion.10.refs_9_), channel_id=1, source_target_pairs={{0,64},{64,128},{128,192},{192,0},{1,65},{65,129},{129,193},{193,1... | collective-permute-start | bytes 2359304 | tf_op jit(solution)/shard_map/ppermute | solution.py:36
  65.5 17.2 %collective-permute-start.21 = (bf16[8,16,3072]{2,1,0:T(8,128)(2,1)}, bf16[8,16,3072]{2,1,0:T(8,128)(2,1)S(1)}, u32[]{:S(2)}, u32[]{:S(2)}) collective-permute-start(bf16[8,16,3072]{2,1,0:T(8,128)(2,1)} %fusion.10.refs_9_), channel_id=1, source_target_pairs={{0,192},{64,0},{128,64},{192,128},{1,193},{65,1},{129,65},{193,129... | collective-permute-start | bytes 2359304 | tf_op jit(solution)/shard_map/ppermute | solution.py:36
  69.7 8.1 %collective-permute-start.6 = (bf16[4,16,3072]{2,1,0:T(8,128)(2,1)S(1)}, bf16[4,16,3072]{2,1,0:T(8,128)(2,1)}, u32[]{:S(2)}, u32[]{:S(2)}) collective-permute-start(bf16[4,16,3072]{2,1,0:T(8,128)(2,1)S(1)} %collective-permute-done.4.refs_1_), channel_id=1, source_target_pairs={{0,8},{8,16},{16,24},{24,32},{32,40},{40,48},{48,56},{56,0},{1,9},... | collective-permute-start | bytes 1179656 | tf_op jit(solution)/shard_map/ppermute | solution.py:36
  69.7 0.7 copy-start.20
  70.5 7.4 %collective-permute-start.7 = (bf16[4,16,3072]{2,1,0:T(8,128)(2,1)S(1)}, bf16[4,16,3072]{2,1,0:T(8,128)(2,1)}, u32[]{:S(2)}, u32[]{:S(2)}) collective-permute-start(bf16[4,16,3072]{2,1,0:T(8,128)(2,1)S(1)} %collective-permute-done.5.refs_2_), channel_id=1, source_target_pairs={{0,56},{8,0},{16,8},{24,16},{32,24},{40,32},{48,40},{56,48},{1,57}... | collective-permute-start | bytes 1179656 | tf_op jit(solution)/shard_map/ppermute | solution.py:36
  73.1 0.8 copy-start.22
  77.8 17.7 %collective-permute-start.8 = (bf16[4,16,3072]{2,1,0:T(8,128)(2,1)}, bf16[4,16,3072]{2,1,0:T(8,128)(2,1)}, u32[]{:S(2)}, u32[]{:S(2)}) collective-permute-start(bf16[4,16,3072]{2,1,0:T(8,128)(2,1)} %collective-permute-done.6.refs_3_), channel_id=1, source_target_pairs={{0,8},{8,16},{16,24},{24,32},{32,40},{40,48},{48,56},{56,0},{1,9},... | collective-permute-start | bytes 1179656 | tf_op jit(solution)/shard_map/ppermute | solution.py:36
  77.9 18.7 %collective-permute-start.9 = (bf16[4,16,3072]{2,1,0:T(8,128)(2,1)}, bf16[4,16,3072]{2,1,0:T(8,128)(2,1)}, u32[]{:S(2)}, u32[]{:S(2)}) collective-permute-start(bf16[4,16,3072]{2,1,0:T(8,128)(2,1)} %collective-permute-done.7.refs_4_), channel_id=1, source_target_pairs={{0,56},{8,0},{16,8},{24,16},{32,24},{40,32},{48,40},{56,48},{1,57}... | collective-permute-start | bytes 1179656 | tf_op jit(solution)/shard_map/ppermute | solution.py:36
  81.8 24.5 %copy-start.8 = (bf16[8,16,3072]{2,1,0:T(8,128)(2,1)}, bf16[8,16,3072]{2,1,0:T(8,128)(2,1)S(1)}, u32[]{:S(2)}) copy-start(bf16[8,16,3072]{2,1,0:T(8,128)(2,1)S(1)} %collective-permute-done.20.refs_10_) | copy-start | bytes 2359300
  82.7 21.0 %collective-permute-start.22 = (bf16[8,8,3072]{2,1,0:T(8,128)(2,1)}, bf16[8,8,3072]{2,1,0:T(8,128)(2,1)}, u32[]{:S(2)}, u32[]{:S(2)}) collective-permute-start(bf16[8,8,3072]{2,1,0:T(8,128)(2,1)} %slice.150), channel_id=1, source_target_pairs={{0,64},{64,128},{128,192},{192,0},{1,65},{65,129},{129,193},{193,1... | collective-permute-start | bytes 1179656 | tf_op jit(solution)/shard_map/ppermute | solution.py:36
  82.7 23.6 %copy-start.10 = (bf16[8,16,3072]{2,1,0:T(8,128)(2,1)}, bf16[8,16,3072]{2,1,0:T(8,128)(2,1)S(1)}, u32[]{:S(2)}) copy-start(bf16[8,16,3072]{2,1,0:T(8,128)(2,1)S(1)} %collective-permute-done.21.refs_11_) | copy-start | bytes 2359300
  83.5 20.6 %collective-permute-start.23 = (bf16[8,8,3072]{2,1,0:T(8,128)(2,1)}, bf16[8,8,3072]{2,1,0:T(8,128)(2,1)}, u32[]{:S(2)}, u32[]{:S(2)}) collective-permute-start(bf16[8,8,3072]{2,1,0:T(8,128)(2,1)} %slice.151), channel_id=1, source_target_pairs={{0,192},{64,0},{128,64},{192,128},{1,193},{65,1},{129,65},{193,129... | collective-permute-start | bytes 1179656 | tf_op jit(solution)/shard_map/ppermute | solution.py:36
  96.5 9.8 %collective-permute-start.10 = (bf16[4,8,3072]{2,1,0:T(8,128)(2,1)S(1)}, bf16[4,8,3072]{2,1,0:T(8,128)(2,1)S(1)}, u32[]{:S(2)}, u32[]{:S(2)}) collective-permute-start(bf16[4,8,3072]{2,1,0:T(8,128)(2,1)S(1)} %slice.145), channel_id=1, source_target_pairs={{0,8},{8,16},{16,24},{24,32},{32,40},{40,48},{48,56},{56,0},{1,9},... | collective-permute-start | bytes 589832 | tf_op jit(solution)/shard_map/ppermute | solution.py:36
  97.5 11.2 %collective-permute-start.11 = (bf16[4,8,3072]{2,1,0:T(8,128)(2,1)S(1)}, bf16[4,8,3072]{2,1,0:T(8,128)(2,1)S(1)}, u32[]{:S(2)}, u32[]{:S(2)}) collective-permute-start(bf16[4,8,3072]{2,1,0:T(8,128)(2,1)S(1)} %slice.146), channel_id=1, source_target_pairs={{0,56},{8,0},{16,8},{24,16},{32,24},{40,32},{48,40},{56,48},{1,57}... | collective-permute-start | bytes 589832 | tf_op jit(solution)/shard_map/ppermute | solution.py:36
  108.7 1.0 copy-start.7
  109.7 1.1 copy-start.9
  110.9 1.2 copy-start.11
  112.0 1.4 copy-start.12
  113.5 1.4 copy-start.13
  114.9 1.0 copy-start.21
  115.9 1.0 copy-start.23
  127.9 1.0 copy-start.4
  130.6 111.2 %reduce-scatter.5.cloned.1.call-start = ((), (), s32[]{:S(2)}) async-start(), calls=%async_computation.8 | async-start | bytes 1769472 | tf_op jit(solution)/shard_map/reduce_scatter | solution.py:385
  130.7 12.6 %copy-start.5 = (f32[1024,256]{1,0:T(8,128)S(1)}, f32[1024,256]{1,0:T(8,128)}, u32[]{:S(2)}) copy-start(f32[1024,256]{1,0:T(8,128)} %copy-done.4) | copy-start | bytes 3145732
  132.0 6.1 %collective-permute-start.25 = (bf16[2,32,1536]{2,1,0:T(8,128)(2,1)S(1)}, bf16[2,32,1536]{2,1,0:T(8,128)(2,1)S(1)}, u32[]{:S(2)}, u32[]{:S(2)}) collective-permute-start(bf16[2,32,1536]{2,1,0:T(8,128)(2,1)S(1)} %get-tuple-element.72), channel_id=1, source_target_pairs={{0,56},{8,0},{16,8},{24,16},{32,24},{40,32},{48,40},{56,48},{1,57}... | collective-permute-start | bytes 589832 | tf_op jit(solution)/shard_map/ppermute | solution.py:36
  135.4 5.7 %collective-permute-start.24 = (bf16[2,32,1536]{2,1,0:T(8,128)(2,1)S(1)}, bf16[2,32,1536]{2,1,0:T(8,128)(2,1)S(1)}, u32[]{:S(2)}, u32[]{:S(2)}) collective-permute-start(bf16[2,32,1536]{2,1,0:T(8,128)(2,1)S(1)} %get-tuple-element.74), channel_id=1, source_target_pairs={{0,8},{8,16},{16,24},{24,32},{32,40},{40,48},{48,56},{56,0},{1,9},... | collective-permute-start | bytes 589832 | tf_op jit(solution)/shard_map/ppermute | solution.py:36
  143.3 2.8 %copy-start.1 = (bf16[4,8,32,3072]{3,2,1,0:T(8,128)(2,1)S(1)}, bf16[4,8,32,3072]{3,2,1,0:T(8,128)(2,1)}, u32[]{:S(2)}) copy-start(bf16[4,8,32,3072]{3,2,1,0:T(8,128)(2,1)} %get-tuple-element.38.x_ref) | copy-start | bytes 18874372
  155.1 0.8 copy-start.14
  155.9 0.8 copy-start.16
  156.7 0.8 copy-start.18
  157.5 18.4 %collective-permute-start.27 = (bf16[4,32,1536]{2,1,0:T(8,128)(2,1)}, bf16[4,32,1536]{2,1,0:T(8,128)(2,1)S(1)}, u32[]{:S(2)}, u32[]{:S(2)}) collective-permute-start(bf16[4,32,1536]{2,1,0:T(8,128)(2,1)} %get-tuple-element.44), channel_id=1, source_target_pairs={{0,56},{8,0},{16,8},{24,16},{32,24},{40,32},{48,40},{56,48},{1,57}... | collective-permute-start | bytes 1179656 | tf_op jit(solution)/shard_map/ppermute | solution.py:36
  157.5 18.4 %collective-permute-start.26 = (bf16[4,32,1536]{2,1,0:T(8,128)(2,1)}, bf16[4,32,1536]{2,1,0:T(8,128)(2,1)S(1)}, u32[]{:S(2)}, u32[]{:S(2)}) collective-permute-start(bf16[4,32,1536]{2,1,0:T(8,128)(2,1)} %get-tuple-element.43), channel_id=1, source_target_pairs={{0,8},{8,16},{16,24},{24,32},{32,40},{40,48},{48,56},{56,0},{1,9},... | collective-permute-start | bytes 1179656 | tf_op jit(solution)/shard_map/ppermute | solution.py:36
  177.3 27.9 %collective-permute-start.29 = (bf16[4,32,1536]{2,1,0:T(8,128)(2,1)S(1)}, bf16[4,32,1536]{2,1,0:T(8,128)(2,1)S(1)}, u32[]{:S(2)}, u32[]{:S(2)}) collective-permute-start(bf16[4,32,1536]{2,1,0:T(8,128)(2,1)S(1)} %get-tuple-element.47), channel_id=1, source_target_pairs={{0,56},{8,0},{16,8},{24,16},{32,24},{40,32},{48,40},{56,48},{1,57}... | collective-permute-start | bytes 1179656 | tf_op jit(solution)/shard_map/ppermute | solution.py:36
  177.6 27.6 %collective-permute-start.28 = (bf16[4,32,1536]{2,1,0:T(8,128)(2,1)S(1)}, bf16[4,32,1536]{2,1,0:T(8,128)(2,1)}, u32[]{:S(2)}, u32[]{:S(2)}) collective-permute-start(bf16[4,32,1536]{2,1,0:T(8,128)(2,1)S(1)} %get-tuple-element.46), channel_id=1, source_target_pairs={{0,8},{8,16},{16,24},{24,32},{32,40},{40,48},{48,56},{56,0},{1,9},... | collective-permute-start | bytes 1179656 | tf_op jit(solution)/shard_map/ppermute | solution.py:36
  205.1 6.9 %copy-start.15 = (bf16[1024,256]{1,0:T(8,128)(2,1)S(1)}, bf16[1024,256]{1,0:T(8,128)(2,1)}, u32[]{:S(2)}) copy-start(bf16[1024,256]{1,0:T(8,128)(2,1)} %copy-done.14) | copy-start | bytes 1572868
  205.1 6.9 %copy-start.17 = (bf16[1024,256]{1,0:T(8,128)(2,1)S(1)}, bf16[1024,256]{1,0:T(8,128)(2,1)}, u32[]{:S(2)}) copy-start(bf16[1024,256]{1,0:T(8,128)(2,1)} %copy-done.16) | copy-start | bytes 1572868
  205.1 6.9 %copy-start.19 = (f32[1024,1]{1,0:T(8,128)S(1)}, f32[1024,1]{1,0:T(8,128)}, u32[]{:S(2)}) copy-start(f32[1024,1]{1,0:T(8,128)} %copy-done.18) | copy-start | bytes 12292
  209.2 16.0 %collective-permute-start.30 = (bf16[4,32,1536]{2,1,0:T(8,128)(2,1)S(1)}, bf16[4,32,1536]{2,1,0:T(8,128)(2,1)S(1)}, u32[]{:S(2)}, u32[]{:S(2)}) collective-permute-start(bf16[4,32,1536]{2,1,0:T(8,128)(2,1)S(1)} %get-tuple-element.50), channel_id=1, source_target_pairs={{0,8},{8,16},{16,24},{24,32},{32,40},{40,48},{48,56},{56,0},{1,9},... | collective-permute-start | bytes 1179656 | tf_op jit(solution)/shard_map/ppermute | solution.py:36
  209.6 15.6 %collective-permute-start.31 = (bf16[4,32,1536]{2,1,0:T(8,128)(2,1)S(1)}, bf16[4,32,1536]{2,1,0:T(8,128)(2,1)S(1)}, u32[]{:S(2)}, u32[]{:S(2)}) collective-permute-start(bf16[4,32,1536]{2,1,0:T(8,128)(2,1)S(1)} %get-tuple-element.51), channel_id=1, source_target_pairs={{0,56},{8,0},{16,8},{24,16},{32,24},{40,32},{48,40},{56,48},{1,57}... | collective-permute-start | bytes 1179656 | tf_op jit(solution)/shard_map/ppermute | solution.py:36
  212.0 2.8 %copy-start.2 = (bf16[4,8,32,3072]{3,2,1,0:T(8,128)(2,1)S(1)}, bf16[4,8,32,3072]{3,2,1,0:T(8,128)(2,1)}, u32[]{:S(2)}) copy-start(bf16[4,8,32,3072]{3,2,1,0:T(8,128)(2,1)} %get-tuple-element.38.x_ref) | copy-start | bytes 18874372
  226.4 5.1 %collective-permute-start.34 = (bf16[32,1536]{1,0:T(8,128)(2,1)S(1)}, bf16[32,1536]{1,0:T(8,128)(2,1)S(1)}, u32[]{:S(2)}, u32[]{:S(2)}) collective-permute-start(bf16[32,1536]{1,0:T(8,128)(2,1)S(1)} %get-tuple-element.80), channel_id=1, source_target_pairs={{0,128},{64,192},{128,0},{192,64},{1,129},{65,193},{129,1},{193,65... | collective-permute-start | bytes 294920 | tf_op jit(solution)/shard_map/ppermute | solution.py:36
  227.5 5.6 %collective-permute-start.33 = (bf16[32,1536]{1,0:T(8,128)(2,1)S(1)}, bf16[32,1536]{1,0:T(8,128)(2,1)S(1)}, u32[]{:S(2)}, u32[]{:S(2)}) collective-permute-start(bf16[32,1536]{1,0:T(8,128)(2,1)S(1)} %get-tuple-element.81), channel_id=1, source_target_pairs={{0,64},{64,128},{128,192},{192,0},{1,65},{65,129},{129,193},{193,1... | collective-permute-start | bytes 294920 | tf_op jit(solution)/shard_map/ppermute | solution.py:36
  228.0 5.1 %collective-permute-start.32 = (bf16[32,1536]{1,0:T(8,128)(2,1)S(1)}, bf16[32,1536]{1,0:T(8,128)(2,1)S(1)}, u32[]{:S(2)}, u32[]{:S(2)}) collective-permute-start(bf16[32,1536]{1,0:T(8,128)(2,1)S(1)} %get-tuple-element.79), channel_id=1, source_target_pairs={{0,192},{64,0},{128,64},{192,128},{1,193},{65,1},{129,65},{193,129... | collective-permute-start | bytes 294920 | tf_op jit(solution)/shard_map/ppermute | solution.py:36
  243.5 13.9 %all-to-all-start.3 = ((bf16[8,4,3072]{2,1,0:T(4,128)(2,1)}), bf16[8,4,3072]{2,1,0:T(4,128)(2,1)S(1)}, u32[]{:S(2)}, u32[]{:S(2)}) async-start(bf16[8,4,3072]{2,1,0:T(4,128)(2,1)} %reshape.86), calls=%async_computation.5 | async-start | bytes 393216 | tf_op jit(solution)/shard_map/all_to_all | solution.py:388
  (1 other events, 0.7 us)
Sparse Core Ops, SparseCore 0:
  27.0 103.4 all-gather.1
  133.1 51.5 reduce-scatter.2
  209.4 32.4 reduce-scatter.4
where the time goes:
time: 266 us; the launch traced here: 265 us
  starting transfers between devices  60.1 us (23%)
  blocking collectives  57.1 us (21%)
  waiting for transfers between devices  55.5 us (21%)
  local copies, waits for them, and re-layouts  32.7 us (12%)
  Pallas kernels  30.4 us (11%)
  between operations  14.2 us (5%)
  other arithmetic  12.7 us (5%)
    ppermute x35, starting transfers between devices, shift(): return lax.ppermute(a, axis, [(i, (i + step) % n) for i in range(n)])  52 us
    all_to_all x2, blocking collectives, spread(): lax.all_to_all(jnp.broadcast_to(a[None], (n,) + a.shape), axes, 0, 0, til...  43.1 us
    ppermute x35, waiting for transfers between devices, shift(): return lax.ppermute(a, axis, [(i, (i + step) % n) for i in range(n)])  39.8 us
    unnamed x60, local copies, waits for them, and re-layouts  24.7 us
    all_to_all x1, blocking collectives, on_device(): got = lax.all_to_all(send, EXPERT, split_axis=0, concat_axis=0, tiled=True)  14 us
    pallas_call x1, Pallas kernels, forward(): pl.pallas_call(forward_kernel, grid_spec=pltpu.PrefetchScalarGridSpec(num...  11 us
    pallas_call x1, Pallas kernels, gradients(): pl.pallas_call(grads_kernel, grid_spec=pltpu.PrefetchScalarGridSpec(num_s...  10.4 us
    pallas_call x1, Pallas kernels, backward(): pl.pallas_call(backward_kernel, grid_spec=pltpu.PrefetchScalarGridSpec(nu...  9.01 us
  transfers between devices with their start and end apart: 39, of which 18 were waited for; matrix products, arithmetic and copies ran while one was open for 7% of the time, Pallas kernels for 11%

commit v1 on v0

--- a/solution.py
+++ b/solution.py
@@ -55,26 +55,25 @@
     return (a.astype(F32) + b.astype(F32)).astype(BF)
 
 
-def ring_sum(parts, axis, hook):
+def ring_sum(far_up, far_down, parts, axis, hook):
     half = SIZE[axis] // 2
     place = ORDER[axis].index
 
     def get(k):
         return parts[place(k)]
 
-    far = get(half)
-    mid = far.shape[0] // 2
-    up, down = shift(far[:mid], axis, 1), shift(far[mid:], axis, -1)
-    own_up, own_down = get(half - 1), get(1 - half)
+    mid = far_up.shape[0]
+    up, down = shift(far_up, axis, 1), shift(far_down, axis, -1)
+    own_up, own_down = hook(1, (get(half - 1), get(1 - half)))
     up = jnp.concatenate([plus(up, own_up[:mid]), own_up[mid:]], axis=0)
     down = jnp.concatenate([own_down[:mid], plus(down, own_down[mid:])], axis=0)
     for k in range(half - 1, 0, -1):
-        up, down = hook(half - k, (up, down))
         up, down = shift(up, axis, 1), shift(down, axis, -1)
         if k > 1:
-            up, down = plus(up, get(k - 1)), plus(down, get(1 - k))
-    up, down = hook(half, (up, down))
-    return (up.astype(F32) + down.astype(F32) + get(0).astype(F32)).astype(BF)
+            own_up, own_down = hook(half - k + 1, (get(k - 1), get(1 - k)))
+            up, down = plus(up, own_up), plus(down, own_down)
+    own = hook(half, get(0))
+    return (up.astype(F32) + down.astype(F32) + own.astype(F32)).astype(BF)
 
 
 def direct_sum(parts, axis):
@@ -96,7 +95,7 @@
 def forward_kernel(where_ref, *refs):
     a_refs, refs = refs[: NZ + 1], refs[NZ + 1 :]
     b_refs, refs = refs[: NX + 1], refs[NX + 1 :]
-    wg_ref, wu_ref, wd_ref, x_out, gate_ref, up_ref, hidden_ref, left_ref, right_ref, rows_ref, in_sems, out_sems = refs
+    wg_ref, wu_ref, wd_ref, x_out, gate_ref, up_ref, hidden_ref, far_up, far_down, left_ref, right_ref, rows_ref, in_sems, out_sems = refs
     step = pl.program_id(0)
     quarter = MID // 2
     arrivals = []
@@ -132,7 +131,16 @@
     up_ref[...] = up
     hidden_ref[...] = hidden
     out = dot(hidden, wd_ref[0, :, :LEFT], ((1,), (0,))).astype(BF)
-    left_ref[...] = out.reshape(NZ, 1, SLOTS, LEFT)
+    left_ref[...] = out[: TILE - SLOTS].reshape(NZ - 1, 1, SLOTS, LEFT)
+
+    @pl.when(step < NX // 2)
+    def _():
+        far_up[0] = out[TILE - SLOTS :]
+
+    @pl.when(step >= NX // 2)
+    def _():
+        far_down[0] = out[TILE - SLOTS :]
+
     out = dot(hidden, wd_ref[0, :, LEFT:], ((1,), (0,))).astype(BF)
     for j in range(NZ):
         right_ref[0, where_ref[NX + j]] = out[j * SLOTS : (j + 1) * SLOTS]
@@ -163,7 +171,9 @@
                 tall(HID),
                 tall(HID),
                 tall(HID),
-                pl.BlockSpec((NZ, 1, SLOTS, LEFT), lambda i, where: (0, i, 0, 0)),
+                pl.BlockSpec((1, SLOTS, LEFT), lambda i, where: (jnp.minimum(i, NX // 2 - 1), 0, 0)),
+                pl.BlockSpec((1, SLOTS, LEFT), lambda i, where: (jnp.maximum(i - NX // 2, 0), 0, 0)),
+                pl.BlockSpec((NZ - 1, 1, SLOTS, LEFT), lambda i, where: (0, i, 0, 0)),
                 pl.BlockSpec((1, NZ, SLOTS, D - LEFT), lambda i, where: (where[i], 0, 0, 0)),
             ],
             scratch_shapes=[
@@ -177,10 +187,12 @@
             jax.ShapeDtypeStruct((ROWS, HID), F32),
             jax.ShapeDtypeStruct((ROWS, HID), F32),
             jax.ShapeDtypeStruct((ROWS, HID), BF),
-            jax.ShapeDtypeStruct((NZ, NX, SLOTS, LEFT), BF),
+            jax.ShapeDtypeStruct((NX // 2, SLOTS, LEFT), BF),
+            jax.ShapeDtypeStruct((NX // 2, SLOTS, LEFT), BF),
+            jax.ShapeDtypeStruct((NZ - 1, NX, SLOTS, LEFT), BF),
             jax.ShapeDtypeStruct((NX, NZ, SLOTS, D - LEFT), BF),
         ],
-        compiler_params=pltpu.CompilerParams(vmem_limit_bytes=40 * MIB),
+        compiler_params=pltpu.CompilerParams(vmem_limit_bytes=60 * MIB),
         cost_estimate=pl.CostEstimate(flops=6 * ROWS * D * HID, bytes_accessed=20 * MIB, transcendentals=ROWS * HID),
         name="forward",
     )(where, *a_pieces, *b_pieces, w_gate, w_up, w_down)
@@ -251,7 +263,7 @@
             jax.ShapeDtypeStruct((ROWS, 1), F32),
             jax.ShapeDtypeStruct((2, LANES), F32),
         ],
-        compiler_params=pltpu.CompilerParams(vmem_limit_bytes=40 * MIB),
+        compiler_params=pltpu.CompilerParams(vmem_limit_bytes=60 * MIB),
         cost_estimate=pl.CostEstimate(flops=5 * ROWS * D * HID, bytes_accessed=20 * MIB, transcendentals=ROWS * HID),
         name="backward",
     )(where, wide_y, wide_y, x, w_down, gate, up, hidden)
@@ -321,7 +333,7 @@
             jax.ShapeDtypeStruct((1, D, HID), BF),
             jax.ShapeDtypeStruct((1, HID, D), BF),
         ],
-        compiler_params=pltpu.CompilerParams(vmem_limit_bytes=40 * MIB),
+        compiler_params=pltpu.CompilerParams(vmem_limit_bytes=60 * MIB),
         cost_estimate=pl.CostEstimate(flops=6 * ROWS * D * HID, bytes_accessed=18 * MIB, transcendentals=0),
         name="gradients",
     )(where, x, wide_y, hidden, d_gate, d_up, spot, factors)
@@ -358,31 +370,33 @@
     line_z = line_of(ring_gather(local_x[MID:], "z"))
     a_pieces = ring_gather(line_x, "z")
     b_pieces = ring_gather(line_z, "x")
-    x, gate, up_part, hidden, left, right = forward(where, a_pieces, b_pieces, w_gate, w_up, w_down)
+    x, gate, up_part, hidden, far_up, far_down, left, right = forward(
+        where, a_pieces, b_pieces, w_gate, w_up, w_down
+    )
     right, wide_y = lax.optimization_barrier((right, wide_y))
     right_line = lax.psum_scatter(right.reshape(ROWS, D - LEFT), "x", scatter_dimension=0, tiled=True)
     kept = {}
 
-    def hook(step, pair):
+    def hook(step, sent):
         if step == 1:
             kept["back"] = backward(where, wide_y, x, w_down, gate, up_part, hidden)
-            pair, kept["sum"] = lax.optimization_barrier((pair, kept["back"][3]))
+            sent, kept["sum"] = lax.optimization_barrier((sent, kept["back"][3]))
         elif step == 2:
             total = jnp.sum(spread(kept["sum"], ("x", "z"), BLOCKS).reshape(BLOCKS, 2, LANES), axis=0)
-            pair, kept["sum"] = lax.optimization_barrier((pair, total))
+            sent, kept["sum"], line = lax.optimization_barrier((sent, total, right_line))
+            kept["line"] = lax.psum_scatter(line.astype(F32), "z", scatter_dimension=0, tiled=True)
         elif step == 3:
             total = jnp.sum(spread(kept["sum"], EXPERT, NE).reshape(NE, 2, LANES), axis=0)
-            pair, norms, line = lax.optimization_barrier((pair, jnp.sqrt(total), right_line.astype(F32)))
-            kept["norms"], kept["line"] = norms, line
+            sent, kept["norms"] = lax.optimization_barrier((sent, jnp.sqrt(total)))
         else:
             d_gate, d_up, spot, _ = kept["back"]
             factors = RADIUS / (kept["norms"] + GAMMA)
             grads = gradients(where, x, wide_y, hidden, d_gate, d_up, spot, factors)
-            pair, kept["grads"] = lax.optimization_barrier((pair, grads))
-        return pair
-
-    left_line = ring_sum(left, "z", hook)
-    right_out = lax.psum_scatter(kept["line"], "z", scatter_dimension=0, tiled=True).astype(BF)
+            sent, kept["grads"] = lax.optimization_barrier((sent, grads))
+        return sent
+
+    left_line = ring_sum(far_up, far_down, left, "z", hook)
+    right_out = kept["line"].astype(BF)
     left_out = direct_sum(left_line, "x")
     own_out = jnp.concatenate([left_out, right_out], axis=1)
     returned = lax.all_to_all(own_out.reshape(NE, CAP, width), EXPERT, split_axis=0, concat_axis=0, tiled=True)

time: 266 us -> 244 us (0.917)
  blocking collectives: 57.1 us -> 14 us
  waiting for transfers between devices: 55.5 us -> 79.9 us
  local copies, waits for them, and re-layouts: 32.7 us -> 14.4 us
  starting transfers between devices: 60.1 us -> 73.5 us
  Pallas kernels: 30.4 us -> 37.5 us
  other arithmetic: 12.7 us -> 7.62 us
    all_to_all x2 -> x0, blocking collectives: 43.1 us -> none  [spread(): lax.all_to_all(jnp.broadcast_to(a[None], (n,) + a.shape), axes, 0, 0, til...]
    unnamed x60 -> x42, local copies, waits for them, and re-layouts: 24.7 us -> 6.06 us
    reduce_scatter x1, waiting for transfers between devices: 0.02 us -> 12 us  [on_device(): lax.psum_scatter(right.reshape(ROWS, D - LEFT), 'x', scatter_dimension=0,...]
    all_to_all x0 -> x2, starting transfers between devices: none -> 11.7 us  [spread(): lax.all_to_all(jnp.broadcast_to(a[None], (n,) + a.shape), axes, 0, 0, til...]
    ppermute x35, waiting for transfers between devices: 39.8 us -> 50 us  [shift(): return lax.ppermute(a, axis, [(i, (i + step) % n) for i in range(n)])]
    reduce_scatter x1, waiting for transfers between devices: 8.62 us -> 0.02 us  [hook(): lax.psum_scatter(line.astype(F32), 'z', scatter_dimension=0, tiled=True)]
    all_gather x1, waiting for transfers between devices: 1.66 us -> 7.41 us  [on_device(): wide_y = lax.all_gather(local_dy, ('x', 'z'), axis=0)]
    all_to_all x0 -> x2, waiting for transfers between devices: none -> 5.16 us  [spread(): lax.all_to_all(jnp.broadcast_to(a[None], (n,) + a.shape), axes, 0, 0, til...]
  transfers between devices with their start and end apart: 39 -> 41, of which waited for: 18 -> 20; matrix products, arithmetic and copies ran while one was open for 7% -> 6% of each run, Pallas kernels for 11% -> 15%
where the time goes in v1:
time: 244 us; the launch traced here: 243 us
  waiting for transfers between devices  79.9 us (33%)
  starting transfers between devices  73.5 us (30%)
  Pallas kernels  37.5 us (15%)
  local copies, waits for them, and re-layouts  14.4 us (6%)
  between operations  14.3 us (6%)
  blocking collectives  14 us (6%)
  other arithmetic  7.62 us (3%)
    ppermute x35, starting transfers between devices, shift(): return lax.ppermute(a, axis, [(i, (i + step) % n) for i in range(n)])  54.9 us
    ppermute x35, waiting for transfers between devices, shift(): return lax.ppermute(a, axis, [(i, (i + step) % n) for i in range(n)])  50 us
    all_to_all x1, blocking collectives, on_device(): got = lax.all_to_all(send, EXPERT, split_axis=0, concat_axis=0, tiled=True)  14 us
    pallas_call x1, Pallas kernels, forward(): pl.pallas_call(forward_kernel, grid_spec=pltpu.PrefetchScalarGridSpec(num...  13.7 us
    pallas_call x1, Pallas kernels, gradients(): pl.pallas_call(grads_kernel, grid_spec=pltpu.PrefetchScalarGridSpec(num_s...  12.1 us
    reduce_scatter x1, waiting for transfers between devices, on_device(): lax.psum_scatter(right.reshape(ROWS, D - LEFT), 'x', scatter_dimension=0,...  12 us
    pallas_call x1, Pallas kernels, backward(): pl.pallas_call(backward_kernel, grid_spec=pltpu.PrefetchScalarGridSpec(nu...  11.7 us
    all_to_all x2, starting transfers between devices, spread(): lax.all_to_all(jnp.broadcast_to(a[None], (n,) + a.shape), axes, 0, 0, til...  11.7 us
  transfers between devices with their start and end apart: 41, of which 20 were waited for; matrix products, arithmetic and copies ran while one was open for 6% of the time, Pallas kernels for 15%

profile of v1, /device:TPU:1, one launch (start us, length us, event | category | flops | bytes accessed | tf_op | source)
XLA Modules:
  0.0 243.4 jit_solution(7428619319540107266)
XLA Ops:
  7.2 0.8 copy.31
  8.6 0.7 multiply_add_fusion
  9.5 0.7 multiply_reduce_fusion
  10.4 1.1 convolution_convert_fusion
  12.0 14.0 %all_to_all.20 = bf16[8,8,3200]{2,1,0:T(8,128)(2,1)S(1)} all-to-all(bf16[8,8,3200]{2,1,0:T(8,128)(2,1)S(1)} %pad_maximum_fusion), channel_id=1, replica_groups=mesh['x'=4,'z'=8,'y'=4,'c'=2] {'y','c'}, dimensions={0} | all-to-all | bytes 819200 | tf_op jit(solution)/shard_map/all_to_all | solution.py:365
  26.2 0.7 all_gather_reshape.3
  27.1 2.5 %collective-permute-start.1 = (bf16[16,3072]{1,0:T(8,128)(2,1)S(1)}, bf16[16,3072]{1,0:T(8,128)(2,1)S(1)}, u32[]{:S(2)}, u32[]{:S(2)}) collective-permute-start(bf16[16,3072]{1,0:T(8,128)(2,1)S(1)} %slice.88), channel_id=1, source_target_pairs={{0,192},{64,0},{128,64},{192,128},{1,193},{65,1},{129,65},{193,129... | collective-permute-start | bytes 294920 | tf_op jit(solution)/shard_map/ppermute | solution.py:36
  29.7 1.7 collective-permute-start.12
  31.4 4.0 %collective-permute-start.13 = (bf16[16,3072]{1,0:T(8,128)(2,1)S(1)}, bf16[16,3072]{1,0:T(8,128)(2,1)S(1)}, u32[]{:S(2)}, u32[]{:S(2)}) collective-permute-start(bf16[16,3072]{1,0:T(8,128)(2,1)S(1)} %slice.94), channel_id=1, source_target_pairs={{0,56},{8,0},{16,8},{24,16},{32,24},{40,32},{48,40},{56,48},{1,57}... | collective-permute-start | bytes 294920 | tf_op jit(solution)/shard_map/ppermute | solution.py:36
  35.4 0.6 constant_dynamic-update-slice_fusion
  36.1 2.8 %collective-permute-start.3 = (bf16[8,3072]{1,0:T(8,128)(2,1)S(1)}, bf16[8,3072]{1,0:T(8,128)(2,1)S(1)}, u32[]{:S(2)}, u32[]{:S(2)}) collective-permute-start(bf16[8,3072]{1,0:T(8,128)(2,1)S(1)} %slice.117), channel_id=1, source_target_pairs={{0,192},{64,0},{128,64},{192,128},{1,193},{65,1},{129,65},{193,129... | collective-permute-start | bytes 147464 | tf_op jit(solution)/shard_map/ppermute | solution.py:36
  39.1 2.7 %collective-permute-start.15 = (bf16[16,3072]{1,0:T(8,128)(2,1)S(1)}, bf16[16,3072]{1,0:T(8,128)(2,1)S(1)}, u32[]{:S(2)}, u32[]{:S(2)}) collective-permute-start(bf16[16,3072]{1,0:T(8,128)(2,1)S(1)} %collective-permute-done.13), channel_id=1, source_target_pairs={{0,56},{8,0},{16,8},{24,16},{32,24},{40,32},{48,40},{56,48},{1,57}... | collective-permute-start | bytes 294920 | tf_op jit(solution)/shard_map/ppermute | solution.py:36
  41.7 0.6 bitcast_dynamic-update-slice_fusion.5
  42.4 0.6 bitcast_dynamic-update-slice_fusion.4
  43.3 2.7 %collective-permute-start.5 = (bf16[4,16,3072]{2,1,0:T(8,128)(2,1)S(1)}, bf16[4,16,3072]{2,1,0:T(8,128)(2,1)S(1)}, u32[]{:S(2)}, u32[]{:S(2)}) collective-permute-start(bf16[4,16,3072]{2,1,0:T(8,128)(2,1)S(1)} %pad_maximum_fusion.1.refs_0_), channel_id=1, source_target_pairs={{0,56},{8,0},{16,8},{24,16},{32,24},{40,32},{48,40},{56,48},{1,57}... | collective-permute-start | bytes 1179656 | tf_op jit(solution)/shard_map/ppermute | solution.py:36
  46.0 2.7 %collective-permute-start.17 = (bf16[16,3072]{1,0:T(8,128)(2,1)S(1)}, bf16[16,3072]{1,0:T(8,128)(2,1)S(1)}, u32[]{:S(2)}, u32[]{:S(2)}) collective-permute-start(bf16[16,3072]{1,0:T(8,128)(2,1)S(1)} %collective-permute-done.15), channel_id=1, source_target_pairs={{0,56},{8,0},{16,8},{24,16},{32,24},{40,32},{48,40},{56,48},{1,57}... | collective-permute-start | bytes 294920 | tf_op jit(solution)/shard_map/ppermute | solution.py:36
  48.6 0.6 bitcast_dynamic-update-slice_fusion.3
  49.3 0.6 bitcast_dynamic-update-slice_fusion.2
  49.9 6.7 %collective-permute-done.17 = bf16[16,3072]{1,0:T(8,128)(2,1)S(1)} collective-permute-done((bf16[16,3072]{1,0:T(8,128)(2,1)S(1)}, bf16[16,3072]{1,0:T(8,128)(2,1)S(1)}, u32[]{:S(2)}, u32[]{:S(2)}) %collective-permute-start.17) | collective-permute-done | bytes 98336 | tf_op jit(solution)/shard_map/ppermute | solution.py:36
  56.6 3.5 %collective-permute-start.19 = (bf16[8,3072]{1,0:T(8,128)(2,1)S(1)}, bf16[8,3072]{1,0:T(8,128)(2,1)S(1)}, u32[]{:S(2)}, u32[]{:S(2)}) collective-permute-start(bf16[8,3072]{1,0:T(8,128)(2,1)S(1)} %slice.122), channel_id=1, source_target_pairs={{0,56},{8,0},{16,8},{24,16},{32,24},{40,32},{48,40},{56,48},{1,57}... | collective-permute-start | bytes 147464 | tf_op jit(solution)/shard_map/ppermute | solution.py:36
  60.4 0.7 bitcast_dynamic-update-slice_fusion.1
  62.2 2.4 collective-permute-done.18
  64.6 0.6 fusion.3.refs_9_
  65.3 4.2 %collective-permute-start.21 = (bf16[8,16,3072]{2,1,0:T(8,128)(2,1)}, bf16[8,16,3072]{2,1,0:T(8,128)(2,1)S(1)}, u32[]{:S(2)}, u32[]{:S(2)}) collective-permute-start(bf16[8,16,3072]{2,1,0:T(8,128)(2,1)} %fusion.3.refs_9_), channel_id=1, source_target_pairs={{0,192},{64,0},{128,64},{192,128},{1,193},{65,1},{129,65},{193,129... | collective-permute-start | bytes 2359304 | tf_op jit(solution)/shard_map/ppermute | solution.py:36
  69.5 2.7 %collective-permute-start.7 = (bf16[4,16,3072]{2,1,0:T(8,128)(2,1)S(1)}, bf16[4,16,3072]{2,1,0:T(8,128)(2,1)}, u32[]{:S(2)}, u32[]{:S(2)}) collective-permute-start(bf16[4,16,3072]{2,1,0:T(8,128)(2,1)S(1)} %collective-permute-done.5.refs_2_), channel_id=1, source_target_pairs={{0,56},{8,0},{16,8},{24,16},{32,24},{40,32},{48,40},{56,48},{1,57}... | collective-permute-start | bytes 1179656 | tf_op jit(solution)/shard_map/ppermute | solution.py:36
  72.2 5.4 %collective-permute-done.6.refs_3_ = bf16[4,16,3072]{2,1,0:T(8,128)(2,1)} collective-permute-done((bf16[4,16,3072]{2,1,0:T(8,128)(2,1)S(1)}, bf16[4,16,3072]{2,1,0:T(8,128)(2,1)}, u32[]{:S(2)}, u32[]{:S(2)}) %collective-permute-start.6) | collective-permute-done | bytes 393248 | tf_op jit(solution)/shard_map/ppermute | solution.py:36
  77.7 2.7 %collective-permute-start.9 = (bf16[4,16,3072]{2,1,0:T(8,128)(2,1)}, bf16[4,16,3072]{2,1,0:T(8,128)(2,1)}, u32[]{:S(2)}, u32[]{:S(2)}) collective-permute-start(bf16[4,16,3072]{2,1,0:T(8,128)(2,1)} %collective-permute-done.7.refs_4_), channel_id=1, source_target_pairs={{0,56},{8,0},{16,8},{24,16},{32,24},{40,32},{48,40},{56,48},{1,57}... | collective-permute-start | bytes 1179656 | tf_op jit(solution)/shard_map/ppermute | solution.py:36
  80.3 1.1 collective-permute-done.20.refs_10_
  81.7 3.1 %collective-permute-start.23 = (bf16[8,8,3072]{2,1,0:T(8,128)(2,1)S(1)}, bf16[8,8,3072]{2,1,0:T(8,128)(2,1)}, u32[]{:S(2)}, u32[]{:S(2)}) collective-permute-start(bf16[8,8,3072]{2,1,0:T(8,128)(2,1)S(1)} %slice.124), channel_id=1, source_target_pairs={{0,192},{64,0},{128,64},{192,128},{1,193},{65,1},{129,65},{193,129... | collective-permute-start | bytes 1179656 | tf_op jit(solution)/shard_map/ppermute | solution.py:36
  84.8 10.7 %collective-permute-done.8.refs_5_ = bf16[4,16,3072]{2,1,0:T(8,128)(2,1)} collective-permute-done((bf16[4,16,3072]{2,1,0:T(8,128)(2,1)}, bf16[4,16,3072]{2,1,0:T(8,128)(2,1)}, u32[]{:S(2)}, u32[]{:S(2)}) %collective-permute-start.8) | collective-permute-done | bytes 393248 | tf_op jit(solution)/shard_map/ppermute | solution.py:36
  95.5 1.0 slice.118
  96.6 0.9 slice.119
  97.5 2.7 %collective-permute-start.11 = (bf16[4,8,3072]{2,1,0:T(8,128)(2,1)S(1)}, bf16[4,8,3072]{2,1,0:T(8,128)(2,1)S(1)}, u32[]{:S(2)}, u32[]{:S(2)}) collective-permute-start(bf16[4,8,3072]{2,1,0:T(8,128)(2,1)S(1)} %slice.119), channel_id=1, source_target_pairs={{0,56},{8,0},{16,8},{24,16},{32,24},{40,32},{48,40},{56,48},{1,57}... | collective-permute-start | bytes 589832 | tf_op jit(solution)/shard_map/ppermute | solution.py:36
  100.8 1.5 collective-permute-done.22.refs_12_
  102.4 4.5 %collective-permute-done.10.refs_7_ = bf16[4,8,3072]{2,1,0:T(8,128)(2,1)S(1)} collective-permute-done((bf16[4,8,3072]{2,1,0:T(8,128)(2,1)S(1)}, bf16[4,8,3072]{2,1,0:T(8,128)(2,1)S(1)}, u32[]{:S(2)}, u32[]{:S(2)}) %collective-permute-start.10) | collective-permute-done | bytes 196640 | tf_op jit(solution)/shard_map/ppermute | solution.py:36
  106.9 1.9 collective-permute-done.11.refs_8_
  108.8 0.7 copy-done.14
  109.5 13.7 %forward.1 = (bf16[4,8,32,3072]{3,2,1,0:T(8,128)(2,1)}, f32[1024,256]{1,0:T(8,128)}, f32[1024,256]{1,0:T(8,128)}, bf16[1024,256]{1,0:T(8,128)(2,1)}, bf16[2,32,1...) custom-call(s32[12]{0:T(128)} %pad_add_fusion.where_ref, ...), custom_call_target="tpu_custom_call" | custom-call | flops 4831838208 | bytes 20971520 | tf_op jit(solution)/shard_map/forward/pallas_call | solution.py:163
  123.2 7.4 %all-gather.2.cloned.1.call-done.y_ref.id_ref = bf16[32,32,3200]{2,1,0:T(8,128)(2,1)} async-done(((bf16[1,32,3200]{2,1,0:T(8,128)(2,1)}), bf16[32,32,3200]{2,1,0:T(8,128)(2,1)}) %all-gather.2.cloned.1.call-update) | async-done | bytes 6553616 | tf_op jit(solution)/shard_map/all_gather | solution.py:368
  130.6 4.1 %collective-permute-start.28 = (bf16[2,32,1536]{2,1,0:T(8,128)(2,1)}, bf16[2,32,1536]{2,1,0:T(8,128)(2,1)}, u32[]{:S(2)}, u32[]{:S(2)}) collective-permute-start(bf16[2,32,1536]{2,1,0:T(8,128)(2,1)} %get-tuple-element.52), channel_id=1, source_target_pairs={{0,56},{8,0},{16,8},{24,16},{32,24},{40,32},{48,40},{56,48},{1,57}... | collective-permute-start | bytes 589832 | tf_op jit(solution)/shard_map/ppermute | solution.py:36
  134.7 1.4 slice_bitcast_fusion.1
  136.1 11.7 %backward.1 = (bf16[1024,256]{1,0:T(8,128)(2,1)}, bf16[1024,256]{1,0:T(8,128)(2,1)}, f32[1024,1]{1,0:T(8,128)}, f32[2,128]{1,0:T(2,128)}) custom-call(s32[12]{0:T(128)} %pad_add_fusion.where_ref, bf16[32,32,3200]{2,1,0:T(8,128)(2,1)} %all-gather.2.cloned.1.call-done.y_ref.id_ref, bf16[32,32,3200]{2,1,0:T(8,128)(2,1)} %all-gather.2.cloned.1.call-done.y_ref.id_ref, ...), custom_call_target="tpu_custom_call" | custom-call | flops 4026531840 | bytes 20971520 | tf_op jit(solution)/shard_map/backward/pallas_call | solution.py:243
  147.9 1.3 broadcast_in_dim.12
  149.2 6.8 %all-to-all-start.1 = ((f32[32,2,128]{2,1,0:T(2,128)}), f32[32,2,128]{2,1,0:T(2,128)S(1)}, u32[]{:S(2)}, u32[]{:S(2)}) async-start(f32[32,2,128]{2,1,0:T(2,128)} %broadcast_in_dim.12), calls=%async_computation.1 | async-start | bytes 65536 | tf_op jit(solution)/shard_map/all_to_all | solution.py:88
  156.1 1.0 add_convert_fusion.5
  157.1 2.5 %collective-permute-start.29 = (bf16[4,32,1536]{2,1,0:T(8,128)(2,1)S(1)}, bf16[4,32,1536]{2,1,0:T(8,128)(2,1)S(1)}, u32[]{:S(2)}, u32[]{:S(2)}) collective-permute-start(bf16[4,32,1536]{2,1,0:T(8,128)(2,1)S(1)} %pad_maximum_fusion.3), channel_id=1, source_target_pairs={{0,56},{8,0},{16,8},{24,16},{32,24},{40,32},{48,40},{56,48},{1,57}... | collective-permute-start | bytes 1179656 | tf_op jit(solution)/shard_map/ppermute | solution.py:36
  159.9 5.0 %all-to-all-done.1 = f32[32,2,128]{2,1,0:T(2,128)S(1)} async-done(((f32[32,2,128]{2,1,0:T(2,128)}), f32[32,2,128]{2,1,0:T(2,128)S(1)}, u32[]{:S(2)}, u32[]{:S(2)}) %all-to-all-start.1) | async-done | bytes 32800 | tf_op jit(solution)/shard_map/all_to_all | solution.py:88
  164.9 12.0 %reduce-scatter.3.cloned.1.call-done = bf16[256,1536]{1,0:T(8,128)(2,1)} async-done(((bf16[1024,1536]{1,0:T(8,128)(2,1)}), bf16[256,1536]{1,0:T(8,128)(2,1)}) %reduce-scatter.3.cloned.1.call-update) | async-done | bytes 786448 | tf_op jit(solution)/shard_map/reduce_scatter | solution.py:377
  177.5 4.9 %all-to-all-start.2 = ((f32[8,2,128]{2,1,0:T(2,128)}), f32[8,2,128]{2,1,0:T(2,128)S(1)}, u32[]{:S(2)}, u32[]{:S(2)}) async-start(f32[8,2,128]{2,1,0:T(2,128)} %broadcast_in_dim.13), calls=%async_computation.3 | async-start | bytes 16384 | tf_op jit(solution)/shard_map/all_to_all | solution.py:88
  182.6 3.1 %collective-permute-start.30 = (bf16[4,32,1536]{2,1,0:T(8,128)(2,1)S(1)}, bf16[4,32,1536]{2,1,0:T(8,128)(2,1)S(1)}, u32[]{:S(2)}, u32[]{:S(2)}) collective-permute-start(bf16[4,32,1536]{2,1,0:T(8,128)(2,1)S(1)} %add_convert_fusion.2), channel_id=1, source_target_pairs={{0,56},{8,0},{16,8},{24,16},{32,24},{40,32},{48,40},{56,48},{1,57}... | collective-permute-start | bytes 1179656 | tf_op jit(solution)/shard_map/ppermute | solution.py:36
  185.7 1.1 add_convert_fusion.4
  187.7 7.6 %collective-permute-done.30 = bf16[4,32,1536]{2,1,0:T(8,128)(2,1)S(1)} collective-permute-done((bf16[4,32,1536]{2,1,0:T(8,128)(2,1)S(1)}, bf16[4,32,1536]{2,1,0:T(8,128)(2,1)S(1)}, u32[]{:S(2)}, u32[]{:S(2)}) %collective-permute-start.30) | collective-permute-done | bytes 393248 | tf_op jit(solution)/shard_map/ppermute | solution.py:36
  195.3 3.5 %collective-permute-start.31 = (bf16[4,32,1536]{2,1,0:T(8,128)(2,1)S(1)}, bf16[4,32,1536]{2,1,0:T(8,128)(2,1)S(1)}, u32[]{:S(2)}, u32[]{:S(2)}) collective-permute-start(bf16[4,32,1536]{2,1,0:T(8,128)(2,1)S(1)} %add_convert_fusion.1), channel_id=1, source_target_pairs={{0,56},{8,0},{16,8},{24,16},{32,24},{40,32},{48,40},{56,48},{1,57}... | collective-permute-start | bytes 1179656 | tf_op jit(solution)/shard_map/ppermute | solution.py:36
  198.8 1.8 collective-permute-done.26
  200.8 12.1 %gradients.1 = (bf16[1,3072,256]{2,1,0:T(8,128)(2,1)}, bf16[1,3072,256]{2,1,0:T(8,128)(2,1)}, bf16[1,256,3072]{2,1,0:T(8,128)(2,1)}) custom-call(s32[12]{0:T(128)} %pad_add_fusion.where_ref, bf16[4,8,32,3072]{3,2,1,0:T(8,128)(2,1)} %get-tuple-element.40.x_ref, bf16[32,32,3200]{2,1,0:T(8,128)(2,1)} %all-gather.2.cloned.1.call-done.y_ref.id_ref, ...), custom_call_target="tpu_custom_call" | custom-call | flops 4831838208 | bytes 18874368 | tf_op jit(solution)/shard_map/gradients/pallas_call | solution.py:305
  213.0 2.5 %collective-permute-done.27 = bf16[4,32,1536]{2,1,0:T(8,128)(2,1)S(1)} collective-permute-done((bf16[4,32,1536]{2,1,0:T(8,128)(2,1)S(1)}, bf16[4,32,1536]{2,1,0:T(8,128)(2,1)S(1)}, u32[]{:S(2)}, u32[]{:S(2)}) %collective-permute-start.27) | collective-permute-done | bytes 393248 | tf_op jit(solution)/shard_map/ppermute | solution.py:36
  215.9 2.7 %collective-permute-start.32 = (bf16[32,1536]{1,0:T(8,128)(2,1)S(1)}, bf16[32,1536]{1,0:T(8,128)(2,1)S(1)}, u32[]{:S(2)}, u32[]{:S(2)}) collective-permute-start(bf16[32,1536]{1,0:T(8,128)(2,1)S(1)} %get-tuple-element.78), channel_id=1, source_target_pairs={{0,192},{64,0},{128,64},{192,128},{1,193},{65,1},{129,65},{193,129... | collective-permute-start | bytes 294920 | tf_op jit(solution)/shard_map/ppermute | solution.py:36
  218.5 2.3 collective-permute-done.34
  220.8 0.7 collective-permute-done.33
  221.7 0.9 pad_maximum_fusion.6
  222.6 0.8 reshape.66
  223.3 6.8 %all-to-all-start.3 = ((bf16[8,4,3072]{2,1,0:T(4,128)(2,1)}), bf16[8,4,3072]{2,1,0:T(4,128)(2,1)S(1)}, u32[]{:S(2)}, u32[]{:S(2)}) async-start(bf16[8,4,3072]{2,1,0:T(4,128)(2,1)} %reshape.66), calls=%async_computation.5 | async-start | bytes 393216 | tf_op jit(solution)/shard_map/all_to_all | solution.py:402
  230.7 5.3 %all-to-all-done.3 = bf16[8,4,3072]{2,1,0:T(4,128)(2,1)S(1)} async-done(((bf16[8,4,3072]{2,1,0:T(4,128)(2,1)}), bf16[8,4,3072]{2,1,0:T(4,128)(2,1)S(1)}, u32[]{:S(2)}, u32[]{:S(2)}) %all-to-all-start.3) | async-done | bytes 196640 | tf_op jit(solution)/shard_map/all_to_all | solution.py:402
  236.1 0.8 convolution_convert_fusion.2
  (132 shorter events, 7.9 us)
Async XLA Ops:
  7.2 3.0 %copy-start = (bf16[12,3072]{1,0:T(8,128)(2,1)S(1)}, bf16[12,3072]{1,0:T(8,128)(2,1)}, u32[]{:S(2)}) copy-start(bf16[12,3072]{1,0:T(8,128)(2,1)} %param.9) | copy-start | bytes 221188
  7.2 123.4 %all-gather.2.cloned.1.call-start = ((), (), s32[]{:S(2)}) async-start(), calls=%async_computation.6 | async-start | bytes 6758400 | tf_op jit(solution)/shard_map/all_gather | solution.py:368
  26.9 150.0 %reduce-scatter.3.cloned.1.call-start = ((), (), s32[]{:S(2)}) async-start(), calls=%async_computation.7 | async-start | bytes 3932160 | tf_op jit(solution)/shard_map/reduce_scatter | solution.py:377
  27.1 9.0 %collective-permute-start.1 = (bf16[16,3072]{1,0:T(8,128)(2,1)S(1)}, bf16[16,3072]{1,0:T(8,128)(2,1)S(1)}, u32[]{:S(2)}, u32[]{:S(2)}) collective-permute-start(bf16[16,3072]{1,0:T(8,128)(2,1)S(1)} %slice.88), channel_id=1, source_target_pairs={{0,192},{64,0},{128,64},{192,128},{1,193},{65,1},{129,65},{193,129... | collective-permute-start | bytes 294920 | tf_op jit(solution)/shard_map/ppermute | solution.py:36
  29.6 9.3 %collective-permute-start = (bf16[16,3072]{1,0:T(8,128)(2,1)S(1)}, bf16[16,3072]{1,0:T(8,128)(2,1)S(1)}, u32[]{:S(2)}, u32[]{:S(2)}) collective-permute-start(bf16[16,3072]{1,0:T(8,128)(2,1)S(1)} %slice.88), channel_id=1, source_target_pairs={{0,64},{64,128},{128,192},{192,0},{1,65},{65,129},{129,193},{193,1... | collective-permute-start | bytes 294920 | tf_op jit(solution)/shard_map/ppermute | solution.py:36
  29.7 9.3 %collective-permute-start.12 = (bf16[16,3072]{1,0:T(8,128)(2,1)S(1)}, bf16[16,3072]{1,0:T(8,128)(2,1)S(1)}, u32[]{:S(2)}, u32[]{:S(2)}) collective-permute-start(bf16[16,3072]{1,0:T(8,128)(2,1)S(1)} %slice.94), channel_id=1, source_target_pairs={{0,8},{8,16},{16,24},{24,32},{32,40},{40,48},{48,56},{56,0},{1,9},... | collective-permute-start | bytes 294920 | tf_op jit(solution)/shard_map/ppermute | solution.py:36
  31.4 7.7 %collective-permute-start.13 = (bf16[16,3072]{1,0:T(8,128)(2,1)S(1)}, bf16[16,3072]{1,0:T(8,128)(2,1)S(1)}, u32[]{:S(2)}, u32[]{:S(2)}) collective-permute-start(bf16[16,3072]{1,0:T(8,128)(2,1)S(1)} %slice.94), channel_id=1, source_target_pairs={{0,56},{8,0},{16,8},{24,16},{32,24},{40,32},{48,40},{56,48},{1,57}... | collective-permute-start | bytes 294920 | tf_op jit(solution)/shard_map/ppermute | solution.py:36
  36.1 6.9 %collective-permute-start.3 = (bf16[8,3072]{1,0:T(8,128)(2,1)S(1)}, bf16[8,3072]{1,0:T(8,128)(2,1)S(1)}, u32[]{:S(2)}, u32[]{:S(2)}) collective-permute-start(bf16[8,3072]{1,0:T(8,128)(2,1)S(1)} %slice.117), channel_id=1, source_target_pairs={{0,192},{64,0},{128,64},{192,128},{1,193},{65,1},{129,65},{193,129... | collective-permute-start | bytes 147464 | tf_op jit(solution)/shard_map/ppermute | solution.py:36
  38.9 4.2 %collective-permute-start.2 = (bf16[8,3072]{1,0:T(8,128)(2,1)S(1)}, bf16[8,3072]{1,0:T(8,128)(2,1)S(1)}, u32[]{:S(2)}, u32[]{:S(2)}) collective-permute-start(bf16[8,3072]{1,0:T(8,128)(2,1)S(1)} %slice.116), channel_id=1, source_target_pairs={{0,64},{64,128},{128,192},{192,0},{1,65},{65,129},{129,193},{193,1... | collective-permute-start | bytes 147464 | tf_op jit(solution)/shard_map/ppermute | solution.py:36
  39.0 7.0 %collective-permute-start.14 = (bf16[16,3072]{1,0:T(8,128)(2,1)S(1)}, bf16[16,3072]{1,0:T(8,128)(2,1)S(1)}, u32[]{:S(2)}, u32[]{:S(2)}) collective-permute-start(bf16[16,3072]{1,0:T(8,128)(2,1)S(1)} %collective-permute-done.12), channel_id=1, source_target_pairs={{0,8},{8,16},{16,24},{24,32},{32,40},{40,48},{48,56},{56,0},{1,9},... | collective-permute-start | bytes 294920 | tf_op jit(solution)/shard_map/ppermute | solution.py:36
  39.1 6.9 %collective-permute-start.15 = (bf16[16,3072]{1,0:T(8,128)(2,1)S(1)}, bf16[16,3072]{1,0:T(8,128)(2,1)S(1)}, u32[]{:S(2)}, u32[]{:S(2)}) collective-permute-start(bf16[16,3072]{1,0:T(8,128)(2,1)S(1)} %collective-permute-done.13), channel_id=1, source_target_pairs={{0,56},{8,0},{16,8},{24,16},{32,24},{40,32},{48,40},{56,48},{1,57}... | collective-permute-start | bytes 294920 | tf_op jit(solution)/shard_map/ppermute | solution.py:36
  43.2 53.3 %copy-start.8 = (bf16[4,16,3072]{2,1,0:T(8,128)(2,1)}, bf16[4,16,3072]{2,1,0:T(8,128)(2,1)S(1)}, u32[]{:S(2)}) copy-start(bf16[4,16,3072]{2,1,0:T(8,128)(2,1)S(1)} %pad_maximum_fusion.1.refs_0_) | copy-start | bytes 1179652
  43.2 41.6 %copy-start.16 = (s32[8]{0:T(128)S(1)}, s32[8]{0:T(128)}, u32[]{:S(2)}) copy-start(s32[8]{0:T(128)} %constant.61.clone) | copy-start | bytes 100
  43.2 26.3 %collective-permute-start.4 = (bf16[4,16,3072]{2,1,0:T(8,128)(2,1)S(1)}, bf16[4,16,3072]{2,1,0:T(8,128)(2,1)S(1)}, u32[]{:S(2)}, u32[]{:S(2)}) collective-permute-start(bf16[4,16,3072]{2,1,0:T(8,128)(2,1)S(1)} %pad_maximum_fusion.1.refs_0_), channel_id=1, source_target_pairs={{0,8},{8,16},{16,24},{24,32},{32,40},{40,48},{48,56},{56,0},{1,9},... | collective-permute-start | bytes 1179656 | tf_op jit(solution)/shard_map/ppermute | solution.py:36
  43.3 26.2 %collective-permute-start.5 = (bf16[4,16,3072]{2,1,0:T(8,128)(2,1)S(1)}, bf16[4,16,3072]{2,1,0:T(8,128)(2,1)S(1)}, u32[]{:S(2)}, u32[]{:S(2)}) collective-permute-start(bf16[4,16,3072]{2,1,0:T(8,128)(2,1)S(1)} %pad_maximum_fusion.1.refs_0_), channel_id=1, source_target_pairs={{0,56},{8,0},{16,8},{24,16},{32,24},{40,32},{48,40},{56,48},{1,57}... | collective-permute-start | bytes 1179656 | tf_op jit(solution)/shard_map/ppermute | solution.py:36
  45.9 14.2 %collective-permute-start.16 = (bf16[16,3072]{1,0:T(8,128)(2,1)S(1)}, bf16[16,3072]{1,0:T(8,128)(2,1)S(1)}, u32[]{:S(2)}, u32[]{:S(2)}) collective-permute-start(bf16[16,3072]{1,0:T(8,128)(2,1)S(1)} %collective-permute-done.14), channel_id=1, source_target_pairs={{0,8},{8,16},{16,24},{24,32},{32,40},{40,48},{48,56},{56,0},{1,9},... | collective-permute-start | bytes 294920 | tf_op jit(solution)/shard_map/ppermute | solution.py:36
  46.0 10.7 %collective-permute-start.17 = (bf16[16,3072]{1,0:T(8,128)(2,1)S(1)}, bf16[16,3072]{1,0:T(8,128)(2,1)S(1)}, u32[]{:S(2)}, u32[]{:S(2)}) collective-permute-start(bf16[16,3072]{1,0:T(8,128)(2,1)S(1)} %collective-permute-done.15), channel_id=1, source_target_pairs={{0,56},{8,0},{16,8},{24,16},{32,24},{40,32},{48,40},{56,48},{1,57}... | collective-permute-start | bytes 294920 | tf_op jit(solution)/shard_map/ppermute | solution.py:36
  49.9 50.3 %copy-start.15 = (s32[4]{0:T(128)S(1)}, s32[4]{0:T(128)}, u32[]{:S(2)}) copy-start(s32[4]{0:T(128)} %constant.60.clone) | copy-start | bytes 52
  56.6 5.6 %collective-permute-start.19 = (bf16[8,3072]{1,0:T(8,128)(2,1)S(1)}, bf16[8,3072]{1,0:T(8,128)(2,1)S(1)}, u32[]{:S(2)}, u32[]{:S(2)}) collective-permute-start(bf16[8,3072]{1,0:T(8,128)(2,1)S(1)} %slice.122), channel_id=1, source_target_pairs={{0,56},{8,0},{16,8},{24,16},{32,24},{40,32},{48,40},{56,48},{1,57}... | collective-permute-start | bytes 147464 | tf_op jit(solution)/shard_map/ppermute | solution.py:36
  60.1 4.5 %collective-permute-start.18 = (bf16[8,3072]{1,0:T(8,128)(2,1)S(1)}, bf16[8,3072]{1,0:T(8,128)(2,1)S(1)}, u32[]{:S(2)}, u32[]{:S(2)}) collective-permute-start(bf16[8,3072]{1,0:T(8,128)(2,1)S(1)} %slice.121), channel_id=1, source_target_pairs={{0,8},{8,16},{16,24},{24,32},{32,40},{40,48},{48,56},{56,0},{1,9},... | collective-permute-start | bytes 147464 | tf_op jit(solution)/shard_map/ppermute | solution.py:36
  65.3 16.2 %collective-permute-start.20 = (bf16[8,16,3072]{2,1,0:T(8,128)(2,1)}, bf16[8,16,3072]{2,1,0:T(8,128)(2,1)S(1)}, u32[]{:S(2)}, u32[]{:S(2)}) collective-permute-start(bf16[8,16,3072]{2,1,0:T(8,128)(2,1)} %fusion.3.refs_9_), channel_id=1, source_target_pairs={{0,64},{64,128},{128,192},{192,0},{1,65},{65,129},{129,193},{193,1... | collective-permute-start | bytes 2359304 | tf_op jit(solution)/shard_map/ppermute | solution.py:36
  65.3 16.3 %collective-permute-start.21 = (bf16[8,16,3072]{2,1,0:T(8,128)(2,1)}, bf16[8,16,3072]{2,1,0:T(8,128)(2,1)S(1)}, u32[]{:S(2)}, u32[]{:S(2)}) collective-permute-start(bf16[8,16,3072]{2,1,0:T(8,128)(2,1)} %fusion.3.refs_9_), channel_id=1, source_target_pairs={{0,192},{64,0},{128,64},{192,128},{1,193},{65,1},{129,65},{193,129... | collective-permute-start | bytes 2359304 | tf_op jit(solution)/shard_map/ppermute | solution.py:36
  69.5 15.3 %copy-start.11 = (bf16[4,16,3072]{2,1,0:T(8,128)(2,1)}, bf16[4,16,3072]{2,1,0:T(8,128)(2,1)S(1)}, u32[]{:S(2)}) copy-start(bf16[4,16,3072]{2,1,0:T(8,128)(2,1)S(1)} %collective-permute-done.4.refs_1_) | copy-start | bytes 1179652
  69.5 8.1 %collective-permute-start.6 = (bf16[4,16,3072]{2,1,0:T(8,128)(2,1)S(1)}, bf16[4,16,3072]{2,1,0:T(8,128)(2,1)}, u32[]{:S(2)}, u32[]{:S(2)}) collective-permute-start(bf16[4,16,3072]{2,1,0:T(8,128)(2,1)S(1)} %collective-permute-done.4.refs_1_), channel_id=1, source_target_pairs={{0,8},{8,16},{16,24},{24,32},{32,40},{40,48},{48,56},{56,0},{1,9},... | collective-permute-start | bytes 1179656 | tf_op jit(solution)/shard_map/ppermute | solution.py:36
  69.5 8.1 %copy-start.12 = (bf16[4,16,3072]{2,1,0:T(8,128)(2,1)}, bf16[4,16,3072]{2,1,0:T(8,128)(2,1)S(1)}, u32[]{:S(2)}) copy-start(bf16[4,16,3072]{2,1,0:T(8,128)(2,1)S(1)} %collective-permute-done.5.refs_2_) | copy-start | bytes 1179652
  69.5 8.1 %collective-permute-start.7 = (bf16[4,16,3072]{2,1,0:T(8,128)(2,1)S(1)}, bf16[4,16,3072]{2,1,0:T(8,128)(2,1)}, u32[]{:S(2)}, u32[]{:S(2)}) collective-permute-start(bf16[4,16,3072]{2,1,0:T(8,128)(2,1)S(1)} %collective-permute-done.5.refs_2_), channel_id=1, source_target_pairs={{0,56},{8,0},{16,8},{24,16},{32,24},{40,32},{48,40},{56,48},{1,57}... | collective-permute-start | bytes 1179656 | tf_op jit(solution)/shard_map/ppermute | solution.py:36
  77.7 17.8 %collective-permute-start.8 = (bf16[4,16,3072]{2,1,0:T(8,128)(2,1)}, bf16[4,16,3072]{2,1,0:T(8,128)(2,1)}, u32[]{:S(2)}, u32[]{:S(2)}) collective-permute-start(bf16[4,16,3072]{2,1,0:T(8,128)(2,1)} %collective-permute-done.6.refs_3_), channel_id=1, source_target_pairs={{0,8},{8,16},{16,24},{24,32},{32,40},{40,48},{48,56},{56,0},{1,9},... | collective-permute-start | bytes 1179656 | tf_op jit(solution)/shard_map/ppermute | solution.py:36
  77.7 18.9 %collective-permute-start.9 = (bf16[4,16,3072]{2,1,0:T(8,128)(2,1)}, bf16[4,16,3072]{2,1,0:T(8,128)(2,1)}, u32[]{:S(2)}, u32[]{:S(2)}) collective-permute-start(bf16[4,16,3072]{2,1,0:T(8,128)(2,1)} %collective-permute-done.7.refs_4_), channel_id=1, source_target_pairs={{0,56},{8,0},{16,8},{24,16},{32,24},{40,32},{48,40},{56,48},{1,57}... | collective-permute-start | bytes 1179656 | tf_op jit(solution)/shard_map/ppermute | solution.py:36
  81.5 27.3 %copy-start.9 = (bf16[8,16,3072]{2,1,0:T(8,128)(2,1)}, bf16[8,16,3072]{2,1,0:T(8,128)(2,1)S(1)}, u32[]{:S(2)}) copy-start(bf16[8,16,3072]{2,1,0:T(8,128)(2,1)S(1)} %collective-permute-done.20.refs_10_) | copy-start | bytes 2359300
  81.5 20.9 %collective-permute-start.22 = (bf16[8,8,3072]{2,1,0:T(8,128)(2,1)S(1)}, bf16[8,8,3072]{2,1,0:T(8,128)(2,1)}, u32[]{:S(2)}, u32[]{:S(2)}) collective-permute-start(bf16[8,8,3072]{2,1,0:T(8,128)(2,1)S(1)} %slice.123), channel_id=1, source_target_pairs={{0,64},{64,128},{128,192},{192,0},{1,65},{65,129},{129,193},{193,1... | collective-permute-start | bytes 1179656 | tf_op jit(solution)/shard_map/ppermute | solution.py:36
  81.6 27.2 %copy-start.10 = (bf16[8,16,3072]{2,1,0:T(8,128)(2,1)}, bf16[8,16,3072]{2,1,0:T(8,128)(2,1)S(1)}, u32[]{:S(2)}) copy-start(bf16[8,16,3072]{2,1,0:T(8,128)(2,1)S(1)} %collective-permute-done.21.refs_11_) | copy-start | bytes 2359300
  81.7 20.7 %collective-permute-start.23 = (bf16[8,8,3072]{2,1,0:T(8,128)(2,1)S(1)}, bf16[8,8,3072]{2,1,0:T(8,128)(2,1)}, u32[]{:S(2)}, u32[]{:S(2)}) collective-permute-start(bf16[8,8,3072]{2,1,0:T(8,128)(2,1)S(1)} %slice.124), channel_id=1, source_target_pairs={{0,192},{64,0},{128,64},{192,128},{1,193},{65,1},{129,65},{193,129... | collective-permute-start | bytes 1179656 | tf_op jit(solution)/shard_map/ppermute | solution.py:36
  96.5 10.4 %collective-permute-start.10 = (bf16[4,8,3072]{2,1,0:T(8,128)(2,1)S(1)}, bf16[4,8,3072]{2,1,0:T(8,128)(2,1)S(1)}, u32[]{:S(2)}, u32[]{:S(2)}) collective-permute-start(bf16[4,8,3072]{2,1,0:T(8,128)(2,1)S(1)} %slice.118), channel_id=1, source_target_pairs={{0,8},{8,16},{16,24},{24,32},{32,40},{40,48},{48,56},{56,0},{1,9},... | collective-permute-start | bytes 589832 | tf_op jit(solution)/shard_map/ppermute | solution.py:36
  97.5 11.3 %collective-permute-start.11 = (bf16[4,8,3072]{2,1,0:T(8,128)(2,1)S(1)}, bf16[4,8,3072]{2,1,0:T(8,128)(2,1)S(1)}, u32[]{:S(2)}, u32[]{:S(2)}) collective-permute-start(bf16[4,8,3072]{2,1,0:T(8,128)(2,1)S(1)} %slice.119), channel_id=1, source_target_pairs={{0,56},{8,0},{16,8},{24,16},{32,24},{40,32},{48,40},{56,48},{1,57}... | collective-permute-start | bytes 589832 | tf_op jit(solution)/shard_map/ppermute | solution.py:36
  106.9 1.9 copy-start.13
  108.8 0.7 copy-start.14
  130.6 4.1 %copy-start.1 = (bf16[7,4,32,1536]{3,2,1,0:T(8,128)(2,1)S(1)}, bf16[7,4,32,1536]{3,2,1,0:T(8,128)(2,1)}, u32[]{:S(2)}) copy-start(bf16[7,4,32,1536]{3,2,1,0:T(8,128)(2,1)} %get-tuple-element.37) | copy-start | bytes 8257540
  130.6 25.5 %collective-permute-start.28 = (bf16[2,32,1536]{2,1,0:T(8,128)(2,1)}, bf16[2,32,1536]{2,1,0:T(8,128)(2,1)}, u32[]{:S(2)}, u32[]{:S(2)}) collective-permute-start(bf16[2,32,1536]{2,1,0:T(8,128)(2,1)} %get-tuple-element.52), channel_id=1, source_target_pairs={{0,56},{8,0},{16,8},{24,16},{32,24},{40,32},{48,40},{56,48},{1,57}... | collective-permute-start | bytes 589832 | tf_op jit(solution)/shard_map/ppermute | solution.py:36
  134.7 25.0 %collective-permute-start.24 = (bf16[2,32,1536]{2,1,0:T(8,128)(2,1)}, bf16[2,32,1536]{2,1,0:T(8,128)(2,1)S(1)}, u32[]{:S(2)}, u32[]{:S(2)}) collective-permute-start(bf16[2,32,1536]{2,1,0:T(8,128)(2,1)} %get-tuple-element.36), channel_id=1, source_target_pairs={{0,8},{8,16},{16,24},{24,32},{32,40},{40,48},{48,56},{56,0},{1,9},... | collective-permute-start | bytes 589832 | tf_op jit(solution)/shard_map/ppermute | solution.py:36
  136.1 19.9 %copy-start.7 = (bf16[4,32,1536]{2,1,0:T(8,128)(2,1)S(1)}, bf16[4,32,1536]{2,1,0:T(8,128)(2,1)}, u32[]{:S(2)}) copy-start(bf16[4,32,1536]{2,1,0:T(8,128)(2,1)} %get-tuple-element.51) | copy-start | bytes 1179652
  147.9 11.8 %copy-start.6 = (bf16[4,32,1536]{2,1,0:T(8,128)(2,1)S(1)}, bf16[4,32,1536]{2,1,0:T(8,128)(2,1)}, u32[]{:S(2)}) copy-start(bf16[4,32,1536]{2,1,0:T(8,128)(2,1)} %get-tuple-element.45) | copy-start | bytes 1179652
  149.2 15.6 %all-to-all-start.1 = ((f32[32,2,128]{2,1,0:T(2,128)}), f32[32,2,128]{2,1,0:T(2,128)S(1)}, u32[]{:S(2)}, u32[]{:S(2)}) async-start(f32[32,2,128]{2,1,0:T(2,128)} %broadcast_in_dim.12), calls=%async_computation.1 | async-start | bytes 65536 | tf_op jit(solution)/shard_map/all_to_all | solution.py:88
  156.0 65.7 %reduce-scatter.5.cloned.1.call-start = ((), (), s32[]{:S(2)}) async-start(), calls=%async_computation.8 | async-start | bytes 884736 | tf_op jit(solution)/shard_map/reduce_scatter | solution.py:387
  157.1 25.4 %copy-start.5 = (bf16[4,32,1536]{2,1,0:T(8,128)(2,1)S(1)}, bf16[4,32,1536]{2,1,0:T(8,128)(2,1)}, u32[]{:S(2)}) copy-start(bf16[4,32,1536]{2,1,0:T(8,128)(2,1)} %get-tuple-element.53) | copy-start | bytes 1179652
  157.1 25.3 %collective-permute-start.29 = (bf16[4,32,1536]{2,1,0:T(8,128)(2,1)S(1)}, bf16[4,32,1536]{2,1,0:T(8,128)(2,1)S(1)}, u32[]{:S(2)}, u32[]{:S(2)}) collective-permute-start(bf16[4,32,1536]{2,1,0:T(8,128)(2,1)S(1)} %pad_maximum_fusion.3), channel_id=1, source_target_pairs={{0,56},{8,0},{16,8},{24,16},{32,24},{40,32},{48,40},{56,48},{1,57}... | collective-permute-start | bytes 1179656 | tf_op jit(solution)/shard_map/ppermute | solution.py:36
  159.7 26.0 %copy-start.4 = (bf16[4,32,1536]{2,1,0:T(8,128)(2,1)S(1)}, bf16[4,32,1536]{2,1,0:T(8,128)(2,1)}, u32[]{:S(2)}) copy-start(bf16[4,32,1536]{2,1,0:T(8,128)(2,1)} %get-tuple-element.48) | copy-start | bytes 1179652
  159.8 25.9 %collective-permute-start.25 = (bf16[4,32,1536]{2,1,0:T(8,128)(2,1)S(1)}, bf16[4,32,1536]{2,1,0:T(8,128)(2,1)}, u32[]{:S(2)}, u32[]{:S(2)}) collective-permute-start(bf16[4,32,1536]{2,1,0:T(8,128)(2,1)S(1)} %pad_maximum_fusion.2), channel_id=1, source_target_pairs={{0,8},{8,16},{16,24},{24,32},{32,40},{40,48},{48,56},{56,0},{1,9},... | collective-permute-start | bytes 1179656 | tf_op jit(solution)/shard_map/ppermute | solution.py:36
  176.9 18.4 %copy-start.3 = (bf16[4,32,1536]{2,1,0:T(8,128)(2,1)S(1)}, bf16[4,32,1536]{2,1,0:T(8,128)(2,1)}, u32[]{:S(2)}) copy-start(bf16[4,32,1536]{2,1,0:T(8,128)(2,1)} %get-tuple-element.54) | copy-start | bytes 1179652
  177.5 9.5 %all-to-all-start.2 = ((f32[8,2,128]{2,1,0:T(2,128)}), f32[8,2,128]{2,1,0:T(2,128)S(1)}, u32[]{:S(2)}, u32[]{:S(2)}) async-start(f32[8,2,128]{2,1,0:T(2,128)} %broadcast_in_dim.13), calls=%async_computation.3 | async-start | bytes 16384 | tf_op jit(solution)/shard_map/all_to_all | solution.py:88
  182.4 18.2 %copy-start.2 = (bf16[4,32,1536]{2,1,0:T(8,128)(2,1)S(1)}, bf16[4,32,1536]{2,1,0:T(8,128)(2,1)}, u32[]{:S(2)}) copy-start(bf16[4,32,1536]{2,1,0:T(8,128)(2,1)} %get-tuple-element.50) | copy-start | bytes 1179652
  182.6 12.7 %collective-permute-start.30 = (bf16[4,32,1536]{2,1,0:T(8,128)(2,1)S(1)}, bf16[4,32,1536]{2,1,0:T(8,128)(2,1)S(1)}, u32[]{:S(2)}, u32[]{:S(2)}) collective-permute-start(bf16[4,32,1536]{2,1,0:T(8,128)(2,1)S(1)} %add_convert_fusion.2), channel_id=1, source_target_pairs={{0,56},{8,0},{16,8},{24,16},{32,24},{40,32},{48,40},{56,48},{1,57}... | collective-permute-start | bytes 1179656 | tf_op jit(solution)/shard_map/ppermute | solution.py:36
  186.8 13.9 %collective-permute-start.26 = (bf16[4,32,1536]{2,1,0:T(8,128)(2,1)S(1)}, bf16[4,32,1536]{2,1,0:T(8,128)(2,1)S(1)}, u32[]{:S(2)}, u32[]{:S(2)}) collective-permute-start(bf16[4,32,1536]{2,1,0:T(8,128)(2,1)S(1)} %add_convert_fusion.4), channel_id=1, source_target_pairs={{0,8},{8,16},{16,24},{24,32},{32,40},{40,48},{48,56},{56,0},{1,9},... | collective-permute-start | bytes 1179656 | tf_op jit(solution)/shard_map/ppermute | solution.py:36
  195.3 17.6 %collective-permute-start.31 = (bf16[4,32,1536]{2,1,0:T(8,128)(2,1)S(1)}, bf16[4,32,1536]{2,1,0:T(8,128)(2,1)S(1)}, u32[]{:S(2)}, u32[]{:S(2)}) collective-permute-start(bf16[4,32,1536]{2,1,0:T(8,128)(2,1)S(1)} %add_convert_fusion.1), channel_id=1, source_target_pairs={{0,56},{8,0},{16,8},{24,16},{32,24},{40,32},{48,40},{56,48},{1,57}... | collective-permute-start | bytes 1179656 | tf_op jit(solution)/shard_map/ppermute | solution.py:36
  200.7 14.8 %collective-permute-start.27 = (bf16[4,32,1536]{2,1,0:T(8,128)(2,1)S(1)}, bf16[4,32,1536]{2,1,0:T(8,128)(2,1)S(1)}, u32[]{:S(2)}, u32[]{:S(2)}) collective-permute-start(bf16[4,32,1536]{2,1,0:T(8,128)(2,1)S(1)} %add_convert_fusion.3), channel_id=1, source_target_pairs={{0,8},{8,16},{16,24},{24,32},{32,40},{40,48},{48,56},{56,0},{1,9},... | collective-permute-start | bytes 1179656 | tf_op jit(solution)/shard_map/ppermute | solution.py:36
  215.7 5.2 %collective-permute-start.34 = (bf16[32,1536]{1,0:T(8,128)(2,1)S(1)}, bf16[32,1536]{1,0:T(8,128)(2,1)S(1)}, u32[]{:S(2)}, u32[]{:S(2)}) collective-permute-start(bf16[32,1536]{1,0:T(8,128)(2,1)S(1)} %get-tuple-element.79), channel_id=1, source_target_pairs={{0,128},{64,192},{128,0},{192,64},{1,129},{65,193},{129,1},{193,65... | collective-permute-start | bytes 294920 | tf_op jit(solution)/shard_map/ppermute | solution.py:36
  215.8 5.8 %collective-permute-start.33 = (bf16[32,1536]{1,0:T(8,128)(2,1)S(1)}, bf16[32,1536]{1,0:T(8,128)(2,1)S(1)}, u32[]{:S(2)}, u32[]{:S(2)}) collective-permute-start(bf16[32,1536]{1,0:T(8,128)(2,1)S(1)} %get-tuple-element.80), channel_id=1, source_target_pairs={{0,64},{64,128},{128,192},{192,0},{1,65},{65,129},{129,193},{193,1... | collective-permute-start | bytes 294920 | tf_op jit(solution)/shard_map/ppermute | solution.py:36
  215.9 5.7 %collective-permute-start.32 = (bf16[32,1536]{1,0:T(8,128)(2,1)S(1)}, bf16[32,1536]{1,0:T(8,128)(2,1)S(1)}, u32[]{:S(2)}, u32[]{:S(2)}) collective-permute-start(bf16[32,1536]{1,0:T(8,128)(2,1)S(1)} %get-tuple-element.78), channel_id=1, source_target_pairs={{0,192},{64,0},{128,64},{192,128},{1,193},{65,1},{129,65},{193,129... | collective-permute-start | bytes 294920 | tf_op jit(solution)/shard_map/ppermute | solution.py:36
  223.3 12.7 %all-to-all-start.3 = ((bf16[8,4,3072]{2,1,0:T(4,128)(2,1)}), bf16[8,4,3072]{2,1,0:T(4,128)(2,1)S(1)}, u32[]{:S(2)}, u32[]{:S(2)}) async-start(bf16[8,4,3072]{2,1,0:T(4,128)(2,1)} %reshape.66), calls=%async_computation.5 | async-start | bytes 393216 | tf_op jit(solution)/shard_map/all_to_all | solution.py:402
Sparse Core Ops, SparseCore 0:
  27.0 103.4 all-gather.1
  133.1 43.7 reduce-scatter.2
  179.4 36.5 reduce-scatter.4

commit v2 on v1

--- a/solution.py
+++ b/solution.py
@@ -95,7 +95,7 @@
 def forward_kernel(where_ref, *refs):
     a_refs, refs = refs[: NZ + 1], refs[NZ + 1 :]
     b_refs, refs = refs[: NX + 1], refs[NX + 1 :]
-    wg_ref, wu_ref, wd_ref, x_out, gate_ref, up_ref, hidden_ref, far_up, far_down, left_ref, right_ref, rows_ref, in_sems, out_sems = refs
+    wg_ref, wu_ref, wd_ref, x_out, gate_ref, up_ref, hidden_ref, far_up, far_down, left_ref, right_ref, rows_ref, wg, wu, wd, in_sems, w_sems, out_sems = refs
     step = pl.program_id(0)
     quarter = MID // 2
     arrivals = []
@@ -109,11 +109,16 @@
         arrivals.append([pltpu.make_async_copy(s, d, in_sems.at[i, n]) for n, (s, d) in enumerate(moves)])
     leaving = [pltpu.make_async_copy(rows_ref.at[i], x_out.at[i], out_sems.at[i]) for i in range(NX)]
 
+    weights = [
+        pltpu.make_async_copy(s.at[0], d, w_sems.at[n]) for n, (s, d) in enumerate([(wg_ref, wg), (wu_ref, wu), (wd_ref, wd)])
+    ]
+
     @pl.when(step == 0)
     def _():
-        for group in arrivals:
-            for copy in group:
-                copy.start()
+        for copy in arrivals[0] + weights[:2] + arrivals[1] + weights[2:] + arrivals[2] + arrivals[3]:
+            copy.start()
+        for copy in weights[:2]:
+            copy.wait()
 
     for i in range(NX):
 
@@ -124,13 +129,18 @@
             leaving[i].start()
 
     x = rows_ref[step].reshape(TILE, D)
-    gate = dot(x, wg_ref[0], ((1,), (0,)))
-    up = dot(x, wu_ref[0], ((1,), (0,)))
+    gate = dot(x, wg[...], ((1,), (0,)))
+    up = dot(x, wu[...], ((1,), (0,)))
     hidden = (gate * jax.nn.sigmoid(gate) * up).astype(BF)
     gate_ref[...] = gate
     up_ref[...] = up
     hidden_ref[...] = hidden
-    out = dot(hidden, wd_ref[0, :, :LEFT], ((1,), (0,))).astype(BF)
+
+    @pl.when(step == 0)
+    def _():
+        weights[2].wait()
+
+    out = dot(hidden, wd[:, :LEFT], ((1,), (0,))).astype(BF)
     left_ref[...] = out[: TILE - SLOTS].reshape(NZ - 1, 1, SLOTS, LEFT)
 
     @pl.when(step < NX // 2)
@@ -141,7 +151,7 @@
     def _():
         far_down[0] = out[TILE - SLOTS :]
 
-    out = dot(hidden, wd_ref[0, :, LEFT:], ((1,), (0,))).astype(BF)
+    out = dot(hidden, wd[:, LEFT:], ((1,), (0,))).astype(BF)
     for j in range(NZ):
         right_ref[0, where_ref[NX + j]] = out[j * SLOTS : (j + 1) * SLOTS]
 
@@ -153,9 +163,6 @@
 
 def forward(where, a_pieces, b_pieces, w_gate, w_up, w_down):
     outside = pl.BlockSpec(memory_space=pltpu.HBM)
-
-    def whole(a):
-        return pl.BlockSpec(a.shape, lambda i, where: (0, 0, 0), pipeline_mode=pl.Buffered(1))
 
     def tall(n):
         return pl.BlockSpec((TILE, n), lambda i, where: (i, 0))
@@ -165,7 +172,7 @@
         grid_spec=pltpu.PrefetchScalarGridSpec(
             num_scalar_prefetch=1,
             grid=(NX,),
-            in_specs=[outside] * (NZ + NX + 2) + [whole(w_gate), whole(w_up), whole(w_down)],
+            in_specs=[outside] * (NZ + NX + 5),
             out_specs=[
                 outside,
                 tall(HID),
@@ -178,7 +185,11 @@
             ],
             scratch_shapes=[
                 pltpu.VMEM((NX, NZ, SLOTS, D), BF),
+                pltpu.VMEM((D, HID), BF),
+                pltpu.VMEM((D, HID), BF),
+                pltpu.VMEM((HID, D), BF),
                 pltpu.SemaphoreType.DMA((NX, NZ + 3)),
+                pltpu.SemaphoreType.DMA((3,)),
                 pltpu.SemaphoreType.DMA((NX,)),
             ],
         ),
@@ -198,21 +209,23 @@
     )(where, *a_pieces, *b_pieces, w_gate, w_up, w_down)
 
 
-def backward_kernel(where_ref, y_ref, id_ref, x_ref, wd_ref, gate_ref, up_ref, hidden_ref, dg_ref, du_ref, spot_ref, sum_ref, y_rows):
+def backward_kernel(where_ref, y_ref, note_ref, wd_ref, gate_ref, up_ref, hidden_ref, dg_ref, du_ref, spot_ref, sum_ref, y_rows):
     i = pl.program_id(0)
     at_x = where_ref[i]
-    spots = []
+    spots, notes = [], []
     for j in range(NZ):
         at_z = where_ref[NX + j]
         y_rows[j] = y_ref[at_z]
-        block_id = id_ref[at_z].astype(F32)
+        note = note_ref[at_z].astype(F32)
         start = ((at_x * NZ + at_z) * 8).astype(F32)
-        spots.append(jnp.where(block_id >= 0.0, block_id + start, -1.0))
+        spots.append(jnp.where(note[:, :LANES] >= 0.0, note[:, :LANES] + start, -1.0))
+        notes.append(note[:, LANES:])
     spot = jnp.concatenate(spots, axis=0)
     spot_ref[...] = spot[:, :1]
-    y = y_rows[...].reshape(TILE, D)
-    x = x_ref[0].reshape(TILE, D)
-    back = dot(y, wd_ref[0], ((1,), (1,)))
+    notes = jnp.concatenate(notes, axis=0)
+    xx = jnp.concatenate([notes[:, :SLOTS] + notes[:, SLOTS : 2 * SLOTS]] * NZ, axis=1)
+    yy = jnp.concatenate([notes[:, 2 * SLOTS : 3 * SLOTS] + notes[:, 3 * SLOTS :]] * NZ, axis=1)
+    back = dot(y_rows[...].reshape(TILE, D), wd_ref[0], ((1,), (1,)))
     gate, up, hidden = gate_ref[...], up_ref[...], hidden_ref[...]
     sig = jax.nn.sigmoid(gate)
     d_gate = (back * up * sig * (1.0 + gate * (1.0 - sig))).astype(BF)
@@ -220,8 +233,7 @@
     dg_ref[...] = d_gate
     du_ref[...] = d_up
     last = ((1,), (1,))
-    pair = dot(x, x, last) * (dot(d_gate, d_gate, last) + dot(d_up, d_up, last))
-    pair = pair + dot(y, y, last) * dot(hidden, hidden, last)
+    pair = xx * (dot(d_gate, d_gate, last) + dot(d_up, d_up, last)) + yy * dot(hidden, hidden, last)
     same = (spot[:, :1] == spot.T[:1, :]) & (spot[:, :1] >= 0.0)
     row_sums = jnp.sum(jnp.where(same, pair, 0.0), axis=1, keepdims=True)
     lane = lax.broadcasted_iota(jnp.int32, (TILE, LANES), 1).astype(F32)
@@ -235,11 +247,10 @@
         sum_ref[half : half + 1, :] += jnp.sum(jnp.where(hot, row_sums, 0.0), axis=0, keepdims=True)
 
 
-def backward(where, wide_y, x, w_down, gate, up, hidden):
+def backward(where, wide_y, w_down, gate, up, hidden):
     def tall(n):
         return pl.BlockSpec((TILE, n), lambda i, where: (i, 0))
 
-    rows = pl.BlockSpec((1, NZ, SLOTS, D), lambda i, where: (i, 0, 0, 0))
     return pl.pallas_call(
         backward_kernel,
         grid_spec=pltpu.PrefetchScalarGridSpec(
@@ -247,8 +258,7 @@
             grid=(NX,),
             in_specs=[
                 pl.BlockSpec((NZ, SLOTS, D), lambda i, where: (where[i], 0, 0)),
-                pl.BlockSpec((NZ, SLOTS, LANES), lambda i, where: (where[i], 0, D // LANES)),
-                rows,
+                pl.BlockSpec((NZ, SLOTS, 2 * LANES), lambda i, where: (where[i], 0, D // (2 * LANES))),
                 pl.BlockSpec(w_down.shape, lambda i, where: (0, 0, 0), pipeline_mode=pl.Buffered(1)),
                 tall(HID),
                 tall(HID),
@@ -264,24 +274,59 @@
             jax.ShapeDtypeStruct((2, LANES), F32),
         ],
         compiler_params=pltpu.CompilerParams(vmem_limit_bytes=60 * MIB),
-        cost_estimate=pl.CostEstimate(flops=5 * ROWS * D * HID, bytes_accessed=20 * MIB, transcendentals=ROWS * HID),
+        cost_estimate=pl.CostEstimate(flops=3 * ROWS * D * HID, bytes_accessed=12 * MIB, transcendentals=ROWS * HID),
         name="backward",
-    )(where, wide_y, wide_y, x, w_down, gate, up, hidden)
-
-
-def grads_kernel(
-    where_ref, x_ref, y_ref, hidden_ref, dg_ref, du_ref, spot_ref, factor_ref, gg_ref, gu_ref, gd_ref, scaled, turned, moved, by_row
-):
+    )(where, wide_y, wide_y, w_down, gate, up, hidden)
+
+
+def factor_by_row(spot, factors):
+    lane = lax.broadcasted_iota(jnp.int32, (ROWS, LANES), 1).astype(F32)
+    factor = jnp.zeros((ROWS, 1), F32)
+    for half in range(2):
+        chosen = jnp.where(spot == lane + half * LANES, factors[half : half + 1, :], 0.0)
+        factor = factor + jnp.sum(chosen, axis=1, keepdims=True)
+    return factor
+
+
+def wide_grads_kernel(x_ref, dg_ref, du_ref, spot_ref, factor_ref, gg_ref, gu_ref, scaled):
     @pl.when(pl.program_id(0) == 0)
     def _():
-        spot = spot_ref[...]
-        lane = lax.broadcasted_iota(jnp.int32, (ROWS, LANES), 1).astype(F32)
-        factor = jnp.zeros((ROWS, 1), F32)
-        for half in range(2):
-            chosen = jnp.where(spot == lane + half * LANES, factor_ref[half : half + 1, :], 0.0)
-            factor = factor + jnp.sum(chosen, axis=1, keepdims=True)
+        factor = factor_by_row(spot_ref[...], factor_ref[...])
         scaled[:, :HID] = (factor * dg_ref[...].astype(F32)).astype(BF)
         scaled[:, HID:] = (factor * du_ref[...].astype(F32)).astype(BF)
+
+    both = dot(x_ref[...].reshape(ROWS, COLS), scaled[...], ((0,), (0,))).astype(BF)
+    gg_ref[0] = both[:, :HID]
+    gu_ref[0] = both[:, HID:]
+
+
+def wide_gradients(x, d_gate, d_up, spot, factors):
+    def whole(a):
+        return pl.BlockSpec(a.shape, lambda i: (0, 0), pipeline_mode=pl.Buffered(1))
+
+    return pl.pallas_call(
+        wide_grads_kernel,
+        grid=(D // COLS,),
+        in_specs=[
+            pl.BlockSpec((NX, NZ, SLOTS, COLS), lambda i: (0, 0, 0, i)),
+            whole(d_gate),
+            whole(d_up),
+            whole(spot),
+            whole(factors),
+        ],
+        out_specs=[pl.BlockSpec((1, COLS, HID), lambda i: (0, i, 0))] * 2,
+        out_shape=[jax.ShapeDtypeStruct((1, D, HID), BF)] * 2,
+        scratch_shapes=[pltpu.VMEM((ROWS, 2 * HID), BF)],
+        compiler_params=pltpu.CompilerParams(vmem_limit_bytes=60 * MIB),
+        cost_estimate=pl.CostEstimate(flops=4 * ROWS * D * HID, bytes_accessed=11 * MIB, transcendentals=0),
+        name="wide_gradients",
+    )(x, d_gate, d_up, spot, factors)
+
+
+def down_grad_kernel(where_ref, y_ref, hidden_ref, spot_ref, factor_ref, gd_ref, turned, moved, by_row):
+    @pl.when(pl.program_id(0) == 0)
+    def _():
+        factor = factor_by_row(spot_ref[...], factor_ref[...])
         for i in range(NX):
             for j in range(NZ):
                 block = where_ref[i] * NZ + where_ref[NX + j]
@@ -290,53 +335,37 @@
                 by_row[block] = factor[first : first + SLOTS]
         turned[...] = moved[...].reshape(ROWS, HID).T
 
-    x = x_ref[...].reshape(ROWS, COLS)
-    both = dot(x, scaled[...], ((0,), (0,))).astype(BF)
-    gg_ref[0] = both[:, :HID]
-    gu_ref[0] = both[:, HID:]
     cot = (by_row[...] * y_ref[...].astype(F32)).astype(BF).reshape(ROWS, COLS)
     gd_ref[0] = dot(turned[...], cot, ((1,), (0,))).astype(BF)
 
 
-def gradients(where, x, wide_y, hidden, d_gate, d_up, spot, factors):
+def down_gradient(where, wide_y, hidden, spot, factors):
     def whole(a):
         return pl.BlockSpec(a.shape, lambda i, where: (0, 0), pipeline_mode=pl.Buffered(1))
 
     return pl.pallas_call(
-        grads_kernel,
+        down_grad_kernel,
         grid_spec=pltpu.PrefetchScalarGridSpec(
             num_scalar_prefetch=1,
             grid=(D // COLS,),
             in_specs=[
-                pl.BlockSpec((NX, NZ, SLOTS, COLS), lambda i, where: (0, 0, 0, i)),
                 pl.BlockSpec((BLOCKS, SLOTS, COLS), lambda i, where: (0, 0, i)),
                 whole(hidden),
-                whole(d_gate),
-                whole(d_up),
                 whole(spot),
                 whole(factors),
             ],
-            out_specs=[
-                pl.BlockSpec((1, COLS, HID), lambda i, where: (0, i, 0)),
-                pl.BlockSpec((1, COLS, HID), lambda i, where: (0, i, 0)),
-                pl.BlockSpec((1, HID, COLS), lambda i, where: (0, 0, i)),
-            ],
+            out_specs=pl.BlockSpec((1, HID, COLS), lambda i, where: (0, 0, i)),
             scratch_shapes=[
-                pltpu.VMEM((ROWS, 2 * HID), BF),
                 pltpu.VMEM((HID, ROWS), BF),
                 pltpu.VMEM((BLOCKS, SLOTS, HID), BF),
                 pltpu.VMEM((BLOCKS, SLOTS, 1), F32),
             ],
         ),
-        out_shape=[
-            jax.ShapeDtypeStruct((1, D, HID), BF),
-            jax.ShapeDtypeStruct((1, D, HID), BF),
-            jax.ShapeDtypeStruct((1, HID, D), BF),
-        ],
+        out_shape=jax.ShapeDtypeStruct((1, HID, D), BF),
         compiler_params=pltpu.CompilerParams(vmem_limit_bytes=60 * MIB),
-        cost_estimate=pl.CostEstimate(flops=6 * ROWS * D * HID, bytes_accessed=18 * MIB, transcendentals=0),
-        name="gradients",
-    )(where, x, wide_y, hidden, d_gate, d_up, spot, factors)
+        cost_estimate=pl.CostEstimate(flops=2 * ROWS * D * HID, bytes_accessed=8 * MIB, transcendentals=0),
+        name="down_gradient",
+    )(where, wide_y, hidden, spot, factors)
 
 
 def on_device(tokens, cotangent, routes, example_ids, w_gate, w_up, w_down):
@@ -365,7 +394,13 @@
     got = lax.all_to_all(send, EXPERT, split_axis=0, concat_axis=0, tiled=True)
     local_x = got[:, :CAP, :width].reshape(SLOTS, width)
     local_dy = got[:, CAP:].reshape(SLOTS, width + LANES)
-    wide_y = lax.all_gather(local_dy, ("x", "z"), axis=0)
+    last = ((1,), (1,))
+    parts = []
+    for rows in (local_x, local_dy[:, :width]):
+        gram = dot(rows, rows, last)
+        high = lax.reduce_precision(gram, 8, 7)
+        parts += [high.astype(BF), (gram - high).astype(BF)]
+    wide_y = lax.all_gather(jnp.concatenate([local_dy] + parts, axis=1), ("x", "z"), axis=0)
     line_x = line_of(ring_gather(local_x[:MID], "x"))
     line_z = line_of(ring_gather(local_x[MID:], "z"))
     a_pieces = ring_gather(line_x, "z")
@@ -379,31 +414,34 @@
 
     def hook(step, sent):
         if step == 1:
-            kept["back"] = backward(where, wide_y, x, w_down, gate, up_part, hidden)
+            kept["back"] = backward(where, wide_y, w_down, gate, up_part, hidden)
             sent, kept["sum"] = lax.optimization_barrier((sent, kept["back"][3]))
         elif step == 2:
             total = jnp.sum(spread(kept["sum"], ("x", "z"), BLOCKS).reshape(BLOCKS, 2, LANES), axis=0)
             sent, kept["sum"], line = lax.optimization_barrier((sent, total, right_line))
-            kept["line"] = lax.psum_scatter(line.astype(F32), "z", scatter_dimension=0, tiled=True)
+            line = lax.optimization_barrier(line.astype(F32))
+            kept["line"] = lax.optimization_barrier(lax.psum_scatter(line, "z", scatter_dimension=0, tiled=True))
         elif step == 3:
             total = jnp.sum(spread(kept["sum"], EXPERT, NE).reshape(NE, 2, LANES), axis=0)
             sent, kept["norms"] = lax.optimization_barrier((sent, jnp.sqrt(total)))
         else:
             d_gate, d_up, spot, _ = kept["back"]
-            factors = RADIUS / (kept["norms"] + GAMMA)
-            grads = gradients(where, x, wide_y, hidden, d_gate, d_up, spot, factors)
-            sent, kept["grads"] = lax.optimization_barrier((sent, grads))
+            kept["factors"] = RADIUS / (kept["norms"] + GAMMA)
+            grads = wide_gradients(x, d_gate, d_up, spot, kept["factors"])
+            sent, kept["grads"] = lax.optimization_barrier((sent, tuple(grads)))
         return sent
 
     left_line = ring_sum(far_up, far_down, left, "z", hook)
     right_out = kept["line"].astype(BF)
     left_out = direct_sum(left_line, "x")
     own_out = jnp.concatenate([left_out, right_out], axis=1)
+    own_out, late = lax.optimization_barrier((own_out, hidden))
+    grad_down = down_gradient(where, wide_y, late, kept["back"][2], kept["factors"])
     returned = lax.all_to_all(own_out.reshape(NE, CAP, width), EXPERT, split_axis=0, concat_axis=0, tiled=True)
     mixed = jnp.dot(placed_bf.T, returned.reshape(SLOTS, width), preferred_element_type=F32).astype(BF)
     norms = kept["norms"]
     own_norms = lax.dynamic_slice(norms.reshape(BLOCKS, 8), (ix * NZ + iz, 0), (1, EX_ROW))
-    return (mixed, own_norms, *kept["grads"])
+    return (mixed, own_norms, *kept["grads"], grad_down)
 
 
 def solution(mesh):

time: 244 us -> 258 us (1.057)
  waiting for transfers between devices: 79.9 us -> 85 us
  Pallas kernels: 37.5 us -> 41.2 us
  starting transfers between devices: 73.5 us -> 76.4 us
  other arithmetic: 7.62 us -> 10.3 us
    ppermute x35, waiting for transfers between devices: 50 us -> 58.5 us  [shift(): return lax.ppermute(a, axis, [(i, (i + step) % n) for i in range(n)])]
    pallas_call x1 -> x2, Pallas kernels: 12.1 us -> 17.9 us  [the longest x1 9.11 us: wide_gradients(): pl.pallas_call(wide_grads_kernel, grid=(D // COLS,), in_specs=[pl.BlockSp...]
    all_to_all x1, waiting for transfers between devices: 5.28 us -> 0.01 us  [on_device(): lax.all_to_all(own_out.reshape(NE, CAP, width), EXPERT, split_axis=0, con...]
    convert_element_type x0 -> x2, other arithmetic: none -> 3.45 us  [the longest x1 2.51 us: hook(): line = lax.optimization_barrier(line.astype(F32))]
    unnamed x42 -> x44, local copies, waits for them, and re-layouts: 6.06 us -> 6.05 us
  transfers between devices with their start and end apart: 41 -> 41, of which waited for: 20 -> 22; matrix products, arithmetic and copies ran while one was open for 6% -> 7% of each run, Pallas kernels for 15% -> 16%
where the time goes in v2:
time: 258 us; the launch traced here: 257 us
  waiting for transfers between devices  85 us (33%)
  starting transfers between devices  76.4 us (30%)
  Pallas kernels  41.2 us (16%)
  between operations  14.3 us (6%)
  blocking collectives  14 us (5%)
  local copies, waits for them, and re-layouts  13.7 us (5%)
  other arithmetic  10.3 us (4%)
    ppermute x35, waiting for transfers between devices, shift(): return lax.ppermute(a, axis, [(i, (i + step) % n) for i in range(n)])  58.5 us
    ppermute x35, starting transfers between devices, shift(): return lax.ppermute(a, axis, [(i, (i + step) % n) for i in range(n)])  56.2 us
    all_to_all x1, blocking collectives, on_device(): got = lax.all_to_all(send, EXPERT, split_axis=0, concat_axis=0, tiled=True)  14 us
    pallas_call x1, Pallas kernels, forward(): pl.pallas_call(forward_kernel, grid_spec=pltpu.PrefetchScalarGridSpec(num...  13.9 us
    reduce_scatter x1, waiting for transfers between devices, on_device(): lax.psum_scatter(right.reshape(ROWS, D - LEFT), 'x', scatter_dimension=0,...  13.1 us
    all_to_all x2, starting transfers between devices, spread(): lax.all_to_all(jnp.broadcast_to(a[None], (n,) + a.shape), axes, 0, 0, til...  12.5 us
    pallas_call x1, Pallas kernels, backward(): pl.pallas_call(backward_kernel, grid_spec=pltpu.PrefetchScalarGridSpec(nu...  9.42 us
    pallas_call x1, Pallas kernels, wide_gradients(): pl.pallas_call(wide_grads_kernel, grid=(D // COLS,), in_specs=[pl.BlockSp...  9.11 us
  transfers between devices with their start and end apart: 41, of which 22 were waited for; matrix products, arithmetic and copies ran while one was open for 7% of the time, Pallas kernels for 16%

profile of v2, /device:TPU:1, one launch (start us, length us, event | category | flops | bytes accessed | tf_op | source)
XLA Modules:
  0.0 257.4 jit_solution(18348141290274596777)
XLA Ops:
  7.2 0.8 copy.28
  8.6 0.7 multiply_add_fusion
  9.5 0.7 multiply_reduce_fusion
  10.4 1.1 convolution_convert_fusion
  12.0 14.0 %all_to_all.20 = bf16[8,8,3200]{2,1,0:T(8,128)(2,1)S(1)} all-to-all(bf16[8,8,3200]{2,1,0:T(8,128)(2,1)S(1)} %pad_maximum_fusion), channel_id=1, replica_groups=mesh['x'=4,'z'=8,'y'=4,'c'=2] {'y','c'}, dimensions={0} | all-to-all | bytes 819200 | tf_op jit(solution)/shard_map/all_to_all | solution.py:394
  26.7 0.8 concatenate.36
  27.7 2.6 collective-permute-start.1
  30.3 1.7 collective-permute-start.12
  32.0 4.0 %collective-permute-start.13 = (bf16[16,3072]{1,0:T(8,128)(2,1)S(1)}, bf16[16,3072]{1,0:T(8,128)(2,1)S(1)}, u32[]{:S(2)}, u32[]{:S(2)}) collective-permute-start(bf16[16,3072]{1,0:T(8,128)(2,1)S(1)} %slice.99), channel_id=1, source_target_pairs={{0,56},{8,0},{16,8},{24,16},{32,24},{40,32},{48,40},{56,48},{1,57}... | collective-permute-start | bytes 294920 | tf_op jit(solution)/shard_map/ppermute | solution.py:36
  36.0 0.6 constant_dynamic-update-slice_fusion
  36.7 2.8 %collective-permute-start.3 = (bf16[8,3072]{1,0:T(8,128)(2,1)S(1)}, bf16[8,3072]{1,0:T(8,128)(2,1)S(1)}, u32[]{:S(2)}, u32[]{:S(2)}) collective-permute-start(bf16[8,3072]{1,0:T(8,128)(2,1)S(1)} %slice.124), channel_id=1, source_target_pairs={{0,192},{64,0},{128,64},{192,128},{1,193},{65,1},{129,65},{193,129... | collective-permute-start | bytes 147464 | tf_op jit(solution)/shard_map/ppermute | solution.py:36
  39.7 2.7 %collective-permute-start.15 = (bf16[16,3072]{1,0:T(8,128)(2,1)S(1)}, bf16[16,3072]{1,0:T(8,128)(2,1)S(1)}, u32[]{:S(2)}, u32[]{:S(2)}) collective-permute-start(bf16[16,3072]{1,0:T(8,128)(2,1)S(1)} %collective-permute-done.13), channel_id=1, source_target_pairs={{0,56},{8,0},{16,8},{24,16},{32,24},{40,32},{48,40},{56,48},{1,57}... | collective-permute-start | bytes 294920 | tf_op jit(solution)/shard_map/ppermute | solution.py:36
  42.3 0.6 bitcast_dynamic-update-slice_fusion.5
  43.0 0.6 bitcast_dynamic-update-slice_fusion.4
  43.9 2.7 %collective-permute-start.5 = (bf16[4,16,3072]{2,1,0:T(8,128)(2,1)S(1)}, bf16[4,16,3072]{2,1,0:T(8,128)(2,1)S(1)}, u32[]{:S(2)}, u32[]{:S(2)}) collective-permute-start(bf16[4,16,3072]{2,1,0:T(8,128)(2,1)S(1)} %pad_maximum_fusion.1.refs_0_), channel_id=1, source_target_pairs={{0,56},{8,0},{16,8},{24,16},{32,24},{40,32},{48,40},{56,48},{1,57}... | collective-permute-start | bytes 1179656 | tf_op jit(solution)/shard_map/ppermute | solution.py:36
  46.6 2.7 %collective-permute-start.17 = (bf16[16,3072]{1,0:T(8,128)(2,1)S(1)}, bf16[16,3072]{1,0:T(8,128)(2,1)S(1)}, u32[]{:S(2)}, u32[]{:S(2)}) collective-permute-start(bf16[16,3072]{1,0:T(8,128)(2,1)S(1)} %collective-permute-done.15), channel_id=1, source_target_pairs={{0,56},{8,0},{16,8},{24,16},{32,24},{40,32},{48,40},{56,48},{1,57}... | collective-permute-start | bytes 294920 | tf_op jit(solution)/shard_map/ppermute | solution.py:36
  50.5 7.0 %collective-permute-done.17 = bf16[16,3072]{1,0:T(8,128)(2,1)S(1)} collective-permute-done((bf16[16,3072]{1,0:T(8,128)(2,1)S(1)}, bf16[16,3072]{1,0:T(8,128)(2,1)S(1)}, u32[]{:S(2)}, u32[]{:S(2)}) %collective-permute-start.17) | collective-permute-done | bytes 98336 | tf_op jit(solution)/shard_map/ppermute | solution.py:36
  57.5 3.6 %collective-permute-start.19 = (bf16[8,3072]{1,0:T(8,128)(2,1)S(1)}, bf16[8,3072]{1,0:T(8,128)(2,1)S(1)}, u32[]{:S(2)}, u32[]{:S(2)}) collective-permute-start(bf16[8,3072]{1,0:T(8,128)(2,1)S(1)} %slice.129), channel_id=1, source_target_pairs={{0,56},{8,0},{16,8},{24,16},{32,24},{40,32},{48,40},{56,48},{1,57}... | collective-permute-start | bytes 147464 | tf_op jit(solution)/shard_map/ppermute | solution.py:36
  61.4 0.7 bitcast_dynamic-update-slice_fusion.1
  63.3 2.3 collective-permute-done.18
  65.6 0.6 fusion.5.refs_9_
  66.2 4.3 %collective-permute-start.21 = (bf16[8,16,3072]{2,1,0:T(8,128)(2,1)}, bf16[8,16,3072]{2,1,0:T(8,128)(2,1)S(1)}, u32[]{:S(2)}, u32[]{:S(2)}) collective-permute-start(bf16[8,16,3072]{2,1,0:T(8,128)(2,1)} %fusion.5.refs_9_), channel_id=1, source_target_pairs={{0,192},{64,0},{128,64},{192,128},{1,193},{65,1},{129,65},{193,129... | collective-permute-start | bytes 2359304 | tf_op jit(solution)/shard_map/ppermute | solution.py:36
  70.5 2.7 %collective-permute-start.7 = (bf16[4,16,3072]{2,1,0:T(8,128)(2,1)S(1)}, bf16[4,16,3072]{2,1,0:T(8,128)(2,1)}, u32[]{:S(2)}, u32[]{:S(2)}) collective-permute-start(bf16[4,16,3072]{2,1,0:T(8,128)(2,1)S(1)} %collective-permute-done.5.refs_2_), channel_id=1, source_target_pairs={{0,56},{8,0},{16,8},{24,16},{32,24},{40,32},{48,40},{56,48},{1,57}... | collective-permute-start | bytes 1179656 | tf_op jit(solution)/shard_map/ppermute | solution.py:36
  73.2 5.4 %collective-permute-done.6.refs_3_ = bf16[4,16,3072]{2,1,0:T(8,128)(2,1)} collective-permute-done((bf16[4,16,3072]{2,1,0:T(8,128)(2,1)S(1)}, bf16[4,16,3072]{2,1,0:T(8,128)(2,1)}, u32[]{:S(2)}, u32[]{:S(2)}) %collective-permute-start.6) | collective-permute-done | bytes 393248 | tf_op jit(solution)/shard_map/ppermute | solution.py:36
  78.7 2.7 %collective-permute-start.9 = (bf16[4,16,3072]{2,1,0:T(8,128)(2,1)}, bf16[4,16,3072]{2,1,0:T(8,128)(2,1)}, u32[]{:S(2)}, u32[]{:S(2)}) collective-permute-start(bf16[4,16,3072]{2,1,0:T(8,128)(2,1)} %collective-permute-done.7.refs_4_), channel_id=1, source_target_pairs={{0,56},{8,0},{16,8},{24,16},{32,24},{40,32},{48,40},{56,48},{1,57}... | collective-permute-start | bytes 1179656 | tf_op jit(solution)/shard_map/ppermute | solution.py:36
  81.3 1.3 collective-permute-done.20.refs_10_
  83.0 3.5 %collective-permute-start.23 = (bf16[8,8,3072]{2,1,0:T(8,128)(2,1)S(1)}, bf16[8,8,3072]{2,1,0:T(8,128)(2,1)}, u32[]{:S(2)}, u32[]{:S(2)}) collective-permute-start(bf16[8,8,3072]{2,1,0:T(8,128)(2,1)S(1)} %slice.131), channel_id=1, source_target_pairs={{0,192},{64,0},{128,64},{192,128},{1,193},{65,1},{129,65},{193,129... | collective-permute-start | bytes 1179656 | tf_op jit(solution)/shard_map/ppermute | solution.py:36
  86.5 10.1 %collective-permute-done.8.refs_5_ = bf16[4,16,3072]{2,1,0:T(8,128)(2,1)S(1)} collective-permute-done((bf16[4,16,3072]{2,1,0:T(8,128)(2,1)}, bf16[4,16,3072]{2,1,0:T(8,128)(2,1)S(1)}, u32[]{:S(2)}, u32[]{:S(2)}) %collective-permute-start.8) | collective-permute-done | bytes 393248 | tf_op jit(solution)/shard_map/ppermute | solution.py:36
  96.7 1.0 slice.126
  97.7 3.2 %collective-permute-start.11 = (bf16[4,8,3072]{2,1,0:T(8,128)(2,1)S(1)}, bf16[4,8,3072]{2,1,0:T(8,128)(2,1)S(1)}, u32[]{:S(2)}, u32[]{:S(2)}) collective-permute-start(bf16[4,8,3072]{2,1,0:T(8,128)(2,1)S(1)} %slice.126), channel_id=1, source_target_pairs={{0,56},{8,0},{16,8},{24,16},{32,24},{40,32},{48,40},{56,48},{1,57}... | collective-permute-start | bytes 589832 | tf_op jit(solution)/shard_map/ppermute | solution.py:36
  100.9 0.7 pad_add_fusion.where_ref
  101.6 2.0 collective-permute-done.22.refs_12_
  103.8 4.1 %collective-permute-done.10.refs_7_ = bf16[4,8,3072]{2,1,0:T(8,128)(2,1)S(1)} collective-permute-done((bf16[4,8,3072]{2,1,0:T(8,128)(2,1)S(1)}, bf16[4,8,3072]{2,1,0:T(8,128)(2,1)S(1)}, u32[]{:S(2)}, u32[]{:S(2)}) %collective-permute-start.10) | collective-permute-done | bytes 196640 | tf_op jit(solution)/shard_map/ppermute | solution.py:36
  107.8 1.8 collective-permute-done.11.refs_8_
  109.7 0.7 copy-done.15
  110.3 13.9 %forward.1 = (bf16[4,8,32,3072]{3,2,1,0:T(8,128)(2,1)}, f32[1024,256]{1,0:T(8,128)}, f32[1024,256]{1,0:T(8,128)}, bf16[1024,256]{1,0:T(8,128)(2,1)}, bf16[2,32,1...) custom-call(s32[12]{0:T(128)} %pad_add_fusion.where_ref, ...), custom_call_target="tpu_custom_call" | custom-call | flops 4831838208 | bytes 20971520 | tf_op jit(solution)/shard_map/forward/pallas_call | solution.py:170
  124.3 8.1 %all-gather.3.cloned.1.call-done = bf16[1024,3328]{1,0:T(8,128)(2,1)} async-done(((bf16[32,3328]{1,0:T(8,128)(2,1)}), bf16[1024,3328]{1,0:T(8,128)(2,1)}) %all-gather.3.cloned.1.call-update) | async-done | bytes 6815760 | tf_op jit(solution)/shard_map/all_gather | solution.py:403
  132.4 4.1 %collective-permute-start.28 = (bf16[2,32,1536]{2,1,0:T(8,128)(2,1)}, bf16[2,32,1536]{2,1,0:T(8,128)(2,1)}, u32[]{:S(2)}, u32[]{:S(2)}) collective-permute-start(bf16[2,32,1536]{2,1,0:T(8,128)(2,1)} %get-tuple-element.51), channel_id=1, source_target_pairs={{0,56},{8,0},{16,8},{24,16},{32,24},{40,32},{48,40},{56,48},{1,57}... | collective-permute-start | bytes 589832 | tf_op jit(solution)/shard_map/ppermute | solution.py:36
  136.5 1.4 slice_bitcast_fusion.1
  137.9 9.4 %backward.1 = (bf16[1024,256]{1,0:T(8,128)(2,1)}, bf16[1024,256]{1,0:T(8,128)(2,1)}, f32[1024,1]{1,0:T(8,128)}, f32[2,128]{1,0:T(2,128)}) custom-call(s32[12]{0:T(128)} %pad_add_fusion.where_ref, bf16[32,32,3328]{2,1,0:T(8,128)(2,1)} %bitcast.53, bf16[32,32,3328]{2,1,0:T(8,128)(2,1)} %bitcast.54, bf16[1,256,3072]{2,1,0:T(8,128)(2,1)} %wd_ref.1, ...), custom_call_target="tpu_custom_call" | custom-call | flops 2415919104 | bytes 12582912 | tf_op jit(solution)/shard_map/backward/pallas_call | solution.py:254
  147.3 1.3 broadcast_in_dim.12
  148.7 7.5 %all-to-all-start.1 = ((f32[32,2,128]{2,1,0:T(2,128)}), f32[32,2,128]{2,1,0:T(2,128)S(1)}, u32[]{:S(2)}, u32[]{:S(2)}) async-start(f32[32,2,128]{2,1,0:T(2,128)} %broadcast_in_dim.12), calls=%async_computation.1 | async-start | bytes 65536 | tf_op jit(solution)/shard_map/all_to_all | solution.py:88
  156.3 1.0 add_convert_fusion.5
  157.4 2.5 collective-permute-start.29
  160.1 5.0 %all-to-all-done.1 = f32[32,2,128]{2,1,0:T(2,128)S(1)} async-done(((f32[32,2,128]{2,1,0:T(2,128)}), f32[32,2,128]{2,1,0:T(2,128)S(1)}, u32[]{:S(2)}, u32[]{:S(2)}) %all-to-all-start.1) | async-done | bytes 32800 | tf_op jit(solution)/shard_map/all_to_all | solution.py:88
  165.1 13.1 %reduce-scatter.3.cloned.1.call-done = bf16[256,1536]{1,0:T(8,128)(2,1)} async-done(((bf16[1024,1536]{1,0:T(8,128)(2,1)}), bf16[256,1536]{1,0:T(8,128)(2,1)}) %reduce-scatter.3.cloned.1.call-update) | async-done | bytes 786448 | tf_op jit(solution)/shard_map/reduce_scatter | solution.py:412
  178.3 2.5 convert_element_type.166
  181.4 4.9 %all-to-all-start.2 = ((f32[8,2,128]{2,1,0:T(2,128)}), f32[8,2,128]{2,1,0:T(2,128)S(1)}, u32[]{:S(2)}, u32[]{:S(2)}) async-start(f32[8,2,128]{2,1,0:T(2,128)} %broadcast_in_dim.13), calls=%async_computation.3 | async-start | bytes 16384 | tf_op jit(solution)/shard_map/all_to_all | solution.py:88
  186.5 3.1 %collective-permute-start.30 = (bf16[4,32,1536]{2,1,0:T(8,128)(2,1)S(1)}, bf16[4,32,1536]{2,1,0:T(8,128)(2,1)S(1)}, u32[]{:S(2)}, u32[]{:S(2)}) collective-permute-start(bf16[4,32,1536]{2,1,0:T(8,128)(2,1)S(1)} %add_convert_fusion.2), channel_id=1, source_target_pairs={{0,56},{8,0},{16,8},{24,16},{32,24},{40,32},{48,40},{56,48},{1,57}... | collective-permute-start | bytes 1179656 | tf_op jit(solution)/shard_map/ppermute | solution.py:36
  189.6 1.1 add_convert_fusion.4
  191.0 11.2 %collective-permute-done.30 = bf16[4,32,1536]{2,1,0:T(8,128)(2,1)S(1)} collective-permute-done((bf16[4,32,1536]{2,1,0:T(8,128)(2,1)S(1)}, bf16[4,32,1536]{2,1,0:T(8,128)(2,1)S(1)}, u32[]{:S(2)}, u32[]{:S(2)}) %collective-permute-start.30) | collective-permute-done | bytes 393248 | tf_op jit(solution)/shard_map/ppermute | solution.py:36
  202.3 3.7 %collective-permute-start.31 = (bf16[4,32,1536]{2,1,0:T(8,128)(2,1)S(1)}, bf16[4,32,1536]{2,1,0:T(8,128)(2,1)S(1)}, u32[]{:S(2)}, u32[]{:S(2)}) collective-permute-start(bf16[4,32,1536]{2,1,0:T(8,128)(2,1)S(1)} %add_convert_fusion.1), channel_id=1, source_target_pairs={{0,56},{8,0},{16,8},{24,16},{32,24},{40,32},{48,40},{56,48},{1,57}... | collective-permute-start | bytes 1179656 | tf_op jit(solution)/shard_map/ppermute | solution.py:36
  206.0 2.4 collective-permute-done.26
  209.2 9.1 %wide_gradients.1 = (bf16[1,3072,256]{2,1,0:T(8,128)(2,1)}, bf16[1,3072,256]{2,1,0:T(8,128)(2,1)}) custom-call(bf16[4,8,32,3072]{3,2,1,0:T(8,128)(2,1)} %get-tuple-element.54.x_ref, bf16[1024,256]{1,0:T(8,128)(2,1)} %get-tuple-element.55.dg_ref, bf16[1024,256]{1,0:T(8,128)(2,1)} %get-tuple-element.56.du_ref, f32[1024,1]{1,0:T(8,128)} %get-tuple-element.57.spot_ref, ...), custom_call_target="tpu_custom_call" | custom-call | flops 3221225472 | bytes 11534336 | tf_op jit(solution)/shard_map/wide_gradients/pallas_call | solution.py:307
  218.3 3.2 %collective-permute-done.31 = bf16[4,32,1536]{2,1,0:T(8,128)(2,1)S(1)} collective-permute-done((bf16[4,32,1536]{2,1,0:T(8,128)(2,1)S(1)}, bf16[4,32,1536]{2,1,0:T(8,128)(2,1)S(1)}, u32[]{:S(2)}, u32[]{:S(2)}) %collective-permute-start.31) | collective-permute-done | bytes 393248 | tf_op jit(solution)/shard_map/ppermute | solution.py:36
  221.5 3.7 %collective-permute-done.27 = bf16[4,32,1536]{2,1,0:T(8,128)(2,1)S(1)} collective-permute-done((bf16[4,32,1536]{2,1,0:T(8,128)(2,1)S(1)}, bf16[4,32,1536]{2,1,0:T(8,128)(2,1)S(1)}, u32[]{:S(2)}, u32[]{:S(2)}) %collective-permute-start.27) | collective-permute-done | bytes 393248 | tf_op jit(solution)/shard_map/ppermute | solution.py:36
  225.6 2.7 %collective-permute-start.32 = (bf16[32,1536]{1,0:T(8,128)(2,1)S(1)}, bf16[32,1536]{1,0:T(8,128)(2,1)S(1)}, u32[]{:S(2)}, u32[]{:S(2)}) collective-permute-start(bf16[32,1536]{1,0:T(8,128)(2,1)S(1)} %get-tuple-element.78), channel_id=1, source_target_pairs={{0,192},{64,0},{128,64},{192,128},{1,193},{65,1},{129,65},{193,129... | collective-permute-start | bytes 294920 | tf_op jit(solution)/shard_map/ppermute | solution.py:36
  228.3 2.2 collective-permute-done.34
  230.5 0.7 collective-permute-done.33
  231.4 0.9 convert_element_type.167
  232.3 0.8 reshape.73
  233.1 7.6 %all-to-all-start.3 = ((bf16[8,4,3072]{2,1,0:T(4,128)(2,1)}), bf16[8,4,3072]{2,1,0:T(4,128)(2,1)S(1)}, u32[]{:S(2)}, u32[]{:S(2)}) async-start(bf16[8,4,3072]{2,1,0:T(4,128)(2,1)} %reshape.73), calls=%async_computation.5 | async-start | bytes 393216 | tf_op jit(solution)/shard_map/all_to_all | solution.py:440
  241.2 8.8 %down_gradient.1 = bf16[1,256,3072]{2,1,0:T(8,128)(2,1)} custom-call(s32[12]{0:T(128)} %pad_add_fusion.where_ref, bf16[32,32,3328]{2,1,0:T(8,128)(2,1)} %bitcast.55, bf16[1024,256]{1,0:T(8,128)(2,1)} %get-tuple-element.66.hidden_ref, f32[1024,1]{1,0:T(8,128)} %get-tuple-element.57.spot_ref, f32[2,128]{1,0:T(2,128)} %add_divide_fusion.factor_ref), custom_call_target="tpu_custom_call" | custom-call | flops 1610612736 | bytes 8388608 | tf_op jit(solution)/shard_map/down_gradient/pallas_call | solution.py:346
  250.1 0.8 convolution_convert_fusion.2
  (142 shorter events, 9.4 us)
Async XLA Ops:
  7.2 3.0 %copy-start = (bf16[12,3072]{1,0:T(8,128)(2,1)S(1)}, bf16[12,3072]{1,0:T(8,128)(2,1)}, u32[]{:S(2)}) copy-start(bf16[12,3072]{1,0:T(8,128)(2,1)} %param.9) | copy-start | bytes 221188
  7.2 125.2 %all-gather.3.cloned.1.call-start = ((), (), s32[]{:S(2)}) async-start(), calls=%async_computation.8 | async-start | bytes 7028736 | tf_op jit(solution)/shard_map/all_gather | solution.py:403
  27.5 150.8 %reduce-scatter.3.cloned.1.call-start = ((), (), s32[]{:S(2)}) async-start(), calls=%async_computation.6 | async-start | bytes 3932160 | tf_op jit(solution)/shard_map/reduce_scatter | solution.py:412
  27.7 9.0 %collective-permute-start.1 = (bf16[16,3072]{1,0:T(8,128)(2,1)S(1)}, bf16[16,3072]{1,0:T(8,128)(2,1)S(1)}, u32[]{:S(2)}, u32[]{:S(2)}) collective-permute-start(bf16[16,3072]{1,0:T(8,128)(2,1)S(1)} %slice.93), channel_id=1, source_target_pairs={{0,192},{64,0},{128,64},{192,128},{1,193},{65,1},{129,65},{193,129... | collective-permute-start | bytes 294920 | tf_op jit(solution)/shard_map/ppermute | solution.py:36
  30.2 9.3 %collective-permute-start = (bf16[16,3072]{1,0:T(8,128)(2,1)S(1)}, bf16[16,3072]{1,0:T(8,128)(2,1)S(1)}, u32[]{:S(2)}, u32[]{:S(2)}) collective-permute-start(bf16[16,3072]{1,0:T(8,128)(2,1)S(1)} %slice.93), channel_id=1, source_target_pairs={{0,64},{64,128},{128,192},{192,0},{1,65},{65,129},{129,193},{193,1... | collective-permute-start | bytes 294920 | tf_op jit(solution)/shard_map/ppermute | solution.py:36
  30.3 9.3 %collective-permute-start.12 = (bf16[16,3072]{1,0:T(8,128)(2,1)S(1)}, bf16[16,3072]{1,0:T(8,128)(2,1)S(1)}, u32[]{:S(2)}, u32[]{:S(2)}) collective-permute-start(bf16[16,3072]{1,0:T(8,128)(2,1)S(1)} %slice.99), channel_id=1, source_target_pairs={{0,8},{8,16},{16,24},{24,32},{32,40},{40,48},{48,56},{56,0},{1,9},... | collective-permute-start | bytes 294920 | tf_op jit(solution)/shard_map/ppermute | solution.py:36
  32.0 7.7 %collective-permute-start.13 = (bf16[16,3072]{1,0:T(8,128)(2,1)S(1)}, bf16[16,3072]{1,0:T(8,128)(2,1)S(1)}, u32[]{:S(2)}, u32[]{:S(2)}) collective-permute-start(bf16[16,3072]{1,0:T(8,128)(2,1)S(1)} %slice.99), channel_id=1, source_target_pairs={{0,56},{8,0},{16,8},{24,16},{32,24},{40,32},{48,40},{56,48},{1,57}... | collective-permute-start | bytes 294920 | tf_op jit(solution)/shard_map/ppermute | solution.py:36
  36.7 6.9 %collective-permute-start.3 = (bf16[8,3072]{1,0:T(8,128)(2,1)S(1)}, bf16[8,3072]{1,0:T(8,128)(2,1)S(1)}, u32[]{:S(2)}, u32[]{:S(2)}) collective-permute-start(bf16[8,3072]{1,0:T(8,128)(2,1)S(1)} %slice.124), channel_id=1, source_target_pairs={{0,192},{64,0},{128,64},{192,128},{1,193},{65,1},{129,65},{193,129... | collective-permute-start | bytes 147464 | tf_op jit(solution)/shard_map/ppermute | solution.py:36
  39.5 4.2 %collective-permute-start.2 = (bf16[8,3072]{1,0:T(8,128)(2,1)S(1)}, bf16[8,3072]{1,0:T(8,128)(2,1)S(1)}, u32[]{:S(2)}, u32[]{:S(2)}) collective-permute-start(bf16[8,3072]{1,0:T(8,128)(2,1)S(1)} %slice.123), channel_id=1, source_target_pairs={{0,64},{64,128},{128,192},{192,0},{1,65},{65,129},{129,193},{193,1... | collective-permute-start | bytes 147464 | tf_op jit(solution)/shard_map/ppermute | solution.py:36
  39.6 7.0 %collective-permute-start.14 = (bf16[16,3072]{1,0:T(8,128)(2,1)S(1)}, bf16[16,3072]{1,0:T(8,128)(2,1)S(1)}, u32[]{:S(2)}, u32[]{:S(2)}) collective-permute-start(bf16[16,3072]{1,0:T(8,128)(2,1)S(1)} %collective-permute-done.12), channel_id=1, source_target_pairs={{0,8},{8,16},{16,24},{24,32},{32,40},{40,48},{48,56},{56,0},{1,9},... | collective-permute-start | bytes 294920 | tf_op jit(solution)/shard_map/ppermute | solution.py:36
  39.7 6.9 %collective-permute-start.15 = (bf16[16,3072]{1,0:T(8,128)(2,1)S(1)}, bf16[16,3072]{1,0:T(8,128)(2,1)S(1)}, u32[]{:S(2)}, u32[]{:S(2)}) collective-permute-start(bf16[16,3072]{1,0:T(8,128)(2,1)S(1)} %collective-permute-done.13), channel_id=1, source_target_pairs={{0,56},{8,0},{16,8},{24,16},{32,24},{40,32},{48,40},{56,48},{1,57}... | collective-permute-start | bytes 294920 | tf_op jit(solution)/shard_map/ppermute | solution.py:36
  43.8 52.8 %copy-start.8 = (bf16[4,16,3072]{2,1,0:T(8,128)(2,1)}, bf16[4,16,3072]{2,1,0:T(8,128)(2,1)S(1)}, u32[]{:S(2)}) copy-start(bf16[4,16,3072]{2,1,0:T(8,128)(2,1)S(1)} %pad_maximum_fusion.1.refs_0_) | copy-start | bytes 1179652
  43.8 42.7 %copy-start.17 = (s32[8]{0:T(128)S(1)}, s32[8]{0:T(128)}, u32[]{:S(2)}) copy-start(s32[8]{0:T(128)} %constant.61.clone) | copy-start | bytes 100
  43.8 26.7 %collective-permute-start.4 = (bf16[4,16,3072]{2,1,0:T(8,128)(2,1)S(1)}, bf16[4,16,3072]{2,1,0:T(8,128)(2,1)S(1)}, u32[]{:S(2)}, u32[]{:S(2)}) collective-permute-start(bf16[4,16,3072]{2,1,0:T(8,128)(2,1)S(1)} %pad_maximum_fusion.1.refs_0_), channel_id=1, source_target_pairs={{0,8},{8,16},{16,24},{24,32},{32,40},{40,48},{48,56},{56,0},{1,9},... | collective-permute-start | bytes 1179656 | tf_op jit(solution)/shard_map/ppermute | solution.py:36
  43.9 26.6 %collective-permute-start.5 = (bf16[4,16,3072]{2,1,0:T(8,128)(2,1)S(1)}, bf16[4,16,3072]{2,1,0:T(8,128)(2,1)S(1)}, u32[]{:S(2)}, u32[]{:S(2)}) collective-permute-start(bf16[4,16,3072]{2,1,0:T(8,128)(2,1)S(1)} %pad_maximum_fusion.1.refs_0_), channel_id=1, source_target_pairs={{0,56},{8,0},{16,8},{24,16},{32,24},{40,32},{48,40},{56,48},{1,57}... | collective-permute-start | bytes 1179656 | tf_op jit(solution)/shard_map/ppermute | solution.py:36
  46.6 14.6 %collective-permute-start.16 = (bf16[16,3072]{1,0:T(8,128)(2,1)S(1)}, bf16[16,3072]{1,0:T(8,128)(2,1)S(1)}, u32[]{:S(2)}, u32[]{:S(2)}) collective-permute-start(bf16[16,3072]{1,0:T(8,128)(2,1)S(1)} %collective-permute-done.14), channel_id=1, source_target_pairs={{0,8},{8,16},{16,24},{24,32},{32,40},{40,48},{48,56},{56,0},{1,9},... | collective-permute-start | bytes 294920 | tf_op jit(solution)/shard_map/ppermute | solution.py:36
  46.6 10.9 %collective-permute-start.17 = (bf16[16,3072]{1,0:T(8,128)(2,1)S(1)}, bf16[16,3072]{1,0:T(8,128)(2,1)S(1)}, u32[]{:S(2)}, u32[]{:S(2)}) collective-permute-start(bf16[16,3072]{1,0:T(8,128)(2,1)S(1)} %collective-permute-done.15), channel_id=1, source_target_pairs={{0,56},{8,0},{16,8},{24,16},{32,24},{40,32},{48,40},{56,48},{1,57}... | collective-permute-start | bytes 294920 | tf_op jit(solution)/shard_map/ppermute | solution.py:36
  50.5 50.4 %copy-start.16 = (s32[4]{0:T(128)S(1)}, s32[4]{0:T(128)}, u32[]{:S(2)}) copy-start(s32[4]{0:T(128)} %constant.60.clone) | copy-start | bytes 52
  57.5 5.8 %collective-permute-start.19 = (bf16[8,3072]{1,0:T(8,128)(2,1)S(1)}, bf16[8,3072]{1,0:T(8,128)(2,1)S(1)}, u32[]{:S(2)}, u32[]{:S(2)}) collective-permute-start(bf16[8,3072]{1,0:T(8,128)(2,1)S(1)} %slice.129), channel_id=1, source_target_pairs={{0,56},{8,0},{16,8},{24,16},{32,24},{40,32},{48,40},{56,48},{1,57}... | collective-permute-start | bytes 147464 | tf_op jit(solution)/shard_map/ppermute | solution.py:36
  61.1 4.4 %collective-permute-start.18 = (bf16[8,3072]{1,0:T(8,128)(2,1)S(1)}, bf16[8,3072]{1,0:T(8,128)(2,1)S(1)}, u32[]{:S(2)}, u32[]{:S(2)}) collective-permute-start(bf16[8,3072]{1,0:T(8,128)(2,1)S(1)} %slice.128), channel_id=1, source_target_pairs={{0,8},{8,16},{16,24},{24,32},{32,40},{40,48},{48,56},{56,0},{1,9},... | collective-permute-start | bytes 147464 | tf_op jit(solution)/shard_map/ppermute | solution.py:36
  66.2 16.5 %collective-permute-start.20 = (bf16[8,16,3072]{2,1,0:T(8,128)(2,1)}, bf16[8,16,3072]{2,1,0:T(8,128)(2,1)S(1)}, u32[]{:S(2)}, u32[]{:S(2)}) collective-permute-start(bf16[8,16,3072]{2,1,0:T(8,128)(2,1)} %fusion.5.refs_9_), channel_id=1, source_target_pairs={{0,64},{64,128},{128,192},{192,0},{1,65},{65,129},{129,193},{193,1... | collective-permute-start | bytes 2359304 | tf_op jit(solution)/shard_map/ppermute | solution.py:36
  66.2 16.7 %collective-permute-start.21 = (bf16[8,16,3072]{2,1,0:T(8,128)(2,1)}, bf16[8,16,3072]{2,1,0:T(8,128)(2,1)S(1)}, u32[]{:S(2)}, u32[]{:S(2)}) collective-permute-start(bf16[8,16,3072]{2,1,0:T(8,128)(2,1)} %fusion.5.refs_9_), channel_id=1, source_target_pairs={{0,192},{64,0},{128,64},{192,128},{1,193},{65,1},{129,65},{193,129... | collective-permute-start | bytes 2359304 | tf_op jit(solution)/shard_map/ppermute | solution.py:36
  70.5 2.7 %copy-start.12 = (bf16[4,16,3072]{2,1,0:T(8,128)(2,1)}, bf16[4,16,3072]{2,1,0:T(8,128)(2,1)S(1)}, u32[]{:S(2)}) copy-start(bf16[4,16,3072]{2,1,0:T(8,128)(2,1)S(1)} %collective-permute-done.4.refs_1_) | copy-start | bytes 1179652
  70.5 8.1 %collective-permute-start.6 = (bf16[4,16,3072]{2,1,0:T(8,128)(2,1)S(1)}, bf16[4,16,3072]{2,1,0:T(8,128)(2,1)}, u32[]{:S(2)}, u32[]{:S(2)}) collective-permute-start(bf16[4,16,3072]{2,1,0:T(8,128)(2,1)S(1)} %collective-permute-done.4.refs_1_), channel_id=1, source_target_pairs={{0,8},{8,16},{16,24},{24,32},{32,40},{40,48},{48,56},{56,0},{1,9},... | collective-permute-start | bytes 1179656 | tf_op jit(solution)/shard_map/ppermute | solution.py:36
  70.5 10.8 %copy-start.13 = (bf16[4,16,3072]{2,1,0:T(8,128)(2,1)}, bf16[4,16,3072]{2,1,0:T(8,128)(2,1)S(1)}, u32[]{:S(2)}) copy-start(bf16[4,16,3072]{2,1,0:T(8,128)(2,1)S(1)} %collective-permute-done.5.refs_2_) | copy-start | bytes 1179652
  70.5 8.1 %collective-permute-start.7 = (bf16[4,16,3072]{2,1,0:T(8,128)(2,1)S(1)}, bf16[4,16,3072]{2,1,0:T(8,128)(2,1)}, u32[]{:S(2)}, u32[]{:S(2)}) collective-permute-start(bf16[4,16,3072]{2,1,0:T(8,128)(2,1)S(1)} %collective-permute-done.5.refs_2_), channel_id=1, source_target_pairs={{0,56},{8,0},{16,8},{24,16},{32,24},{40,32},{48,40},{56,48},{1,57}... | collective-permute-start | bytes 1179656 | tf_op jit(solution)/shard_map/ppermute | solution.py:36
  78.7 17.9 %collective-permute-start.8 = (bf16[4,16,3072]{2,1,0:T(8,128)(2,1)}, bf16[4,16,3072]{2,1,0:T(8,128)(2,1)S(1)}, u32[]{:S(2)}, u32[]{:S(2)}) collective-permute-start(bf16[4,16,3072]{2,1,0:T(8,128)(2,1)} %collective-permute-done.6.refs_3_), channel_id=1, source_target_pairs={{0,8},{8,16},{16,24},{24,32},{32,40},{40,48},{48,56},{56,0},{1,9},... | collective-permute-start | bytes 1179656 | tf_op jit(solution)/shard_map/ppermute | solution.py:36
  78.7 18.0 %collective-permute-start.9 = (bf16[4,16,3072]{2,1,0:T(8,128)(2,1)}, bf16[4,16,3072]{2,1,0:T(8,128)(2,1)}, u32[]{:S(2)}, u32[]{:S(2)}) collective-permute-start(bf16[4,16,3072]{2,1,0:T(8,128)(2,1)} %collective-permute-done.7.refs_4_), channel_id=1, source_target_pairs={{0,56},{8,0},{16,8},{24,16},{32,24},{40,32},{48,40},{56,48},{1,57}... | collective-permute-start | bytes 1179656 | tf_op jit(solution)/shard_map/ppermute | solution.py:36
  82.7 27.0 %copy-start.9 = (bf16[8,16,3072]{2,1,0:T(8,128)(2,1)}, bf16[8,16,3072]{2,1,0:T(8,128)(2,1)S(1)}, u32[]{:S(2)}) copy-start(bf16[8,16,3072]{2,1,0:T(8,128)(2,1)S(1)} %collective-permute-done.20.refs_10_) | copy-start | bytes 2359300
  82.7 20.9 %collective-permute-start.22 = (bf16[8,8,3072]{2,1,0:T(8,128)(2,1)S(1)}, bf16[8,8,3072]{2,1,0:T(8,128)(2,1)}, u32[]{:S(2)}, u32[]{:S(2)}) collective-permute-start(bf16[8,8,3072]{2,1,0:T(8,128)(2,1)S(1)} %slice.130), channel_id=1, source_target_pairs={{0,64},{64,128},{128,192},{192,0},{1,65},{65,129},{129,193},{193,1... | collective-permute-start | bytes 1179656 | tf_op jit(solution)/shard_map/ppermute | solution.py:36
  82.9 26.7 %copy-start.10 = (bf16[8,16,3072]{2,1,0:T(8,128)(2,1)}, bf16[8,16,3072]{2,1,0:T(8,128)(2,1)S(1)}, u32[]{:S(2)}) copy-start(bf16[8,16,3072]{2,1,0:T(8,128)(2,1)S(1)} %collective-permute-done.21.refs_11_) | copy-start | bytes 2359300
  83.0 20.8 %collective-permute-start.23 = (bf16[8,8,3072]{2,1,0:T(8,128)(2,1)S(1)}, bf16[8,8,3072]{2,1,0:T(8,128)(2,1)}, u32[]{:S(2)}, u32[]{:S(2)}) collective-permute-start(bf16[8,8,3072]{2,1,0:T(8,128)(2,1)S(1)} %slice.131), channel_id=1, source_target_pairs={{0,192},{64,0},{128,64},{192,128},{1,193},{65,1},{129,65},{193,129... | collective-permute-start | bytes 1179656 | tf_op jit(solution)/shard_map/ppermute | solution.py:36
  96.6 13.1 %copy-start.11 = (bf16[4,16,3072]{2,1,0:T(8,128)(2,1)}, bf16[4,16,3072]{2,1,0:T(8,128)(2,1)S(1)}, u32[]{:S(2)}) copy-start(bf16[4,16,3072]{2,1,0:T(8,128)(2,1)S(1)} %collective-permute-done.8.refs_5_) | copy-start | bytes 1179652
  96.6 11.2 %collective-permute-start.10 = (bf16[4,8,3072]{2,1,0:T(8,128)(2,1)S(1)}, bf16[4,8,3072]{2,1,0:T(8,128)(2,1)S(1)}, u32[]{:S(2)}, u32[]{:S(2)}) collective-permute-start(bf16[4,8,3072]{2,1,0:T(8,128)(2,1)S(1)} %slice.125), channel_id=1, source_target_pairs={{0,8},{8,16},{16,24},{24,32},{32,40},{40,48},{48,56},{56,0},{1,9},... | collective-permute-start | bytes 589832 | tf_op jit(solution)/shard_map/ppermute | solution.py:36
  97.7 11.9 %collective-permute-start.11 = (bf16[4,8,3072]{2,1,0:T(8,128)(2,1)S(1)}, bf16[4,8,3072]{2,1,0:T(8,128)(2,1)S(1)}, u32[]{:S(2)}, u32[]{:S(2)}) collective-permute-start(bf16[4,8,3072]{2,1,0:T(8,128)(2,1)S(1)} %slice.126), channel_id=1, source_target_pairs={{0,56},{8,0},{16,8},{24,16},{32,24},{40,32},{48,40},{56,48},{1,57}... | collective-permute-start | bytes 589832 | tf_op jit(solution)/shard_map/ppermute | solution.py:36
  107.8 1.8 copy-start.14
  109.7 0.7 copy-start.15
  132.4 4.1 %copy-start.1 = (bf16[7,4,32,1536]{3,2,1,0:T(8,128)(2,1)S(1)}, bf16[7,4,32,1536]{3,2,1,0:T(8,128)(2,1)}, u32[]{:S(2)}) copy-start(bf16[7,4,32,1536]{3,2,1,0:T(8,128)(2,1)} %get-tuple-element.37) | copy-start | bytes 8257540
  132.4 23.9 %collective-permute-start.28 = (bf16[2,32,1536]{2,1,0:T(8,128)(2,1)}, bf16[2,32,1536]{2,1,0:T(8,128)(2,1)}, u32[]{:S(2)}, u32[]{:S(2)}) collective-permute-start(bf16[2,32,1536]{2,1,0:T(8,128)(2,1)} %get-tuple-element.51), channel_id=1, source_target_pairs={{0,56},{8,0},{16,8},{24,16},{32,24},{40,32},{48,40},{56,48},{1,57}... | collective-permute-start | bytes 589832 | tf_op jit(solution)/shard_map/ppermute | solution.py:36
  136.5 23.4 %collective-permute-start.24 = (bf16[2,32,1536]{2,1,0:T(8,128)(2,1)}, bf16[2,32,1536]{2,1,0:T(8,128)(2,1)S(1)}, u32[]{:S(2)}, u32[]{:S(2)}) collective-permute-start(bf16[2,32,1536]{2,1,0:T(8,128)(2,1)} %get-tuple-element.36), channel_id=1, source_target_pairs={{0,8},{8,16},{16,24},{24,32},{32,40},{40,48},{48,56},{56,0},{1,9},... | collective-permute-start | bytes 589832 | tf_op jit(solution)/shard_map/ppermute | solution.py:36
  137.9 18.4 %copy-start.7 = (bf16[4,32,1536]{2,1,0:T(8,128)(2,1)S(1)}, bf16[4,32,1536]{2,1,0:T(8,128)(2,1)}, u32[]{:S(2)}) copy-start(bf16[4,32,1536]{2,1,0:T(8,128)(2,1)} %get-tuple-element.50) | copy-start | bytes 1179652
  147.3 12.5 %copy-start.6 = (bf16[4,32,1536]{2,1,0:T(8,128)(2,1)S(1)}, bf16[4,32,1536]{2,1,0:T(8,128)(2,1)}, u32[]{:S(2)}) copy-start(bf16[4,32,1536]{2,1,0:T(8,128)(2,1)} %get-tuple-element.44) | copy-start | bytes 1179652
  148.7 16.4 %all-to-all-start.1 = ((f32[32,2,128]{2,1,0:T(2,128)}), f32[32,2,128]{2,1,0:T(2,128)S(1)}, u32[]{:S(2)}, u32[]{:S(2)}) async-start(f32[32,2,128]{2,1,0:T(2,128)} %broadcast_in_dim.12), calls=%async_computation.1 | async-start | bytes 65536 | tf_op jit(solution)/shard_map/all_to_all | solution.py:88
  156.2 75.1 %reduce-scatter.5.cloned.1.call-start = ((), (), s32[]{:S(2)}) async-start(), calls=%async_computation.7 | async-start | bytes 1769472 | tf_op jit(solution)/shard_map/reduce_scatter | solution.py:423
  157.4 29.0 %collective-permute-start.29 = (bf16[4,32,1536]{2,1,0:T(8,128)(2,1)S(1)}, bf16[4,32,1536]{2,1,0:T(8,128)(2,1)S(1)}, u32[]{:S(2)}, u32[]{:S(2)}) collective-permute-start(bf16[4,32,1536]{2,1,0:T(8,128)(2,1)S(1)} %pad_maximum_fusion.3), channel_id=1, source_target_pairs={{0,56},{8,0},{16,8},{24,16},{32,24},{40,32},{48,40},{56,48},{1,57}... | collective-permute-start | bytes 1179656 | tf_op jit(solution)/shard_map/ppermute | solution.py:36
  160.0 29.5 %collective-permute-start.25 = (bf16[4,32,1536]{2,1,0:T(8,128)(2,1)S(1)}, bf16[4,32,1536]{2,1,0:T(8,128)(2,1)}, u32[]{:S(2)}, u32[]{:S(2)}) collective-permute-start(bf16[4,32,1536]{2,1,0:T(8,128)(2,1)S(1)} %pad_maximum_fusion.2), channel_id=1, source_target_pairs={{0,8},{8,16},{16,24},{24,32},{32,40},{40,48},{48,56},{56,0},{1,9},... | collective-permute-start | bytes 1179656 | tf_op jit(solution)/shard_map/ppermute | solution.py:36
  178.3 8.1 %copy-start.5 = (bf16[4,32,1536]{2,1,0:T(8,128)(2,1)S(1)}, bf16[4,32,1536]{2,1,0:T(8,128)(2,1)}, u32[]{:S(2)}) copy-start(bf16[4,32,1536]{2,1,0:T(8,128)(2,1)} %get-tuple-element.52) | copy-start | bytes 1179652
  180.8 8.8 %copy-start.4 = (bf16[4,32,1536]{2,1,0:T(8,128)(2,1)S(1)}, bf16[4,32,1536]{2,1,0:T(8,128)(2,1)}, u32[]{:S(2)}) copy-start(bf16[4,32,1536]{2,1,0:T(8,128)(2,1)} %get-tuple-element.47) | copy-start | bytes 1179652
  180.8 21.4 %copy-start.3 = (bf16[4,32,1536]{2,1,0:T(8,128)(2,1)S(1)}, bf16[4,32,1536]{2,1,0:T(8,128)(2,1)}, u32[]{:S(2)}) copy-start(bf16[4,32,1536]{2,1,0:T(8,128)(2,1)} %get-tuple-element.53) | copy-start | bytes 1179652
  181.4 9.5 %all-to-all-start.2 = ((f32[8,2,128]{2,1,0:T(2,128)}), f32[8,2,128]{2,1,0:T(2,128)S(1)}, u32[]{:S(2)}, u32[]{:S(2)}) async-start(f32[8,2,128]{2,1,0:T(2,128)} %broadcast_in_dim.13), calls=%async_computation.3 | async-start | bytes 16384 | tf_op jit(solution)/shard_map/all_to_all | solution.py:88
  186.3 22.1 %copy-start.2 = (bf16[4,32,1536]{2,1,0:T(8,128)(2,1)S(1)}, bf16[4,32,1536]{2,1,0:T(8,128)(2,1)}, u32[]{:S(2)}) copy-start(bf16[4,32,1536]{2,1,0:T(8,128)(2,1)} %get-tuple-element.49) | copy-start | bytes 1179652
  186.5 15.7 %collective-permute-start.30 = (bf16[4,32,1536]{2,1,0:T(8,128)(2,1)S(1)}, bf16[4,32,1536]{2,1,0:T(8,128)(2,1)S(1)}, u32[]{:S(2)}, u32[]{:S(2)}) collective-permute-start(bf16[4,32,1536]{2,1,0:T(8,128)(2,1)S(1)} %add_convert_fusion.2), channel_id=1, source_target_pairs={{0,56},{8,0},{16,8},{24,16},{32,24},{40,32},{48,40},{56,48},{1,57}... | collective-permute-start | bytes 1179656 | tf_op jit(solution)/shard_map/ppermute | solution.py:36
  190.7 17.7 %collective-permute-start.26 = (bf16[4,32,1536]{2,1,0:T(8,128)(2,1)S(1)}, bf16[4,32,1536]{2,1,0:T(8,128)(2,1)S(1)}, u32[]{:S(2)}, u32[]{:S(2)}) collective-permute-start(bf16[4,32,1536]{2,1,0:T(8,128)(2,1)S(1)} %add_convert_fusion.4), channel_id=1, source_target_pairs={{0,8},{8,16},{16,24},{24,32},{32,40},{40,48},{48,56},{56,0},{1,9},... | collective-permute-start | bytes 1179656 | tf_op jit(solution)/shard_map/ppermute | solution.py:36
  202.3 19.2 %collective-permute-start.31 = (bf16[4,32,1536]{2,1,0:T(8,128)(2,1)S(1)}, bf16[4,32,1536]{2,1,0:T(8,128)(2,1)S(1)}, u32[]{:S(2)}, u32[]{:S(2)}) collective-permute-start(bf16[4,32,1536]{2,1,0:T(8,128)(2,1)S(1)} %add_convert_fusion.1), channel_id=1, source_target_pairs={{0,56},{8,0},{16,8},{24,16},{32,24},{40,32},{48,40},{56,48},{1,57}... | collective-permute-start | bytes 1179656 | tf_op jit(solution)/shard_map/ppermute | solution.py:36
  208.5 16.7 %collective-permute-start.27 = (bf16[4,32,1536]{2,1,0:T(8,128)(2,1)S(1)}, bf16[4,32,1536]{2,1,0:T(8,128)(2,1)S(1)}, u32[]{:S(2)}, u32[]{:S(2)}) collective-permute-start(bf16[4,32,1536]{2,1,0:T(8,128)(2,1)S(1)} %add_convert_fusion.3), channel_id=1, source_target_pairs={{0,8},{8,16},{16,24},{24,32},{32,40},{40,48},{48,56},{56,0},{1,9},... | collective-permute-start | bytes 1179656 | tf_op jit(solution)/shard_map/ppermute | solution.py:36
  225.4 5.2 %collective-permute-start.34 = (bf16[32,1536]{1,0:T(8,128)(2,1)S(1)}, bf16[32,1536]{1,0:T(8,128)(2,1)S(1)}, u32[]{:S(2)}, u32[]{:S(2)}) collective-permute-start(bf16[32,1536]{1,0:T(8,128)(2,1)S(1)} %get-tuple-element.79), channel_id=1, source_target_pairs={{0,128},{64,192},{128,0},{192,64},{1,129},{65,193},{129,1},{193,65... | collective-permute-start | bytes 294920 | tf_op jit(solution)/shard_map/ppermute | solution.py:36
  225.5 5.8 %collective-permute-start.33 = (bf16[32,1536]{1,0:T(8,128)(2,1)S(1)}, bf16[32,1536]{1,0:T(8,128)(2,1)S(1)}, u32[]{:S(2)}, u32[]{:S(2)}) collective-permute-start(bf16[32,1536]{1,0:T(8,128)(2,1)S(1)} %get-tuple-element.80), channel_id=1, source_target_pairs={{0,64},{64,128},{128,192},{192,0},{1,65},{65,129},{129,193},{193,1... | collective-permute-start | bytes 294920 | tf_op jit(solution)/shard_map/ppermute | solution.py:36
  225.6 5.7 %collective-permute-start.32 = (bf16[32,1536]{1,0:T(8,128)(2,1)S(1)}, bf16[32,1536]{1,0:T(8,128)(2,1)S(1)}, u32[]{:S(2)}, u32[]{:S(2)}) collective-permute-start(bf16[32,1536]{1,0:T(8,128)(2,1)S(1)} %get-tuple-element.78), channel_id=1, source_target_pairs={{0,192},{64,0},{128,64},{192,128},{1,193},{65,1},{129,65},{193,129... | collective-permute-start | bytes 294920 | tf_op jit(solution)/shard_map/ppermute | solution.py:36
  233.1 16.9 %all-to-all-start.3 = ((bf16[8,4,3072]{2,1,0:T(4,128)(2,1)}), bf16[8,4,3072]{2,1,0:T(4,128)(2,1)S(1)}, u32[]{:S(2)}, u32[]{:S(2)}) async-start(bf16[8,4,3072]{2,1,0:T(4,128)(2,1)} %reshape.73), calls=%async_computation.5 | async-start | bytes 393216 | tf_op jit(solution)/shard_map/all_to_all | solution.py:440
Sparse Core Ops, SparseCore 0:
  27.6 104.6 all-gather.2
  134.9 43.3 reduce-scatter.2
  181.4 44.0 reduce-scatter.4

commit v3 on v2

--- a/solution.py
+++ b/solution.py
@@ -36,7 +36,7 @@
     return lax.ppermute(a, axis, [(i, (i + step) % n) for i in range(n)])
 
 
-def ring_gather(a, axis):
+def ring_gather(a, axis, split):
     half = SIZE[axis] // 2
     mid = a.shape[-2] // 2
     pieces = [a]
@@ -44,35 +44,31 @@
     for _ in range(1, half):
         up, down = shift(up, axis, 1), shift(down, axis, -1)
         pieces += [up, down]
-    return pieces + [shift(up[..., :mid, :], axis, 1), shift(down[..., mid:, :], axis, -1)]
-
-
-def line_of(pieces):
-    return jnp.stack(pieces[:-2] + [jnp.concatenate(pieces[-2:], axis=-2)], axis=0)
+    if split:
+        return pieces + [shift(up[..., :mid, :], axis, 1), shift(down[..., mid:, :], axis, -1)]
+    return pieces + [shift(up, axis, 1)]
 
 
 def plus(a, b):
     return (a.astype(F32) + b.astype(F32)).astype(BF)
 
 
-def ring_sum(far_up, far_down, parts, axis, hook):
+def ring_sum(far, parts, axis, hook):
     half = SIZE[axis] // 2
     place = ORDER[axis].index
 
     def get(k):
         return parts[place(k)]
 
-    mid = far_up.shape[0]
-    up, down = shift(far_up, axis, 1), shift(far_down, axis, -1)
-    own_up, own_down = hook(1, (get(half - 1), get(1 - half)))
-    up = jnp.concatenate([plus(up, own_up[:mid]), own_up[mid:]], axis=0)
-    down = jnp.concatenate([own_down[:mid], plus(down, own_down[mid:])], axis=0)
+    own_up, down = hook(1, (get(half - 1), get(1 - half)), far)
+    up = plus(shift(far, axis, 1), own_up)
     for k in range(half - 1, 0, -1):
+        going = up
         up, down = shift(up, axis, 1), shift(down, axis, -1)
         if k > 1:
-            own_up, own_down = hook(half - k + 1, (get(k - 1), get(1 - k)))
+            own_up, own_down = hook(half - k + 1, (get(k - 1), get(1 - k)), going)
             up, down = plus(up, own_up), plus(down, own_down)
-    own = hook(half, get(0))
+    own = hook(half, get(0), going)
     return (up.astype(F32) + down.astype(F32) + own.astype(F32)).astype(BF)
 
 
@@ -95,7 +91,7 @@
 def forward_kernel(where_ref, *refs):
     a_refs, refs = refs[: NZ + 1], refs[NZ + 1 :]
     b_refs, refs = refs[: NX + 1], refs[NX + 1 :]
-    wg_ref, wu_ref, wd_ref, x_out, gate_ref, up_ref, hidden_ref, far_up, far_down, left_ref, right_ref, rows_ref, wg, wu, wd, in_sems, w_sems, out_sems = refs
+    wg_ref, wu_ref, wd_ref, x_out, gate_ref, up_ref, hidden_ref, far_ref, left_ref, right_ref, rows_ref, wg, wu, wd, in_sems, w_sems, out_sems = refs
     step = pl.program_id(0)
     quarter = MID // 2
     arrivals = []
@@ -142,15 +138,7 @@
 
     out = dot(hidden, wd[:, :LEFT], ((1,), (0,))).astype(BF)
     left_ref[...] = out[: TILE - SLOTS].reshape(NZ - 1, 1, SLOTS, LEFT)
-
-    @pl.when(step < NX // 2)
-    def _():
-        far_up[0] = out[TILE - SLOTS :]
-
-    @pl.when(step >= NX // 2)
-    def _():
-        far_down[0] = out[TILE - SLOTS :]
-
+    far_ref[0] = out[TILE - SLOTS :]
     out = dot(hidden, wd[:, LEFT:], ((1,), (0,))).astype(BF)
     for j in range(NZ):
         right_ref[0, where_ref[NX + j]] = out[j * SLOTS : (j + 1) * SLOTS]
@@ -178,8 +166,7 @@
                 tall(HID),
                 tall(HID),
                 tall(HID),
-                pl.BlockSpec((1, SLOTS, LEFT), lambda i, where: (jnp.minimum(i, NX // 2 - 1), 0, 0)),
-                pl.BlockSpec((1, SLOTS, LEFT), lambda i, where: (jnp.maximum(i - NX // 2, 0), 0, 0)),
+                pl.BlockSpec((1, SLOTS, LEFT), lambda i, where: (i, 0, 0)),
                 pl.BlockSpec((NZ - 1, 1, SLOTS, LEFT), lambda i, where: (0, i, 0, 0)),
                 pl.BlockSpec((1, NZ, SLOTS, D - LEFT), lambda i, where: (where[i], 0, 0, 0)),
             ],
@@ -198,8 +185,7 @@
             jax.ShapeDtypeStruct((ROWS, HID), F32),
             jax.ShapeDtypeStruct((ROWS, HID), F32),
             jax.ShapeDtypeStruct((ROWS, HID), BF),
-            jax.ShapeDtypeStruct((NX // 2, SLOTS, LEFT), BF),
-            jax.ShapeDtypeStruct((NX // 2, SLOTS, LEFT), BF),
+            jax.ShapeDtypeStruct((NX, SLOTS, LEFT), BF),
             jax.ShapeDtypeStruct((NZ - 1, NX, SLOTS, LEFT), BF),
             jax.ShapeDtypeStruct((NX, NZ, SLOTS, D - LEFT), BF),
         ],
@@ -318,7 +304,7 @@
         out_shape=[jax.ShapeDtypeStruct((1, D, HID), BF)] * 2,
         scratch_shapes=[pltpu.VMEM((ROWS, 2 * HID), BF)],
         compiler_params=pltpu.CompilerParams(vmem_limit_bytes=60 * MIB),
-        cost_estimate=pl.CostEstimate(flops=4 * ROWS * D * HID, bytes_accessed=11 * MIB, transcendentals=0),
+        cost_estimate=pl.CostEstimate(flops=ROWS * D, bytes_accessed=MIB, transcendentals=0),
         name="wide_gradients",
     )(x, d_gate, d_up, spot, factors)
 
@@ -363,7 +349,7 @@
         ),
         out_shape=jax.ShapeDtypeStruct((1, HID, D), BF),
         compiler_params=pltpu.CompilerParams(vmem_limit_bytes=60 * MIB),
-        cost_estimate=pl.CostEstimate(flops=2 * ROWS * D * HID, bytes_accessed=8 * MIB, transcendentals=0),
+        cost_estimate=pl.CostEstimate(flops=ROWS * D, bytes_accessed=MIB, transcendentals=0),
         name="down_gradient",
     )(where, wide_y, hidden, spot, factors)
 
@@ -401,47 +387,49 @@
         high = lax.reduce_precision(gram, 8, 7)
         parts += [high.astype(BF), (gram - high).astype(BF)]
     wide_y = lax.all_gather(jnp.concatenate([local_dy] + parts, axis=1), ("x", "z"), axis=0)
-    line_x = line_of(ring_gather(local_x[:MID], "x"))
-    line_z = line_of(ring_gather(local_x[MID:], "z"))
-    a_pieces = ring_gather(line_x, "z")
-    b_pieces = ring_gather(line_z, "x")
-    x, gate, up_part, hidden, far_up, far_down, left, right = forward(
+    line_x = jnp.stack(ring_gather(local_x[:MID], "x", False))
+    line_z = jnp.stack(ring_gather(local_x[MID:], "z", False))
+    a_pieces = ring_gather(line_x, "z", True)
+    b_pieces = ring_gather(line_z, "x", True)
+    x, gate, up_part, hidden, far, left, right = forward(
         where, a_pieces, b_pieces, w_gate, w_up, w_down
     )
     right, wide_y = lax.optimization_barrier((right, wide_y))
     right_line = lax.psum_scatter(right.reshape(ROWS, D - LEFT), "x", scatter_dimension=0, tiled=True)
     kept = {}
 
-    def hook(step, sent):
+    def hook(step, sent, going):
         if step == 1:
             kept["back"] = backward(where, wide_y, w_down, gate, up_part, hidden)
             sent, kept["sum"] = lax.optimization_barrier((sent, kept["back"][3]))
         elif step == 2:
-            total = jnp.sum(spread(kept["sum"], ("x", "z"), BLOCKS).reshape(BLOCKS, 2, LANES), axis=0)
-            sent, kept["sum"], line = lax.optimization_barrier((sent, total, right_line))
-            line = lax.optimization_barrier(line.astype(F32))
-            kept["line"] = lax.optimization_barrier(lax.psum_scatter(line, "z", scatter_dimension=0, tiled=True))
+            total, _ = lax.optimization_barrier((kept["sum"], going))
+            total = jnp.sum(spread(total, ("x", "z"), BLOCKS).reshape(BLOCKS, 2, LANES), axis=0)
+            total = jnp.sum(spread(total, EXPERT, NE).reshape(NE, 2, LANES), axis=0)
+            sent, total, line = lax.optimization_barrier((sent, total, right_line))
+            kept["line"] = lax.psum_scatter(line, "z", scatter_dimension=0, tiled=True)
+            kept["norms"] = jnp.sqrt(total)
+            kept["factors"] = RADIUS / (kept["norms"] + GAMMA)
         elif step == 3:
-            total = jnp.sum(spread(kept["sum"], EXPERT, NE).reshape(NE, 2, LANES), axis=0)
-            sent, kept["norms"] = lax.optimization_barrier((sent, jnp.sqrt(total)))
+            factors, _ = lax.optimization_barrier((kept["factors"], going))
+            grad = down_gradient(where, wide_y, hidden, kept["back"][2], factors)
+            sent, kept["down"] = lax.optimization_barrier((sent, grad))
         else:
             d_gate, d_up, spot, _ = kept["back"]
-            kept["factors"] = RADIUS / (kept["norms"] + GAMMA)
-            grads = wide_gradients(x, d_gate, d_up, spot, kept["factors"])
+            factors, _ = lax.optimization_barrier((kept["factors"], going))
+            grads = wide_gradients(x, d_gate, d_up, spot, factors)
             sent, kept["grads"] = lax.optimization_barrier((sent, tuple(grads)))
         return sent
 
-    left_line = ring_sum(far_up, far_down, left, "z", hook)
-    right_out = kept["line"].astype(BF)
+    left_line = ring_sum(far, left, "z", hook)
+    right_out = kept["line"]
     left_out = direct_sum(left_line, "x")
     own_out = jnp.concatenate([left_out, right_out], axis=1)
-    own_out, late = lax.optimization_barrier((own_out, hidden))
-    grad_down = down_gradient(where, wide_y, late, kept["back"][2], kept["factors"])
     returned = lax.all_to_all(own_out.reshape(NE, CAP, width), EXPERT, split_axis=0, concat_axis=0, tiled=True)
     mixed = jnp.dot(placed_bf.T, returned.reshape(SLOTS, width), preferred_element_type=F32).astype(BF)
     norms = kept["norms"]
     own_norms = lax.dynamic_slice(norms.reshape(BLOCKS, 8), (ix * NZ + iz, 0), (1, EX_ROW))
-    return (mixed, own_norms, *kept["grads"], grad_down)
+    return (mixed, own_norms, *kept["grads"], kept["down"])
 
 
 def solution(mesh):

time: 258 us -> 250 us (0.969)
  starting transfers between devices: 76.4 us -> 55.8 us
  blocking collectives: 14 us -> 31.3 us
  other arithmetic: 10.3 us -> 5.99 us
  local copies, waits for them, and re-layouts: 13.7 us -> 10.7 us
  waiting for transfers between devices: 85 us -> 87.9 us
    all_to_all x0 -> x1, blocking collectives: none -> 17.3 us  [spread(): lax.all_to_all(jnp.broadcast_to(a[None], (n,) + a.shape), axes, 0, 0, til...]
    reduce_scatter x1, waiting for transfers between devices: 0.02 us -> 15.8 us  [hook(): kept['line'] = lax.psum_scatter(line, 'z', scatter_dimension=0, tiled=True)]
    ppermute x35 -> x32, starting transfers between devices: 56.2 us -> 40.8 us  [shift(): return lax.ppermute(a, axis, [(i, (i + step) % n) for i in range(n)])]
    reduce_scatter x1, waiting for transfers between devices: 13.1 us -> 0.02 us  [on_device(): lax.psum_scatter(right.reshape(ROWS, D - LEFT), 'x', scatter_dimension=0,...]
    ppermute x35 -> x32, waiting for transfers between devices: 58.5 us -> 48 us  [shift(): return lax.ppermute(a, axis, [(i, (i + step) % n) for i in range(n)])]
    all_to_all x2 -> x1, starting transfers between devices: 12.5 us -> 5.77 us  [spread(): lax.all_to_all(jnp.broadcast_to(a[None], (n,) + a.shape), axes, 0, 0, til...]
    all_gather x1, waiting for transfers between devices: 8.1 us -> 14.5 us  [on_device(): lax.all_gather(jnp.concatenate([local_dy] + parts, axis=1), ('x', 'z'), a...]
    all_to_all x1, waiting for transfers between devices: 0.01 us -> 5.28 us  [on_device(): lax.all_to_all(own_out.reshape(NE, CAP, width), EXPERT, split_axis=0, con...]
  transfers between devices with their start and end apart: 41 -> 37, of which waited for: 22 -> 18; matrix products, arithmetic and copies ran while one was open for 7% -> 3% of each run, Pallas kernels for 16% -> 16%
where the time goes in v3:
time: 250 us; the launch traced here: 249 us
  waiting for transfers between devices  87.9 us (35%)
  starting transfers between devices  55.8 us (22%)
  Pallas kernels  40.6 us (16%)
  blocking collectives  31.3 us (13%)
  between operations  14.2 us (6%)
  local copies, waits for them, and re-layouts  10.7 us (4%)
  other arithmetic  5.99 us (2%)
  matrix products  2.51 us (1%)
    ppermute x32, waiting for transfers between devices, shift(): return lax.ppermute(a, axis, [(i, (i + step) % n) for i in range(n)])  48 us
    ppermute x32, starting transfers between devices, shift(): return lax.ppermute(a, axis, [(i, (i + step) % n) for i in range(n)])  40.8 us
    all_to_all x1, blocking collectives, spread(): lax.all_to_all(jnp.broadcast_to(a[None], (n,) + a.shape), axes, 0, 0, til...  17.3 us
    reduce_scatter x1, waiting for transfers between devices, hook(): kept['line'] = lax.psum_scatter(line, 'z', scatter_dimension=0, tiled=True)  15.8 us
    all_gather x1, waiting for transfers between devices, on_device(): lax.all_gather(jnp.concatenate([local_dy] + parts, axis=1), ('x', 'z'), a...  14.5 us
    all_to_all x1, blocking collectives, on_device(): got = lax.all_to_all(send, EXPERT, split_axis=0, concat_axis=0, tiled=True)  14 us
    pallas_call x1, Pallas kernels, forward(): pl.pallas_call(forward_kernel, grid_spec=pltpu.PrefetchScalarGridSpec(num...  13.1 us
    pallas_call x1, Pallas kernels, backward(): pl.pallas_call(backward_kernel, grid_spec=pltpu.PrefetchScalarGridSpec(nu...  9.44 us
  transfers between devices with their start and end apart: 37, of which 18 were waited for; matrix products, arithmetic and copies ran while one was open for 3% of the time, Pallas kernels for 16%

profile of v3, /device:TPU:1, one launch (start us, length us, event | category | flops | bytes accessed | tf_op | source)
XLA Modules:
  0.0 249.0 jit_solution(8646547051085482158)
XLA Ops:
  7.2 0.8 copy.28
  8.6 0.7 multiply_add_fusion
  9.5 0.7 multiply_reduce_fusion
  10.4 1.1 convolution_convert_fusion
  12.0 14.0 %all_to_all.20 = bf16[8,8,3200]{2,1,0:T(8,128)(2,1)S(1)} all-to-all(bf16[8,8,3200]{2,1,0:T(8,128)(2,1)S(1)} %pad_maximum_fusion), channel_id=1, replica_groups=mesh['x'=4,'z'=8,'y'=4,'c'=2] {'y','c'}, dimensions={0} | all-to-all | bytes 819200 | tf_op jit(solution)/shard_map/all_to_all | solution.py:380
  26.7 0.8 concatenate.22
  27.7 1.3 collective-permute-start
  29.0 1.5 collective-permute-start.1
  30.5 1.7 collective-permute-start.11
  32.2 4.0 %collective-permute-start.12 = (bf16[16,3072]{1,0:T(8,128)(2,1)S(1)}, bf16[16,3072]{1,0:T(8,128)(2,1)S(1)}, u32[]{:S(2)}, u32[]{:S(2)}) collective-permute-start(bf16[16,3072]{1,0:T(8,128)(2,1)S(1)} %slice.73), channel_id=1, source_target_pairs={{0,56},{8,0},{16,8},{24,16},{32,24},{40,32},{48,40},{56,48},{1,57}... | collective-permute-start | bytes 294920 | tf_op jit(solution)/shard_map/ppermute | solution.py:36
  36.4 1.8 collective-permute-done.11
  38.2 2.8 %collective-permute-start.14 = (bf16[16,3072]{1,0:T(8,128)(2,1)S(1)}, bf16[16,3072]{1,0:T(8,128)(2,1)S(1)}, u32[]{:S(2)}, u32[]{:S(2)}) collective-permute-start(bf16[16,3072]{1,0:T(8,128)(2,1)S(1)} %collective-permute-done.12), channel_id=1, source_target_pairs={{0,56},{8,0},{16,8},{24,16},{32,24},{40,32},{48,40},{56,48},{1,57}... | collective-permute-start | bytes 294920 | tf_op jit(solution)/shard_map/ppermute | solution.py:36
  41.2 2.7 %collective-permute-start.4 = (bf16[4,16,3072]{2,1,0:T(8,128)(2,1)S(1)}, bf16[4,16,3072]{2,1,0:T(8,128)(2,1)S(1)}, u32[]{:S(2)}, u32[]{:S(2)}) collective-permute-start(bf16[4,16,3072]{2,1,0:T(8,128)(2,1)S(1)} %pad_maximum_fusion.1.refs_0_), channel_id=1, source_target_pairs={{0,56},{8,0},{16,8},{24,16},{32,24},{40,32},{48,40},{56,48},{1,57}... | collective-permute-start | bytes 1179656 | tf_op jit(solution)/shard_map/ppermute | solution.py:36
  43.9 2.7 %collective-permute-start.16 = (bf16[16,3072]{1,0:T(8,128)(2,1)S(1)}, bf16[16,3072]{1,0:T(8,128)(2,1)S(1)}, u32[]{:S(2)}, u32[]{:S(2)}) collective-permute-start(bf16[16,3072]{1,0:T(8,128)(2,1)S(1)} %collective-permute-done.14), channel_id=1, source_target_pairs={{0,56},{8,0},{16,8},{24,16},{32,24},{40,32},{48,40},{56,48},{1,57}... | collective-permute-start | bytes 294920 | tf_op jit(solution)/shard_map/ppermute | solution.py:36
  46.6 12.5 %collective-permute-done.15 = bf16[16,3072]{1,0:T(8,128)(2,1)S(1)} collective-permute-done((bf16[16,3072]{1,0:T(8,128)(2,1)S(1)}, bf16[16,3072]{1,0:T(8,128)(2,1)S(1)}, u32[]{:S(2)}, u32[]{:S(2)}) %collective-permute-start.15) | collective-permute-done | bytes 98336 | tf_op jit(solution)/shard_map/ppermute | solution.py:36
  59.2 5.4 %collective-permute-done.17 = bf16[16,3072]{1,0:T(8,128)(2,1)S(1)} collective-permute-done((bf16[16,3072]{1,0:T(8,128)(2,1)S(1)}, bf16[16,3072]{1,0:T(8,128)(2,1)S(1)}, u32[]{:S(2)}, u32[]{:S(2)}) %collective-permute-start.17) | collective-permute-done | bytes 98336 | tf_op jit(solution)/shard_map/ppermute | solution.py:36
  64.6 2.7 %collective-permute-start.19 = (bf16[8,16,3072]{2,1,0:T(8,128)(2,1)S(1)}, bf16[8,16,3072]{2,1,0:T(8,128)(2,1)S(1)}, u32[]{:S(2)}, u32[]{:S(2)}) collective-permute-start(bf16[8,16,3072]{2,1,0:T(8,128)(2,1)S(1)} %bitcast_dynamic-update-slice_fusion.refs_9_), channel_id=1, source_target_pairs={{0,192},{64,0},{128,64},{192,128},{1,193},{65,1},{129,65},{193,129... | collective-permute-start | bytes 2359304 | tf_op jit(solution)/shard_map/ppermute | solution.py:36
  67.3 2.7 %collective-permute-start.6 = (bf16[4,16,3072]{2,1,0:T(8,128)(2,1)S(1)}, bf16[4,16,3072]{2,1,0:T(8,128)(2,1)}, u32[]{:S(2)}, u32[]{:S(2)}) collective-permute-start(bf16[4,16,3072]{2,1,0:T(8,128)(2,1)S(1)} %collective-permute-done.4.refs_2_), channel_id=1, source_target_pairs={{0,56},{8,0},{16,8},{24,16},{32,24},{40,32},{48,40},{56,48},{1,57}... | collective-permute-start | bytes 1179656 | tf_op jit(solution)/shard_map/ppermute | solution.py:36
  70.0 5.5 %collective-permute-done.5.refs_3_ = bf16[4,16,3072]{2,1,0:T(8,128)(2,1)} collective-permute-done((bf16[4,16,3072]{2,1,0:T(8,128)(2,1)S(1)}, bf16[4,16,3072]{2,1,0:T(8,128)(2,1)}, u32[]{:S(2)}, u32[]{:S(2)}) %collective-permute-start.5) | collective-permute-done | bytes 393248 | tf_op jit(solution)/shard_map/ppermute | solution.py:36
  75.5 2.7 %collective-permute-start.8 = (bf16[4,16,3072]{2,1,0:T(8,128)(2,1)}, bf16[4,16,3072]{2,1,0:T(8,128)(2,1)}, u32[]{:S(2)}, u32[]{:S(2)}) collective-permute-start(bf16[4,16,3072]{2,1,0:T(8,128)(2,1)} %collective-permute-done.6.refs_4_), channel_id=1, source_target_pairs={{0,56},{8,0},{16,8},{24,16},{32,24},{40,32},{48,40},{56,48},{1,57}... | collective-permute-start | bytes 1179656 | tf_op jit(solution)/shard_map/ppermute | solution.py:36
  78.2 2.9 %collective-permute-done.18.refs_10_ = bf16[8,16,3072]{2,1,0:T(8,128)(2,1)S(1)} collective-permute-done((bf16[8,16,3072]{2,1,0:T(8,128)(2,1)S(1)}, bf16[8,16,3072]{2,1,0:T(8,128)(2,1)S(1)}, u32[]{:S(2)}, u32[]{:S(2)}) %collective-permute-start.18) | collective-permute-done | bytes 786464 | tf_op jit(solution)/shard_map/ppermute | solution.py:36
  81.2 2.7 %collective-permute-start.21 = (bf16[8,8,3072]{2,1,0:T(8,128)(2,1)S(1)}, bf16[8,8,3072]{2,1,0:T(8,128)(2,1)S(1)}, u32[]{:S(2)}, u32[]{:S(2)}) collective-permute-start(bf16[8,8,3072]{2,1,0:T(8,128)(2,1)S(1)} %slice.95), channel_id=1, source_target_pairs={{0,192},{64,0},{128,64},{192,128},{1,193},{65,1},{129,65},{193,129... | collective-permute-start | bytes 1179656 | tf_op jit(solution)/shard_map/ppermute | solution.py:36
  84.0 1.1 collective-permute-done.7.refs_5_
  85.0 0.9 slice.91
  86.1 6.5 %collective-permute-done.8.refs_6_ = bf16[4,16,3072]{2,1,0:T(8,128)(2,1)} collective-permute-done((bf16[4,16,3072]{2,1,0:T(8,128)(2,1)}, bf16[4,16,3072]{2,1,0:T(8,128)(2,1)}, u32[]{:S(2)}, u32[]{:S(2)}) %collective-permute-start.8) | collective-permute-done | bytes 393248 | tf_op jit(solution)/shard_map/ppermute | solution.py:36
  92.6 1.0 slice.92
  93.5 3.5 %collective-permute-start.10 = (bf16[4,8,3072]{2,1,0:T(8,128)(2,1)S(1)}, bf16[4,8,3072]{2,1,0:T(8,128)(2,1)S(1)}, u32[]{:S(2)}, u32[]{:S(2)}) collective-permute-start(bf16[4,8,3072]{2,1,0:T(8,128)(2,1)S(1)} %slice.92), channel_id=1, source_target_pairs={{0,56},{8,0},{16,8},{24,16},{32,24},{40,32},{48,40},{56,48},{1,57}... | collective-permute-start | bytes 589832 | tf_op jit(solution)/shard_map/ppermute | solution.py:36
  97.0 0.6 pad_add_fusion.where_ref
  97.6 2.0 collective-permute-done.10.refs_8_
  99.6 0.5 collective-permute-done.20.refs_12_
  100.3 0.8 copy-done.13
  101.1 13.1 %forward.1 = (bf16[4,8,32,3072]{3,2,1,0:T(8,128)(2,1)}, f32[1024,256]{1,0:T(8,128)}, f32[1024,256]{1,0:T(8,128)}, bf16[1024,256]{1,0:T(8,128)(2,1)}, bf16[4,32,1...) custom-call(s32[12]{0:T(128)} %pad_add_fusion.where_ref, ...), custom_call_target="tpu_custom_call" | custom-call | flops 4831838208 | bytes 20971520 | tf_op jit(solution)/shard_map/forward/pallas_call | solution.py:158
  114.2 14.5 %all-gather.3.cloned.1.call-done = bf16[1024,3328]{1,0:T(8,128)(2,1)} async-done(((bf16[32,3328]{1,0:T(8,128)(2,1)}), bf16[1024,3328]{1,0:T(8,128)(2,1)}) %all-gather.3.cloned.1.call-update) | async-done | bytes 6815760 | tf_op jit(solution)/shard_map/all_gather | solution.py:389
  128.8 0.6 collective-permute-start.22
  129.4 1.1 copy-done.1
  130.5 1.3 slice_bitcast_fusion.1
  131.8 9.4 %backward.1 = (bf16[1024,256]{1,0:T(8,128)(2,1)}, bf16[1024,256]{1,0:T(8,128)(2,1)}, f32[1024,1]{1,0:T(8,128)}, f32[2,128]{1,0:T(2,128)}) custom-call(s32[12]{0:T(128)} %pad_add_fusion.where_ref, bf16[32,32,3328]{2,1,0:T(8,128)(2,1)} %bitcast.50, bf16[32,32,3328]{2,1,0:T(8,128)(2,1)} %bitcast.51, bf16[1,256,3072]{2,1,0:T(8,128)(2,1)} %wd_ref.1, ...), custom_call_target="tpu_custom_call" | custom-call | flops 2415919104 | bytes 12582912 | tf_op jit(solution)/shard_map/backward/pallas_call | solution.py:240
  141.3 1.8 collective-permute-start.26
  143.1 1.1 add_convert_fusion.5
  144.2 0.7 broadcast_in_dim.12
  144.9 17.3 %all_to_all.21 = f32[32,2,128]{2,1,0:T(2,128)S(1)} all-to-all(f32[32,2,128]{2,1,0:T(2,128)S(1)} %broadcast_in_dim.12), channel_id=1, replica_groups=mesh['x'=4,'z'=8,'y'=4,'c'=2] {'x','z'}, dimensions={0} | all-to-all | bytes 65536 | tf_op jit(solution)/shard_map/all_to_all | solution.py:84
  162.3 0.6 broadcast_in_dim.13
  162.9 5.8 %all-to-all-start.2 = ((f32[8,2,128]{2,1,0:T(2,128)}), f32[8,2,128]{2,1,0:T(2,128)S(1)}, u32[]{:S(2)}, u32[]{:S(2)}) async-start(f32[8,2,128]{2,1,0:T(2,128)} %broadcast_in_dim.13), calls=%async_computation.2 | async-start | bytes 16384 | tf_op jit(solution)/shard_map/all_to_all | solution.py:84
  168.6 0.3 collective-permute-start.23
  169.0 4.3 %all-to-all-done.2 = f32[8,2,128]{2,1,0:T(2,128)S(1)} async-done(((f32[8,2,128]{2,1,0:T(2,128)}), f32[8,2,128]{2,1,0:T(2,128)S(1)}, u32[]{:S(2)}, u32[]{:S(2)}) %all-to-all-start.2) | async-done | bytes 8224 | tf_op jit(solution)/shard_map/all_to_all | solution.py:84
  173.4 0.3 collective-permute-start.27
  173.7 6.4 %collective-permute-done.23 = bf16[4,32,1536]{2,1,0:T(8,128)(2,1)S(1)} collective-permute-done((bf16[4,32,1536]{2,1,0:T(8,128)(2,1)S(1)}, bf16[4,32,1536]{2,1,0:T(8,128)(2,1)S(1)}, u32[]{:S(2)}, u32[]{:S(2)}) %collective-permute-start.23) | collective-permute-done | bytes 393248 | tf_op jit(solution)/shard_map/ppermute | solution.py:36
  180.3 0.6 fusion.17
  180.9 8.9 %down_gradient.1 = bf16[1,256,3072]{2,1,0:T(8,128)(2,1)} custom-call(s32[12]{0:T(128)} %pad_add_fusion.where_ref, bf16[32,32,3328]{2,1,0:T(8,128)(2,1)} %bitcast.52, bf16[1024,256]{1,0:T(8,128)(2,1)} %get-tuple-element.42.hidden_ref, f32[1024,1]{1,0:T(8,128)} %get-tuple-element.49.spot_ref, f32[2,128]{1,0:T(2,128)} %get-tuple-element.59.factor_ref), custom_call_target="tpu_custom_call" | custom-call | flops 3145728 | bytes 1048576 | tf_op jit(solution)/shard_map/down_gradient/pallas_call | solution.py:332
  189.9 2.8 %collective-permute-start.28 = (bf16[4,32,1536]{2,1,0:T(8,128)(2,1)S(1)}, bf16[4,32,1536]{2,1,0:T(8,128)(2,1)S(1)}, u32[]{:S(2)}, u32[]{:S(2)}) collective-permute-start(bf16[4,32,1536]{2,1,0:T(8,128)(2,1)S(1)} %add_convert_fusion.1), channel_id=1, source_target_pairs={{0,56},{8,0},{16,8},{24,16},{32,24},{40,32},{48,40},{56,48},{1,57}... | collective-permute-start | bytes 1179656 | tf_op jit(solution)/shard_map/ppermute | solution.py:36
  192.8 9.1 %wide_gradients.1 = (bf16[1,3072,256]{2,1,0:T(8,128)(2,1)}, bf16[1,3072,256]{2,1,0:T(8,128)(2,1)}) custom-call(bf16[4,8,32,3072]{3,2,1,0:T(8,128)(2,1)} %get-tuple-element.56.x_ref, bf16[1024,256]{1,0:T(8,128)(2,1)} %get-tuple-element.57.dg_ref, bf16[1024,256]{1,0:T(8,128)(2,1)} %get-tuple-element.58.du_ref, f32[1024,1]{1,0:T(8,128)} %get-tuple-element.49.spot_ref, ...), custom_call_target="tpu_custom_call" | custom-call | flops 3145728 | bytes 1048576 | tf_op jit(solution)/shard_map/wide_gradients/pallas_call | solution.py:293
  201.9 0.8 collective-permute-done.25
  203.0 1.0 collective-permute-start.31
  203.9 0.5 collective-permute-start.30
  204.4 2.2 collective-permute-start.29
  206.6 1.5 collective-permute-done.31
  208.1 1.0 collective-permute-done.30
  209.1 15.8 %reduce-scatter.5.cloned.1.call-done = bf16[32,1536]{1,0:T(8,128)(2,1)} async-done(((bf16[256,1536]{1,0:T(8,128)(2,1)}), bf16[32,1536]{1,0:T(8,128)(2,1)}) %reduce-scatter.5.cloned.1.call-update) | async-done | bytes 98320 | tf_op jit(solution)/shard_map/reduce_scatter | solution.py:410
  224.9 0.9 pad_maximum_fusion.4
  225.9 0.8 reshape.73
  226.6 9.2 %all-to-all-start.3 = ((bf16[8,4,3072]{2,1,0:T(4,128)(2,1)}), bf16[8,4,3072]{2,1,0:T(4,128)(2,1)S(1)}, u32[]{:S(2)}, u32[]{:S(2)}) async-start(bf16[8,4,3072]{2,1,0:T(4,128)(2,1)} %reshape.73), calls=%async_computation.5 | async-start | bytes 393216 | tf_op jit(solution)/shard_map/all_to_all | solution.py:428
  235.8 0.5 constant_dynamic-slice_fusion
  236.4 5.3 %all-to-all-done.3 = bf16[8,4,3072]{2,1,0:T(4,128)(2,1)S(1)} async-done(((bf16[8,4,3072]{2,1,0:T(4,128)(2,1)}), bf16[8,4,3072]{2,1,0:T(4,128)(2,1)S(1)}, u32[]{:S(2)}, u32[]{:S(2)}) %all-to-all-start.3) | async-done | bytes 196640 | tf_op jit(solution)/shard_map/all_to_all | solution.py:428
  241.7 0.8 convolution_convert_fusion.2
  (122 shorter events, 4.3 us)
Async XLA Ops:
  7.2 3.0 %copy-start = (bf16[12,3072]{1,0:T(8,128)(2,1)S(1)}, bf16[12,3072]{1,0:T(8,128)(2,1)}, u32[]{:S(2)}) copy-start(bf16[12,3072]{1,0:T(8,128)(2,1)} %param.9) | copy-start | bytes 221188
  7.2 121.5 %all-gather.3.cloned.1.call-start = ((), (), s32[]{:S(2)}) async-start(), calls=%async_computation.8 | async-start | bytes 7028736 | tf_op jit(solution)/shard_map/all_gather | solution.py:389
  27.5 145.8 %reduce-scatter.3.cloned.1.call-start = ((), (), s32[]{:S(2)}) async-start(), calls=%async_computation.6 | async-start | bytes 3932160 | tf_op jit(solution)/shard_map/reduce_scatter | solution.py:398
  27.7 8.6 %collective-permute-start = (bf16[16,3072]{1,0:T(8,128)(2,1)S(1)}, bf16[16,3072]{1,0:T(8,128)(2,1)S(1)}, u32[]{:S(2)}, u32[]{:S(2)}) collective-permute-start(bf16[16,3072]{1,0:T(8,128)(2,1)S(1)} %slice.69), channel_id=1, source_target_pairs={{0,64},{64,128},{128,192},{192,0},{1,65},{65,129},{129,193},{193,1... | collective-permute-start | bytes 294920 | tf_op jit(solution)/shard_map/ppermute | solution.py:36
  29.0 12.0 %collective-permute-start.1 = (bf16[16,3072]{1,0:T(8,128)(2,1)S(1)}, bf16[16,3072]{1,0:T(8,128)(2,1)S(1)}, u32[]{:S(2)}, u32[]{:S(2)}) collective-permute-start(bf16[16,3072]{1,0:T(8,128)(2,1)S(1)} %slice.69), channel_id=1, source_target_pairs={{0,192},{64,0},{128,64},{192,128},{1,193},{65,1},{129,65},{193,129... | collective-permute-start | bytes 294920 | tf_op jit(solution)/shard_map/ppermute | solution.py:36
  30.5 7.7 %collective-permute-start.11 = (bf16[16,3072]{1,0:T(8,128)(2,1)S(1)}, bf16[16,3072]{1,0:T(8,128)(2,1)S(1)}, u32[]{:S(2)}, u32[]{:S(2)}) collective-permute-start(bf16[16,3072]{1,0:T(8,128)(2,1)S(1)} %slice.73), channel_id=1, source_target_pairs={{0,8},{8,16},{16,24},{24,32},{32,40},{40,48},{48,56},{56,0},{1,9},... | collective-permute-start | bytes 294920 | tf_op jit(solution)/shard_map/ppermute | solution.py:36
  32.2 6.0 %collective-permute-start.12 = (bf16[16,3072]{1,0:T(8,128)(2,1)S(1)}, bf16[16,3072]{1,0:T(8,128)(2,1)S(1)}, u32[]{:S(2)}, u32[]{:S(2)}) collective-permute-start(bf16[16,3072]{1,0:T(8,128)(2,1)S(1)} %slice.73), channel_id=1, source_target_pairs={{0,56},{8,0},{16,8},{24,16},{32,24},{40,32},{48,40},{56,48},{1,57}... | collective-permute-start | bytes 294920 | tf_op jit(solution)/shard_map/ppermute | solution.py:36
  36.3 4.8 %collective-permute-start.2 = (bf16[16,3072]{1,0:T(8,128)(2,1)S(1)}, bf16[16,3072]{1,0:T(8,128)(2,1)S(1)}, u32[]{:S(2)}, u32[]{:S(2)}) collective-permute-start(bf16[16,3072]{1,0:T(8,128)(2,1)S(1)} %collective-permute-done), channel_id=1, source_target_pairs={{0,64},{64,128},{128,192},{192,0},{1,65},{65,129},{129,193},{193,1... | collective-permute-start | bytes 294920 | tf_op jit(solution)/shard_map/ppermute | solution.py:36
  38.2 5.7 %collective-permute-start.13 = (bf16[16,3072]{1,0:T(8,128)(2,1)S(1)}, bf16[16,3072]{1,0:T(8,128)(2,1)S(1)}, u32[]{:S(2)}, u32[]{:S(2)}) collective-permute-start(bf16[16,3072]{1,0:T(8,128)(2,1)S(1)} %collective-permute-done.11), channel_id=1, source_target_pairs={{0,8},{8,16},{16,24},{24,32},{32,40},{40,48},{48,56},{56,0},{1,9},... | collective-permute-start | bytes 294920 | tf_op jit(solution)/shard_map/ppermute | solution.py:36
  38.2 5.7 %collective-permute-start.14 = (bf16[16,3072]{1,0:T(8,128)(2,1)S(1)}, bf16[16,3072]{1,0:T(8,128)(2,1)S(1)}, u32[]{:S(2)}, u32[]{:S(2)}) collective-permute-start(bf16[16,3072]{1,0:T(8,128)(2,1)S(1)} %collective-permute-done.12), channel_id=1, source_target_pairs={{0,56},{8,0},{16,8},{24,16},{32,24},{40,32},{48,40},{56,48},{1,57}... | collective-permute-start | bytes 294920 | tf_op jit(solution)/shard_map/ppermute | solution.py:36
  41.0 42.9 %copy-start.17 = (s32[8]{0:T(128)S(1)}, s32[8]{0:T(128)}, u32[]{:S(2)}) copy-start(s32[8]{0:T(128)} %constant.61.clone) | copy-start | bytes 100
  41.1 52.4 %copy-start.6 = (bf16[4,16,3072]{2,1,0:T(8,128)(2,1)}, bf16[4,16,3072]{2,1,0:T(8,128)(2,1)S(1)}, u32[]{:S(2)}) copy-start(bf16[4,16,3072]{2,1,0:T(8,128)(2,1)S(1)} %pad_maximum_fusion.1.refs_0_) | copy-start | bytes 1179652
  41.1 26.2 %collective-permute-start.3 = (bf16[4,16,3072]{2,1,0:T(8,128)(2,1)S(1)}, bf16[4,16,3072]{2,1,0:T(8,128)(2,1)S(1)}, u32[]{:S(2)}, u32[]{:S(2)}) collective-permute-start(bf16[4,16,3072]{2,1,0:T(8,128)(2,1)S(1)} %pad_maximum_fusion.1.refs_0_), channel_id=1, source_target_pairs={{0,8},{8,16},{16,24},{24,32},{32,40},{40,48},{48,56},{56,0},{1,9},... | collective-permute-start | bytes 1179656 | tf_op jit(solution)/shard_map/ppermute | solution.py:36
  41.2 26.1 %collective-permute-start.4 = (bf16[4,16,3072]{2,1,0:T(8,128)(2,1)S(1)}, bf16[4,16,3072]{2,1,0:T(8,128)(2,1)S(1)}, u32[]{:S(2)}, u32[]{:S(2)}) collective-permute-start(bf16[4,16,3072]{2,1,0:T(8,128)(2,1)S(1)} %pad_maximum_fusion.1.refs_0_), channel_id=1, source_target_pairs={{0,56},{8,0},{16,8},{24,16},{32,24},{40,32},{48,40},{56,48},{1,57}... | collective-permute-start | bytes 1179656 | tf_op jit(solution)/shard_map/ppermute | solution.py:36
  43.9 15.2 %collective-permute-start.15 = (bf16[16,3072]{1,0:T(8,128)(2,1)S(1)}, bf16[16,3072]{1,0:T(8,128)(2,1)S(1)}, u32[]{:S(2)}, u32[]{:S(2)}) collective-permute-start(bf16[16,3072]{1,0:T(8,128)(2,1)S(1)} %collective-permute-done.13), channel_id=1, source_target_pairs={{0,8},{8,16},{16,24},{24,32},{32,40},{40,48},{48,56},{56,0},{1,9},... | collective-permute-start | bytes 294920 | tf_op jit(solution)/shard_map/ppermute | solution.py:36
  43.9 15.3 %collective-permute-start.16 = (bf16[16,3072]{1,0:T(8,128)(2,1)S(1)}, bf16[16,3072]{1,0:T(8,128)(2,1)S(1)}, u32[]{:S(2)}, u32[]{:S(2)}) collective-permute-start(bf16[16,3072]{1,0:T(8,128)(2,1)S(1)} %collective-permute-done.14), channel_id=1, source_target_pairs={{0,56},{8,0},{16,8},{24,16},{32,24},{40,32},{48,40},{56,48},{1,57}... | collective-permute-start | bytes 294920 | tf_op jit(solution)/shard_map/ppermute | solution.py:36
  46.6 50.5 %copy-start.16 = (s32[4]{0:T(128)S(1)}, s32[4]{0:T(128)}, u32[]{:S(2)}) copy-start(s32[4]{0:T(128)} %constant.60.clone) | copy-start | bytes 52
  59.1 5.4 %collective-permute-start.17 = (bf16[16,3072]{1,0:T(8,128)(2,1)S(1)}, bf16[16,3072]{1,0:T(8,128)(2,1)S(1)}, u32[]{:S(2)}, u32[]{:S(2)}) collective-permute-start(bf16[16,3072]{1,0:T(8,128)(2,1)S(1)} %collective-permute-done.15), channel_id=1, source_target_pairs={{0,8},{8,16},{16,24},{24,32},{32,40},{40,48},{48,56},{56,0},{1,9},... | collective-permute-start | bytes 294920 | tf_op jit(solution)/shard_map/ppermute | solution.py:36
  64.5 16.6 %copy-start.10 = (bf16[8,16,3072]{2,1,0:T(8,128)(2,1)}, bf16[8,16,3072]{2,1,0:T(8,128)(2,1)S(1)}, u32[]{:S(2)}) copy-start(bf16[8,16,3072]{2,1,0:T(8,128)(2,1)S(1)} %bitcast_dynamic-update-slice_fusion.refs_9_) | copy-start | bytes 2359300
  64.5 16.5 %collective-permute-start.18 = (bf16[8,16,3072]{2,1,0:T(8,128)(2,1)S(1)}, bf16[8,16,3072]{2,1,0:T(8,128)(2,1)S(1)}, u32[]{:S(2)}, u32[]{:S(2)}) collective-permute-start(bf16[8,16,3072]{2,1,0:T(8,128)(2,1)S(1)} %bitcast_dynamic-update-slice_fusion.refs_9_), channel_id=1, source_target_pairs={{0,64},{64,128},{128,192},{192,0},{1,65},{65,129},{129,193},{193,1... | collective-permute-start | bytes 2359304 | tf_op jit(solution)/shard_map/ppermute | solution.py:36
  64.6 16.6 %collective-permute-start.19 = (bf16[8,16,3072]{2,1,0:T(8,128)(2,1)S(1)}, bf16[8,16,3072]{2,1,0:T(8,128)(2,1)S(1)}, u32[]{:S(2)}, u32[]{:S(2)}) collective-permute-start(bf16[8,16,3072]{2,1,0:T(8,128)(2,1)S(1)} %bitcast_dynamic-update-slice_fusion.refs_9_), channel_id=1, source_target_pairs={{0,192},{64,0},{128,64},{192,128},{1,193},{65,1},{129,65},{193,129... | collective-permute-start | bytes 2359304 | tf_op jit(solution)/shard_map/ppermute | solution.py:36
  67.3 10.9 %copy-start.11 = (bf16[4,16,3072]{2,1,0:T(8,128)(2,1)}, bf16[4,16,3072]{2,1,0:T(8,128)(2,1)S(1)}, u32[]{:S(2)}) copy-start(bf16[4,16,3072]{2,1,0:T(8,128)(2,1)S(1)} %collective-permute-done.3.refs_1_) | copy-start | bytes 1179652
  67.3 8.2 %collective-permute-start.5 = (bf16[4,16,3072]{2,1,0:T(8,128)(2,1)S(1)}, bf16[4,16,3072]{2,1,0:T(8,128)(2,1)}, u32[]{:S(2)}, u32[]{:S(2)}) collective-permute-start(bf16[4,16,3072]{2,1,0:T(8,128)(2,1)S(1)} %collective-permute-done.3.refs_1_), channel_id=1, source_target_pairs={{0,8},{8,16},{16,24},{24,32},{32,40},{40,48},{48,56},{56,0},{1,9},... | collective-permute-start | bytes 1179656 | tf_op jit(solution)/shard_map/ppermute | solution.py:36
  67.3 8.2 %copy-start.12 = (bf16[4,16,3072]{2,1,0:T(8,128)(2,1)}, bf16[4,16,3072]{2,1,0:T(8,128)(2,1)S(1)}, u32[]{:S(2)}) copy-start(bf16[4,16,3072]{2,1,0:T(8,128)(2,1)S(1)} %collective-permute-done.4.refs_2_) | copy-start | bytes 1179652
  67.3 8.1 %collective-permute-start.6 = (bf16[4,16,3072]{2,1,0:T(8,128)(2,1)S(1)}, bf16[4,16,3072]{2,1,0:T(8,128)(2,1)}, u32[]{:S(2)}, u32[]{:S(2)}) collective-permute-start(bf16[4,16,3072]{2,1,0:T(8,128)(2,1)S(1)} %collective-permute-done.4.refs_2_), channel_id=1, source_target_pairs={{0,56},{8,0},{16,8},{24,16},{32,24},{40,32},{48,40},{56,48},{1,57}... | collective-permute-start | bytes 1179656 | tf_op jit(solution)/shard_map/ppermute | solution.py:36
  75.5 9.6 %collective-permute-start.7 = (bf16[4,16,3072]{2,1,0:T(8,128)(2,1)}, bf16[4,16,3072]{2,1,0:T(8,128)(2,1)}, u32[]{:S(2)}, u32[]{:S(2)}) collective-permute-start(bf16[4,16,3072]{2,1,0:T(8,128)(2,1)} %collective-permute-done.5.refs_3_), channel_id=1, source_target_pairs={{0,8},{8,16},{16,24},{24,32},{32,40},{40,48},{48,56},{56,0},{1,9},... | collective-permute-start | bytes 1179656 | tf_op jit(solution)/shard_map/ppermute | solution.py:36
  75.5 17.1 %collective-permute-start.8 = (bf16[4,16,3072]{2,1,0:T(8,128)(2,1)}, bf16[4,16,3072]{2,1,0:T(8,128)(2,1)}, u32[]{:S(2)}, u32[]{:S(2)}) collective-permute-start(bf16[4,16,3072]{2,1,0:T(8,128)(2,1)} %collective-permute-done.6.refs_4_), channel_id=1, source_target_pairs={{0,56},{8,0},{16,8},{24,16},{32,24},{40,32},{48,40},{56,48},{1,57}... | collective-permute-start | bytes 1179656 | tf_op jit(solution)/shard_map/ppermute | solution.py:36
  81.1 19.1 %copy-start.8 = (bf16[8,16,3072]{2,1,0:T(8,128)(2,1)}, bf16[8,16,3072]{2,1,0:T(8,128)(2,1)S(1)}, u32[]{:S(2)}) copy-start(bf16[8,16,3072]{2,1,0:T(8,128)(2,1)S(1)} %collective-permute-done.18.refs_10_) | copy-start | bytes 2359300
  81.1 19.1 %collective-permute-start.20 = (bf16[8,8,3072]{2,1,0:T(8,128)(2,1)S(1)}, bf16[8,8,3072]{2,1,0:T(8,128)(2,1)}, u32[]{:S(2)}, u32[]{:S(2)}) collective-permute-start(bf16[8,8,3072]{2,1,0:T(8,128)(2,1)S(1)} %slice.94), channel_id=1, source_target_pairs={{0,64},{64,128},{128,192},{192,0},{1,65},{65,129},{129,193},{193,1... | collective-permute-start | bytes 1179656 | tf_op jit(solution)/shard_map/ppermute | solution.py:36
  81.2 18.9 %copy-start.9 = (bf16[8,16,3072]{2,1,0:T(8,128)(2,1)}, bf16[8,16,3072]{2,1,0:T(8,128)(2,1)S(1)}, u32[]{:S(2)}) copy-start(bf16[8,16,3072]{2,1,0:T(8,128)(2,1)S(1)} %collective-permute-done.19.refs_11_) | copy-start | bytes 2359300
  81.2 18.9 %collective-permute-start.21 = (bf16[8,8,3072]{2,1,0:T(8,128)(2,1)S(1)}, bf16[8,8,3072]{2,1,0:T(8,128)(2,1)S(1)}, u32[]{:S(2)}, u32[]{:S(2)}) collective-permute-start(bf16[8,8,3072]{2,1,0:T(8,128)(2,1)S(1)} %slice.95), channel_id=1, source_target_pairs={{0,192},{64,0},{128,64},{192,128},{1,193},{65,1},{129,65},{193,129... | collective-permute-start | bytes 1179656 | tf_op jit(solution)/shard_map/ppermute | solution.py:36
  86.0 11.6 %collective-permute-start.9 = (bf16[4,8,3072]{2,1,0:T(8,128)(2,1)S(1)}, bf16[4,8,3072]{2,1,0:T(8,128)(2,1)S(1)}, u32[]{:S(2)}, u32[]{:S(2)}) collective-permute-start(bf16[4,8,3072]{2,1,0:T(8,128)(2,1)S(1)} %slice.91), channel_id=1, source_target_pairs={{0,8},{8,16},{16,24},{24,32},{32,40},{40,48},{48,56},{56,0},{1,9},... | collective-permute-start | bytes 589832 | tf_op jit(solution)/shard_map/ppermute | solution.py:36
  93.5 6.1 %collective-permute-start.10 = (bf16[4,8,3072]{2,1,0:T(8,128)(2,1)S(1)}, bf16[4,8,3072]{2,1,0:T(8,128)(2,1)S(1)}, u32[]{:S(2)}, u32[]{:S(2)}) collective-permute-start(bf16[4,8,3072]{2,1,0:T(8,128)(2,1)S(1)} %slice.92), channel_id=1, source_target_pairs={{0,56},{8,0},{16,8},{24,16},{32,24},{40,32},{48,40},{56,48},{1,57}... | collective-permute-start | bytes 589832 | tf_op jit(solution)/shard_map/ppermute | solution.py:36
  97.6 2.5 %copy-start.14 = (bf16[4,8,3072]{2,1,0:T(8,128)(2,1)}, bf16[4,8,3072]{2,1,0:T(8,128)(2,1)S(1)}, u32[]{:S(2)}) copy-start(bf16[4,8,3072]{2,1,0:T(8,128)(2,1)S(1)} %collective-permute-done.9.refs_7_) | copy-start | bytes 589828
  99.6 0.7 copy-start.15
  100.3 0.8 copy-start.13
  128.7 1.8 copy-start.1
  128.8 14.3 %collective-permute-start.22 = (bf16[4,32,1536]{2,1,0:T(8,128)(2,1)}, bf16[4,32,1536]{2,1,0:T(8,128)(2,1)}, u32[]{:S(2)}, u32[]{:S(2)}) collective-permute-start(bf16[4,32,1536]{2,1,0:T(8,128)(2,1)} %get-tuple-element.36), channel_id=1, source_target_pairs={{0,8},{8,16},{16,24},{24,32},{32,40},{40,48},{48,56},{56,0},{1,9},... | collective-permute-start | bytes 1179656 | tf_op jit(solution)/shard_map/ppermute | solution.py:36
  131.8 9.5 %copy-start.7 = (bf16[4,32,1536]{2,1,0:T(8,128)(2,1)S(1)}, bf16[4,32,1536]{2,1,0:T(8,128)(2,1)}, u32[]{:S(2)}) copy-start(bf16[4,32,1536]{2,1,0:T(8,128)(2,1)} %get-tuple-element.53) | copy-start | bytes 1179652
  141.2 32.1 %copy-start.5 = (bf16[4,32,1536]{2,1,0:T(8,128)(2,1)S(1)}, bf16[4,32,1536]{2,1,0:T(8,128)(2,1)}, u32[]{:S(2)}) copy-start(bf16[4,32,1536]{2,1,0:T(8,128)(2,1)} %get-tuple-element.54) | copy-start | bytes 1179652
  141.2 38.8 %copy-start.4 = (bf16[4,32,1536]{2,1,0:T(8,128)(2,1)S(1)}, bf16[4,32,1536]{2,1,0:T(8,128)(2,1)}, u32[]{:S(2)}) copy-start(bf16[4,32,1536]{2,1,0:T(8,128)(2,1)} %get-tuple-element.48) | copy-start | bytes 1179652
  141.3 32.1 %collective-permute-start.26 = (bf16[4,32,1536]{2,1,0:T(8,128)(2,1)S(1)}, bf16[4,32,1536]{2,1,0:T(8,128)(2,1)S(1)}, u32[]{:S(2)}, u32[]{:S(2)}) collective-permute-start(bf16[4,32,1536]{2,1,0:T(8,128)(2,1)S(1)} %copy-done.7), channel_id=1, source_target_pairs={{0,56},{8,0},{16,8},{24,16},{32,24},{40,32},{48,40},{56,48},{1,57}... | collective-permute-start | bytes 1179656 | tf_op jit(solution)/shard_map/ppermute | solution.py:36
  162.9 10.4 %all-to-all-start.2 = ((f32[8,2,128]{2,1,0:T(2,128)}), f32[8,2,128]{2,1,0:T(2,128)S(1)}, u32[]{:S(2)}, u32[]{:S(2)}) async-start(f32[8,2,128]{2,1,0:T(2,128)} %broadcast_in_dim.13), calls=%async_computation.2 | async-start | bytes 16384 | tf_op jit(solution)/shard_map/all_to_all | solution.py:84
  168.6 56.3 %reduce-scatter.5.cloned.1.call-start = ((), (), s32[]{:S(2)}) async-start(), calls=%async_computation.7 | async-start | bytes 884736 | tf_op jit(solution)/shard_map/reduce_scatter | solution.py:410
  168.6 11.5 %collective-permute-start.23 = (bf16[4,32,1536]{2,1,0:T(8,128)(2,1)S(1)}, bf16[4,32,1536]{2,1,0:T(8,128)(2,1)S(1)}, u32[]{:S(2)}, u32[]{:S(2)}) collective-permute-start(bf16[4,32,1536]{2,1,0:T(8,128)(2,1)S(1)} %add_convert_fusion.5), channel_id=1, source_target_pairs={{0,8},{8,16},{16,24},{24,32},{32,40},{40,48},{48,56},{56,0},{1,9},... | collective-permute-start | bytes 1179656 | tf_op jit(solution)/shard_map/ppermute | solution.py:36
  173.4 16.3 %collective-permute-start.27 = (bf16[4,32,1536]{2,1,0:T(8,128)(2,1)S(1)}, bf16[4,32,1536]{2,1,0:T(8,128)(2,1)S(1)}, u32[]{:S(2)}, u32[]{:S(2)}) collective-permute-start(bf16[4,32,1536]{2,1,0:T(8,128)(2,1)S(1)} %add_convert_fusion.2), channel_id=1, source_target_pairs={{0,56},{8,0},{16,8},{24,16},{32,24},{40,32},{48,40},{56,48},{1,57}... | collective-permute-start | bytes 1179656 | tf_op jit(solution)/shard_map/ppermute | solution.py:36
  180.2 12.4 %collective-permute-start.24 = (bf16[4,32,1536]{2,1,0:T(8,128)(2,1)S(1)}, bf16[4,32,1536]{2,1,0:T(8,128)(2,1)S(1)}, u32[]{:S(2)}, u32[]{:S(2)}) collective-permute-start(bf16[4,32,1536]{2,1,0:T(8,128)(2,1)S(1)} %add_convert_fusion.4), channel_id=1, source_target_pairs={{0,8},{8,16},{16,24},{24,32},{32,40},{40,48},{48,56},{56,0},{1,9},... | collective-permute-start | bytes 1179656 | tf_op jit(solution)/shard_map/ppermute | solution.py:36
  180.9 8.9 %copy-start.3 = (bf16[4,32,1536]{2,1,0:T(8,128)(2,1)S(1)}, bf16[4,32,1536]{2,1,0:T(8,128)(2,1)}, u32[]{:S(2)}) copy-start(bf16[4,32,1536]{2,1,0:T(8,128)(2,1)} %get-tuple-element.55) | copy-start | bytes 1179652
  180.9 11.8 %copy-start.2 = (bf16[4,32,1536]{2,1,0:T(8,128)(2,1)S(1)}, bf16[4,32,1536]{2,1,0:T(8,128)(2,1)}, u32[]{:S(2)}) copy-start(bf16[4,32,1536]{2,1,0:T(8,128)(2,1)} %get-tuple-element.52) | copy-start | bytes 1179652
  189.9 12.1 %collective-permute-start.28 = (bf16[4,32,1536]{2,1,0:T(8,128)(2,1)S(1)}, bf16[4,32,1536]{2,1,0:T(8,128)(2,1)S(1)}, u32[]{:S(2)}, u32[]{:S(2)}) collective-permute-start(bf16[4,32,1536]{2,1,0:T(8,128)(2,1)S(1)} %add_convert_fusion.1), channel_id=1, source_target_pairs={{0,56},{8,0},{16,8},{24,16},{32,24},{40,32},{48,40},{56,48},{1,57}... | collective-permute-start | bytes 1179656 | tf_op jit(solution)/shard_map/ppermute | solution.py:36
  192.7 10.1 %collective-permute-start.25 = (bf16[4,32,1536]{2,1,0:T(8,128)(2,1)S(1)}, bf16[4,32,1536]{2,1,0:T(8,128)(2,1)S(1)}, u32[]{:S(2)}, u32[]{:S(2)}) collective-permute-start(bf16[4,32,1536]{2,1,0:T(8,128)(2,1)S(1)} %add_convert_fusion.3), channel_id=1, source_target_pairs={{0,8},{8,16},{16,24},{24,32},{32,40},{40,48},{48,56},{56,0},{1,9},... | collective-permute-start | bytes 1179656 | tf_op jit(solution)/shard_map/ppermute | solution.py:36
  203.0 5.1 %collective-permute-start.31 = (bf16[32,1536]{1,0:T(8,128)(2,1)S(1)}, bf16[32,1536]{1,0:T(8,128)(2,1)S(1)}, u32[]{:S(2)}, u32[]{:S(2)}) collective-permute-start(bf16[32,1536]{1,0:T(8,128)(2,1)S(1)} %get-tuple-element.79), channel_id=1, source_target_pairs={{0,128},{64,192},{128,0},{192,64},{1,129},{65,193},{129,1},{193,65... | collective-permute-start | bytes 294920 | tf_op jit(solution)/shard_map/ppermute | solution.py:36
  203.9 5.1 %collective-permute-start.30 = (bf16[32,1536]{1,0:T(8,128)(2,1)S(1)}, bf16[32,1536]{1,0:T(8,128)(2,1)S(1)}, u32[]{:S(2)}, u32[]{:S(2)}) collective-permute-start(bf16[32,1536]{1,0:T(8,128)(2,1)S(1)} %get-tuple-element.80), channel_id=1, source_target_pairs={{0,64},{64,128},{128,192},{192,0},{1,65},{65,129},{129,193},{193,1... | collective-permute-start | bytes 294920 | tf_op jit(solution)/shard_map/ppermute | solution.py:36
  204.4 4.7 %collective-permute-start.29 = (bf16[32,1536]{1,0:T(8,128)(2,1)S(1)}, bf16[32,1536]{1,0:T(8,128)(2,1)S(1)}, u32[]{:S(2)}, u32[]{:S(2)}) collective-permute-start(bf16[32,1536]{1,0:T(8,128)(2,1)S(1)} %get-tuple-element.78), channel_id=1, source_target_pairs={{0,192},{64,0},{128,64},{192,128},{1,193},{65,1},{129,65},{193,129... | collective-permute-start | bytes 294920 | tf_op jit(solution)/shard_map/ppermute | solution.py:36
  226.6 15.0 %all-to-all-start.3 = ((bf16[8,4,3072]{2,1,0:T(4,128)(2,1)}), bf16[8,4,3072]{2,1,0:T(4,128)(2,1)S(1)}, u32[]{:S(2)}, u32[]{:S(2)}) async-start(bf16[8,4,3072]{2,1,0:T(4,128)(2,1)} %reshape.73), calls=%async_computation.5 | async-start | bytes 393216 | tf_op jit(solution)/shard_map/all_to_all | solution.py:428
Sparse Core Ops, SparseCore 0:
  27.7 101.0 all-gather.2
  131.3 39.0 reduce-scatter.2
  193.0 31.9 reduce-scatter.4

commit v4 on v3

--- a/solution.py
+++ b/solution.py
@@ -28,7 +28,7 @@
 TILE = NZ * SLOTS
 MID = SLOTS // 2
 COLS = 512
-LEFT = D // 2
+LEFT = 1792
 
 
 def shift(a, axis, step):
@@ -405,31 +405,32 @@
         elif step == 2:
             total, _ = lax.optimization_barrier((kept["sum"], going))
             total = jnp.sum(spread(total, ("x", "z"), BLOCKS).reshape(BLOCKS, 2, LANES), axis=0)
+            sent, kept["sum"], line = lax.optimization_barrier((sent, total, right_line))
+            kept["line"] = lax.psum_scatter(line, "z", scatter_dimension=0, tiled=True)
+        elif step == 3:
+            total, _ = lax.optimization_barrier((kept["sum"], going))
             total = jnp.sum(spread(total, EXPERT, NE).reshape(NE, 2, LANES), axis=0)
-            sent, total, line = lax.optimization_barrier((sent, total, right_line))
-            kept["line"] = lax.psum_scatter(line, "z", scatter_dimension=0, tiled=True)
+            sent, total = lax.optimization_barrier((sent, total))
             kept["norms"] = jnp.sqrt(total)
             kept["factors"] = RADIUS / (kept["norms"] + GAMMA)
-        elif step == 3:
-            factors, _ = lax.optimization_barrier((kept["factors"], going))
-            grad = down_gradient(where, wide_y, hidden, kept["back"][2], factors)
-            sent, kept["down"] = lax.optimization_barrier((sent, grad))
         else:
             d_gate, d_up, spot, _ = kept["back"]
             factors, _ = lax.optimization_barrier((kept["factors"], going))
             grads = wide_gradients(x, d_gate, d_up, spot, factors)
-            sent, kept["grads"] = lax.optimization_barrier((sent, tuple(grads)))
+            sent, kept["grads"], kept["line"] = lax.optimization_barrier((sent, tuple(grads), kept["line"]))
         return sent
 
     left_line = ring_sum(far, left, "z", hook)
     right_out = kept["line"]
     left_out = direct_sum(left_line, "x")
     own_out = jnp.concatenate([left_out, right_out], axis=1)
+    own_out, late = lax.optimization_barrier((own_out, hidden))
+    grad_down = down_gradient(where, wide_y, late, kept["back"][2], kept["factors"])
     returned = lax.all_to_all(own_out.reshape(NE, CAP, width), EXPERT, split_axis=0, concat_axis=0, tiled=True)
     mixed = jnp.dot(placed_bf.T, returned.reshape(SLOTS, width), preferred_element_type=F32).astype(BF)
     norms = kept["norms"]
     own_norms = lax.dynamic_slice(norms.reshape(BLOCKS, 8), (ix * NZ + iz, 0), (1, EX_ROW))
-    return (mixed, own_norms, *kept["grads"], kept["down"])
+    return (mixed, own_norms, *kept["grads"], grad_down)
 
 
 def solution(mesh):

time: 250 us -> 248 us (level)
  blocking collectives: 31.3 us -> 14 us
  starting transfers between devices: 55.8 us -> 68.1 us
  local copies, waits for them, and re-layouts: 10.7 us -> 15.8 us
  waiting for transfers between devices: 87.9 us -> 84.5 us
    all_to_all x1 -> x0, blocking collectives: 17.3 us -> none  [spread(): lax.all_to_all(jnp.broadcast_to(a[None], (n,) + a.shape), axes, 0, 0, til...]
    all_to_all x1 -> x2, starting transfers between devices: 5.77 us -> 13.2 us  [spread(): lax.all_to_all(jnp.broadcast_to(a[None], (n,) + a.shape), axes, 0, 0, til...]
    all_to_all x1 -> x2, waiting for transfers between devices: 4.29 us -> 11.4 us  [spread(): lax.all_to_all(jnp.broadcast_to(a[None], (n,) + a.shape), axes, 0, 0, til...]
    all_to_all x1, waiting for transfers between devices: 5.28 us -> 0.01 us  [on_device(): lax.all_to_all(own_out.reshape(NE, CAP, width), EXPERT, split_axis=0, con...]
    ppermute x32, waiting for transfers between devices: 48 us -> 43 us  [shift(): return lax.ppermute(a, axis, [(i, (i + step) % n) for i in range(n)])]
    ppermute x32, starting transfers between devices: 40.8 us -> 44.9 us  [shift(): return lax.ppermute(a, axis, [(i, (i + step) % n) for i in range(n)])]
    reduce_scatter x1, waiting for transfers between devices: 15.8 us -> 12.5 us  [hook(): kept['line'] = lax.psum_scatter(line, 'z', scatter_dimension=0, tiled=True)]
    reduce_scatter x1, waiting for transfers between devices: 0.02 us -> 3.04 us  [on_device(): lax.psum_scatter(right.reshape(ROWS, D - LEFT), 'x', scatter_dimension=0,...]
  transfers between devices with their start and end apart: 37 -> 38, of which waited for: 18 -> 17; matrix products, arithmetic and copies ran while one was open for 3% -> 7% of each run, Pallas kernels for 16% -> 16%
where the time goes in v4:
time: 248 us; the launch traced here: 247 us
  waiting for transfers between devices  84.5 us (34%)
  starting transfers between devices  68.1 us (27%)
  Pallas kernels  40.2 us (16%)
  local copies, waits for them, and re-layouts  15.8 us (6%)
  between operations  14.1 us (6%)
  blocking collectives  14 us (6%)
  other arithmetic  8.06 us (3%)
  matrix products  2.51 us (1%)
    ppermute x32, starting transfers between devices, shift(): return lax.ppermute(a, axis, [(i, (i + step) % n) for i in range(n)])  44.9 us
    ppermute x32, waiting for transfers between devices, shift(): return lax.ppermute(a, axis, [(i, (i + step) % n) for i in range(n)])  43 us
    all_to_all x1, blocking collectives, on_device(): got = lax.all_to_all(send, EXPERT, split_axis=0, concat_axis=0, tiled=True)  14 us
    all_gather x1, waiting for transfers between devices, on_device(): lax.all_gather(jnp.concatenate([local_dy] + parts, axis=1), ('x', 'z'), a...  13.8 us
    all_to_all x2, starting transfers between devices, spread(): lax.all_to_all(jnp.broadcast_to(a[None], (n,) + a.shape), axes, 0, 0, til...  13.2 us
    pallas_call x1, Pallas kernels, forward(): pl.pallas_call(forward_kernel, grid_spec=pltpu.PrefetchScalarGridSpec(num...  13.1 us
    reduce_scatter x1, waiting for transfers between devices, hook(): kept['line'] = lax.psum_scatter(line, 'z', scatter_dimension=0, tiled=True)  12.5 us
    all_to_all x2, waiting for transfers between devices, spread(): lax.all_to_all(jnp.broadcast_to(a[None], (n,) + a.shape), axes, 0, 0, til...  11.4 us
  transfers between devices with their start and end apart: 38, of which 17 were waited for; matrix products, arithmetic and copies ran while one was open for 7% of the time, Pallas kernels for 16%

profile of v4, /device:TPU:1, one launch (start us, length us, event | category | flops | bytes accessed | tf_op | source)
XLA Modules:
  0.0 247.3 jit_solution(57748631906400472)
XLA Ops:
  7.2 0.8 copy.28
  8.6 0.7 multiply_add_fusion
  9.5 0.7 multiply_reduce_fusion
  10.4 1.1 convolution_convert_fusion
  12.0 14.0 %all_to_all.20 = bf16[8,8,3200]{2,1,0:T(8,128)(2,1)S(1)} all-to-all(bf16[8,8,3200]{2,1,0:T(8,128)(2,1)S(1)} %pad_maximum_fusion), channel_id=1, replica_groups=mesh['x'=4,'z'=8,'y'=4,'c'=2] {'y','c'}, dimensions={0} | all-to-all | bytes 819200 | tf_op jit(solution)/shard_map/all_to_all | solution.py:380
  26.7 0.8 concatenate.22
  27.7 1.3 collective-permute-start
  28.9 1.5 collective-permute-start.1
  30.5 1.7 collective-permute-start.11
  32.2 4.0 %collective-permute-start.12 = (bf16[16,3072]{1,0:T(8,128)(2,1)S(1)}, bf16[16,3072]{1,0:T(8,128)(2,1)S(1)}, u32[]{:S(2)}, u32[]{:S(2)}) collective-permute-start(bf16[16,3072]{1,0:T(8,128)(2,1)S(1)} %slice.73), channel_id=1, source_target_pairs={{0,56},{8,0},{16,8},{24,16},{32,24},{40,32},{48,40},{56,48},{1,57}... | collective-permute-start | bytes 294920 | tf_op jit(solution)/shard_map/ppermute | solution.py:36
  36.2 0.6 constant_dynamic-update-slice_fusion
  37.0 1.1 collective-permute-done.11
  38.1 2.8 %collective-permute-start.14 = (bf16[16,3072]{1,0:T(8,128)(2,1)S(1)}, bf16[16,3072]{1,0:T(8,128)(2,1)S(1)}, u32[]{:S(2)}, u32[]{:S(2)}) collective-permute-start(bf16[16,3072]{1,0:T(8,128)(2,1)S(1)} %collective-permute-done.12), channel_id=1, source_target_pairs={{0,56},{8,0},{16,8},{24,16},{32,24},{40,32},{48,40},{56,48},{1,57}... | collective-permute-start | bytes 294920 | tf_op jit(solution)/shard_map/ppermute | solution.py:36
  40.9 0.6 bitcast_dynamic-update-slice_fusion.6
  42.4 2.7 %collective-permute-start.4 = (bf16[4,16,3072]{2,1,0:T(8,128)(2,1)S(1)}, bf16[4,16,3072]{2,1,0:T(8,128)(2,1)S(1)}, u32[]{:S(2)}, u32[]{:S(2)}) collective-permute-start(bf16[4,16,3072]{2,1,0:T(8,128)(2,1)S(1)} %pad_maximum_fusion.1.refs_0_), channel_id=1, source_target_pairs={{0,56},{8,0},{16,8},{24,16},{32,24},{40,32},{48,40},{56,48},{1,57}... | collective-permute-start | bytes 1179656 | tf_op jit(solution)/shard_map/ppermute | solution.py:36
  45.0 2.7 %collective-permute-start.16 = (bf16[16,3072]{1,0:T(8,128)(2,1)S(1)}, bf16[16,3072]{1,0:T(8,128)(2,1)S(1)}, u32[]{:S(2)}, u32[]{:S(2)}) collective-permute-start(bf16[16,3072]{1,0:T(8,128)(2,1)S(1)} %collective-permute-done.14), channel_id=1, source_target_pairs={{0,56},{8,0},{16,8},{24,16},{32,24},{40,32},{48,40},{56,48},{1,57}... | collective-permute-start | bytes 294920 | tf_op jit(solution)/shard_map/ppermute | solution.py:36
  49.0 9.2 %collective-permute-done.15 = bf16[16,3072]{1,0:T(8,128)(2,1)S(1)} collective-permute-done((bf16[16,3072]{1,0:T(8,128)(2,1)S(1)}, bf16[16,3072]{1,0:T(8,128)(2,1)S(1)}, u32[]{:S(2)}, u32[]{:S(2)}) %collective-permute-start.15) | collective-permute-done | bytes 98336 | tf_op jit(solution)/shard_map/ppermute | solution.py:36
  58.2 0.6 bitcast_dynamic-update-slice_fusion.2
  58.9 0.6 bitcast_dynamic-update-slice_fusion.1
  59.5 4.3 %collective-permute-done.17 = bf16[16,3072]{1,0:T(8,128)(2,1)S(1)} collective-permute-done((bf16[16,3072]{1,0:T(8,128)(2,1)S(1)}, bf16[16,3072]{1,0:T(8,128)(2,1)S(1)}, u32[]{:S(2)}, u32[]{:S(2)}) %collective-permute-start.17) | collective-permute-done | bytes 98336 | tf_op jit(solution)/shard_map/ppermute | solution.py:36
  63.9 0.6 bitcast_dynamic-update-slice_fusion.refs_9_
  64.5 2.7 %collective-permute-start.19 = (bf16[8,16,3072]{2,1,0:T(8,128)(2,1)}, bf16[8,16,3072]{2,1,0:T(8,128)(2,1)S(1)}, u32[]{:S(2)}, u32[]{:S(2)}) collective-permute-start(bf16[8,16,3072]{2,1,0:T(8,128)(2,1)} %bitcast_dynamic-update-slice_fusion.refs_9_), channel_id=1, source_target_pairs={{0,192},{64,0},{128,64},{192,128},{1,193},{65,1},{129,65},{193,129... | collective-permute-start | bytes 2359304 | tf_op jit(solution)/shard_map/ppermute | solution.py:36
  67.2 2.7 %collective-permute-start.6 = (bf16[4,16,3072]{2,1,0:T(8,128)(2,1)S(1)}, bf16[4,16,3072]{2,1,0:T(8,128)(2,1)}, u32[]{:S(2)}, u32[]{:S(2)}) collective-permute-start(bf16[4,16,3072]{2,1,0:T(8,128)(2,1)S(1)} %collective-permute-done.4.refs_2_), channel_id=1, source_target_pairs={{0,56},{8,0},{16,8},{24,16},{32,24},{40,32},{48,40},{56,48},{1,57}... | collective-permute-start | bytes 1179656 | tf_op jit(solution)/shard_map/ppermute | solution.py:36
  69.9 5.5 %collective-permute-done.5.refs_3_ = bf16[4,16,3072]{2,1,0:T(8,128)(2,1)} collective-permute-done((bf16[4,16,3072]{2,1,0:T(8,128)(2,1)S(1)}, bf16[4,16,3072]{2,1,0:T(8,128)(2,1)}, u32[]{:S(2)}, u32[]{:S(2)}) %collective-permute-start.5) | collective-permute-done | bytes 393248 | tf_op jit(solution)/shard_map/ppermute | solution.py:36
  75.4 2.7 %collective-permute-start.8 = (bf16[4,16,3072]{2,1,0:T(8,128)(2,1)}, bf16[4,16,3072]{2,1,0:T(8,128)(2,1)}, u32[]{:S(2)}, u32[]{:S(2)}) collective-permute-start(bf16[4,16,3072]{2,1,0:T(8,128)(2,1)} %collective-permute-done.6.refs_4_), channel_id=1, source_target_pairs={{0,56},{8,0},{16,8},{24,16},{32,24},{40,32},{48,40},{56,48},{1,57}... | collective-permute-start | bytes 1179656 | tf_op jit(solution)/shard_map/ppermute | solution.py:36
  78.0 2.3 collective-permute-done.18.refs_10_
  80.5 2.7 %collective-permute-start.21 = (bf16[8,8,3072]{2,1,0:T(8,128)(2,1)S(1)}, bf16[8,8,3072]{2,1,0:T(8,128)(2,1)}, u32[]{:S(2)}, u32[]{:S(2)}) collective-permute-start(bf16[8,8,3072]{2,1,0:T(8,128)(2,1)S(1)} %slice.95), channel_id=1, source_target_pairs={{0,192},{64,0},{128,64},{192,128},{1,193},{65,1},{129,65},{193,129... | collective-permute-start | bytes 1179656 | tf_op jit(solution)/shard_map/ppermute | solution.py:36
  83.2 4.3 %collective-permute-done.7.refs_5_ = bf16[4,16,3072]{2,1,0:T(8,128)(2,1)} collective-permute-done((bf16[4,16,3072]{2,1,0:T(8,128)(2,1)}, bf16[4,16,3072]{2,1,0:T(8,128)(2,1)}, u32[]{:S(2)}, u32[]{:S(2)}) %collective-permute-start.7) | collective-permute-done | bytes 393248 | tf_op jit(solution)/shard_map/ppermute | solution.py:36
  87.5 0.9 slice.91
  88.6 3.8 %collective-permute-done.8.refs_6_ = bf16[4,16,3072]{2,1,0:T(8,128)(2,1)} collective-permute-done((bf16[4,16,3072]{2,1,0:T(8,128)(2,1)}, bf16[4,16,3072]{2,1,0:T(8,128)(2,1)}, u32[]{:S(2)}, u32[]{:S(2)}) %collective-permute-start.8) | collective-permute-done | bytes 393248 | tf_op jit(solution)/shard_map/ppermute | solution.py:36
  92.4 0.9 slice.92
  93.3 3.5 %collective-permute-start.10 = (bf16[4,8,3072]{2,1,0:T(8,128)(2,1)S(1)}, bf16[4,8,3072]{2,1,0:T(8,128)(2,1)S(1)}, u32[]{:S(2)}, u32[]{:S(2)}) collective-permute-start(bf16[4,8,3072]{2,1,0:T(8,128)(2,1)S(1)} %slice.92), channel_id=1, source_target_pairs={{0,56},{8,0},{16,8},{24,16},{32,24},{40,32},{48,40},{56,48},{1,57}... | collective-permute-start | bytes 589832 | tf_op jit(solution)/shard_map/ppermute | solution.py:36
  96.8 0.7 pad_add_fusion.where_ref
  97.5 1.7 collective-permute-done.9.refs_7_
  99.2 1.1 collective-permute-done.10.refs_8_
  101.0 13.1 %forward.1 = (bf16[4,8,32,3072]{3,2,1,0:T(8,128)(2,1)}, f32[1024,256]{1,0:T(8,128)}, f32[1024,256]{1,0:T(8,128)}, bf16[1024,256]{1,0:T(8,128)(2,1)}, bf16[4,32,1...) custom-call(s32[12]{0:T(128)} %pad_add_fusion.where_ref, ...), custom_call_target="tpu_custom_call" | custom-call | flops 4831838208 | bytes 20971520 | tf_op jit(solution)/shard_map/forward/pallas_call | solution.py:158
  114.1 13.8 %all-gather.3.cloned.1.call-done = bf16[1024,3328]{1,0:T(8,128)(2,1)} async-done(((bf16[32,3328]{1,0:T(8,128)(2,1)}), bf16[1024,3328]{1,0:T(8,128)(2,1)}) %all-gather.3.cloned.1.call-update) | async-done | bytes 6815760 | tf_op jit(solution)/shard_map/all_gather | solution.py:389
  127.9 1.5 collective-permute-start.22
  129.5 2.2 slice_bitcast_fusion.5
  131.6 9.3 %backward.1 = (bf16[1024,256]{1,0:T(8,128)(2,1)}, bf16[1024,256]{1,0:T(8,128)(2,1)}, f32[1024,1]{1,0:T(8,128)}, f32[2,128]{1,0:T(2,128)}) custom-call(s32[12]{0:T(128)} %pad_add_fusion.where_ref, bf16[32,32,3328]{2,1,0:T(8,128)(2,1)} %bitcast.50, bf16[32,32,3328]{2,1,0:T(8,128)(2,1)} %bitcast.51, bf16[1,256,3072]{2,1,0:T(8,128)(2,1)} %wd_ref.1, ...), custom_call_target="tpu_custom_call" | custom-call | flops 2415919104 | bytes 12582912 | tf_op jit(solution)/shard_map/backward/pallas_call | solution.py:240
  141.0 1.2 collective-permute-start.26
  142.2 1.9 add_convert_fusion.5
  144.1 1.3 broadcast_in_dim.12
  145.4 8.1 %all-to-all-start.1 = ((f32[32,2,128]{2,1,0:T(2,128)}), f32[32,2,128]{2,1,0:T(2,128)S(1)}, u32[]{:S(2)}, u32[]{:S(2)}) async-start(f32[32,2,128]{2,1,0:T(2,128)} %broadcast_in_dim.12), calls=%async_computation.1 | async-start | bytes 65536 | tf_op jit(solution)/shard_map/all_to_all | solution.py:84
  153.5 1.5 collective-permute-start.23
  155.0 7.5 %all-to-all-done.1 = f32[32,2,128]{2,1,0:T(2,128)S(1)} async-done(((f32[32,2,128]{2,1,0:T(2,128)}), f32[32,2,128]{2,1,0:T(2,128)S(1)}, u32[]{:S(2)}, u32[]{:S(2)}) %all-to-all-start.1) | async-done | bytes 32800 | tf_op jit(solution)/shard_map/all_to_all | solution.py:84
  162.5 3.0 %reduce-scatter.3.cloned.1.call-done = bf16[256,1280]{1,0:T(8,128)(2,1)} async-done(((bf16[1024,1280]{1,0:T(8,128)(2,1)}), bf16[256,1280]{1,0:T(8,128)(2,1)}) %reduce-scatter.3.cloned.1.call-update) | async-done | bytes 655376 | tf_op jit(solution)/shard_map/reduce_scatter | solution.py:398
  165.6 3.1 %collective-permute-start.27 = (bf16[4,32,1792]{2,1,0:T(8,128)(2,1)S(1)}, bf16[4,32,1792]{2,1,0:T(8,128)(2,1)S(1)}, u32[]{:S(2)}, u32[]{:S(2)}) collective-permute-start(bf16[4,32,1792]{2,1,0:T(8,128)(2,1)S(1)} %add_convert_fusion.2), channel_id=1, source_target_pairs={{0,56},{8,0},{16,8},{24,16},{32,24},{40,32},{48,40},{56,48},{1,57}... | collective-permute-start | bytes 1376264 | tf_op jit(solution)/shard_map/ppermute | solution.py:36
  168.8 1.1 add_convert_fusion.4
  170.5 5.2 %all-to-all-start.2 = ((f32[8,2,128]{2,1,0:T(2,128)}), f32[8,2,128]{2,1,0:T(2,128)S(1)}, u32[]{:S(2)}, u32[]{:S(2)}) async-start(f32[8,2,128]{2,1,0:T(2,128)} %broadcast_in_dim.13), calls=%async_computation.3 | async-start | bytes 16384 | tf_op jit(solution)/shard_map/all_to_all | solution.py:84
  175.7 0.7 reduce-scatter.5.cloned.1.call-update
  176.4 4.0 %all-to-all-done.2 = f32[8,2,128]{2,1,0:T(2,128)S(1)} async-done(((f32[8,2,128]{2,1,0:T(2,128)}), f32[8,2,128]{2,1,0:T(2,128)S(1)}, u32[]{:S(2)}, u32[]{:S(2)}) %all-to-all-start.2) | async-done | bytes 8224 | tf_op jit(solution)/shard_map/all_to_all | solution.py:84
  180.5 1.1 collective-permute-start.28
  181.6 7.4 %collective-permute-done.24 = bf16[4,32,1792]{2,1,0:T(8,128)(2,1)} collective-permute-done((bf16[4,32,1792]{2,1,0:T(8,128)(2,1)S(1)}, bf16[4,32,1792]{2,1,0:T(8,128)(2,1)}, u32[]{:S(2)}, u32[]{:S(2)}) %collective-permute-start.24) | collective-permute-done | bytes 458784 | tf_op jit(solution)/shard_map/ppermute | solution.py:36
  189.0 1.1 add_convert_fusion.3
  190.8 9.1 %wide_gradients.1 = (bf16[1,3072,256]{2,1,0:T(8,128)(2,1)}, bf16[1,3072,256]{2,1,0:T(8,128)(2,1)}) custom-call(bf16[4,8,32,3072]{3,2,1,0:T(8,128)(2,1)} %get-tuple-element.58.x_ref, bf16[1024,256]{1,0:T(8,128)(2,1)} %get-tuple-element.59.dg_ref, bf16[1024,256]{1,0:T(8,128)(2,1)} %get-tuple-element.60.du_ref, f32[1024,1]{1,0:T(8,128)} %get-tuple-element.61.spot_ref, ...), custom_call_target="tpu_custom_call" | custom-call | flops 3145728 | bytes 1048576 | tf_op jit(solution)/shard_map/wide_gradients/pallas_call | solution.py:293
  199.9 12.5 %reduce-scatter.5.cloned.1.call-done = bf16[32,1280]{1,0:T(8,128)(2,1)} async-done(((bf16[256,1280]{1,0:T(8,128)(2,1)}), bf16[32,1280]{1,0:T(8,128)(2,1)}) %reduce-scatter.5.cloned.1.call-update) | async-done | bytes 81936 | tf_op jit(solution)/shard_map/reduce_scatter | solution.py:409
  212.5 2.5 %collective-permute-start.31 = (bf16[32,1792]{1,0:T(8,128)(2,1)S(1)}, bf16[32,1792]{1,0:T(8,128)(2,1)S(1)}, u32[]{:S(2)}, u32[]{:S(2)}) collective-permute-start(bf16[32,1792]{1,0:T(8,128)(2,1)S(1)} %get-tuple-element.83), channel_id=1, source_target_pairs={{0,128},{64,192},{128,0},{192,64},{1,129},{65,193},{129,1},{193,65... | collective-permute-start | bytes 344072 | tf_op jit(solution)/shard_map/ppermute | solution.py:36
  215.6 2.1 collective-permute-start.29
  217.8 2.1 collective-permute-done.30
  220.0 0.8 reshape.73
  220.7 9.9 %all-to-all-start.3 = ((bf16[8,4,3072]{2,1,0:T(4,128)(2,1)}), bf16[8,4,3072]{2,1,0:T(4,128)(2,1)S(1)}, u32[]{:S(2)}, u32[]{:S(2)}) async-start(bf16[8,4,3072]{2,1,0:T(4,128)(2,1)} %reshape.73), calls=%async_computation.5 | async-start | bytes 393216 | tf_op jit(solution)/shard_map/all_to_all | solution.py:429
  231.2 8.7 %down_gradient.1 = bf16[1,256,3072]{2,1,0:T(8,128)(2,1)} custom-call(s32[12]{0:T(128)} %pad_add_fusion.where_ref, bf16[32,32,3328]{2,1,0:T(8,128)(2,1)} %bitcast.52, bf16[1024,256]{1,0:T(8,128)(2,1)} %get-tuple-element.72.hidden_ref, f32[1024,1]{1,0:T(8,128)} %get-tuple-element.61.spot_ref, f32[2,128]{1,0:T(2,128)} %get-tuple-element.63.factor_ref), custom_call_target="tpu_custom_call" | custom-call | flops 3145728 | bytes 1048576 | tf_op jit(solution)/shard_map/down_gradient/pallas_call | solution.py:332
  240.0 0.8 convolution_convert_fusion.2
  (109 shorter events, 8.6 us)
Async XLA Ops:
  7.2 3.0 %copy-start = (bf16[12,3072]{1,0:T(8,128)(2,1)S(1)}, bf16[12,3072]{1,0:T(8,128)(2,1)}, u32[]{:S(2)}) copy-start(bf16[12,3072]{1,0:T(8,128)(2,1)} %param.9) | copy-start | bytes 221188
  7.2 120.7 %all-gather.3.cloned.1.call-start = ((), (), s32[]{:S(2)}) async-start(), calls=%async_computation.8 | async-start | bytes 7028736 | tf_op jit(solution)/shard_map/all_gather | solution.py:389
  27.5 138.0 %reduce-scatter.3.cloned.1.call-start = ((), (), s32[]{:S(2)}) async-start(), calls=%async_computation.6 | async-start | bytes 3276800 | tf_op jit(solution)/shard_map/reduce_scatter | solution.py:398
  27.7 9.2 %collective-permute-start = (bf16[16,3072]{1,0:T(8,128)(2,1)S(1)}, bf16[16,3072]{1,0:T(8,128)(2,1)S(1)}, u32[]{:S(2)}, u32[]{:S(2)}) collective-permute-start(bf16[16,3072]{1,0:T(8,128)(2,1)S(1)} %slice.69), channel_id=1, source_target_pairs={{0,64},{64,128},{128,192},{192,0},{1,65},{65,129},{129,193},{193,1... | collective-permute-start | bytes 294920 | tf_op jit(solution)/shard_map/ppermute | solution.py:36
  28.9 13.2 %collective-permute-start.1 = (bf16[16,3072]{1,0:T(8,128)(2,1)S(1)}, bf16[16,3072]{1,0:T(8,128)(2,1)S(1)}, u32[]{:S(2)}, u32[]{:S(2)}) collective-permute-start(bf16[16,3072]{1,0:T(8,128)(2,1)S(1)} %slice.69), channel_id=1, source_target_pairs={{0,192},{64,0},{128,64},{192,128},{1,193},{65,1},{129,65},{193,129... | collective-permute-start | bytes 294920 | tf_op jit(solution)/shard_map/ppermute | solution.py:36
  30.5 7.7 %collective-permute-start.11 = (bf16[16,3072]{1,0:T(8,128)(2,1)S(1)}, bf16[16,3072]{1,0:T(8,128)(2,1)S(1)}, u32[]{:S(2)}, u32[]{:S(2)}) collective-permute-start(bf16[16,3072]{1,0:T(8,128)(2,1)S(1)} %slice.73), channel_id=1, source_target_pairs={{0,8},{8,16},{16,24},{24,32},{32,40},{40,48},{48,56},{56,0},{1,9},... | collective-permute-start | bytes 294920 | tf_op jit(solution)/shard_map/ppermute | solution.py:36
  32.2 5.9 %collective-permute-start.12 = (bf16[16,3072]{1,0:T(8,128)(2,1)S(1)}, bf16[16,3072]{1,0:T(8,128)(2,1)S(1)}, u32[]{:S(2)}, u32[]{:S(2)}) collective-permute-start(bf16[16,3072]{1,0:T(8,128)(2,1)S(1)} %slice.73), channel_id=1, source_target_pairs={{0,56},{8,0},{16,8},{24,16},{32,24},{40,32},{48,40},{56,48},{1,57}... | collective-permute-start | bytes 294920 | tf_op jit(solution)/shard_map/ppermute | solution.py:36
  36.9 5.3 %collective-permute-start.2 = (bf16[16,3072]{1,0:T(8,128)(2,1)S(1)}, bf16[16,3072]{1,0:T(8,128)(2,1)S(1)}, u32[]{:S(2)}, u32[]{:S(2)}) collective-permute-start(bf16[16,3072]{1,0:T(8,128)(2,1)S(1)} %collective-permute-done), channel_id=1, source_target_pairs={{0,64},{64,128},{128,192},{192,0},{1,65},{65,129},{129,193},{193,1... | collective-permute-start | bytes 294920 | tf_op jit(solution)/shard_map/ppermute | solution.py:36
  38.1 6.9 %collective-permute-start.13 = (bf16[16,3072]{1,0:T(8,128)(2,1)S(1)}, bf16[16,3072]{1,0:T(8,128)(2,1)S(1)}, u32[]{:S(2)}, u32[]{:S(2)}) collective-permute-start(bf16[16,3072]{1,0:T(8,128)(2,1)S(1)} %collective-permute-done.11), channel_id=1, source_target_pairs={{0,8},{8,16},{16,24},{24,32},{32,40},{40,48},{48,56},{56,0},{1,9},... | collective-permute-start | bytes 294920 | tf_op jit(solution)/shard_map/ppermute | solution.py:36
  38.1 6.9 %collective-permute-start.14 = (bf16[16,3072]{1,0:T(8,128)(2,1)S(1)}, bf16[16,3072]{1,0:T(8,128)(2,1)S(1)}, u32[]{:S(2)}, u32[]{:S(2)}) collective-permute-start(bf16[16,3072]{1,0:T(8,128)(2,1)S(1)} %collective-permute-done.12), channel_id=1, source_target_pairs={{0,56},{8,0},{16,8},{24,16},{32,24},{40,32},{48,40},{56,48},{1,57}... | collective-permute-start | bytes 294920 | tf_op jit(solution)/shard_map/ppermute | solution.py:36
  42.2 41.0 %copy-start.10 = (s32[8]{0:T(128)S(1)}, s32[8]{0:T(128)}, u32[]{:S(2)}) copy-start(s32[8]{0:T(128)} %constant.61.clone) | copy-start | bytes 100
  42.3 51.1 %copy-start.1 = (bf16[4,16,3072]{2,1,0:T(8,128)(2,1)}, bf16[4,16,3072]{2,1,0:T(8,128)(2,1)S(1)}, u32[]{:S(2)}) copy-start(bf16[4,16,3072]{2,1,0:T(8,128)(2,1)S(1)} %pad_maximum_fusion.1.refs_0_) | copy-start | bytes 1179652
  42.3 24.9 %collective-permute-start.3 = (bf16[4,16,3072]{2,1,0:T(8,128)(2,1)S(1)}, bf16[4,16,3072]{2,1,0:T(8,128)(2,1)S(1)}, u32[]{:S(2)}, u32[]{:S(2)}) collective-permute-start(bf16[4,16,3072]{2,1,0:T(8,128)(2,1)S(1)} %pad_maximum_fusion.1.refs_0_), channel_id=1, source_target_pairs={{0,8},{8,16},{16,24},{24,32},{32,40},{40,48},{48,56},{56,0},{1,9},... | collective-permute-start | bytes 1179656 | tf_op jit(solution)/shard_map/ppermute | solution.py:36
  42.4 24.8 %collective-permute-start.4 = (bf16[4,16,3072]{2,1,0:T(8,128)(2,1)S(1)}, bf16[4,16,3072]{2,1,0:T(8,128)(2,1)S(1)}, u32[]{:S(2)}, u32[]{:S(2)}) collective-permute-start(bf16[4,16,3072]{2,1,0:T(8,128)(2,1)S(1)} %pad_maximum_fusion.1.refs_0_), channel_id=1, source_target_pairs={{0,56},{8,0},{16,8},{24,16},{32,24},{40,32},{48,40},{56,48},{1,57}... | collective-permute-start | bytes 1179656 | tf_op jit(solution)/shard_map/ppermute | solution.py:36
  45.0 13.2 %collective-permute-start.15 = (bf16[16,3072]{1,0:T(8,128)(2,1)S(1)}, bf16[16,3072]{1,0:T(8,128)(2,1)S(1)}, u32[]{:S(2)}, u32[]{:S(2)}) collective-permute-start(bf16[16,3072]{1,0:T(8,128)(2,1)S(1)} %collective-permute-done.13), channel_id=1, source_target_pairs={{0,8},{8,16},{16,24},{24,32},{32,40},{40,48},{48,56},{56,0},{1,9},... | collective-permute-start | bytes 294920 | tf_op jit(solution)/shard_map/ppermute | solution.py:36
  45.0 13.8 %collective-permute-start.16 = (bf16[16,3072]{1,0:T(8,128)(2,1)S(1)}, bf16[16,3072]{1,0:T(8,128)(2,1)S(1)}, u32[]{:S(2)}, u32[]{:S(2)}) collective-permute-start(bf16[16,3072]{1,0:T(8,128)(2,1)S(1)} %collective-permute-done.14), channel_id=1, source_target_pairs={{0,56},{8,0},{16,8},{24,16},{32,24},{40,32},{48,40},{56,48},{1,57}... | collective-permute-start | bytes 294920 | tf_op jit(solution)/shard_map/ppermute | solution.py:36
  48.4 48.5 %copy-start.9 = (s32[4]{0:T(128)S(1)}, s32[4]{0:T(128)}, u32[]{:S(2)}) copy-start(s32[4]{0:T(128)} %constant.60.clone) | copy-start | bytes 52
  58.2 5.6 %collective-permute-start.17 = (bf16[16,3072]{1,0:T(8,128)(2,1)S(1)}, bf16[16,3072]{1,0:T(8,128)(2,1)S(1)}, u32[]{:S(2)}, u32[]{:S(2)}) collective-permute-start(bf16[16,3072]{1,0:T(8,128)(2,1)S(1)} %collective-permute-done.15), channel_id=1, source_target_pairs={{0,8},{8,16},{16,24},{24,32},{32,40},{40,48},{48,56},{56,0},{1,9},... | collective-permute-start | bytes 294920 | tf_op jit(solution)/shard_map/ppermute | solution.py:36
  64.5 15.8 %collective-permute-start.18 = (bf16[8,16,3072]{2,1,0:T(8,128)(2,1)}, bf16[8,16,3072]{2,1,0:T(8,128)(2,1)S(1)}, u32[]{:S(2)}, u32[]{:S(2)}) collective-permute-start(bf16[8,16,3072]{2,1,0:T(8,128)(2,1)} %bitcast_dynamic-update-slice_fusion.refs_9_), channel_id=1, source_target_pairs={{0,64},{64,128},{128,192},{192,0},{1,65},{65,129},{129,193},{193,1... | collective-permute-start | bytes 2359304 | tf_op jit(solution)/shard_map/ppermute | solution.py:36
  64.5 15.9 %collective-permute-start.19 = (bf16[8,16,3072]{2,1,0:T(8,128)(2,1)}, bf16[8,16,3072]{2,1,0:T(8,128)(2,1)S(1)}, u32[]{:S(2)}, u32[]{:S(2)}) collective-permute-start(bf16[8,16,3072]{2,1,0:T(8,128)(2,1)} %bitcast_dynamic-update-slice_fusion.refs_9_), channel_id=1, source_target_pairs={{0,192},{64,0},{128,64},{192,128},{1,193},{65,1},{129,65},{193,129... | collective-permute-start | bytes 2359304 | tf_op jit(solution)/shard_map/ppermute | solution.py:36
  67.2 16.0 %copy-start.5 = (bf16[4,16,3072]{2,1,0:T(8,128)(2,1)}, bf16[4,16,3072]{2,1,0:T(8,128)(2,1)S(1)}, u32[]{:S(2)}) copy-start(bf16[4,16,3072]{2,1,0:T(8,128)(2,1)S(1)} %collective-permute-done.3.refs_1_) | copy-start | bytes 1179652
  67.2 8.1 %collective-permute-start.5 = (bf16[4,16,3072]{2,1,0:T(8,128)(2,1)S(1)}, bf16[4,16,3072]{2,1,0:T(8,128)(2,1)}, u32[]{:S(2)}, u32[]{:S(2)}) collective-permute-start(bf16[4,16,3072]{2,1,0:T(8,128)(2,1)S(1)} %collective-permute-done.3.refs_1_), channel_id=1, source_target_pairs={{0,8},{8,16},{16,24},{24,32},{32,40},{40,48},{48,56},{56,0},{1,9},... | collective-permute-start | bytes 1179656 | tf_op jit(solution)/shard_map/ppermute | solution.py:36
  67.2 8.1 %copy-start.6 = (bf16[4,16,3072]{2,1,0:T(8,128)(2,1)}, bf16[4,16,3072]{2,1,0:T(8,128)(2,1)S(1)}, u32[]{:S(2)}) copy-start(bf16[4,16,3072]{2,1,0:T(8,128)(2,1)S(1)} %collective-permute-done.4.refs_2_) | copy-start | bytes 1179652
  67.2 8.1 %collective-permute-start.6 = (bf16[4,16,3072]{2,1,0:T(8,128)(2,1)S(1)}, bf16[4,16,3072]{2,1,0:T(8,128)(2,1)}, u32[]{:S(2)}, u32[]{:S(2)}) collective-permute-start(bf16[4,16,3072]{2,1,0:T(8,128)(2,1)S(1)} %collective-permute-done.4.refs_2_), channel_id=1, source_target_pairs={{0,56},{8,0},{16,8},{24,16},{32,24},{40,32},{48,40},{56,48},{1,57}... | collective-permute-start | bytes 1179656 | tf_op jit(solution)/shard_map/ppermute | solution.py:36
  75.3 12.2 %collective-permute-start.7 = (bf16[4,16,3072]{2,1,0:T(8,128)(2,1)}, bf16[4,16,3072]{2,1,0:T(8,128)(2,1)}, u32[]{:S(2)}, u32[]{:S(2)}) collective-permute-start(bf16[4,16,3072]{2,1,0:T(8,128)(2,1)} %collective-permute-done.5.refs_3_), channel_id=1, source_target_pairs={{0,8},{8,16},{16,24},{24,32},{32,40},{40,48},{48,56},{56,0},{1,9},... | collective-permute-start | bytes 1179656 | tf_op jit(solution)/shard_map/ppermute | solution.py:36
  75.4 17.0 %collective-permute-start.8 = (bf16[4,16,3072]{2,1,0:T(8,128)(2,1)}, bf16[4,16,3072]{2,1,0:T(8,128)(2,1)}, u32[]{:S(2)}, u32[]{:S(2)}) collective-permute-start(bf16[4,16,3072]{2,1,0:T(8,128)(2,1)} %collective-permute-done.6.refs_4_), channel_id=1, source_target_pairs={{0,56},{8,0},{16,8},{24,16},{32,24},{40,32},{48,40},{56,48},{1,57}... | collective-permute-start | bytes 1179656 | tf_op jit(solution)/shard_map/ppermute | solution.py:36
  80.3 20.1 %copy-start.2 = (bf16[8,16,3072]{2,1,0:T(8,128)(2,1)}, bf16[8,16,3072]{2,1,0:T(8,128)(2,1)S(1)}, u32[]{:S(2)}) copy-start(bf16[8,16,3072]{2,1,0:T(8,128)(2,1)S(1)} %collective-permute-done.18.refs_10_) | copy-start | bytes 2359300
  80.3 20.0 %collective-permute-start.20 = (bf16[8,8,3072]{2,1,0:T(8,128)(2,1)S(1)}, bf16[8,8,3072]{2,1,0:T(8,128)(2,1)}, u32[]{:S(2)}, u32[]{:S(2)}) collective-permute-start(bf16[8,8,3072]{2,1,0:T(8,128)(2,1)S(1)} %slice.94), channel_id=1, source_target_pairs={{0,64},{64,128},{128,192},{192,0},{1,65},{65,129},{129,193},{193,1... | collective-permute-start | bytes 1179656 | tf_op jit(solution)/shard_map/ppermute | solution.py:36
  80.4 19.9 %copy-start.3 = (bf16[8,16,3072]{2,1,0:T(8,128)(2,1)}, bf16[8,16,3072]{2,1,0:T(8,128)(2,1)S(1)}, u32[]{:S(2)}) copy-start(bf16[8,16,3072]{2,1,0:T(8,128)(2,1)S(1)} %collective-permute-done.19.refs_11_) | copy-start | bytes 2359300
  80.5 19.9 %collective-permute-start.21 = (bf16[8,8,3072]{2,1,0:T(8,128)(2,1)S(1)}, bf16[8,8,3072]{2,1,0:T(8,128)(2,1)}, u32[]{:S(2)}, u32[]{:S(2)}) collective-permute-start(bf16[8,8,3072]{2,1,0:T(8,128)(2,1)S(1)} %slice.95), channel_id=1, source_target_pairs={{0,192},{64,0},{128,64},{192,128},{1,193},{65,1},{129,65},{193,129... | collective-permute-start | bytes 1179656 | tf_op jit(solution)/shard_map/ppermute | solution.py:36
  88.5 10.7 %collective-permute-start.9 = (bf16[4,8,3072]{2,1,0:T(8,128)(2,1)S(1)}, bf16[4,8,3072]{2,1,0:T(8,128)(2,1)S(1)}, u32[]{:S(2)}, u32[]{:S(2)}) collective-permute-start(bf16[4,8,3072]{2,1,0:T(8,128)(2,1)S(1)} %slice.91), channel_id=1, source_target_pairs={{0,8},{8,16},{16,24},{24,32},{32,40},{40,48},{48,56},{56,0},{1,9},... | collective-permute-start | bytes 589832 | tf_op jit(solution)/shard_map/ppermute | solution.py:36
  93.3 7.0 %collective-permute-start.10 = (bf16[4,8,3072]{2,1,0:T(8,128)(2,1)S(1)}, bf16[4,8,3072]{2,1,0:T(8,128)(2,1)S(1)}, u32[]{:S(2)}, u32[]{:S(2)}) collective-permute-start(bf16[4,8,3072]{2,1,0:T(8,128)(2,1)S(1)} %slice.92), channel_id=1, source_target_pairs={{0,56},{8,0},{16,8},{24,16},{32,24},{40,32},{48,40},{56,48},{1,57}... | collective-permute-start | bytes 589832 | tf_op jit(solution)/shard_map/ppermute | solution.py:36
  99.2 1.2 copy-start.7
  100.3 0.7 copy-start.8
  127.9 14.3 %collective-permute-start.22 = (bf16[4,32,1792]{2,1,0:T(8,128)(2,1)}, bf16[4,32,1792]{2,1,0:T(8,128)(2,1)}, u32[]{:S(2)}, u32[]{:S(2)}) collective-permute-start(bf16[4,32,1792]{2,1,0:T(8,128)(2,1)} %get-tuple-element.39), channel_id=1, source_target_pairs={{0,8},{8,16},{16,24},{24,32},{32,40},{40,48},{48,56},{56,0},{1,9},... | collective-permute-start | bytes 1376264 | tf_op jit(solution)/shard_map/ppermute | solution.py:36
  141.0 24.6 %collective-permute-start.26 = (bf16[4,32,1792]{2,1,0:T(8,128)(2,1)S(1)}, bf16[4,32,1792]{2,1,0:T(8,128)(2,1)S(1)}, u32[]{:S(2)}, u32[]{:S(2)}) collective-permute-start(bf16[4,32,1792]{2,1,0:T(8,128)(2,1)S(1)} %get-tuple-element.55), channel_id=1, source_target_pairs={{0,56},{8,0},{16,8},{24,16},{32,24},{40,32},{48,40},{56,48},{1,57}... | collective-permute-start | bytes 1376264 | tf_op jit(solution)/shard_map/ppermute | solution.py:36
  145.4 17.0 %all-to-all-start.1 = ((f32[32,2,128]{2,1,0:T(2,128)}), f32[32,2,128]{2,1,0:T(2,128)S(1)}, u32[]{:S(2)}, u32[]{:S(2)}) async-start(f32[32,2,128]{2,1,0:T(2,128)} %broadcast_in_dim.12), calls=%async_computation.1 | async-start | bytes 65536 | tf_op jit(solution)/shard_map/all_to_all | solution.py:84
  153.5 15.3 %collective-permute-start.23 = (bf16[4,32,1792]{2,1,0:T(8,128)(2,1)}, bf16[4,32,1792]{2,1,0:T(8,128)(2,1)}, u32[]{:S(2)}, u32[]{:S(2)}) collective-permute-start(bf16[4,32,1792]{2,1,0:T(8,128)(2,1)} %add_convert_fusion.5), channel_id=1, source_target_pairs={{0,8},{8,16},{16,24},{24,32},{32,40},{40,48},{48,56},{56,0},{1,9},... | collective-permute-start | bytes 1376264 | tf_op jit(solution)/shard_map/ppermute | solution.py:36
  165.6 14.8 %collective-permute-start.27 = (bf16[4,32,1792]{2,1,0:T(8,128)(2,1)S(1)}, bf16[4,32,1792]{2,1,0:T(8,128)(2,1)S(1)}, u32[]{:S(2)}, u32[]{:S(2)}) collective-permute-start(bf16[4,32,1792]{2,1,0:T(8,128)(2,1)S(1)} %add_convert_fusion.2), channel_id=1, source_target_pairs={{0,56},{8,0},{16,8},{24,16},{32,24},{40,32},{48,40},{56,48},{1,57}... | collective-permute-start | bytes 1376264 | tf_op jit(solution)/shard_map/ppermute | solution.py:36
  170.5 9.9 %all-to-all-start.2 = ((f32[8,2,128]{2,1,0:T(2,128)}), f32[8,2,128]{2,1,0:T(2,128)S(1)}, u32[]{:S(2)}, u32[]{:S(2)}) async-start(f32[8,2,128]{2,1,0:T(2,128)} %broadcast_in_dim.13), calls=%async_computation.3 | async-start | bytes 16384 | tf_op jit(solution)/shard_map/all_to_all | solution.py:84
  175.7 36.6 %reduce-scatter.5.cloned.1.call-start = ((), (), s32[]{:S(2)}) async-start(), calls=%async_computation.7 | async-start | bytes 737280 | tf_op jit(solution)/shard_map/reduce_scatter | solution.py:409
  175.7 13.3 %collective-permute-start.24 = (bf16[4,32,1792]{2,1,0:T(8,128)(2,1)S(1)}, bf16[4,32,1792]{2,1,0:T(8,128)(2,1)}, u32[]{:S(2)}, u32[]{:S(2)}) collective-permute-start(bf16[4,32,1792]{2,1,0:T(8,128)(2,1)S(1)} %add_convert_fusion.4), channel_id=1, source_target_pairs={{0,8},{8,16},{16,24},{24,32},{32,40},{40,48},{48,56},{56,0},{1,9},... | collective-permute-start | bytes 1376264 | tf_op jit(solution)/shard_map/ppermute | solution.py:36
  180.5 31.8 %collective-permute-start.28 = (bf16[4,32,1792]{2,1,0:T(8,128)(2,1)S(1)}, bf16[4,32,1792]{2,1,0:T(8,128)(2,1)S(1)}, u32[]{:S(2)}, u32[]{:S(2)}) collective-permute-start(bf16[4,32,1792]{2,1,0:T(8,128)(2,1)S(1)} %add_convert_fusion.1), channel_id=1, source_target_pairs={{0,56},{8,0},{16,8},{24,16},{32,24},{40,32},{48,40},{56,48},{1,57}... | collective-permute-start | bytes 1376264 | tf_op jit(solution)/shard_map/ppermute | solution.py:36
  190.1 22.2 %collective-permute-start.25 = (bf16[4,32,1792]{2,1,0:T(8,128)(2,1)S(1)}, bf16[4,32,1792]{2,1,0:T(8,128)(2,1)S(1)}, u32[]{:S(2)}, u32[]{:S(2)}) collective-permute-start(bf16[4,32,1792]{2,1,0:T(8,128)(2,1)S(1)} %add_convert_fusion.3), channel_id=1, source_target_pairs={{0,8},{8,16},{16,24},{24,32},{32,40},{40,48},{48,56},{56,0},{1,9},... | collective-permute-start | bytes 1376264 | tf_op jit(solution)/shard_map/ppermute | solution.py:36
  212.3 7.6 %copy-start.4 = (bf16[32,1280]{1,0:T(8,128)(2,1)S(1)}, bf16[32,1280]{1,0:T(8,128)(2,1)}, u32[]{:S(2)}) copy-start(bf16[32,1280]{1,0:T(8,128)(2,1)} %reduce-scatter.5.cloned.1.call-done) | copy-start | bytes 245764
  212.5 5.2 %collective-permute-start.31 = (bf16[32,1792]{1,0:T(8,128)(2,1)S(1)}, bf16[32,1792]{1,0:T(8,128)(2,1)S(1)}, u32[]{:S(2)}, u32[]{:S(2)}) collective-permute-start(bf16[32,1792]{1,0:T(8,128)(2,1)S(1)} %get-tuple-element.83), channel_id=1, source_target_pairs={{0,128},{64,192},{128,0},{192,64},{1,129},{65,193},{129,1},{193,65... | collective-permute-start | bytes 344072 | tf_op jit(solution)/shard_map/ppermute | solution.py:36
  215.0 4.9 %collective-permute-start.30 = (bf16[32,1792]{1,0:T(8,128)(2,1)S(1)}, bf16[32,1792]{1,0:T(8,128)(2,1)S(1)}, u32[]{:S(2)}, u32[]{:S(2)}) collective-permute-start(bf16[32,1792]{1,0:T(8,128)(2,1)S(1)} %get-tuple-element.84), channel_id=1, source_target_pairs={{0,64},{64,128},{128,192},{192,0},{1,65},{65,129},{129,193},{193,1... | collective-permute-start | bytes 344072 | tf_op jit(solution)/shard_map/ppermute | solution.py:36
  215.6 4.3 %collective-permute-start.29 = (bf16[32,1792]{1,0:T(8,128)(2,1)S(1)}, bf16[32,1792]{1,0:T(8,128)(2,1)S(1)}, u32[]{:S(2)}, u32[]{:S(2)}) collective-permute-start(bf16[32,1792]{1,0:T(8,128)(2,1)S(1)} %get-tuple-element.82), channel_id=1, source_target_pairs={{0,192},{64,0},{128,64},{192,128},{1,193},{65,1},{129,65},{193,129... | collective-permute-start | bytes 344072 | tf_op jit(solution)/shard_map/ppermute | solution.py:36
  220.7 19.2 %all-to-all-start.3 = ((bf16[8,4,3072]{2,1,0:T(4,128)(2,1)}), bf16[8,4,3072]{2,1,0:T(4,128)(2,1)S(1)}, u32[]{:S(2)}, u32[]{:S(2)}) async-start(bf16[8,4,3072]{2,1,0:T(4,128)(2,1)} %reshape.73), calls=%async_computation.5 | async-start | bytes 393216 | tf_op jit(solution)/shard_map/all_to_all | solution.py:429
Sparse Core Ops, SparseCore 0:
  27.6 100.2 all-gather.2
  130.5 35.0 reduce-scatter.2
  179.0 33.2 reduce-scatter.4

commit v5 on v4

--- a/solution.py
+++ b/solution.py
@@ -28,7 +28,7 @@
 TILE = NZ * SLOTS
 MID = SLOTS // 2
 COLS = 512
-LEFT = 1792
+LEFT = 2304
 
 
 def shift(a, axis, step):

time: 248 us -> 253 us (1.020)
  waiting for transfers between devices: 84.5 us -> 87.5 us
    ppermute x32, waiting for transfers between devices: 43 us -> 52.1 us  [shift(): return lax.ppermute(a, axis, [(i, (i + step) % n) for i in range(n)])]
    reduce_scatter x1, waiting for transfers between devices: 3.04 us -> 0.01 us  [on_device(): lax.psum_scatter(right.reshape(ROWS, D - LEFT), 'x', scatter_dimension=0,...]
    reduce_scatter x1, waiting for transfers between devices: 12.5 us -> 9.79 us  [hook(): kept['line'] = lax.psum_scatter(line, 'z', scatter_dimension=0, tiled=True)]
    unnamed x30 -> x36, local copies, waits for them, and re-layouts: 5.98 us -> 5.98 us
  transfers between devices with their start and end apart: 38 -> 38, of which waited for: 17 -> 16; matrix products, arithmetic and copies ran while one was open for 7% -> 8% of each run, Pallas kernels for 16% -> 16%
where the time goes in v5:
time: 253 us; the launch traced here: 252 us
  waiting for transfers between devices  87.5 us (35%)
  starting transfers between devices  68.2 us (27%)
  Pallas kernels  40.2 us (16%)
  local copies, waits for them, and re-layouts  15.5 us (6%)
  between operations  14.2 us (6%)
  blocking collectives  14 us (6%)
  other arithmetic  10.3 us (4%)
    ppermute x32, waiting for transfers between devices, shift(): return lax.ppermute(a, axis, [(i, (i + step) % n) for i in range(n)])  52.1 us
    ppermute x32, starting transfers between devices, shift(): return lax.ppermute(a, axis, [(i, (i + step) % n) for i in range(n)])  43.2 us
    all_to_all x2, starting transfers between devices, spread(): lax.all_to_all(jnp.broadcast_to(a[None], (n,) + a.shape), axes, 0, 0, til...  14.5 us
    all_to_all x1, blocking collectives, on_device(): got = lax.all_to_all(send, EXPERT, split_axis=0, concat_axis=0, tiled=True)  14 us
    all_gather x1, waiting for transfers between devices, on_device(): lax.all_gather(jnp.concatenate([local_dy] + parts, axis=1), ('x', 'z'), a...  13.6 us
    pallas_call x1, Pallas kernels, forward(): pl.pallas_call(forward_kernel, grid_spec=pltpu.PrefetchScalarGridSpec(num...  13.1 us
    all_to_all x2, waiting for transfers between devices, spread(): lax.all_to_all(jnp.broadcast_to(a[None], (n,) + a.shape), axes, 0, 0, til...  11.3 us
    all_to_all x1, starting transfers between devices, on_device(): lax.all_to_all(own_out.reshape(NE, CAP, width), EXPERT, split_axis=0, con...  10.4 us
  transfers between devices with their start and end apart: 38, of which 16 were waited for; matrix products, arithmetic and copies ran while one was open for 8% of the time, Pallas kernels for 16%

profile of v5, /device:TPU:1, one launch (start us, length us, event | category | flops | bytes accessed | tf_op | source)
XLA Modules:
  0.0 252.5 jit_solution(1509363526180499696)
XLA Ops:
  7.2 0.8 copy.28
  8.6 0.7 multiply_add_fusion
  9.5 0.7 multiply_reduce_fusion
  10.4 1.1 convolution_convert_fusion
  12.0 14.0 %all_to_all.20 = bf16[8,8,3200]{2,1,0:T(8,128)(2,1)S(1)} all-to-all(bf16[8,8,3200]{2,1,0:T(8,128)(2,1)S(1)} %pad_maximum_fusion), channel_id=1, replica_groups=mesh['x'=4,'z'=8,'y'=4,'c'=2] {'y','c'}, dimensions={0} | all-to-all | bytes 819200 | tf_op jit(solution)/shard_map/all_to_all | solution.py:380
  26.7 0.8 concatenate.22
  27.7 1.3 collective-permute-start
  29.0 1.5 collective-permute-start.1
  30.5 1.7 collective-permute-start.11
  32.2 4.0 %collective-permute-start.12 = (bf16[16,3072]{1,0:T(8,128)(2,1)S(1)}, bf16[16,3072]{1,0:T(8,128)(2,1)S(1)}, u32[]{:S(2)}, u32[]{:S(2)}) collective-permute-start(bf16[16,3072]{1,0:T(8,128)(2,1)S(1)} %slice.73), channel_id=1, source_target_pairs={{0,56},{8,0},{16,8},{24,16},{32,24},{40,32},{48,40},{56,48},{1,57}... | collective-permute-start | bytes 294920 | tf_op jit(solution)/shard_map/ppermute | solution.py:36
  36.2 0.7 constant_dynamic-update-slice_fusion
  37.0 1.1 collective-permute-done.11
  38.2 2.8 %collective-permute-start.14 = (bf16[16,3072]{1,0:T(8,128)(2,1)S(1)}, bf16[16,3072]{1,0:T(8,128)(2,1)S(1)}, u32[]{:S(2)}, u32[]{:S(2)}) collective-permute-start(bf16[16,3072]{1,0:T(8,128)(2,1)S(1)} %collective-permute-done.12), channel_id=1, source_target_pairs={{0,56},{8,0},{16,8},{24,16},{32,24},{40,32},{48,40},{56,48},{1,57}... | collective-permute-start | bytes 294920 | tf_op jit(solution)/shard_map/ppermute | solution.py:36
  40.9 0.6 bitcast_dynamic-update-slice_fusion.6
  41.6 0.6 bitcast_dynamic-update-slice_fusion.5
  42.4 2.7 %collective-permute-start.4 = (bf16[4,16,3072]{2,1,0:T(8,128)(2,1)S(1)}, bf16[4,16,3072]{2,1,0:T(8,128)(2,1)S(1)}, u32[]{:S(2)}, u32[]{:S(2)}) collective-permute-start(bf16[4,16,3072]{2,1,0:T(8,128)(2,1)S(1)} %pad_maximum_fusion.1.refs_0_), channel_id=1, source_target_pairs={{0,56},{8,0},{16,8},{24,16},{32,24},{40,32},{48,40},{56,48},{1,57}... | collective-permute-start | bytes 1179656 | tf_op jit(solution)/shard_map/ppermute | solution.py:36
  45.0 2.7 %collective-permute-start.16 = (bf16[16,3072]{1,0:T(8,128)(2,1)S(1)}, bf16[16,3072]{1,0:T(8,128)(2,1)S(1)}, u32[]{:S(2)}, u32[]{:S(2)}) collective-permute-start(bf16[16,3072]{1,0:T(8,128)(2,1)S(1)} %collective-permute-done.14), channel_id=1, source_target_pairs={{0,56},{8,0},{16,8},{24,16},{32,24},{40,32},{48,40},{56,48},{1,57}... | collective-permute-start | bytes 294920 | tf_op jit(solution)/shard_map/ppermute | solution.py:36
  47.7 0.6 bitcast_dynamic-update-slice_fusion.4
  49.0 9.3 %collective-permute-done.15 = bf16[16,3072]{1,0:T(8,128)(2,1)S(1)} collective-permute-done((bf16[16,3072]{1,0:T(8,128)(2,1)S(1)}, bf16[16,3072]{1,0:T(8,128)(2,1)S(1)}, u32[]{:S(2)}, u32[]{:S(2)}) %collective-permute-start.15) | collective-permute-done | bytes 98336 | tf_op jit(solution)/shard_map/ppermute | solution.py:36
  59.5 4.3 %collective-permute-done.17 = bf16[16,3072]{1,0:T(8,128)(2,1)S(1)} collective-permute-done((bf16[16,3072]{1,0:T(8,128)(2,1)S(1)}, bf16[16,3072]{1,0:T(8,128)(2,1)S(1)}, u32[]{:S(2)}, u32[]{:S(2)}) %collective-permute-start.17) | collective-permute-done | bytes 98336 | tf_op jit(solution)/shard_map/ppermute | solution.py:36
  63.9 0.6 bitcast_dynamic-update-slice_fusion.refs_9_
  64.5 2.6 %collective-permute-start.19 = (bf16[8,16,3072]{2,1,0:T(8,128)(2,1)}, bf16[8,16,3072]{2,1,0:T(8,128)(2,1)S(1)}, u32[]{:S(2)}, u32[]{:S(2)}) collective-permute-start(bf16[8,16,3072]{2,1,0:T(8,128)(2,1)} %bitcast_dynamic-update-slice_fusion.refs_9_), channel_id=1, source_target_pairs={{0,192},{64,0},{128,64},{192,128},{1,193},{65,1},{129,65},{193,129... | collective-permute-start | bytes 2359304 | tf_op jit(solution)/shard_map/ppermute | solution.py:36
  67.2 2.7 %collective-permute-start.6 = (bf16[4,16,3072]{2,1,0:T(8,128)(2,1)S(1)}, bf16[4,16,3072]{2,1,0:T(8,128)(2,1)}, u32[]{:S(2)}, u32[]{:S(2)}) collective-permute-start(bf16[4,16,3072]{2,1,0:T(8,128)(2,1)S(1)} %collective-permute-done.4.refs_2_), channel_id=1, source_target_pairs={{0,56},{8,0},{16,8},{24,16},{32,24},{40,32},{48,40},{56,48},{1,57}... | collective-permute-start | bytes 1179656 | tf_op jit(solution)/shard_map/ppermute | solution.py:36
  69.9 5.4 %collective-permute-done.5.refs_3_ = bf16[4,16,3072]{2,1,0:T(8,128)(2,1)} collective-permute-done((bf16[4,16,3072]{2,1,0:T(8,128)(2,1)S(1)}, bf16[4,16,3072]{2,1,0:T(8,128)(2,1)}, u32[]{:S(2)}, u32[]{:S(2)}) %collective-permute-start.5) | collective-permute-done | bytes 393248 | tf_op jit(solution)/shard_map/ppermute | solution.py:36
  75.3 2.7 %collective-permute-start.8 = (bf16[4,16,3072]{2,1,0:T(8,128)(2,1)}, bf16[4,16,3072]{2,1,0:T(8,128)(2,1)}, u32[]{:S(2)}, u32[]{:S(2)}) collective-permute-start(bf16[4,16,3072]{2,1,0:T(8,128)(2,1)} %collective-permute-done.6.refs_4_), channel_id=1, source_target_pairs={{0,56},{8,0},{16,8},{24,16},{32,24},{40,32},{48,40},{56,48},{1,57}... | collective-permute-start | bytes 1179656 | tf_op jit(solution)/shard_map/ppermute | solution.py:36
  78.0 2.2 collective-permute-done.18.refs_10_
  80.4 2.7 %collective-permute-start.21 = (bf16[8,8,3072]{2,1,0:T(8,128)(2,1)S(1)}, bf16[8,8,3072]{2,1,0:T(8,128)(2,1)}, u32[]{:S(2)}, u32[]{:S(2)}) collective-permute-start(bf16[8,8,3072]{2,1,0:T(8,128)(2,1)S(1)} %slice.95), channel_id=1, source_target_pairs={{0,192},{64,0},{128,64},{192,128},{1,193},{65,1},{129,65},{193,129... | collective-permute-start | bytes 1179656 | tf_op jit(solution)/shard_map/ppermute | solution.py:36
  83.1 5.9 %collective-permute-done.7.refs_5_ = bf16[4,16,3072]{2,1,0:T(8,128)(2,1)S(1)} collective-permute-done((bf16[4,16,3072]{2,1,0:T(8,128)(2,1)}, bf16[4,16,3072]{2,1,0:T(8,128)(2,1)S(1)}, u32[]{:S(2)}, u32[]{:S(2)}) %collective-permute-start.7) | collective-permute-done | bytes 393248 | tf_op jit(solution)/shard_map/ppermute | solution.py:36
  89.2 3.3 %collective-permute-done.8.refs_6_ = bf16[4,16,3072]{2,1,0:T(8,128)(2,1)} collective-permute-done((bf16[4,16,3072]{2,1,0:T(8,128)(2,1)}, bf16[4,16,3072]{2,1,0:T(8,128)(2,1)}, u32[]{:S(2)}, u32[]{:S(2)}) %collective-permute-start.8) | collective-permute-done | bytes 393248 | tf_op jit(solution)/shard_map/ppermute | solution.py:36
  92.5 0.9 slice.92
  93.4 3.5 %collective-permute-start.10 = (bf16[4,8,3072]{2,1,0:T(8,128)(2,1)S(1)}, bf16[4,8,3072]{2,1,0:T(8,128)(2,1)S(1)}, u32[]{:S(2)}, u32[]{:S(2)}) collective-permute-start(bf16[4,8,3072]{2,1,0:T(8,128)(2,1)S(1)} %slice.92), channel_id=1, source_target_pairs={{0,56},{8,0},{16,8},{24,16},{32,24},{40,32},{48,40},{56,48},{1,57}... | collective-permute-start | bytes 589832 | tf_op jit(solution)/shard_map/ppermute | solution.py:36
  96.9 0.7 pad_add_fusion.where_ref
  97.6 1.9 collective-permute-done.9.refs_7_
  99.4 1.0 collective-permute-done.10.refs_8_
  100.4 0.7 copy-done.11
  101.1 13.1 %forward.1 = (bf16[4,8,32,3072]{3,2,1,0:T(8,128)(2,1)}, f32[1024,256]{1,0:T(8,128)}, f32[1024,256]{1,0:T(8,128)}, bf16[1024,256]{1,0:T(8,128)(2,1)}, bf16[4,32,2...) custom-call(s32[12]{0:T(128)} %pad_add_fusion.where_ref, ...), custom_call_target="tpu_custom_call" | custom-call | flops 4831838208 | bytes 20971520 | tf_op jit(solution)/shard_map/forward/pallas_call | solution.py:158
  114.2 13.6 %all-gather.3.cloned.1.call-done = bf16[1024,3328]{1,0:T(8,128)(2,1)} async-done(((bf16[32,3328]{1,0:T(8,128)(2,1)}), bf16[1024,3328]{1,0:T(8,128)(2,1)}) %all-gather.3.cloned.1.call-update) | async-done | bytes 6815760 | tf_op jit(solution)/shard_map/all_gather | solution.py:389
  127.8 1.6 collective-permute-start.22
  129.5 3.5 %slice_bitcast_fusion.5 = (bf16[4,32,2304]{2,1,0:T(8,128)(2,1)}, bf16[4,32,2304]{2,1,0:T(8,128)(2,1)}, bf16[4,32,2304]{2,1,0:T(8,128)(2,1)S(1)}, bf16[4,32,2304]...) fusion(bf16[7,4,32,2304]{3,2,1,0:T(8,128)(2,1)} %get-tuple-elem, ...), kind=kLoop, calls=%fused_computation.14 | loop fusion | bytes 8257536 | tf_op jit(solution)/shard_map/squeeze | solution.py:61
  132.9 9.3 %backward.1 = (bf16[1024,256]{1,0:T(8,128)(2,1)}, bf16[1024,256]{1,0:T(8,128)(2,1)}, f32[1024,1]{1,0:T(8,128)}, f32[2,128]{1,0:T(2,128)}) custom-call(s32[12]{0:T(128)} %pad_add_fusion.where_ref, bf16[32,32,3328]{2,1,0:T(8,128)(2,1)} %bitcast.50, bf16[32,32,3328]{2,1,0:T(8,128)(2,1)} %bitcast.51, bf16[1,256,3072]{2,1,0:T(8,128)(2,1)} %wd_ref.1, ...), custom_call_target="tpu_custom_call" | custom-call | flops 2415919104 | bytes 12582912 | tf_op jit(solution)/shard_map/backward/pallas_call | solution.py:240
  142.2 1.3 collective-permute-start.26
  143.5 2.0 add_convert_fusion.5
  146.1 8.9 %all-to-all-start.1 = ((f32[32,2,128]{2,1,0:T(2,128)}), f32[32,2,128]{2,1,0:T(2,128)S(1)}, u32[]{:S(2)}, u32[]{:S(2)}) async-start(f32[32,2,128]{2,1,0:T(2,128)} %broadcast_in_dim.12), calls=%async_computation.1 | async-start | bytes 65536 | tf_op jit(solution)/shard_map/all_to_all | solution.py:84
  155.1 1.5 collective-permute-start.23
  156.6 7.3 %all-to-all-done.1 = f32[32,2,128]{2,1,0:T(2,128)S(1)} async-done(((f32[32,2,128]{2,1,0:T(2,128)}), f32[32,2,128]{2,1,0:T(2,128)S(1)}, u32[]{:S(2)}, u32[]{:S(2)}) %all-to-all-start.1) | async-done | bytes 32800 | tf_op jit(solution)/shard_map/all_to_all | solution.py:84
  164.0 1.2 add_convert_fusion.2
  165.2 0.7 collective-permute-start.27
  166.0 4.9 %collective-permute-done.23 = bf16[4,32,2304]{2,1,0:T(8,128)(2,1)} collective-permute-done((bf16[4,32,2304]{2,1,0:T(8,128)(2,1)}, bf16[4,32,2304]{2,1,0:T(8,128)(2,1)}, u32[]{:S(2)}, u32[]{:S(2)}) %collective-permute-start.23) | collective-permute-done | bytes 589856 | tf_op jit(solution)/shard_map/ppermute | solution.py:36
  170.9 2.0 add_convert_fusion.4
  173.5 5.5 %all-to-all-start.2 = ((f32[8,2,128]{2,1,0:T(2,128)}), f32[8,2,128]{2,1,0:T(2,128)S(1)}, u32[]{:S(2)}, u32[]{:S(2)}) async-start(f32[8,2,128]{2,1,0:T(2,128)} %broadcast_in_dim.13), calls=%async_computation.3 | async-start | bytes 16384 | tf_op jit(solution)/shard_map/all_to_all | solution.py:84
  179.1 0.7 reduce-scatter.5.cloned.1.call-update
  179.8 3.9 %all-to-all-done.2 = f32[8,2,128]{2,1,0:T(2,128)S(1)} async-done(((f32[8,2,128]{2,1,0:T(2,128)}), f32[8,2,128]{2,1,0:T(2,128)S(1)}, u32[]{:S(2)}, u32[]{:S(2)}) %all-to-all-start.2) | async-done | bytes 8224 | tf_op jit(solution)/shard_map/all_to_all | solution.py:84
  183.9 1.3 collective-permute-start.28
  185.1 10.2 %collective-permute-done.24 = bf16[4,32,2304]{2,1,0:T(8,128)(2,1)} collective-permute-done((bf16[4,32,2304]{2,1,0:T(8,128)(2,1)}, bf16[4,32,2304]{2,1,0:T(8,128)(2,1)}, u32[]{:S(2)}, u32[]{:S(2)}) %collective-permute-start.24) | collective-permute-done | bytes 589856 | tf_op jit(solution)/shard_map/ppermute | solution.py:36
  195.3 1.2 add_convert_fusion.3
  197.2 9.1 %wide_gradients.1 = (bf16[1,3072,256]{2,1,0:T(8,128)(2,1)}, bf16[1,3072,256]{2,1,0:T(8,128)(2,1)}) custom-call(bf16[4,8,32,3072]{3,2,1,0:T(8,128)(2,1)} %get-tuple-element.58.x_ref, bf16[1024,256]{1,0:T(8,128)(2,1)} %get-tuple-element.59.dg_ref, bf16[1024,256]{1,0:T(8,128)(2,1)} %get-tuple-element.60.du_ref, f32[1024,1]{1,0:T(8,128)} %get-tuple-element.61.spot_ref, ...), custom_call_target="tpu_custom_call" | custom-call | flops 3145728 | bytes 1048576 | tf_op jit(solution)/shard_map/wide_gradients/pallas_call | solution.py:293
  206.3 9.8 %reduce-scatter.5.cloned.1.call-done = bf16[32,768]{1,0:T(8,128)(2,1)} async-done(((bf16[256,768]{1,0:T(8,128)(2,1)}), bf16[32,768]{1,0:T(8,128)(2,1)}) %reduce-scatter.5.cloned.1.call-update) | async-done | bytes 49168 | tf_op jit(solution)/shard_map/reduce_scatter | solution.py:409
  216.4 2.9 %collective-permute-start.31 = (bf16[32,2304]{1,0:T(8,128)(2,1)S(1)}, bf16[32,2304]{1,0:T(8,128)(2,1)S(1)}, u32[]{:S(2)}, u32[]{:S(2)}) collective-permute-start(bf16[32,2304]{1,0:T(8,128)(2,1)S(1)} %get-tuple-element.83), channel_id=1, source_target_pairs={{0,128},{64,192},{128,0},{192,64},{1,129},{65,193},{129,1},{193,65... | collective-permute-start | bytes 442376 | tf_op jit(solution)/shard_map/ppermute | solution.py:36
  219.5 2.5 collective-permute-start.29
  222.0 2.5 collective-permute-done.30
  224.6 0.8 reshape.73
  225.4 10.4 %all-to-all-start.3 = ((bf16[8,4,3072]{2,1,0:T(4,128)(2,1)}), bf16[8,4,3072]{2,1,0:T(4,128)(2,1)S(1)}, u32[]{:S(2)}, u32[]{:S(2)}) async-start(bf16[8,4,3072]{2,1,0:T(4,128)(2,1)} %reshape.73), calls=%async_computation.5 | async-start | bytes 393216 | tf_op jit(solution)/shard_map/all_to_all | solution.py:429
  236.4 8.7 %down_gradient.1 = bf16[1,256,3072]{2,1,0:T(8,128)(2,1)} custom-call(s32[12]{0:T(128)} %pad_add_fusion.where_ref, bf16[32,32,3328]{2,1,0:T(8,128)(2,1)} %bitcast.52, bf16[1024,256]{1,0:T(8,128)(2,1)} %get-tuple-element.72.hidden_ref, f32[1024,1]{1,0:T(8,128)} %get-tuple-element.61.spot_ref, f32[2,128]{1,0:T(2,128)} %get-tuple-element.63.factor_ref), custom_call_target="tpu_custom_call" | custom-call | flops 3145728 | bytes 1048576 | tf_op jit(solution)/shard_map/down_gradient/pallas_call | solution.py:332
  245.2 0.8 convolution_convert_fusion.2
  (115 shorter events, 8.2 us)
Async XLA Ops:
  7.2 3.0 %copy-start = (bf16[12,3072]{1,0:T(8,128)(2,1)S(1)}, bf16[12,3072]{1,0:T(8,128)(2,1)}, u32[]{:S(2)}) copy-start(bf16[12,3072]{1,0:T(8,128)(2,1)} %param.9) | copy-start | bytes 221188
  7.2 120.6 %all-gather.3.cloned.1.call-start = ((), (), s32[]{:S(2)}) async-start(), calls=%async_computation.8 | async-start | bytes 7028736 | tf_op jit(solution)/shard_map/all_gather | solution.py:389
  27.5 136.5 %reduce-scatter.3.cloned.1.call-start = ((), (), s32[]{:S(2)}) async-start(), calls=%async_computation.6 | async-start | bytes 1966080 | tf_op jit(solution)/shard_map/reduce_scatter | solution.py:398
  27.7 9.2 %collective-permute-start = (bf16[16,3072]{1,0:T(8,128)(2,1)S(1)}, bf16[16,3072]{1,0:T(8,128)(2,1)S(1)}, u32[]{:S(2)}, u32[]{:S(2)}) collective-permute-start(bf16[16,3072]{1,0:T(8,128)(2,1)S(1)} %slice.69), channel_id=1, source_target_pairs={{0,64},{64,128},{128,192},{192,0},{1,65},{65,129},{129,193},{193,1... | collective-permute-start | bytes 294920 | tf_op jit(solution)/shard_map/ppermute | solution.py:36
  29.0 13.2 %collective-permute-start.1 = (bf16[16,3072]{1,0:T(8,128)(2,1)S(1)}, bf16[16,3072]{1,0:T(8,128)(2,1)S(1)}, u32[]{:S(2)}, u32[]{:S(2)}) collective-permute-start(bf16[16,3072]{1,0:T(8,128)(2,1)S(1)} %slice.69), channel_id=1, source_target_pairs={{0,192},{64,0},{128,64},{192,128},{1,193},{65,1},{129,65},{193,129... | collective-permute-start | bytes 294920 | tf_op jit(solution)/shard_map/ppermute | solution.py:36
  30.5 7.7 %collective-permute-start.11 = (bf16[16,3072]{1,0:T(8,128)(2,1)S(1)}, bf16[16,3072]{1,0:T(8,128)(2,1)S(1)}, u32[]{:S(2)}, u32[]{:S(2)}) collective-permute-start(bf16[16,3072]{1,0:T(8,128)(2,1)S(1)} %slice.73), channel_id=1, source_target_pairs={{0,8},{8,16},{16,24},{24,32},{32,40},{40,48},{48,56},{56,0},{1,9},... | collective-permute-start | bytes 294920 | tf_op jit(solution)/shard_map/ppermute | solution.py:36
  32.2 5.9 %collective-permute-start.12 = (bf16[16,3072]{1,0:T(8,128)(2,1)S(1)}, bf16[16,3072]{1,0:T(8,128)(2,1)S(1)}, u32[]{:S(2)}, u32[]{:S(2)}) collective-permute-start(bf16[16,3072]{1,0:T(8,128)(2,1)S(1)} %slice.73), channel_id=1, source_target_pairs={{0,56},{8,0},{16,8},{24,16},{32,24},{40,32},{48,40},{56,48},{1,57}... | collective-permute-start | bytes 294920 | tf_op jit(solution)/shard_map/ppermute | solution.py:36
  36.9 5.3 %collective-permute-start.2 = (bf16[16,3072]{1,0:T(8,128)(2,1)S(1)}, bf16[16,3072]{1,0:T(8,128)(2,1)S(1)}, u32[]{:S(2)}, u32[]{:S(2)}) collective-permute-start(bf16[16,3072]{1,0:T(8,128)(2,1)S(1)} %collective-permute-done), channel_id=1, source_target_pairs={{0,64},{64,128},{128,192},{192,0},{1,65},{65,129},{129,193},{193,1... | collective-permute-start | bytes 294920 | tf_op jit(solution)/shard_map/ppermute | solution.py:36
  38.2 6.9 %collective-permute-start.13 = (bf16[16,3072]{1,0:T(8,128)(2,1)S(1)}, bf16[16,3072]{1,0:T(8,128)(2,1)S(1)}, u32[]{:S(2)}, u32[]{:S(2)}) collective-permute-start(bf16[16,3072]{1,0:T(8,128)(2,1)S(1)} %collective-permute-done.11), channel_id=1, source_target_pairs={{0,8},{8,16},{16,24},{24,32},{32,40},{40,48},{48,56},{56,0},{1,9},... | collective-permute-start | bytes 294920 | tf_op jit(solution)/shard_map/ppermute | solution.py:36
  38.2 6.9 %collective-permute-start.14 = (bf16[16,3072]{1,0:T(8,128)(2,1)S(1)}, bf16[16,3072]{1,0:T(8,128)(2,1)S(1)}, u32[]{:S(2)}, u32[]{:S(2)}) collective-permute-start(bf16[16,3072]{1,0:T(8,128)(2,1)S(1)} %collective-permute-done.12), channel_id=1, source_target_pairs={{0,56},{8,0},{16,8},{24,16},{32,24},{40,32},{48,40},{56,48},{1,57}... | collective-permute-start | bytes 294920 | tf_op jit(solution)/shard_map/ppermute | solution.py:36
  42.3 38.1 %copy-start.2 = (bf16[4,16,3072]{2,1,0:T(8,128)(2,1)}, bf16[4,16,3072]{2,1,0:T(8,128)(2,1)S(1)}, u32[]{:S(2)}) copy-start(bf16[4,16,3072]{2,1,0:T(8,128)(2,1)S(1)} %pad_maximum_fusion.1.refs_0_) | copy-start | bytes 1179652
  42.3 24.9 %collective-permute-start.3 = (bf16[4,16,3072]{2,1,0:T(8,128)(2,1)S(1)}, bf16[4,16,3072]{2,1,0:T(8,128)(2,1)S(1)}, u32[]{:S(2)}, u32[]{:S(2)}) collective-permute-start(bf16[4,16,3072]{2,1,0:T(8,128)(2,1)S(1)} %pad_maximum_fusion.1.refs_0_), channel_id=1, source_target_pairs={{0,8},{8,16},{16,24},{24,32},{32,40},{40,48},{48,56},{56,0},{1,9},... | collective-permute-start | bytes 1179656 | tf_op jit(solution)/shard_map/ppermute | solution.py:36
  42.4 24.8 %collective-permute-start.4 = (bf16[4,16,3072]{2,1,0:T(8,128)(2,1)S(1)}, bf16[4,16,3072]{2,1,0:T(8,128)(2,1)S(1)}, u32[]{:S(2)}, u32[]{:S(2)}) collective-permute-start(bf16[4,16,3072]{2,1,0:T(8,128)(2,1)S(1)} %pad_maximum_fusion.1.refs_0_), channel_id=1, source_target_pairs={{0,56},{8,0},{16,8},{24,16},{32,24},{40,32},{48,40},{56,48},{1,57}... | collective-permute-start | bytes 1179656 | tf_op jit(solution)/shard_map/ppermute | solution.py:36
  45.0 13.2 %collective-permute-start.15 = (bf16[16,3072]{1,0:T(8,128)(2,1)S(1)}, bf16[16,3072]{1,0:T(8,128)(2,1)S(1)}, u32[]{:S(2)}, u32[]{:S(2)}) collective-permute-start(bf16[16,3072]{1,0:T(8,128)(2,1)S(1)} %collective-permute-done.13), channel_id=1, source_target_pairs={{0,8},{8,16},{16,24},{24,32},{32,40},{40,48},{48,56},{56,0},{1,9},... | collective-permute-start | bytes 294920 | tf_op jit(solution)/shard_map/ppermute | solution.py:36
  45.0 13.9 %collective-permute-start.16 = (bf16[16,3072]{1,0:T(8,128)(2,1)S(1)}, bf16[16,3072]{1,0:T(8,128)(2,1)S(1)}, u32[]{:S(2)}, u32[]{:S(2)}) collective-permute-start(bf16[16,3072]{1,0:T(8,128)(2,1)S(1)} %collective-permute-done.14), channel_id=1, source_target_pairs={{0,56},{8,0},{16,8},{24,16},{32,24},{40,32},{48,40},{56,48},{1,57}... | collective-permute-start | bytes 294920 | tf_op jit(solution)/shard_map/ppermute | solution.py:36
  48.4 34.8 %copy-start.13 = (s32[8]{0:T(128)S(1)}, s32[8]{0:T(128)}, u32[]{:S(2)}) copy-start(s32[8]{0:T(128)} %constant.61.clone) | copy-start | bytes 100
  58.3 5.6 %collective-permute-start.17 = (bf16[16,3072]{1,0:T(8,128)(2,1)S(1)}, bf16[16,3072]{1,0:T(8,128)(2,1)S(1)}, u32[]{:S(2)}, u32[]{:S(2)}) collective-permute-start(bf16[16,3072]{1,0:T(8,128)(2,1)S(1)} %collective-permute-done.15), channel_id=1, source_target_pairs={{0,8},{8,16},{16,24},{24,32},{32,40},{40,48},{48,56},{56,0},{1,9},... | collective-permute-start | bytes 294920 | tf_op jit(solution)/shard_map/ppermute | solution.py:36
  64.5 15.7 %collective-permute-start.18 = (bf16[8,16,3072]{2,1,0:T(8,128)(2,1)}, bf16[8,16,3072]{2,1,0:T(8,128)(2,1)S(1)}, u32[]{:S(2)}, u32[]{:S(2)}) collective-permute-start(bf16[8,16,3072]{2,1,0:T(8,128)(2,1)} %bitcast_dynamic-update-slice_fusion.refs_9_), channel_id=1, source_target_pairs={{0,64},{64,128},{128,192},{192,0},{1,65},{65,129},{129,193},{193,1... | collective-permute-start | bytes 2359304 | tf_op jit(solution)/shard_map/ppermute | solution.py:36
  64.5 15.8 %collective-permute-start.19 = (bf16[8,16,3072]{2,1,0:T(8,128)(2,1)}, bf16[8,16,3072]{2,1,0:T(8,128)(2,1)S(1)}, u32[]{:S(2)}, u32[]{:S(2)}) collective-permute-start(bf16[8,16,3072]{2,1,0:T(8,128)(2,1)} %bitcast_dynamic-update-slice_fusion.refs_9_), channel_id=1, source_target_pairs={{0,192},{64,0},{128,64},{192,128},{1,193},{65,1},{129,65},{193,129... | collective-permute-start | bytes 2359304 | tf_op jit(solution)/shard_map/ppermute | solution.py:36
  67.2 2.7 %copy-start.8 = (bf16[4,16,3072]{2,1,0:T(8,128)(2,1)}, bf16[4,16,3072]{2,1,0:T(8,128)(2,1)S(1)}, u32[]{:S(2)}) copy-start(bf16[4,16,3072]{2,1,0:T(8,128)(2,1)S(1)} %collective-permute-done.3.refs_1_) | copy-start | bytes 1179652
  67.2 8.1 %collective-permute-start.5 = (bf16[4,16,3072]{2,1,0:T(8,128)(2,1)S(1)}, bf16[4,16,3072]{2,1,0:T(8,128)(2,1)}, u32[]{:S(2)}, u32[]{:S(2)}) collective-permute-start(bf16[4,16,3072]{2,1,0:T(8,128)(2,1)S(1)} %collective-permute-done.3.refs_1_), channel_id=1, source_target_pairs={{0,8},{8,16},{16,24},{24,32},{32,40},{40,48},{48,56},{56,0},{1,9},... | collective-permute-start | bytes 1179656 | tf_op jit(solution)/shard_map/ppermute | solution.py:36
  67.2 8.1 %copy-start.9 = (bf16[4,16,3072]{2,1,0:T(8,128)(2,1)}, bf16[4,16,3072]{2,1,0:T(8,128)(2,1)S(1)}, u32[]{:S(2)}) copy-start(bf16[4,16,3072]{2,1,0:T(8,128)(2,1)S(1)} %collective-permute-done.4.refs_2_) | copy-start | bytes 1179652
  67.2 8.1 %collective-permute-start.6 = (bf16[4,16,3072]{2,1,0:T(8,128)(2,1)S(1)}, bf16[4,16,3072]{2,1,0:T(8,128)(2,1)}, u32[]{:S(2)}, u32[]{:S(2)}) collective-permute-start(bf16[4,16,3072]{2,1,0:T(8,128)(2,1)S(1)} %collective-permute-done.4.refs_2_), channel_id=1, source_target_pairs={{0,56},{8,0},{16,8},{24,16},{32,24},{40,32},{48,40},{56,48},{1,57}... | collective-permute-start | bytes 1179656 | tf_op jit(solution)/shard_map/ppermute | solution.py:36
  75.3 13.7 %collective-permute-start.7 = (bf16[4,16,3072]{2,1,0:T(8,128)(2,1)}, bf16[4,16,3072]{2,1,0:T(8,128)(2,1)S(1)}, u32[]{:S(2)}, u32[]{:S(2)}) collective-permute-start(bf16[4,16,3072]{2,1,0:T(8,128)(2,1)} %collective-permute-done.5.refs_3_), channel_id=1, source_target_pairs={{0,8},{8,16},{16,24},{24,32},{32,40},{40,48},{48,56},{56,0},{1,9},... | collective-permute-start | bytes 1179656 | tf_op jit(solution)/shard_map/ppermute | solution.py:36
  75.3 17.1 %collective-permute-start.8 = (bf16[4,16,3072]{2,1,0:T(8,128)(2,1)}, bf16[4,16,3072]{2,1,0:T(8,128)(2,1)}, u32[]{:S(2)}, u32[]{:S(2)}) collective-permute-start(bf16[4,16,3072]{2,1,0:T(8,128)(2,1)} %collective-permute-done.6.refs_4_), channel_id=1, source_target_pairs={{0,56},{8,0},{16,8},{24,16},{32,24},{40,32},{48,40},{56,48},{1,57}... | collective-permute-start | bytes 1179656 | tf_op jit(solution)/shard_map/ppermute | solution.py:36
  78.0 18.9 %copy-start.12 = (s32[4]{0:T(128)S(1)}, s32[4]{0:T(128)}, u32[]{:S(2)}) copy-start(s32[4]{0:T(128)} %constant.60.clone) | copy-start | bytes 52
  80.2 13.2 %copy-start.3 = (bf16[8,16,3072]{2,1,0:T(8,128)(2,1)}, bf16[8,16,3072]{2,1,0:T(8,128)(2,1)S(1)}, u32[]{:S(2)}) copy-start(bf16[8,16,3072]{2,1,0:T(8,128)(2,1)S(1)} %collective-permute-done.18.refs_10_) | copy-start | bytes 2359300
  80.2 20.2 %collective-permute-start.20 = (bf16[8,8,3072]{2,1,0:T(8,128)(2,1)S(1)}, bf16[8,8,3072]{2,1,0:T(8,128)(2,1)}, u32[]{:S(2)}, u32[]{:S(2)}) collective-permute-start(bf16[8,8,3072]{2,1,0:T(8,128)(2,1)S(1)} %slice.94), channel_id=1, source_target_pairs={{0,64},{64,128},{128,192},{192,0},{1,65},{65,129},{129,193},{193,1... | collective-permute-start | bytes 1179656 | tf_op jit(solution)/shard_map/ppermute | solution.py:36
  80.3 20.1 %copy-start.4 = (bf16[8,16,3072]{2,1,0:T(8,128)(2,1)}, bf16[8,16,3072]{2,1,0:T(8,128)(2,1)S(1)}, u32[]{:S(2)}) copy-start(bf16[8,16,3072]{2,1,0:T(8,128)(2,1)S(1)} %collective-permute-done.19.refs_11_) | copy-start | bytes 2359300
  80.4 20.0 %collective-permute-start.21 = (bf16[8,8,3072]{2,1,0:T(8,128)(2,1)S(1)}, bf16[8,8,3072]{2,1,0:T(8,128)(2,1)}, u32[]{:S(2)}, u32[]{:S(2)}) collective-permute-start(bf16[8,8,3072]{2,1,0:T(8,128)(2,1)S(1)} %slice.95), channel_id=1, source_target_pairs={{0,192},{64,0},{128,64},{192,128},{1,193},{65,1},{129,65},{193,129... | collective-permute-start | bytes 1179656 | tf_op jit(solution)/shard_map/ppermute | solution.py:36
  89.1 11.4 %copy-start.5 = (bf16[4,16,3072]{2,1,0:T(8,128)(2,1)}, bf16[4,16,3072]{2,1,0:T(8,128)(2,1)S(1)}, u32[]{:S(2)}) copy-start(bf16[4,16,3072]{2,1,0:T(8,128)(2,1)S(1)} %collective-permute-done.7.refs_5_) | copy-start | bytes 1179652
  89.1 10.4 %collective-permute-start.9 = (bf16[4,8,3072]{2,1,0:T(8,128)(2,1)S(1)}, bf16[4,8,3072]{2,1,0:T(8,128)(2,1)S(1)}, u32[]{:S(2)}, u32[]{:S(2)}) collective-permute-start(bf16[4,8,3072]{2,1,0:T(8,128)(2,1)S(1)} %slice.91), channel_id=1, source_target_pairs={{0,8},{8,16},{16,24},{24,32},{32,40},{40,48},{48,56},{56,0},{1,9},... | collective-permute-start | bytes 589832 | tf_op jit(solution)/shard_map/ppermute | solution.py:36
  93.4 7.0 %collective-permute-start.10 = (bf16[4,8,3072]{2,1,0:T(8,128)(2,1)S(1)}, bf16[4,8,3072]{2,1,0:T(8,128)(2,1)S(1)}, u32[]{:S(2)}, u32[]{:S(2)}) collective-permute-start(bf16[4,8,3072]{2,1,0:T(8,128)(2,1)S(1)} %slice.92), channel_id=1, source_target_pairs={{0,56},{8,0},{16,8},{24,16},{32,24},{40,32},{48,40},{56,48},{1,57}... | collective-permute-start | bytes 589832 | tf_op jit(solution)/shard_map/ppermute | solution.py:36
  99.4 1.0 copy-start.10
  100.4 0.7 copy-start.11
  127.8 15.7 %collective-permute-start.22 = (bf16[4,32,2304]{2,1,0:T(8,128)(2,1)}, bf16[4,32,2304]{2,1,0:T(8,128)(2,1)}, u32[]{:S(2)}, u32[]{:S(2)}) collective-permute-start(bf16[4,32,2304]{2,1,0:T(8,128)(2,1)} %get-tuple-element.39), channel_id=1, source_target_pairs={{0,8},{8,16},{16,24},{24,32},{32,40},{40,48},{48,56},{56,0},{1,9},... | collective-permute-start | bytes 1769480 | tf_op jit(solution)/shard_map/ppermute | solution.py:36
  142.2 3.3 %copy-start.7 = (f32[2,128]{1,0:T(2,128)S(1)}, f32[2,128]{1,0:T(2,128)}, u32[]{:S(2)}) copy-start(f32[2,128]{1,0:T(2,128)} %get-tuple-element.49) | copy-start | bytes 3076
  142.2 21.8 %collective-permute-start.26 = (bf16[4,32,2304]{2,1,0:T(8,128)(2,1)}, bf16[4,32,2304]{2,1,0:T(8,128)(2,1)}, u32[]{:S(2)}, u32[]{:S(2)}) collective-permute-start(bf16[4,32,2304]{2,1,0:T(8,128)(2,1)} %get-tuple-element.55), channel_id=1, source_target_pairs={{0,56},{8,0},{16,8},{24,16},{32,24},{40,32},{48,40},{56,48},{1,57}... | collective-permute-start | bytes 1769480 | tf_op jit(solution)/shard_map/ppermute | solution.py:36
  146.1 17.8 %all-to-all-start.1 = ((f32[32,2,128]{2,1,0:T(2,128)}), f32[32,2,128]{2,1,0:T(2,128)S(1)}, u32[]{:S(2)}, u32[]{:S(2)}) async-start(f32[32,2,128]{2,1,0:T(2,128)} %broadcast_in_dim.12), calls=%async_computation.1 | async-start | bytes 65536 | tf_op jit(solution)/shard_map/all_to_all | solution.py:84
  155.1 15.8 %collective-permute-start.23 = (bf16[4,32,2304]{2,1,0:T(8,128)(2,1)}, bf16[4,32,2304]{2,1,0:T(8,128)(2,1)}, u32[]{:S(2)}, u32[]{:S(2)}) collective-permute-start(bf16[4,32,2304]{2,1,0:T(8,128)(2,1)} %add_convert_fusion.5), channel_id=1, source_target_pairs={{0,8},{8,16},{16,24},{24,32},{32,40},{40,48},{48,56},{56,0},{1,9},... | collective-permute-start | bytes 1769480 | tf_op jit(solution)/shard_map/ppermute | solution.py:36
  165.2 18.5 %collective-permute-start.27 = (bf16[4,32,2304]{2,1,0:T(8,128)(2,1)S(1)}, bf16[4,32,2304]{2,1,0:T(8,128)(2,1)S(1)}, u32[]{:S(2)}, u32[]{:S(2)}) collective-permute-start(bf16[4,32,2304]{2,1,0:T(8,128)(2,1)S(1)} %add_convert_fusion.2), channel_id=1, source_target_pairs={{0,56},{8,0},{16,8},{24,16},{32,24},{40,32},{48,40},{56,48},{1,57}... | collective-permute-start | bytes 1769480 | tf_op jit(solution)/shard_map/ppermute | solution.py:36
  173.5 10.2 %all-to-all-start.2 = ((f32[8,2,128]{2,1,0:T(2,128)}), f32[8,2,128]{2,1,0:T(2,128)S(1)}, u32[]{:S(2)}, u32[]{:S(2)}) async-start(f32[8,2,128]{2,1,0:T(2,128)} %broadcast_in_dim.13), calls=%async_computation.3 | async-start | bytes 16384 | tf_op jit(solution)/shard_map/all_to_all | solution.py:84
  179.1 37.0 %reduce-scatter.5.cloned.1.call-start = ((), (), s32[]{:S(2)}) async-start(), calls=%async_computation.7 | async-start | bytes 442368 | tf_op jit(solution)/shard_map/reduce_scatter | solution.py:409
  179.1 16.2 %collective-permute-start.24 = (bf16[4,32,2304]{2,1,0:T(8,128)(2,1)}, bf16[4,32,2304]{2,1,0:T(8,128)(2,1)}, u32[]{:S(2)}, u32[]{:S(2)}) collective-permute-start(bf16[4,32,2304]{2,1,0:T(8,128)(2,1)} %add_convert_fusion.4), channel_id=1, source_target_pairs={{0,8},{8,16},{16,24},{24,32},{32,40},{40,48},{48,56},{56,0},{1,9},... | collective-permute-start | bytes 1769480 | tf_op jit(solution)/shard_map/ppermute | solution.py:36
  183.9 32.2 %collective-permute-start.28 = (bf16[4,32,2304]{2,1,0:T(8,128)(2,1)S(1)}, bf16[4,32,2304]{2,1,0:T(8,128)(2,1)S(1)}, u32[]{:S(2)}, u32[]{:S(2)}) collective-permute-start(bf16[4,32,2304]{2,1,0:T(8,128)(2,1)S(1)} %add_convert_fusion.1), channel_id=1, source_target_pairs={{0,56},{8,0},{16,8},{24,16},{32,24},{40,32},{48,40},{56,48},{1,57}... | collective-permute-start | bytes 1769480 | tf_op jit(solution)/shard_map/ppermute | solution.py:36
  196.5 19.6 %collective-permute-start.25 = (bf16[4,32,2304]{2,1,0:T(8,128)(2,1)S(1)}, bf16[4,32,2304]{2,1,0:T(8,128)(2,1)S(1)}, u32[]{:S(2)}, u32[]{:S(2)}) collective-permute-start(bf16[4,32,2304]{2,1,0:T(8,128)(2,1)S(1)} %add_convert_fusion.3), channel_id=1, source_target_pairs={{0,8},{8,16},{16,24},{24,32},{32,40},{40,48},{48,56},{56,0},{1,9},... | collective-permute-start | bytes 1769480 | tf_op jit(solution)/shard_map/ppermute | solution.py:36
  197.2 18.9 %copy-start.1 = (bf16[4,32,2304]{2,1,0:T(8,128)(2,1)S(1)}, bf16[4,32,2304]{2,1,0:T(8,128)(2,1)}, u32[]{:S(2)}) copy-start(bf16[4,32,2304]{2,1,0:T(8,128)(2,1)} %get-tuple-element.67) | copy-start | bytes 1769476
  216.4 8.2 %copy-start.6 = (bf16[32,768]{1,0:T(8,128)(2,1)S(1)}, bf16[32,768]{1,0:T(8,128)(2,1)}, u32[]{:S(2)}) copy-start(bf16[32,768]{1,0:T(8,128)(2,1)} %reduce-scatter.5.cloned.1.call-done) | copy-start | bytes 147460
  216.4 5.6 %collective-permute-start.31 = (bf16[32,2304]{1,0:T(8,128)(2,1)S(1)}, bf16[32,2304]{1,0:T(8,128)(2,1)S(1)}, u32[]{:S(2)}, u32[]{:S(2)}) collective-permute-start(bf16[32,2304]{1,0:T(8,128)(2,1)S(1)} %get-tuple-element.83), channel_id=1, source_target_pairs={{0,128},{64,192},{128,0},{192,64},{1,129},{65,193},{129,1},{193,65... | collective-permute-start | bytes 442376 | tf_op jit(solution)/shard_map/ppermute | solution.py:36
  219.3 5.2 %collective-permute-start.30 = (bf16[32,2304]{1,0:T(8,128)(2,1)S(1)}, bf16[32,2304]{1,0:T(8,128)(2,1)S(1)}, u32[]{:S(2)}, u32[]{:S(2)}) collective-permute-start(bf16[32,2304]{1,0:T(8,128)(2,1)S(1)} %get-tuple-element.84), channel_id=1, source_target_pairs={{0,64},{64,128},{128,192},{192,0},{1,65},{65,129},{129,193},{193,1... | collective-permute-start | bytes 442376 | tf_op jit(solution)/shard_map/ppermute | solution.py:36
  219.5 5.0 %collective-permute-start.29 = (bf16[32,2304]{1,0:T(8,128)(2,1)S(1)}, bf16[32,2304]{1,0:T(8,128)(2,1)S(1)}, u32[]{:S(2)}, u32[]{:S(2)}) collective-permute-start(bf16[32,2304]{1,0:T(8,128)(2,1)S(1)} %get-tuple-element.82), channel_id=1, source_target_pairs={{0,192},{64,0},{128,64},{192,128},{1,193},{65,1},{129,65},{193,129... | collective-permute-start | bytes 442376 | tf_op jit(solution)/shard_map/ppermute | solution.py:36
  225.4 19.7 %all-to-all-start.3 = ((bf16[8,4,3072]{2,1,0:T(4,128)(2,1)}), bf16[8,4,3072]{2,1,0:T(4,128)(2,1)S(1)}, u32[]{:S(2)}, u32[]{:S(2)}) async-start(bf16[8,4,3072]{2,1,0:T(4,128)(2,1)} %reshape.73), calls=%async_computation.5 | async-start | bytes 393216 | tf_op jit(solution)/shard_map/all_to_all | solution.py:429
Sparse Core Ops, SparseCore 0:
  27.7 100.1 all-gather.2
  130.9 25.5 reduce-scatter.2
  182.4 33.6 reduce-scatter.4

commit v6 on v5

--- a/solution.py
+++ b/solution.py
@@ -28,7 +28,7 @@
 TILE = NZ * SLOTS
 MID = SLOTS // 2
 COLS = 512
-LEFT = 2304
+LEFT = 2048
 
 
 def shift(a, axis, step):
@@ -410,27 +410,26 @@
         elif step == 3:
             total, _ = lax.optimization_barrier((kept["sum"], going))
             total = jnp.sum(spread(total, EXPERT, NE).reshape(NE, 2, LANES), axis=0)
-            sent, total = lax.optimization_barrier((sent, total))
             kept["norms"] = jnp.sqrt(total)
             kept["factors"] = RADIUS / (kept["norms"] + GAMMA)
+            grad = down_gradient(where, wide_y, hidden, kept["back"][2], kept["factors"])
+            sent, kept["down"], kept["line"] = lax.optimization_barrier((sent, grad, kept["line"]))
         else:
             d_gate, d_up, spot, _ = kept["back"]
             factors, _ = lax.optimization_barrier((kept["factors"], going))
             grads = wide_gradients(x, d_gate, d_up, spot, factors)
-            sent, kept["grads"], kept["line"] = lax.optimization_barrier((sent, tuple(grads), kept["line"]))
+            sent, kept["grads"] = lax.optimization_barrier((sent, tuple(grads)))
         return sent
 
     left_line = ring_sum(far, left, "z", hook)
     right_out = kept["line"]
     left_out = direct_sum(left_line, "x")
     own_out = jnp.concatenate([left_out, right_out], axis=1)
-    own_out, late = lax.optimization_barrier((own_out, hidden))
-    grad_down = down_gradient(where, wide_y, late, kept["back"][2], kept["factors"])
     returned = lax.all_to_all(own_out.reshape(NE, CAP, width), EXPERT, split_axis=0, concat_axis=0, tiled=True)
     mixed = jnp.dot(placed_bf.T, returned.reshape(SLOTS, width), preferred_element_type=F32).astype(BF)
     norms = kept["norms"]
     own_norms = lax.dynamic_slice(norms.reshape(BLOCKS, 8), (ix * NZ + iz, 0), (1, EX_ROW))
-    return (mixed, own_norms, *kept["grads"], grad_down)
+    return (mixed, own_norms, *kept["grads"], kept["down"])
 
 
 def solution(mesh):

time: 253 us -> 244 us (0.964)
  waiting for transfers between devices: 87.5 us -> 77.7 us
    ppermute x32, waiting for transfers between devices: 52.1 us -> 38.7 us  [shift(): return lax.ppermute(a, axis, [(i, (i + step) % n) for i in range(n)])]
    all_to_all x1, waiting for transfers between devices: 0.01 us -> 5.28 us  [on_device(): lax.all_to_all(own_out.reshape(NE, CAP, width), EXPERT, split_axis=0, con...]
    unnamed x36 -> x32, local copies, waits for them, and re-layouts: 5.98 us -> 6 us
  transfers between devices with their start and end apart: 38 -> 38, of which waited for: 16 -> 17; matrix products, arithmetic and copies ran while one was open for 8% -> 7% of each run, Pallas kernels for 16% -> 17%
where the time goes in v6:
time: 244 us; the launch traced here: 243 us
  waiting for transfers between devices  77.7 us (32%)
  starting transfers between devices  69.9 us (29%)
  Pallas kernels  40.2 us (16%)
  local copies, waits for them, and re-layouts  15.3 us (6%)
  between operations  14.2 us (6%)
  blocking collectives  14 us (6%)
  other arithmetic  9.07 us (4%)
  matrix products  2.51 us (1%)
    ppermute x32, starting transfers between devices, shift(): return lax.ppermute(a, axis, [(i, (i + step) % n) for i in range(n)])  45 us
    ppermute x32, waiting for transfers between devices, shift(): return lax.ppermute(a, axis, [(i, (i + step) % n) for i in range(n)])  38.7 us
    all_to_all x1, blocking collectives, on_device(): got = lax.all_to_all(send, EXPERT, split_axis=0, concat_axis=0, tiled=True)  14 us
    all_gather x1, waiting for transfers between devices, on_device(): lax.all_gather(jnp.concatenate([local_dy] + parts, axis=1), ('x', 'z'), a...  13.9 us
    all_to_all x2, starting transfers between devices, spread(): lax.all_to_all(jnp.broadcast_to(a[None], (n,) + a.shape), axes, 0, 0, til...  13.6 us
    pallas_call x1, Pallas kernels, forward(): pl.pallas_call(forward_kernel, grid_spec=pltpu.PrefetchScalarGridSpec(num...  13 us
    all_to_all x2, waiting for transfers between devices, spread(): lax.all_to_all(jnp.broadcast_to(a[None], (n,) + a.shape), axes, 0, 0, til...  11.9 us
    all_to_all x1, starting transfers between devices, on_device(): lax.all_to_all(own_out.reshape(NE, CAP, width), EXPERT, split_axis=0, con...  11.2 us
  transfers between devices with their start and end apart: 38, of which 17 were waited for; matrix products, arithmetic and copies ran while one was open for 7% of the time, Pallas kernels for 17%

profile of v6, /device:TPU:1, one launch (start us, length us, event | category | flops | bytes accessed | tf_op | source)
XLA Modules:
  0.0 242.8 jit_solution(11466861925148346717)
XLA Ops:
  7.2 0.8 copy.28
  8.6 0.7 multiply_add_fusion
  9.5 0.7 multiply_reduce_fusion
  10.4 1.1 convolution_convert_fusion
  12.0 14.0 %all_to_all.20 = bf16[8,8,3200]{2,1,0:T(8,128)(2,1)S(1)} all-to-all(bf16[8,8,3200]{2,1,0:T(8,128)(2,1)S(1)} %pad_maximum_fusion), channel_id=1, replica_groups=mesh['x'=4,'z'=8,'y'=4,'c'=2] {'y','c'}, dimensions={0} | all-to-all | bytes 819200 | tf_op jit(solution)/shard_map/all_to_all | solution.py:380
  26.7 0.8 concatenate.22
  27.7 1.3 collective-permute-start
  28.9 1.5 collective-permute-start.1
  30.5 1.7 collective-permute-start.11
  32.2 4.0 %collective-permute-start.12 = (bf16[16,3072]{1,0:T(8,128)(2,1)S(1)}, bf16[16,3072]{1,0:T(8,128)(2,1)S(1)}, u32[]{:S(2)}, u32[]{:S(2)}) collective-permute-start(bf16[16,3072]{1,0:T(8,128)(2,1)S(1)} %slice.73), channel_id=1, source_target_pairs={{0,56},{8,0},{16,8},{24,16},{32,24},{40,32},{48,40},{56,48},{1,57}... | collective-permute-start | bytes 294920 | tf_op jit(solution)/shard_map/ppermute | solution.py:36
  36.2 0.6 constant_dynamic-update-slice_fusion
  37.0 1.1 collective-permute-done.11
  38.1 2.8 %collective-permute-start.14 = (bf16[16,3072]{1,0:T(8,128)(2,1)S(1)}, bf16[16,3072]{1,0:T(8,128)(2,1)S(1)}, u32[]{:S(2)}, u32[]{:S(2)}) collective-permute-start(bf16[16,3072]{1,0:T(8,128)(2,1)S(1)} %collective-permute-done.12), channel_id=1, source_target_pairs={{0,56},{8,0},{16,8},{24,16},{32,24},{40,32},{48,40},{56,48},{1,57}... | collective-permute-start | bytes 294920 | tf_op jit(solution)/shard_map/ppermute | solution.py:36
  40.9 0.6 bitcast_dynamic-update-slice_fusion.6
  41.5 0.6 bitcast_dynamic-update-slice_fusion.5
  42.4 2.7 %collective-permute-start.4 = (bf16[4,16,3072]{2,1,0:T(8,128)(2,1)S(1)}, bf16[4,16,3072]{2,1,0:T(8,128)(2,1)S(1)}, u32[]{:S(2)}, u32[]{:S(2)}) collective-permute-start(bf16[4,16,3072]{2,1,0:T(8,128)(2,1)S(1)} %pad_maximum_fusion.1.refs_0_), channel_id=1, source_target_pairs={{0,56},{8,0},{16,8},{24,16},{32,24},{40,32},{48,40},{56,48},{1,57}... | collective-permute-start | bytes 1179656 | tf_op jit(solution)/shard_map/ppermute | solution.py:36
  45.0 2.7 %collective-permute-start.16 = (bf16[16,3072]{1,0:T(8,128)(2,1)S(1)}, bf16[16,3072]{1,0:T(8,128)(2,1)S(1)}, u32[]{:S(2)}, u32[]{:S(2)}) collective-permute-start(bf16[16,3072]{1,0:T(8,128)(2,1)S(1)} %collective-permute-done.14), channel_id=1, source_target_pairs={{0,56},{8,0},{16,8},{24,16},{32,24},{40,32},{48,40},{56,48},{1,57}... | collective-permute-start | bytes 294920 | tf_op jit(solution)/shard_map/ppermute | solution.py:36
  49.0 9.2 %collective-permute-done.15 = bf16[16,3072]{1,0:T(8,128)(2,1)S(1)} collective-permute-done((bf16[16,3072]{1,0:T(8,128)(2,1)S(1)}, bf16[16,3072]{1,0:T(8,128)(2,1)S(1)}, u32[]{:S(2)}, u32[]{:S(2)}) %collective-permute-start.15) | collective-permute-done | bytes 98336 | tf_op jit(solution)/shard_map/ppermute | solution.py:36
  58.2 0.6 bitcast_dynamic-update-slice_fusion.2
  58.9 0.6 bitcast_dynamic-update-slice_fusion.1
  59.5 4.3 %collective-permute-done.17 = bf16[16,3072]{1,0:T(8,128)(2,1)S(1)} collective-permute-done((bf16[16,3072]{1,0:T(8,128)(2,1)S(1)}, bf16[16,3072]{1,0:T(8,128)(2,1)S(1)}, u32[]{:S(2)}, u32[]{:S(2)}) %collective-permute-start.17) | collective-permute-done | bytes 98336 | tf_op jit(solution)/shard_map/ppermute | solution.py:36
  63.9 0.6 bitcast_dynamic-update-slice_fusion.refs_9_
  64.5 2.7 %collective-permute-start.19 = (bf16[8,16,3072]{2,1,0:T(8,128)(2,1)}, bf16[8,16,3072]{2,1,0:T(8,128)(2,1)S(1)}, u32[]{:S(2)}, u32[]{:S(2)}) collective-permute-start(bf16[8,16,3072]{2,1,0:T(8,128)(2,1)} %bitcast_dynamic-update-slice_fusion.refs_9_), channel_id=1, source_target_pairs={{0,192},{64,0},{128,64},{192,128},{1,193},{65,1},{129,65},{193,129... | collective-permute-start | bytes 2359304 | tf_op jit(solution)/shard_map/ppermute | solution.py:36
  67.2 2.7 %collective-permute-start.6 = (bf16[4,16,3072]{2,1,0:T(8,128)(2,1)S(1)}, bf16[4,16,3072]{2,1,0:T(8,128)(2,1)}, u32[]{:S(2)}, u32[]{:S(2)}) collective-permute-start(bf16[4,16,3072]{2,1,0:T(8,128)(2,1)S(1)} %collective-permute-done.4.refs_2_), channel_id=1, source_target_pairs={{0,56},{8,0},{16,8},{24,16},{32,24},{40,32},{48,40},{56,48},{1,57}... | collective-permute-start | bytes 1179656 | tf_op jit(solution)/shard_map/ppermute | solution.py:36
  69.9 5.5 %collective-permute-done.5.refs_3_ = bf16[4,16,3072]{2,1,0:T(8,128)(2,1)} collective-permute-done((bf16[4,16,3072]{2,1,0:T(8,128)(2,1)S(1)}, bf16[4,16,3072]{2,1,0:T(8,128)(2,1)}, u32[]{:S(2)}, u32[]{:S(2)}) %collective-permute-start.5) | collective-permute-done | bytes 393248 | tf_op jit(solution)/shard_map/ppermute | solution.py:36
  75.3 2.7 %collective-permute-start.8 = (bf16[4,16,3072]{2,1,0:T(8,128)(2,1)}, bf16[4,16,3072]{2,1,0:T(8,128)(2,1)}, u32[]{:S(2)}, u32[]{:S(2)}) collective-permute-start(bf16[4,16,3072]{2,1,0:T(8,128)(2,1)} %collective-permute-done.6.refs_4_), channel_id=1, source_target_pairs={{0,56},{8,0},{16,8},{24,16},{32,24},{40,32},{48,40},{56,48},{1,57}... | collective-permute-start | bytes 1179656 | tf_op jit(solution)/shard_map/ppermute | solution.py:36
  78.0 2.3 collective-permute-done.18.refs_10_
  80.5 2.7 %collective-permute-start.21 = (bf16[8,8,3072]{2,1,0:T(8,128)(2,1)S(1)}, bf16[8,8,3072]{2,1,0:T(8,128)(2,1)}, u32[]{:S(2)}, u32[]{:S(2)}) collective-permute-start(bf16[8,8,3072]{2,1,0:T(8,128)(2,1)S(1)} %slice.95), channel_id=1, source_target_pairs={{0,192},{64,0},{128,64},{192,128},{1,193},{65,1},{129,65},{193,129... | collective-permute-start | bytes 1179656 | tf_op jit(solution)/shard_map/ppermute | solution.py:36
  83.2 4.3 %collective-permute-done.7.refs_5_ = bf16[4,16,3072]{2,1,0:T(8,128)(2,1)} collective-permute-done((bf16[4,16,3072]{2,1,0:T(8,128)(2,1)}, bf16[4,16,3072]{2,1,0:T(8,128)(2,1)}, u32[]{:S(2)}, u32[]{:S(2)}) %collective-permute-start.7) | collective-permute-done | bytes 393248 | tf_op jit(solution)/shard_map/ppermute | solution.py:36
  87.5 0.9 slice.91
  88.6 3.8 %collective-permute-done.8.refs_6_ = bf16[4,16,3072]{2,1,0:T(8,128)(2,1)} collective-permute-done((bf16[4,16,3072]{2,1,0:T(8,128)(2,1)}, bf16[4,16,3072]{2,1,0:T(8,128)(2,1)}, u32[]{:S(2)}, u32[]{:S(2)}) %collective-permute-start.8) | collective-permute-done | bytes 393248 | tf_op jit(solution)/shard_map/ppermute | solution.py:36
  92.4 0.9 slice.92
  93.3 3.5 %collective-permute-start.10 = (bf16[4,8,3072]{2,1,0:T(8,128)(2,1)S(1)}, bf16[4,8,3072]{2,1,0:T(8,128)(2,1)S(1)}, u32[]{:S(2)}, u32[]{:S(2)}) collective-permute-start(bf16[4,8,3072]{2,1,0:T(8,128)(2,1)S(1)} %slice.92), channel_id=1, source_target_pairs={{0,56},{8,0},{16,8},{24,16},{32,24},{40,32},{48,40},{56,48},{1,57}... | collective-permute-start | bytes 589832 | tf_op jit(solution)/shard_map/ppermute | solution.py:36
  97.4 1.8 collective-permute-done.9.refs_7_
  99.2 1.1 collective-permute-done.10.refs_8_
  100.4 0.7 copy-done.9
  101.0 13.0 %forward.1 = (bf16[4,8,32,3072]{3,2,1,0:T(8,128)(2,1)}, f32[1024,256]{1,0:T(8,128)}, f32[1024,256]{1,0:T(8,128)}, bf16[1024,256]{1,0:T(8,128)(2,1)}, bf16[4,32,2...) custom-call(s32[12]{0:T(128)} %pad_add_fusion.where_ref, ...), custom_call_target="tpu_custom_call" | custom-call | flops 4831838208 | bytes 20971520 | tf_op jit(solution)/shard_map/forward/pallas_call | solution.py:158
  114.1 13.9 %all-gather.3.cloned.1.call-done = bf16[1024,3328]{1,0:T(8,128)(2,1)} async-done(((bf16[32,3328]{1,0:T(8,128)(2,1)}), bf16[1024,3328]{1,0:T(8,128)(2,1)}) %all-gather.3.cloned.1.call-update) | async-done | bytes 6815760 | tf_op jit(solution)/shard_map/all_gather | solution.py:389
  128.0 1.5 collective-permute-start.22
  129.5 2.3 slice_bitcast_fusion
  131.8 9.3 %backward.1 = (bf16[1024,256]{1,0:T(8,128)(2,1)}, bf16[1024,256]{1,0:T(8,128)(2,1)}, f32[1024,1]{1,0:T(8,128)}, f32[2,128]{1,0:T(2,128)}) custom-call(s32[12]{0:T(128)} %pad_add_fusion.where_ref, bf16[32,32,3328]{2,1,0:T(8,128)(2,1)} %bitcast.50, bf16[32,32,3328]{2,1,0:T(8,128)(2,1)} %bitcast.51, bf16[1,256,3072]{2,1,0:T(8,128)(2,1)} %wd_ref.1, ...), custom_call_target="tpu_custom_call" | custom-call | flops 2415919104 | bytes 12582912 | tf_op jit(solution)/shard_map/backward/pallas_call | solution.py:240
  141.1 1.4 collective-permute-start.26
  142.5 2.0 add_convert_fusion.5
  145.1 8.0 %all-to-all-start.1 = ((f32[32,2,128]{2,1,0:T(2,128)}), f32[32,2,128]{2,1,0:T(2,128)S(1)}, u32[]{:S(2)}, u32[]{:S(2)}) async-start(f32[32,2,128]{2,1,0:T(2,128)} %broadcast_in_dim.12), calls=%async_computation.1 | async-start | bytes 65536 | tf_op jit(solution)/shard_map/all_to_all | solution.py:84
  153.1 1.5 collective-permute-start.23
  154.6 7.3 %all-to-all-done.1 = f32[32,2,128]{2,1,0:T(2,128)S(1)} async-done(((f32[32,2,128]{2,1,0:T(2,128)}), f32[32,2,128]{2,1,0:T(2,128)S(1)}, u32[]{:S(2)}, u32[]{:S(2)}) %all-to-all-start.1) | async-done | bytes 32800 | tf_op jit(solution)/shard_map/all_to_all | solution.py:84
  162.0 1.2 add_convert_fusion.2
  163.2 2.3 collective-permute-start.27
  165.5 2.0 collective-permute-done.23
  167.4 2.0 add_convert_fusion.4
  170.0 5.6 %all-to-all-start.2 = ((f32[8,2,128]{2,1,0:T(2,128)}), f32[8,2,128]{2,1,0:T(2,128)S(1)}, u32[]{:S(2)}, u32[]{:S(2)}) async-start(f32[8,2,128]{2,1,0:T(2,128)} %broadcast_in_dim.13), calls=%async_computation.3 | async-start | bytes 16384 | tf_op jit(solution)/shard_map/all_to_all | solution.py:84
  175.6 4.6 %all-to-all-done.2 = f32[8,2,128]{2,1,0:T(2,128)S(1)} async-done(((f32[8,2,128]{2,1,0:T(2,128)}), f32[8,2,128]{2,1,0:T(2,128)S(1)}, u32[]{:S(2)}, u32[]{:S(2)}) %all-to-all-start.2) | async-done | bytes 8224 | tf_op jit(solution)/shard_map/all_to_all | solution.py:84
  180.9 8.7 %down_gradient.1 = bf16[1,256,3072]{2,1,0:T(8,128)(2,1)} custom-call(s32[12]{0:T(128)} %pad_add_fusion.where_ref, bf16[32,32,3328]{2,1,0:T(8,128)(2,1)} %bitcast.52, bf16[1024,256]{1,0:T(8,128)(2,1)} %get-tuple-element.43.hidden_ref, f32[1024,1]{1,0:T(8,128)} %get-tuple-element.50.spot_ref, f32[2,128]{1,0:T(2,128)} %get-tuple-element.61.factor_ref), custom_call_target="tpu_custom_call" | custom-call | flops 3145728 | bytes 1048576 | tf_op jit(solution)/shard_map/down_gradient/pallas_call | solution.py:332
  189.6 7.8 %reduce-scatter.5.cloned.1.call-done = bf16[32,1024]{1,0:T(8,128)(2,1)} async-done(((bf16[256,1024]{1,0:T(8,128)(2,1)}), bf16[32,1024]{1,0:T(8,128)(2,1)}) %reduce-scatter.5.cloned.1.call-update) | async-done | bytes 65552 | tf_op jit(solution)/shard_map/reduce_scatter | solution.py:409
  197.5 1.6 collective-permute-start.28
  199.4 9.1 %wide_gradients.1 = (bf16[1,3072,256]{2,1,0:T(8,128)(2,1)}, bf16[1,3072,256]{2,1,0:T(8,128)(2,1)}) custom-call(bf16[4,8,32,3072]{3,2,1,0:T(8,128)(2,1)} %get-tuple-element.58.x_ref, bf16[1024,256]{1,0:T(8,128)(2,1)} %get-tuple-element.59.dg_ref, bf16[1024,256]{1,0:T(8,128)(2,1)} %get-tuple-element.60.du_ref, f32[1024,1]{1,0:T(8,128)} %get-tuple-element.50.spot_ref, ...), custom_call_target="tpu_custom_call" | custom-call | flops 3145728 | bytes 1048576 | tf_op jit(solution)/shard_map/wide_gradients/pallas_call | solution.py:293
  208.5 0.9 collective-permute-done.25
  209.6 2.9 %collective-permute-start.31 = (bf16[32,2048]{1,0:T(8,128)(2,1)S(1)}, bf16[32,2048]{1,0:T(8,128)(2,1)S(1)}, u32[]{:S(2)}, u32[]{:S(2)}) collective-permute-start(bf16[32,2048]{1,0:T(8,128)(2,1)S(1)} %get-tuple-element.79), channel_id=1, source_target_pairs={{0,128},{64,192},{128,0},{192,64},{1,129},{65,193},{129,1},{193,65... | collective-permute-start | bytes 393224 | tf_op jit(solution)/shard_map/ppermute | solution.py:36
  212.7 2.5 %collective-permute-start.29 = (bf16[32,2048]{1,0:T(8,128)(2,1)S(1)}, bf16[32,2048]{1,0:T(8,128)(2,1)S(1)}, u32[]{:S(2)}, u32[]{:S(2)}) collective-permute-start(bf16[32,2048]{1,0:T(8,128)(2,1)S(1)} %get-tuple-element.78), channel_id=1, source_target_pairs={{0,192},{64,0},{128,64},{192,128},{1,193},{65,1},{129,65},{193,129... | collective-permute-start | bytes 393224 | tf_op jit(solution)/shard_map/ppermute | solution.py:36
  215.2 2.3 collective-permute-done.30
  217.6 0.8 reshape.73
  218.4 11.2 %all-to-all-start.3 = ((bf16[8,4,3072]{2,1,0:T(4,128)(2,1)}), bf16[8,4,3072]{2,1,0:T(4,128)(2,1)S(1)}, u32[]{:S(2)}, u32[]{:S(2)}) async-start(bf16[8,4,3072]{2,1,0:T(4,128)(2,1)} %reshape.73), calls=%async_computation.5 | async-start | bytes 393216 | tf_op jit(solution)/shard_map/all_to_all | solution.py:428
  230.2 5.3 %all-to-all-done.3 = bf16[8,4,3072]{2,1,0:T(4,128)(2,1)S(1)} async-done(((bf16[8,4,3072]{2,1,0:T(4,128)(2,1)}), bf16[8,4,3072]{2,1,0:T(4,128)(2,1)S(1)}, u32[]{:S(2)}, u32[]{:S(2)}) %all-to-all-start.3) | async-done | bytes 196640 | tf_op jit(solution)/shard_map/all_to_all | solution.py:428
  235.5 0.8 convolution_convert_fusion.2
  (111 shorter events, 8.3 us)
Async XLA Ops:
  7.2 3.0 %copy-start = (bf16[12,3072]{1,0:T(8,128)(2,1)S(1)}, bf16[12,3072]{1,0:T(8,128)(2,1)}, u32[]{:S(2)}) copy-start(bf16[12,3072]{1,0:T(8,128)(2,1)} %param.9) | copy-start | bytes 221188
  7.2 120.8 %all-gather.3.cloned.1.call-start = ((), (), s32[]{:S(2)}) async-start(), calls=%async_computation.8 | async-start | bytes 7028736 | tf_op jit(solution)/shard_map/all_gather | solution.py:389
  27.5 134.5 %reduce-scatter.3.cloned.1.call-start = ((), (), s32[]{:S(2)}) async-start(), calls=%async_computation.6 | async-start | bytes 2621440 | tf_op jit(solution)/shard_map/reduce_scatter | solution.py:398
  27.7 9.2 %collective-permute-start = (bf16[16,3072]{1,0:T(8,128)(2,1)S(1)}, bf16[16,3072]{1,0:T(8,128)(2,1)S(1)}, u32[]{:S(2)}, u32[]{:S(2)}) collective-permute-start(bf16[16,3072]{1,0:T(8,128)(2,1)S(1)} %slice.69), channel_id=1, source_target_pairs={{0,64},{64,128},{128,192},{192,0},{1,65},{65,129},{129,193},{193,1... | collective-permute-start | bytes 294920 | tf_op jit(solution)/shard_map/ppermute | solution.py:36
  28.9 13.2 %collective-permute-start.1 = (bf16[16,3072]{1,0:T(8,128)(2,1)S(1)}, bf16[16,3072]{1,0:T(8,128)(2,1)S(1)}, u32[]{:S(2)}, u32[]{:S(2)}) collective-permute-start(bf16[16,3072]{1,0:T(8,128)(2,1)S(1)} %slice.69), channel_id=1, source_target_pairs={{0,192},{64,0},{128,64},{192,128},{1,193},{65,1},{129,65},{193,129... | collective-permute-start | bytes 294920 | tf_op jit(solution)/shard_map/ppermute | solution.py:36
  30.5 7.7 %collective-permute-start.11 = (bf16[16,3072]{1,0:T(8,128)(2,1)S(1)}, bf16[16,3072]{1,0:T(8,128)(2,1)S(1)}, u32[]{:S(2)}, u32[]{:S(2)}) collective-permute-start(bf16[16,3072]{1,0:T(8,128)(2,1)S(1)} %slice.73), channel_id=1, source_target_pairs={{0,8},{8,16},{16,24},{24,32},{32,40},{40,48},{48,56},{56,0},{1,9},... | collective-permute-start | bytes 294920 | tf_op jit(solution)/shard_map/ppermute | solution.py:36
  32.2 5.9 %collective-permute-start.12 = (bf16[16,3072]{1,0:T(8,128)(2,1)S(1)}, bf16[16,3072]{1,0:T(8,128)(2,1)S(1)}, u32[]{:S(2)}, u32[]{:S(2)}) collective-permute-start(bf16[16,3072]{1,0:T(8,128)(2,1)S(1)} %slice.73), channel_id=1, source_target_pairs={{0,56},{8,0},{16,8},{24,16},{32,24},{40,32},{48,40},{56,48},{1,57}... | collective-permute-start | bytes 294920 | tf_op jit(solution)/shard_map/ppermute | solution.py:36
  36.9 5.3 %collective-permute-start.2 = (bf16[16,3072]{1,0:T(8,128)(2,1)S(1)}, bf16[16,3072]{1,0:T(8,128)(2,1)S(1)}, u32[]{:S(2)}, u32[]{:S(2)}) collective-permute-start(bf16[16,3072]{1,0:T(8,128)(2,1)S(1)} %collective-permute-done), channel_id=1, source_target_pairs={{0,64},{64,128},{128,192},{192,0},{1,65},{65,129},{129,193},{193,1... | collective-permute-start | bytes 294920 | tf_op jit(solution)/shard_map/ppermute | solution.py:36
  38.1 6.9 %collective-permute-start.13 = (bf16[16,3072]{1,0:T(8,128)(2,1)S(1)}, bf16[16,3072]{1,0:T(8,128)(2,1)S(1)}, u32[]{:S(2)}, u32[]{:S(2)}) collective-permute-start(bf16[16,3072]{1,0:T(8,128)(2,1)S(1)} %collective-permute-done.11), channel_id=1, source_target_pairs={{0,8},{8,16},{16,24},{24,32},{32,40},{40,48},{48,56},{56,0},{1,9},... | collective-permute-start | bytes 294920 | tf_op jit(solution)/shard_map/ppermute | solution.py:36
  38.1 6.9 %collective-permute-start.14 = (bf16[16,3072]{1,0:T(8,128)(2,1)S(1)}, bf16[16,3072]{1,0:T(8,128)(2,1)S(1)}, u32[]{:S(2)}, u32[]{:S(2)}) collective-permute-start(bf16[16,3072]{1,0:T(8,128)(2,1)S(1)} %collective-permute-done.12), channel_id=1, source_target_pairs={{0,56},{8,0},{16,8},{24,16},{32,24},{40,32},{48,40},{56,48},{1,57}... | collective-permute-start | bytes 294920 | tf_op jit(solution)/shard_map/ppermute | solution.py:36
  42.2 41.0 %copy-start.11 = (s32[8]{0:T(128)S(1)}, s32[8]{0:T(128)}, u32[]{:S(2)}) copy-start(s32[8]{0:T(128)} %constant.61.clone) | copy-start | bytes 100
  42.3 51.1 %copy-start.1 = (bf16[4,16,3072]{2,1,0:T(8,128)(2,1)}, bf16[4,16,3072]{2,1,0:T(8,128)(2,1)S(1)}, u32[]{:S(2)}) copy-start(bf16[4,16,3072]{2,1,0:T(8,128)(2,1)S(1)} %pad_maximum_fusion.1.refs_0_) | copy-start | bytes 1179652
  42.3 24.9 %collective-permute-start.3 = (bf16[4,16,3072]{2,1,0:T(8,128)(2,1)S(1)}, bf16[4,16,3072]{2,1,0:T(8,128)(2,1)S(1)}, u32[]{:S(2)}, u32[]{:S(2)}) collective-permute-start(bf16[4,16,3072]{2,1,0:T(8,128)(2,1)S(1)} %pad_maximum_fusion.1.refs_0_), channel_id=1, source_target_pairs={{0,8},{8,16},{16,24},{24,32},{32,40},{40,48},{48,56},{56,0},{1,9},... | collective-permute-start | bytes 1179656 | tf_op jit(solution)/shard_map/ppermute | solution.py:36
  42.4 24.8 %collective-permute-start.4 = (bf16[4,16,3072]{2,1,0:T(8,128)(2,1)S(1)}, bf16[4,16,3072]{2,1,0:T(8,128)(2,1)S(1)}, u32[]{:S(2)}, u32[]{:S(2)}) collective-permute-start(bf16[4,16,3072]{2,1,0:T(8,128)(2,1)S(1)} %pad_maximum_fusion.1.refs_0_), channel_id=1, source_target_pairs={{0,56},{8,0},{16,8},{24,16},{32,24},{40,32},{48,40},{56,48},{1,57}... | collective-permute-start | bytes 1179656 | tf_op jit(solution)/shard_map/ppermute | solution.py:36
  45.0 13.2 %collective-permute-start.15 = (bf16[16,3072]{1,0:T(8,128)(2,1)S(1)}, bf16[16,3072]{1,0:T(8,128)(2,1)S(1)}, u32[]{:S(2)}, u32[]{:S(2)}) collective-permute-start(bf16[16,3072]{1,0:T(8,128)(2,1)S(1)} %collective-permute-done.13), channel_id=1, source_target_pairs={{0,8},{8,16},{16,24},{24,32},{32,40},{40,48},{48,56},{56,0},{1,9},... | collective-permute-start | bytes 294920 | tf_op jit(solution)/shard_map/ppermute | solution.py:36
  45.0 13.8 %collective-permute-start.16 = (bf16[16,3072]{1,0:T(8,128)(2,1)S(1)}, bf16[16,3072]{1,0:T(8,128)(2,1)S(1)}, u32[]{:S(2)}, u32[]{:S(2)}) collective-permute-start(bf16[16,3072]{1,0:T(8,128)(2,1)S(1)} %collective-permute-done.14), channel_id=1, source_target_pairs={{0,56},{8,0},{16,8},{24,16},{32,24},{40,32},{48,40},{56,48},{1,57}... | collective-permute-start | bytes 294920 | tf_op jit(solution)/shard_map/ppermute | solution.py:36
  48.4 48.5 %copy-start.10 = (s32[4]{0:T(128)S(1)}, s32[4]{0:T(128)}, u32[]{:S(2)}) copy-start(s32[4]{0:T(128)} %constant.60.clone) | copy-start | bytes 52
  58.2 5.6 %collective-permute-start.17 = (bf16[16,3072]{1,0:T(8,128)(2,1)S(1)}, bf16[16,3072]{1,0:T(8,128)(2,1)S(1)}, u32[]{:S(2)}, u32[]{:S(2)}) collective-permute-start(bf16[16,3072]{1,0:T(8,128)(2,1)S(1)} %collective-permute-done.15), channel_id=1, source_target_pairs={{0,8},{8,16},{16,24},{24,32},{32,40},{40,48},{48,56},{56,0},{1,9},... | collective-permute-start | bytes 294920 | tf_op jit(solution)/shard_map/ppermute | solution.py:36
  64.5 15.8 %collective-permute-start.18 = (bf16[8,16,3072]{2,1,0:T(8,128)(2,1)}, bf16[8,16,3072]{2,1,0:T(8,128)(2,1)S(1)}, u32[]{:S(2)}, u32[]{:S(2)}) collective-permute-start(bf16[8,16,3072]{2,1,0:T(8,128)(2,1)} %bitcast_dynamic-update-slice_fusion.refs_9_), channel_id=1, source_target_pairs={{0,64},{64,128},{128,192},{192,0},{1,65},{65,129},{129,193},{193,1... | collective-permute-start | bytes 2359304 | tf_op jit(solution)/shard_map/ppermute | solution.py:36
  64.5 15.9 %collective-permute-start.19 = (bf16[8,16,3072]{2,1,0:T(8,128)(2,1)}, bf16[8,16,3072]{2,1,0:T(8,128)(2,1)S(1)}, u32[]{:S(2)}, u32[]{:S(2)}) collective-permute-start(bf16[8,16,3072]{2,1,0:T(8,128)(2,1)} %bitcast_dynamic-update-slice_fusion.refs_9_), channel_id=1, source_target_pairs={{0,192},{64,0},{128,64},{192,128},{1,193},{65,1},{129,65},{193,129... | collective-permute-start | bytes 2359304 | tf_op jit(solution)/shard_map/ppermute | solution.py:36
  67.2 16.0 %copy-start.6 = (bf16[4,16,3072]{2,1,0:T(8,128)(2,1)}, bf16[4,16,3072]{2,1,0:T(8,128)(2,1)S(1)}, u32[]{:S(2)}) copy-start(bf16[4,16,3072]{2,1,0:T(8,128)(2,1)S(1)} %collective-permute-done.3.refs_1_) | copy-start | bytes 1179652
  67.2 8.1 %collective-permute-start.5 = (bf16[4,16,3072]{2,1,0:T(8,128)(2,1)S(1)}, bf16[4,16,3072]{2,1,0:T(8,128)(2,1)}, u32[]{:S(2)}, u32[]{:S(2)}) collective-permute-start(bf16[4,16,3072]{2,1,0:T(8,128)(2,1)S(1)} %collective-permute-done.3.refs_1_), channel_id=1, source_target_pairs={{0,8},{8,16},{16,24},{24,32},{32,40},{40,48},{48,56},{56,0},{1,9},... | collective-permute-start | bytes 1179656 | tf_op jit(solution)/shard_map/ppermute | solution.py:36
  67.2 8.1 %copy-start.7 = (bf16[4,16,3072]{2,1,0:T(8,128)(2,1)}, bf16[4,16,3072]{2,1,0:T(8,128)(2,1)S(1)}, u32[]{:S(2)}) copy-start(bf16[4,16,3072]{2,1,0:T(8,128)(2,1)S(1)} %collective-permute-done.4.refs_2_) | copy-start | bytes 1179652
  67.2 8.1 %collective-permute-start.6 = (bf16[4,16,3072]{2,1,0:T(8,128)(2,1)S(1)}, bf16[4,16,3072]{2,1,0:T(8,128)(2,1)}, u32[]{:S(2)}, u32[]{:S(2)}) collective-permute-start(bf16[4,16,3072]{2,1,0:T(8,128)(2,1)S(1)} %collective-permute-done.4.refs_2_), channel_id=1, source_target_pairs={{0,56},{8,0},{16,8},{24,16},{32,24},{40,32},{48,40},{56,48},{1,57}... | collective-permute-start | bytes 1179656 | tf_op jit(solution)/shard_map/ppermute | solution.py:36
  75.3 12.2 %collective-permute-start.7 = (bf16[4,16,3072]{2,1,0:T(8,128)(2,1)}, bf16[4,16,3072]{2,1,0:T(8,128)(2,1)}, u32[]{:S(2)}, u32[]{:S(2)}) collective-permute-start(bf16[4,16,3072]{2,1,0:T(8,128)(2,1)} %collective-permute-done.5.refs_3_), channel_id=1, source_target_pairs={{0,8},{8,16},{16,24},{24,32},{32,40},{40,48},{48,56},{56,0},{1,9},... | collective-permute-start | bytes 1179656 | tf_op jit(solution)/shard_map/ppermute | solution.py:36
  75.3 17.0 %collective-permute-start.8 = (bf16[4,16,3072]{2,1,0:T(8,128)(2,1)}, bf16[4,16,3072]{2,1,0:T(8,128)(2,1)}, u32[]{:S(2)}, u32[]{:S(2)}) collective-permute-start(bf16[4,16,3072]{2,1,0:T(8,128)(2,1)} %collective-permute-done.6.refs_4_), channel_id=1, source_target_pairs={{0,56},{8,0},{16,8},{24,16},{32,24},{40,32},{48,40},{56,48},{1,57}... | collective-permute-start | bytes 1179656 | tf_op jit(solution)/shard_map/ppermute | solution.py:36
  80.3 20.1 %copy-start.2 = (bf16[8,16,3072]{2,1,0:T(8,128)(2,1)}, bf16[8,16,3072]{2,1,0:T(8,128)(2,1)S(1)}, u32[]{:S(2)}) copy-start(bf16[8,16,3072]{2,1,0:T(8,128)(2,1)S(1)} %collective-permute-done.18.refs_10_) | copy-start | bytes 2359300
  80.3 20.0 %collective-permute-start.20 = (bf16[8,8,3072]{2,1,0:T(8,128)(2,1)S(1)}, bf16[8,8,3072]{2,1,0:T(8,128)(2,1)}, u32[]{:S(2)}, u32[]{:S(2)}) collective-permute-start(bf16[8,8,3072]{2,1,0:T(8,128)(2,1)S(1)} %slice.94), channel_id=1, source_target_pairs={{0,64},{64,128},{128,192},{192,0},{1,65},{65,129},{129,193},{193,1... | collective-permute-start | bytes 1179656 | tf_op jit(solution)/shard_map/ppermute | solution.py:36
  80.4 19.9 %copy-start.3 = (bf16[8,16,3072]{2,1,0:T(8,128)(2,1)}, bf16[8,16,3072]{2,1,0:T(8,128)(2,1)S(1)}, u32[]{:S(2)}) copy-start(bf16[8,16,3072]{2,1,0:T(8,128)(2,1)S(1)} %collective-permute-done.19.refs_11_) | copy-start | bytes 2359300
  80.5 19.9 %collective-permute-start.21 = (bf16[8,8,3072]{2,1,0:T(8,128)(2,1)S(1)}, bf16[8,8,3072]{2,1,0:T(8,128)(2,1)}, u32[]{:S(2)}, u32[]{:S(2)}) collective-permute-start(bf16[8,8,3072]{2,1,0:T(8,128)(2,1)S(1)} %slice.95), channel_id=1, source_target_pairs={{0,192},{64,0},{128,64},{192,128},{1,193},{65,1},{129,65},{193,129... | collective-permute-start | bytes 1179656 | tf_op jit(solution)/shard_map/ppermute | solution.py:36
  88.5 10.7 %collective-permute-start.9 = (bf16[4,8,3072]{2,1,0:T(8,128)(2,1)S(1)}, bf16[4,8,3072]{2,1,0:T(8,128)(2,1)S(1)}, u32[]{:S(2)}, u32[]{:S(2)}) collective-permute-start(bf16[4,8,3072]{2,1,0:T(8,128)(2,1)S(1)} %slice.91), channel_id=1, source_target_pairs={{0,8},{8,16},{16,24},{24,32},{32,40},{40,48},{48,56},{56,0},{1,9},... | collective-permute-start | bytes 589832 | tf_op jit(solution)/shard_map/ppermute | solution.py:36
  93.3 7.0 %collective-permute-start.10 = (bf16[4,8,3072]{2,1,0:T(8,128)(2,1)S(1)}, bf16[4,8,3072]{2,1,0:T(8,128)(2,1)S(1)}, u32[]{:S(2)}, u32[]{:S(2)}) collective-permute-start(bf16[4,8,3072]{2,1,0:T(8,128)(2,1)S(1)} %slice.92), channel_id=1, source_target_pairs={{0,56},{8,0},{16,8},{24,16},{32,24},{40,32},{48,40},{56,48},{1,57}... | collective-permute-start | bytes 589832 | tf_op jit(solution)/shard_map/ppermute | solution.py:36
  99.2 1.2 copy-start.8
  100.3 0.7 copy-start.9
  128.0 14.5 %collective-permute-start.22 = (bf16[4,32,2048]{2,1,0:T(8,128)(2,1)}, bf16[4,32,2048]{2,1,0:T(8,128)(2,1)}, u32[]{:S(2)}, u32[]{:S(2)}) collective-permute-start(bf16[4,32,2048]{2,1,0:T(8,128)(2,1)} %get-tuple-element.37), channel_id=1, source_target_pairs={{0,8},{8,16},{16,24},{24,32},{32,40},{40,48},{48,56},{56,0},{1,9},... | collective-permute-start | bytes 1572872 | tf_op jit(solution)/shard_map/ppermute | solution.py:36
  141.1 3.3 %copy-start.5 = (f32[2,128]{1,0:T(2,128)S(1)}, f32[2,128]{1,0:T(2,128)}, u32[]{:S(2)}) copy-start(f32[2,128]{1,0:T(2,128)} %get-tuple-element.47) | copy-start | bytes 3076
  141.1 20.9 %collective-permute-start.26 = (bf16[4,32,2048]{2,1,0:T(8,128)(2,1)S(1)}, bf16[4,32,2048]{2,1,0:T(8,128)(2,1)}, u32[]{:S(2)}, u32[]{:S(2)}) collective-permute-start(bf16[4,32,2048]{2,1,0:T(8,128)(2,1)S(1)} %get-tuple-element.55), channel_id=1, source_target_pairs={{0,56},{8,0},{16,8},{24,16},{32,24},{40,32},{48,40},{56,48},{1,57}... | collective-permute-start | bytes 1572872 | tf_op jit(solution)/shard_map/ppermute | solution.py:36
  145.1 16.8 %all-to-all-start.1 = ((f32[32,2,128]{2,1,0:T(2,128)}), f32[32,2,128]{2,1,0:T(2,128)S(1)}, u32[]{:S(2)}, u32[]{:S(2)}) async-start(f32[32,2,128]{2,1,0:T(2,128)} %broadcast_in_dim.12), calls=%async_computation.1 | async-start | bytes 65536 | tf_op jit(solution)/shard_map/all_to_all | solution.py:84
  153.0 44.4 %reduce-scatter.5.cloned.1.call-start = ((), (), s32[]{:S(2)}) async-start(), calls=%async_computation.7 | async-start | bytes 589824 | tf_op jit(solution)/shard_map/reduce_scatter | solution.py:409
  153.1 14.3 %collective-permute-start.23 = (bf16[4,32,2048]{2,1,0:T(8,128)(2,1)}, bf16[4,32,2048]{2,1,0:T(8,128)(2,1)}, u32[]{:S(2)}, u32[]{:S(2)}) collective-permute-start(bf16[4,32,2048]{2,1,0:T(8,128)(2,1)} %add_convert_fusion.5), channel_id=1, source_target_pairs={{0,8},{8,16},{16,24},{24,32},{32,40},{40,48},{48,56},{56,0},{1,9},... | collective-permute-start | bytes 1572872 | tf_op jit(solution)/shard_map/ppermute | solution.py:36
  163.2 34.2 %collective-permute-start.27 = (bf16[4,32,2048]{2,1,0:T(8,128)(2,1)S(1)}, bf16[4,32,2048]{2,1,0:T(8,128)(2,1)S(1)}, u32[]{:S(2)}, u32[]{:S(2)}) collective-permute-start(bf16[4,32,2048]{2,1,0:T(8,128)(2,1)S(1)} %add_convert_fusion.2), channel_id=1, source_target_pairs={{0,56},{8,0},{16,8},{24,16},{32,24},{40,32},{48,40},{56,48},{1,57}... | collective-permute-start | bytes 1572872 | tf_op jit(solution)/shard_map/ppermute | solution.py:36
  170.0 10.3 %all-to-all-start.2 = ((f32[8,2,128]{2,1,0:T(2,128)}), f32[8,2,128]{2,1,0:T(2,128)S(1)}, u32[]{:S(2)}, u32[]{:S(2)}) async-start(f32[8,2,128]{2,1,0:T(2,128)} %broadcast_in_dim.13), calls=%async_computation.3 | async-start | bytes 16384 | tf_op jit(solution)/shard_map/all_to_all | solution.py:84
  175.6 23.5 %collective-permute-start.24 = (bf16[4,32,2048]{2,1,0:T(8,128)(2,1)}, bf16[4,32,2048]{2,1,0:T(8,128)(2,1)S(1)}, u32[]{:S(2)}, u32[]{:S(2)}) collective-permute-start(bf16[4,32,2048]{2,1,0:T(8,128)(2,1)} %add_convert_fusion.4), channel_id=1, source_target_pairs={{0,8},{8,16},{16,24},{24,32},{32,40},{40,48},{48,56},{56,0},{1,9},... | collective-permute-start | bytes 1572872 | tf_op jit(solution)/shard_map/ppermute | solution.py:36
  197.5 10.9 %collective-permute-start.28 = (bf16[4,32,2048]{2,1,0:T(8,128)(2,1)S(1)}, bf16[4,32,2048]{2,1,0:T(8,128)(2,1)S(1)}, u32[]{:S(2)}, u32[]{:S(2)}) collective-permute-start(bf16[4,32,2048]{2,1,0:T(8,128)(2,1)S(1)} %add_convert_fusion.1), channel_id=1, source_target_pairs={{0,56},{8,0},{16,8},{24,16},{32,24},{40,32},{48,40},{56,48},{1,57}... | collective-permute-start | bytes 1572872 | tf_op jit(solution)/shard_map/ppermute | solution.py:36
  199.3 10.1 %collective-permute-start.25 = (bf16[4,32,2048]{2,1,0:T(8,128)(2,1)S(1)}, bf16[4,32,2048]{2,1,0:T(8,128)(2,1)S(1)}, u32[]{:S(2)}, u32[]{:S(2)}) collective-permute-start(bf16[4,32,2048]{2,1,0:T(8,128)(2,1)S(1)} %add_convert_fusion.3), channel_id=1, source_target_pairs={{0,8},{8,16},{16,24},{24,32},{32,40},{40,48},{48,56},{56,0},{1,9},... | collective-permute-start | bytes 1572872 | tf_op jit(solution)/shard_map/ppermute | solution.py:36
  208.5 9.1 %copy-start.4 = (bf16[32,1024]{1,0:T(8,128)(2,1)S(1)}, bf16[32,1024]{1,0:T(8,128)(2,1)}, u32[]{:S(2)}) copy-start(bf16[32,1024]{1,0:T(8,128)(2,1)} %reduce-scatter.5.cloned.1.call-done) | copy-start | bytes 196612
  209.6 5.6 %collective-permute-start.31 = (bf16[32,2048]{1,0:T(8,128)(2,1)S(1)}, bf16[32,2048]{1,0:T(8,128)(2,1)S(1)}, u32[]{:S(2)}, u32[]{:S(2)}) collective-permute-start(bf16[32,2048]{1,0:T(8,128)(2,1)S(1)} %get-tuple-element.79), channel_id=1, source_target_pairs={{0,128},{64,192},{128,0},{192,64},{1,129},{65,193},{129,1},{193,65... | collective-permute-start | bytes 393224 | tf_op jit(solution)/shard_map/ppermute | solution.py:36
  212.5 5.0 %collective-permute-start.30 = (bf16[32,2048]{1,0:T(8,128)(2,1)S(1)}, bf16[32,2048]{1,0:T(8,128)(2,1)S(1)}, u32[]{:S(2)}, u32[]{:S(2)}) collective-permute-start(bf16[32,2048]{1,0:T(8,128)(2,1)S(1)} %get-tuple-element.80), channel_id=1, source_target_pairs={{0,64},{64,128},{128,192},{192,0},{1,65},{65,129},{129,193},{193,1... | collective-permute-start | bytes 393224 | tf_op jit(solution)/shard_map/ppermute | solution.py:36
  212.7 4.8 %collective-permute-start.29 = (bf16[32,2048]{1,0:T(8,128)(2,1)S(1)}, bf16[32,2048]{1,0:T(8,128)(2,1)S(1)}, u32[]{:S(2)}, u32[]{:S(2)}) collective-permute-start(bf16[32,2048]{1,0:T(8,128)(2,1)S(1)} %get-tuple-element.78), channel_id=1, source_target_pairs={{0,192},{64,0},{128,64},{192,128},{1,193},{65,1},{129,65},{193,129... | collective-permute-start | bytes 393224 | tf_op jit(solution)/shard_map/ppermute | solution.py:36
  218.4 17.1 %all-to-all-start.3 = ((bf16[8,4,3072]{2,1,0:T(4,128)(2,1)}), bf16[8,4,3072]{2,1,0:T(4,128)(2,1)S(1)}, u32[]{:S(2)}, u32[]{:S(2)}) async-start(bf16[8,4,3072]{2,1,0:T(4,128)(2,1)} %reshape.73), calls=%async_computation.5 | async-start | bytes 393216 | tf_op jit(solution)/shard_map/all_to_all | solution.py:428
Sparse Core Ops, SparseCore 0:
  27.6 100.3 all-gather.2
  130.5 30.4 reduce-scatter.2
  163.7 33.7 reduce-scatter.4

commit v7 on v6

--- a/solution.py
+++ b/solution.py
@@ -60,15 +60,16 @@
     def get(k):
         return parts[place(k)]
 
-    own_up, down = hook(1, (get(half - 1), get(1 - half)), far)
-    up = plus(shift(far, axis, 1), own_up)
+    up = plus(hook(1, shift(far, axis, 1), far), get(half - 1))
+    down = get(1 - half)
     for k in range(half - 1, 0, -1):
         going = up
         up, down = shift(up, axis, 1), shift(down, axis, -1)
         if k > 1:
-            own_up, own_down = hook(half - k + 1, (get(k - 1), get(1 - k)), going)
-            up, down = plus(up, own_up), plus(down, own_down)
-    own = hook(half, get(0), going)
+            up, down = hook(half - k + 1, (up, down), going)
+            up, down = plus(up, get(k - 1)), plus(down, get(1 - k))
+    up, down = hook(half, (up, down), going)
+    own = get(0)
     return (up.astype(F32) + down.astype(F32) + own.astype(F32)).astype(BF)
 
 

time: 244 us -> 250 us (1.025)
  blocking collectives: 14 us -> 42.6 us
  starting transfers between devices: 69.9 us -> 52.3 us
  waiting for transfers between devices: 77.7 us -> 74.9 us
    all_to_all x0 -> x2, blocking collectives: none -> 28.6 us  [spread(): lax.all_to_all(jnp.broadcast_to(a[None], (n,) + a.shape), axes, 0, 0, til...]
    all_to_all x2 -> x0, starting transfers between devices: 13.6 us -> none  [spread(): lax.all_to_all(jnp.broadcast_to(a[None], (n,) + a.shape), axes, 0, 0, til...]
    all_to_all x2 -> x0, waiting for transfers between devices: 11.9 us -> none  [spread(): lax.all_to_all(jnp.broadcast_to(a[None], (n,) + a.shape), axes, 0, 0, til...]
    ppermute x32, waiting for transfers between devices: 38.7 us -> 49.5 us  [shift(): return lax.ppermute(a, axis, [(i, (i + step) % n) for i in range(n)])]
    all_gather x1, waiting for transfers between devices: 13.9 us -> 9.39 us  [on_device(): lax.all_gather(jnp.concatenate([local_dy] + parts, axis=1), ('x', 'z'), a...]
    ppermute x32, starting transfers between devices: 45 us -> 40.6 us  [shift(): return lax.ppermute(a, axis, [(i, (i + step) % n) for i in range(n)])]
    convert_element_type x5 -> x3, other arithmetic: 5.35 us -> 4.34 us  [plus(): return (a.astype(F32) + b.astype(F32)).astype(BF)]
    unnamed x32 -> x30, local copies, waits for them, and re-layouts: 6 us -> 6.04 us
  transfers between devices with their start and end apart: 38 -> 36, of which waited for: 17 -> 16; matrix products, arithmetic and copies ran while one was open for 7% -> 5% of each run, Pallas kernels for 17% -> 16%
where the time goes in v7:
time: 250 us; the launch traced here: 249 us
  waiting for transfers between devices  74.9 us (30%)
  starting transfers between devices  52.3 us (21%)
  blocking collectives  42.6 us (17%)
  Pallas kernels  40.2 us (16%)
  between operations  14.2 us (6%)
  local copies, waits for them, and re-layouts  13.6 us (5%)
  other arithmetic  9.1 us (4%)
    ppermute x32, waiting for transfers between devices, shift(): return lax.ppermute(a, axis, [(i, (i + step) % n) for i in range(n)])  49.5 us
    ppermute x32, starting transfers between devices, shift(): return lax.ppermute(a, axis, [(i, (i + step) % n) for i in range(n)])  40.6 us
    all_to_all x2, blocking collectives, spread(): lax.all_to_all(jnp.broadcast_to(a[None], (n,) + a.shape), axes, 0, 0, til...  28.6 us
    all_to_all x1, blocking collectives, on_device(): got = lax.all_to_all(send, EXPERT, split_axis=0, concat_axis=0, tiled=True)  14 us
    pallas_call x1, Pallas kernels, forward(): pl.pallas_call(forward_kernel, grid_spec=pltpu.PrefetchScalarGridSpec(num...  13.1 us
    all_to_all x1, starting transfers between devices, on_device(): lax.all_to_all(own_out.reshape(NE, CAP, width), EXPERT, split_axis=0, con...  11.6 us
    all_gather x1, waiting for transfers between devices, on_device(): lax.all_gather(jnp.concatenate([local_dy] + parts, axis=1), ('x', 'z'), a...  9.39 us
    pallas_call x1, Pallas kernels, backward(): pl.pallas_call(backward_kernel, grid_spec=pltpu.PrefetchScalarGridSpec(nu...  9.29 us
  transfers between devices with their start and end apart: 36, of which 16 were waited for; matrix products, arithmetic and copies ran while one was open for 5% of the time, Pallas kernels for 16%

profile of v7, /device:TPU:1, one launch (start us, length us, event | category | flops | bytes accessed | tf_op | source)
XLA Modules:
  0.0 249.4 jit_solution(10381029514692951882)
XLA Ops:
  7.2 0.8 copy.28
  8.6 0.7 multiply_add_fusion
  9.5 0.7 multiply_reduce_fusion
  10.4 1.1 convolution_convert_fusion.1
  12.0 14.0 %all_to_all.20 = bf16[8,8,3200]{2,1,0:T(8,128)(2,1)S(1)} all-to-all(bf16[8,8,3200]{2,1,0:T(8,128)(2,1)S(1)} %pad_maximum_fusion), channel_id=1, replica_groups=mesh['x'=4,'z'=8,'y'=4,'c'=2] {'y','c'}, dimensions={0} | all-to-all | bytes 819200 | tf_op jit(solution)/shard_map/all_to_all | solution.py:381
  26.7 0.8 concatenate.22
  27.7 1.7 collective-permute-start.11
  29.4 4.0 %collective-permute-start.12 = (bf16[16,3072]{1,0:T(8,128)(2,1)S(1)}, bf16[16,3072]{1,0:T(8,128)(2,1)S(1)}, u32[]{:S(2)}, u32[]{:S(2)}) collective-permute-start(bf16[16,3072]{1,0:T(8,128)(2,1)S(1)} %slice.73), channel_id=1, source_target_pairs={{0,56},{8,0},{16,8},{24,16},{32,24},{40,32},{48,40},{56,48},{1,57}... | collective-permute-start | bytes 294920 | tf_op jit(solution)/shard_map/ppermute | solution.py:36
  33.5 1.3 collective-permute-start
  34.8 1.5 collective-permute-start.1
  36.3 0.6 constant_dynamic-update-slice_fusion
  37.0 2.7 %collective-permute-start.14 = (bf16[16,3072]{1,0:T(8,128)(2,1)S(1)}, bf16[16,3072]{1,0:T(8,128)(2,1)S(1)}, u32[]{:S(2)}, u32[]{:S(2)}) collective-permute-start(bf16[16,3072]{1,0:T(8,128)(2,1)S(1)} %collective-permute-done.12), channel_id=1, source_target_pairs={{0,56},{8,0},{16,8},{24,16},{32,24},{40,32},{48,40},{56,48},{1,57}... | collective-permute-start | bytes 294920 | tf_op jit(solution)/shard_map/ppermute | solution.py:36
  39.7 0.6 bitcast_dynamic-update-slice_fusion.6
  40.4 0.6 bitcast_dynamic-update-slice_fusion.5
  41.0 3.4 %collective-permute-done.2 = bf16[16,3072]{1,0:T(8,128)(2,1)S(1)} collective-permute-done((bf16[16,3072]{1,0:T(8,128)(2,1)S(1)}, bf16[16,3072]{1,0:T(8,128)(2,1)S(1)}, u32[]{:S(2)}, u32[]{:S(2)}) %collective-permute-start.2) | collective-permute-done | bytes 98336 | tf_op jit(solution)/shard_map/ppermute | solution.py:36
  44.7 1.3 collective-permute-start.3
  46.0 2.6 %collective-permute-start.16 = (bf16[16,3072]{1,0:T(8,128)(2,1)S(1)}, bf16[16,3072]{1,0:T(8,128)(2,1)S(1)}, u32[]{:S(2)}, u32[]{:S(2)}) collective-permute-start(bf16[16,3072]{1,0:T(8,128)(2,1)S(1)} %collective-permute-done.14), channel_id=1, source_target_pairs={{0,56},{8,0},{16,8},{24,16},{32,24},{40,32},{48,40},{56,48},{1,57}... | collective-permute-start | bytes 294920 | tf_op jit(solution)/shard_map/ppermute | solution.py:36
  48.7 0.6 bitcast_dynamic-update-slice_fusion.4
  50.0 8.9 %collective-permute-done.15 = bf16[16,3072]{1,0:T(8,128)(2,1)S(1)} collective-permute-done((bf16[16,3072]{1,0:T(8,128)(2,1)S(1)}, bf16[16,3072]{1,0:T(8,128)(2,1)S(1)}, u32[]{:S(2)}, u32[]{:S(2)}) %collective-permute-start.15) | collective-permute-done | bytes 98336 | tf_op jit(solution)/shard_map/ppermute | solution.py:36
  58.9 0.6 bitcast_dynamic-update-slice_fusion.2
  59.6 0.6 bitcast_dynamic-update-slice_fusion.1
  60.2 5.2 %collective-permute-done.17 = bf16[16,3072]{1,0:T(8,128)(2,1)S(1)} collective-permute-done((bf16[16,3072]{1,0:T(8,128)(2,1)S(1)}, bf16[16,3072]{1,0:T(8,128)(2,1)S(1)}, u32[]{:S(2)}, u32[]{:S(2)}) %collective-permute-start.17) | collective-permute-done | bytes 98336 | tf_op jit(solution)/shard_map/ppermute | solution.py:36
  65.5 0.6 bitcast_dynamic-update-slice_fusion.refs_9_
  66.3 2.5 %collective-permute-start.19 = (bf16[8,16,3072]{2,1,0:T(8,128)(2,1)}, bf16[8,16,3072]{2,1,0:T(8,128)(2,1)S(1)}, u32[]{:S(2)}, u32[]{:S(2)}) collective-permute-start(bf16[8,16,3072]{2,1,0:T(8,128)(2,1)} %bitcast_dynamic-update-slice_fusion.refs_9_), channel_id=1, source_target_pairs={{0,192},{64,0},{128,64},{192,128},{1,193},{65,1},{129,65},{193,129... | collective-permute-start | bytes 2359304 | tf_op jit(solution)/shard_map/ppermute | solution.py:36
  68.8 1.4 collective-permute-start.5
  70.3 5.3 %collective-permute-done.6.refs_4_ = bf16[4,16,3072]{2,1,0:T(8,128)(2,1)} collective-permute-done((bf16[4,16,3072]{2,1,0:T(8,128)(2,1)S(1)}, bf16[4,16,3072]{2,1,0:T(8,128)(2,1)}, u32[]{:S(2)}, u32[]{:S(2)}) %collective-permute-start.6) | collective-permute-done | bytes 393248 | tf_op jit(solution)/shard_map/ppermute | solution.py:36
  75.5 1.4 collective-permute-start.8
  77.2 3.2 %collective-permute-done.18.refs_10_ = bf16[8,16,3072]{2,1,0:T(8,128)(2,1)S(1)} collective-permute-done((bf16[8,16,3072]{2,1,0:T(8,128)(2,1)}, bf16[8,16,3072]{2,1,0:T(8,128)(2,1)S(1)}, u32[]{:S(2)}, u32[]{:S(2)}) %collective-permute-start.18) | collective-permute-done | bytes 786464 | tf_op jit(solution)/shard_map/ppermute | solution.py:36
  80.6 2.7 %collective-permute-start.21 = (bf16[8,8,3072]{2,1,0:T(8,128)(2,1)S(1)}, bf16[8,8,3072]{2,1,0:T(8,128)(2,1)}, u32[]{:S(2)}, u32[]{:S(2)}) collective-permute-start(bf16[8,8,3072]{2,1,0:T(8,128)(2,1)S(1)} %slice.95), channel_id=1, source_target_pairs={{0,192},{64,0},{128,64},{192,128},{1,193},{65,1},{129,65},{193,129... | collective-permute-start | bytes 1179656 | tf_op jit(solution)/shard_map/ppermute | solution.py:36
  83.3 7.5 %collective-permute-done.8.refs_6_ = bf16[4,16,3072]{2,1,0:T(8,128)(2,1)} collective-permute-done((bf16[4,16,3072]{2,1,0:T(8,128)(2,1)}, bf16[4,16,3072]{2,1,0:T(8,128)(2,1)}, u32[]{:S(2)}, u32[]{:S(2)}) %collective-permute-start.8) | collective-permute-done | bytes 393248 | tf_op jit(solution)/shard_map/ppermute | solution.py:36
  90.8 0.9 slice.92
  91.7 3.3 %collective-permute-start.10 = (bf16[4,8,3072]{2,1,0:T(8,128)(2,1)S(1)}, bf16[4,8,3072]{2,1,0:T(8,128)(2,1)S(1)}, u32[]{:S(2)}, u32[]{:S(2)}) collective-permute-start(bf16[4,8,3072]{2,1,0:T(8,128)(2,1)S(1)} %slice.92), channel_id=1, source_target_pairs={{0,56},{8,0},{16,8},{24,16},{32,24},{40,32},{48,40},{56,48},{1,57}... | collective-permute-start | bytes 589832 | tf_op jit(solution)/shard_map/ppermute | solution.py:36
  95.1 0.9 slice.91
  96.7 3.4 %collective-permute-done.20.refs_12_ = bf16[8,8,3072]{2,1,0:T(8,128)(2,1)} collective-permute-done((bf16[8,8,3072]{2,1,0:T(8,128)(2,1)S(1)}, bf16[8,8,3072]{2,1,0:T(8,128)(2,1)}, u32[]{:S(2)}, u32[]{:S(2)}) %collective-permute-start.20) | collective-permute-done | bytes 393248 | tf_op jit(solution)/shard_map/ppermute | solution.py:36
  101.0 7.0 %collective-permute-done.9.refs_7_ = bf16[4,8,3072]{2,1,0:T(8,128)(2,1)S(1)} collective-permute-done((bf16[4,8,3072]{2,1,0:T(8,128)(2,1)S(1)}, bf16[4,8,3072]{2,1,0:T(8,128)(2,1)S(1)}, u32[]{:S(2)}, u32[]{:S(2)}) %collective-permute-start.9) | collective-permute-done | bytes 196640 | tf_op jit(solution)/shard_map/ppermute | solution.py:36
  108.0 0.7 copy-done.8
  108.7 13.1 %forward.1 = (bf16[4,8,32,3072]{3,2,1,0:T(8,128)(2,1)}, f32[1024,256]{1,0:T(8,128)}, f32[1024,256]{1,0:T(8,128)}, bf16[1024,256]{1,0:T(8,128)(2,1)}, bf16[4,32,2...) custom-call(s32[12]{0:T(128)} %pad_add_fusion.where_ref, ...), custom_call_target="tpu_custom_call" | custom-call | flops 4831838208 | bytes 20971520 | tf_op jit(solution)/shard_map/forward/pallas_call | solution.py:159
  121.8 9.4 %all-gather.3.cloned.1.call-done = bf16[1024,3328]{1,0:T(8,128)(2,1)} async-done(((bf16[32,3328]{1,0:T(8,128)(2,1)}), bf16[1024,3328]{1,0:T(8,128)(2,1)}) %all-gather.3.cloned.1.call-update) | async-done | bytes 6815760 | tf_op jit(solution)/shard_map/all_gather | solution.py:390
  131.3 0.9 collective-permute-start.22
  132.1 1.1 slice_bitcast_fusion
  133.2 2.0 collective-permute-start.24
  135.2 9.3 %backward.1 = (bf16[1024,256]{1,0:T(8,128)(2,1)}, bf16[1024,256]{1,0:T(8,128)(2,1)}, f32[1024,1]{1,0:T(8,128)}, f32[2,128]{1,0:T(2,128)}) custom-call(s32[12]{0:T(128)} %pad_add_fusion.where_ref, bf16[32,32,3328]{2,1,0:T(8,128)(2,1)} %bitcast.56, bf16[32,32,3328]{2,1,0:T(8,128)(2,1)} %bitcast.57, bf16[1,256,3072]{2,1,0:T(8,128)(2,1)} %wd_ref.1, ...), custom_call_target="tpu_custom_call" | custom-call | flops 2415919104 | bytes 12582912 | tf_op jit(solution)/shard_map/backward/pallas_call | solution.py:241
  144.5 1.2 fusion.5
  145.7 0.7 broadcast_in_dim.12
  146.4 16.1 %all_to_all.21 = f32[32,2,128]{2,1,0:T(2,128)S(1)} all-to-all(f32[32,2,128]{2,1,0:T(2,128)S(1)} %broadcast_in_dim.12), channel_id=1, replica_groups=mesh['x'=4,'z'=8,'y'=4,'c'=2] {'x','z'}, dimensions={0} | all-to-all | bytes 65536 | tf_op jit(solution)/shard_map/all_to_all | solution.py:85
  162.6 2.1 reduce-scatter.3.cloned.1.call-done
  164.8 1.6 fusion.3
  166.4 1.3 collective-permute-start.25
  167.7 1.8 collective-permute-start.26
  169.6 12.5 %all_to_all.22 = f32[8,2,128]{2,1,0:T(2,128)S(1)} all-to-all(f32[8,2,128]{2,1,0:T(2,128)S(1)} %broadcast_in_dim.13), channel_id=1, replica_groups=mesh['x'=4,'z'=8,'y'=4,'c'=2] {'y','c'}, dimensions={0} | all-to-all | bytes 16384 | tf_op jit(solution)/shard_map/all_to_all | solution.py:85
  182.6 8.7 %down_gradient.1 = bf16[1,256,3072]{2,1,0:T(8,128)(2,1)} custom-call(s32[12]{0:T(128)} %pad_add_fusion.where_ref, bf16[32,32,3328]{2,1,0:T(8,128)(2,1)} %bitcast.58, bf16[1024,256]{1,0:T(8,128)(2,1)} %get-tuple-element.42.hidden_ref, f32[1024,1]{1,0:T(8,128)} %get-tuple-element.51.spot_ref, f32[2,128]{1,0:T(2,128)} %get-tuple-element.60.factor_ref), custom_call_target="tpu_custom_call" | custom-call | flops 3145728 | bytes 1048576 | tf_op jit(solution)/shard_map/down_gradient/pallas_call | solution.py:333
  191.3 8.6 %reduce-scatter.5.cloned.1.call-done = bf16[32,1024]{1,0:T(8,128)(2,1)} async-done(((bf16[256,1024]{1,0:T(8,128)(2,1)}), bf16[32,1024]{1,0:T(8,128)(2,1)}) %reduce-scatter.5.cloned.1.call-update) | async-done | bytes 65552 | tf_op jit(solution)/shard_map/reduce_scatter | solution.py:410
  199.9 1.6 fusion.1
  201.5 1.1 collective-permute-start.27
  202.6 1.7 collective-permute-start.28
  204.2 9.1 %wide_gradients.1 = (bf16[1,3072,256]{2,1,0:T(8,128)(2,1)}, bf16[1,3072,256]{2,1,0:T(8,128)(2,1)}) custom-call(bf16[4,8,32,3072]{3,2,1,0:T(8,128)(2,1)} %get-tuple-element.57.x_ref, bf16[1024,256]{1,0:T(8,128)(2,1)} %get-tuple-element.58.dg_ref, bf16[1024,256]{1,0:T(8,128)(2,1)} %get-tuple-element.59.du_ref, f32[1024,1]{1,0:T(8,128)} %get-tuple-element.51.spot_ref, ...), custom_call_target="tpu_custom_call" | custom-call | flops 3145728 | bytes 1048576 | tf_op jit(solution)/shard_map/wide_gradients/pallas_call | solution.py:294
  213.4 1.3 fusion
  214.7 2.5 %collective-permute-start.29 = (bf16[32,2048]{1,0:T(8,128)(2,1)S(1)}, bf16[32,2048]{1,0:T(8,128)(2,1)S(1)}, u32[]{:S(2)}, u32[]{:S(2)}) collective-permute-start(bf16[32,2048]{1,0:T(8,128)(2,1)S(1)} %get-tuple-element.75), channel_id=1, source_target_pairs={{0,192},{64,0},{128,64},{192,128},{1,193},{65,1},{129,65},{193,129... | collective-permute-start | bytes 393224 | tf_op jit(solution)/shard_map/ppermute | solution.py:36
  217.2 1.7 collective-permute-start.31
  219.1 4.5 %collective-permute-done.30 = bf16[32,2048]{1,0:T(8,128)(2,1)S(1)} collective-permute-done((bf16[32,2048]{1,0:T(8,128)(2,1)S(1)}, bf16[32,2048]{1,0:T(8,128)(2,1)S(1)}, u32[]{:S(2)}, u32[]{:S(2)}) %collective-permute-start.30) | collective-permute-done | bytes 131104 | tf_op jit(solution)/shard_map/ppermute | solution.py:36
  223.7 0.7 reshape.85
  224.5 11.6 %all-to-all-start.3 = ((bf16[8,4,3072]{2,1,0:T(4,128)(2,1)}), bf16[8,4,3072]{2,1,0:T(4,128)(2,1)S(1)}, u32[]{:S(2)}, u32[]{:S(2)}) async-start(bf16[8,4,3072]{2,1,0:T(4,128)(2,1)} %reshape.85), calls=%async_computation.5 | async-start | bytes 393216 | tf_op jit(solution)/shard_map/all_to_all | solution.py:429
  236.7 5.3 %all-to-all-done.3 = bf16[8,4,3072]{2,1,0:T(4,128)(2,1)S(1)} async-done(((bf16[8,4,3072]{2,1,0:T(4,128)(2,1)}), bf16[8,4,3072]{2,1,0:T(4,128)(2,1)S(1)}, u32[]{:S(2)}, u32[]{:S(2)}) %all-to-all-start.3) | async-done | bytes 196640 | tf_op jit(solution)/shard_map/all_to_all | solution.py:429
  242.1 0.8 convolution_convert_fusion.2
  (105 shorter events, 7.4 us)
Async XLA Ops:
  7.2 3.0 %copy-start = (bf16[12,3072]{1,0:T(8,128)(2,1)S(1)}, bf16[12,3072]{1,0:T(8,128)(2,1)}, u32[]{:S(2)}) copy-start(bf16[12,3072]{1,0:T(8,128)(2,1)} %param.10) | copy-start | bytes 221188
  7.2 124.0 %all-gather.3.cloned.1.call-start = ((), (), s32[]{:S(2)}) async-start(), calls=%async_computation.8 | async-start | bytes 7028736 | tf_op jit(solution)/shard_map/all_gather | solution.py:390
  26.2 57.1 %copy-start.10 = (s32[8]{0:T(128)S(1)}, s32[8]{0:T(128)}, u32[]{:S(2)}) copy-start(s32[8]{0:T(128)} %constant.61.clone) | copy-start | bytes 100
  26.5 69.6 %copy-start.9 = (s32[4]{0:T(128)S(1)}, s32[4]{0:T(128)}, u32[]{:S(2)}) copy-start(s32[4]{0:T(128)} %constant.60.clone) | copy-start | bytes 52
  27.6 137.2 %reduce-scatter.3.cloned.1.call-start = ((), (), s32[]{:S(2)}) async-start(), calls=%async_computation.6 | async-start | bytes 2621440 | tf_op jit(solution)/shard_map/reduce_scatter | solution.py:399
  27.7 9.2 %collective-permute-start.11 = (bf16[16,3072]{1,0:T(8,128)(2,1)S(1)}, bf16[16,3072]{1,0:T(8,128)(2,1)S(1)}, u32[]{:S(2)}, u32[]{:S(2)}) collective-permute-start(bf16[16,3072]{1,0:T(8,128)(2,1)S(1)} %slice.73), channel_id=1, source_target_pairs={{0,8},{8,16},{16,24},{24,32},{32,40},{40,48},{48,56},{56,0},{1,9},... | collective-permute-start | bytes 294920 | tf_op jit(solution)/shard_map/ppermute | solution.py:36
  29.4 7.6 %collective-permute-start.12 = (bf16[16,3072]{1,0:T(8,128)(2,1)S(1)}, bf16[16,3072]{1,0:T(8,128)(2,1)S(1)}, u32[]{:S(2)}, u32[]{:S(2)}) collective-permute-start(bf16[16,3072]{1,0:T(8,128)(2,1)S(1)} %slice.73), channel_id=1, source_target_pairs={{0,56},{8,0},{16,8},{24,16},{32,24},{40,32},{48,40},{56,48},{1,57}... | collective-permute-start | bytes 294920 | tf_op jit(solution)/shard_map/ppermute | solution.py:36
  33.5 6.2 %collective-permute-start = (bf16[16,3072]{1,0:T(8,128)(2,1)S(1)}, bf16[16,3072]{1,0:T(8,128)(2,1)S(1)}, u32[]{:S(2)}, u32[]{:S(2)}) collective-permute-start(bf16[16,3072]{1,0:T(8,128)(2,1)S(1)} %slice.69), channel_id=1, source_target_pairs={{0,64},{64,128},{128,192},{192,0},{1,65},{65,129},{129,193},{193,1... | collective-permute-start | bytes 294920 | tf_op jit(solution)/shard_map/ppermute | solution.py:36
  34.8 6.2 %collective-permute-start.1 = (bf16[16,3072]{1,0:T(8,128)(2,1)S(1)}, bf16[16,3072]{1,0:T(8,128)(2,1)S(1)}, u32[]{:S(2)}, u32[]{:S(2)}) collective-permute-start(bf16[16,3072]{1,0:T(8,128)(2,1)S(1)} %slice.69), channel_id=1, source_target_pairs={{0,192},{64,0},{128,64},{192,128},{1,193},{65,1},{129,65},{193,129... | collective-permute-start | bytes 294920 | tf_op jit(solution)/shard_map/ppermute | solution.py:36
  36.9 9.1 %collective-permute-start.13 = (bf16[16,3072]{1,0:T(8,128)(2,1)S(1)}, bf16[16,3072]{1,0:T(8,128)(2,1)S(1)}, u32[]{:S(2)}, u32[]{:S(2)}) collective-permute-start(bf16[16,3072]{1,0:T(8,128)(2,1)S(1)} %collective-permute-done.11), channel_id=1, source_target_pairs={{0,8},{8,16},{16,24},{24,32},{32,40},{40,48},{48,56},{56,0},{1,9},... | collective-permute-start | bytes 294920 | tf_op jit(solution)/shard_map/ppermute | solution.py:36
  37.0 9.0 %collective-permute-start.14 = (bf16[16,3072]{1,0:T(8,128)(2,1)S(1)}, bf16[16,3072]{1,0:T(8,128)(2,1)S(1)}, u32[]{:S(2)}, u32[]{:S(2)}) collective-permute-start(bf16[16,3072]{1,0:T(8,128)(2,1)S(1)} %collective-permute-done.12), channel_id=1, source_target_pairs={{0,56},{8,0},{16,8},{24,16},{32,24},{40,32},{48,40},{56,48},{1,57}... | collective-permute-start | bytes 294920 | tf_op jit(solution)/shard_map/ppermute | solution.py:36
  39.7 4.7 %collective-permute-start.2 = (bf16[16,3072]{1,0:T(8,128)(2,1)S(1)}, bf16[16,3072]{1,0:T(8,128)(2,1)S(1)}, u32[]{:S(2)}, u32[]{:S(2)}) collective-permute-start(bf16[16,3072]{1,0:T(8,128)(2,1)S(1)} %collective-permute-done), channel_id=1, source_target_pairs={{0,64},{64,128},{128,192},{192,0},{1,65},{65,129},{129,193},{193,1... | collective-permute-start | bytes 294920 | tf_op jit(solution)/shard_map/ppermute | solution.py:36
  44.4 63.6 %copy-start.1 = (bf16[4,16,3072]{2,1,0:T(8,128)(2,1)}, bf16[4,16,3072]{2,1,0:T(8,128)(2,1)S(1)}, u32[]{:S(2)}) copy-start(bf16[4,16,3072]{2,1,0:T(8,128)(2,1)S(1)} %pad_maximum_fusion.1.refs_0_) | copy-start | bytes 1179652
  44.5 24.3 %collective-permute-start.4 = (bf16[4,16,3072]{2,1,0:T(8,128)(2,1)S(1)}, bf16[4,16,3072]{2,1,0:T(8,128)(2,1)S(1)}, u32[]{:S(2)}, u32[]{:S(2)}) collective-permute-start(bf16[4,16,3072]{2,1,0:T(8,128)(2,1)S(1)} %pad_maximum_fusion.1.refs_0_), channel_id=1, source_target_pairs={{0,56},{8,0},{16,8},{24,16},{32,24},{40,32},{48,40},{56,48},{1,57}... | collective-permute-start | bytes 1179656 | tf_op jit(solution)/shard_map/ppermute | solution.py:36
  44.7 24.1 %collective-permute-start.3 = (bf16[4,16,3072]{2,1,0:T(8,128)(2,1)S(1)}, bf16[4,16,3072]{2,1,0:T(8,128)(2,1)S(1)}, u32[]{:S(2)}, u32[]{:S(2)}) collective-permute-start(bf16[4,16,3072]{2,1,0:T(8,128)(2,1)S(1)} %pad_maximum_fusion.1.refs_0_), channel_id=1, source_target_pairs={{0,8},{8,16},{16,24},{24,32},{32,40},{40,48},{48,56},{56,0},{1,9},... | collective-permute-start | bytes 1179656 | tf_op jit(solution)/shard_map/ppermute | solution.py:36
  46.0 12.9 %collective-permute-start.15 = (bf16[16,3072]{1,0:T(8,128)(2,1)S(1)}, bf16[16,3072]{1,0:T(8,128)(2,1)S(1)}, u32[]{:S(2)}, u32[]{:S(2)}) collective-permute-start(bf16[16,3072]{1,0:T(8,128)(2,1)S(1)} %collective-permute-done.13), channel_id=1, source_target_pairs={{0,8},{8,16},{16,24},{24,32},{32,40},{40,48},{48,56},{56,0},{1,9},... | collective-permute-start | bytes 294920 | tf_op jit(solution)/shard_map/ppermute | solution.py:36
  46.0 13.5 %collective-permute-start.16 = (bf16[16,3072]{1,0:T(8,128)(2,1)S(1)}, bf16[16,3072]{1,0:T(8,128)(2,1)S(1)}, u32[]{:S(2)}, u32[]{:S(2)}) collective-permute-start(bf16[16,3072]{1,0:T(8,128)(2,1)S(1)} %collective-permute-done.14), channel_id=1, source_target_pairs={{0,56},{8,0},{16,8},{24,16},{32,24},{40,32},{48,40},{56,48},{1,57}... | collective-permute-start | bytes 294920 | tf_op jit(solution)/shard_map/ppermute | solution.py:36
  58.9 6.5 %collective-permute-start.17 = (bf16[16,3072]{1,0:T(8,128)(2,1)S(1)}, bf16[16,3072]{1,0:T(8,128)(2,1)S(1)}, u32[]{:S(2)}, u32[]{:S(2)}) collective-permute-start(bf16[16,3072]{1,0:T(8,128)(2,1)S(1)} %collective-permute-done.15), channel_id=1, source_target_pairs={{0,8},{8,16},{16,24},{24,32},{32,40},{40,48},{48,56},{56,0},{1,9},... | collective-permute-start | bytes 294920 | tf_op jit(solution)/shard_map/ppermute | solution.py:36
  66.1 14.3 %collective-permute-start.18 = (bf16[8,16,3072]{2,1,0:T(8,128)(2,1)}, bf16[8,16,3072]{2,1,0:T(8,128)(2,1)S(1)}, u32[]{:S(2)}, u32[]{:S(2)}) collective-permute-start(bf16[8,16,3072]{2,1,0:T(8,128)(2,1)} %bitcast_dynamic-update-slice_fusion.refs_9_), channel_id=1, source_target_pairs={{0,64},{64,128},{128,192},{192,0},{1,65},{65,129},{129,193},{193,1... | collective-permute-start | bytes 2359304 | tf_op jit(solution)/shard_map/ppermute | solution.py:36
  66.3 14.2 %collective-permute-start.19 = (bf16[8,16,3072]{2,1,0:T(8,128)(2,1)}, bf16[8,16,3072]{2,1,0:T(8,128)(2,1)S(1)}, u32[]{:S(2)}, u32[]{:S(2)}) collective-permute-start(bf16[8,16,3072]{2,1,0:T(8,128)(2,1)} %bitcast_dynamic-update-slice_fusion.refs_9_), channel_id=1, source_target_pairs={{0,192},{64,0},{128,64},{192,128},{1,193},{65,1},{129,65},{193,129... | collective-permute-start | bytes 2359304 | tf_op jit(solution)/shard_map/ppermute | solution.py:36
  68.8 14.5 %copy-start.5 = (bf16[4,16,3072]{2,1,0:T(8,128)(2,1)}, bf16[4,16,3072]{2,1,0:T(8,128)(2,1)S(1)}, u32[]{:S(2)}) copy-start(bf16[4,16,3072]{2,1,0:T(8,128)(2,1)S(1)} %collective-permute-done.4.refs_2_) | copy-start | bytes 1179652
  68.8 6.7 %collective-permute-start.6 = (bf16[4,16,3072]{2,1,0:T(8,128)(2,1)S(1)}, bf16[4,16,3072]{2,1,0:T(8,128)(2,1)}, u32[]{:S(2)}, u32[]{:S(2)}) collective-permute-start(bf16[4,16,3072]{2,1,0:T(8,128)(2,1)S(1)} %collective-permute-done.4.refs_2_), channel_id=1, source_target_pairs={{0,56},{8,0},{16,8},{24,16},{32,24},{40,32},{48,40},{56,48},{1,57}... | collective-permute-start | bytes 1179656 | tf_op jit(solution)/shard_map/ppermute | solution.py:36
  68.8 6.7 %copy-start.6 = (bf16[4,16,3072]{2,1,0:T(8,128)(2,1)}, bf16[4,16,3072]{2,1,0:T(8,128)(2,1)S(1)}, u32[]{:S(2)}) copy-start(bf16[4,16,3072]{2,1,0:T(8,128)(2,1)S(1)} %collective-permute-done.3.refs_1_) | copy-start | bytes 1179652
  68.8 8.1 %collective-permute-start.5 = (bf16[4,16,3072]{2,1,0:T(8,128)(2,1)S(1)}, bf16[4,16,3072]{2,1,0:T(8,128)(2,1)}, u32[]{:S(2)}, u32[]{:S(2)}) collective-permute-start(bf16[4,16,3072]{2,1,0:T(8,128)(2,1)S(1)} %collective-permute-done.3.refs_1_), channel_id=1, source_target_pairs={{0,8},{8,16},{16,24},{24,32},{32,40},{40,48},{48,56},{56,0},{1,9},... | collective-permute-start | bytes 1179656 | tf_op jit(solution)/shard_map/ppermute | solution.py:36
  75.5 15.3 %collective-permute-start.8 = (bf16[4,16,3072]{2,1,0:T(8,128)(2,1)}, bf16[4,16,3072]{2,1,0:T(8,128)(2,1)}, u32[]{:S(2)}, u32[]{:S(2)}) collective-permute-start(bf16[4,16,3072]{2,1,0:T(8,128)(2,1)} %collective-permute-done.6.refs_4_), channel_id=1, source_target_pairs={{0,56},{8,0},{16,8},{24,16},{32,24},{40,32},{48,40},{56,48},{1,57}... | collective-permute-start | bytes 1179656 | tf_op jit(solution)/shard_map/ppermute | solution.py:36
  76.9 18.1 %collective-permute-start.7 = (bf16[4,16,3072]{2,1,0:T(8,128)(2,1)}, bf16[4,16,3072]{2,1,0:T(8,128)(2,1)}, u32[]{:S(2)}, u32[]{:S(2)}) collective-permute-start(bf16[4,16,3072]{2,1,0:T(8,128)(2,1)} %collective-permute-done.5.refs_3_), channel_id=1, source_target_pairs={{0,8},{8,16},{16,24},{24,32},{32,40},{40,48},{48,56},{56,0},{1,9},... | collective-permute-start | bytes 1179656 | tf_op jit(solution)/shard_map/ppermute | solution.py:36
  80.4 27.6 %copy-start.2 = (bf16[8,16,3072]{2,1,0:T(8,128)(2,1)}, bf16[8,16,3072]{2,1,0:T(8,128)(2,1)S(1)}, u32[]{:S(2)}) copy-start(bf16[8,16,3072]{2,1,0:T(8,128)(2,1)S(1)} %collective-permute-done.18.refs_10_) | copy-start | bytes 2359300
  80.4 19.7 %collective-permute-start.20 = (bf16[8,8,3072]{2,1,0:T(8,128)(2,1)S(1)}, bf16[8,8,3072]{2,1,0:T(8,128)(2,1)}, u32[]{:S(2)}, u32[]{:S(2)}) collective-permute-start(bf16[8,8,3072]{2,1,0:T(8,128)(2,1)S(1)} %slice.94), channel_id=1, source_target_pairs={{0,64},{64,128},{128,192},{192,0},{1,65},{65,129},{129,193},{193,1... | collective-permute-start | bytes 1179656 | tf_op jit(solution)/shard_map/ppermute | solution.py:36
  80.5 27.5 %copy-start.3 = (bf16[8,16,3072]{2,1,0:T(8,128)(2,1)}, bf16[8,16,3072]{2,1,0:T(8,128)(2,1)S(1)}, u32[]{:S(2)}) copy-start(bf16[8,16,3072]{2,1,0:T(8,128)(2,1)S(1)} %collective-permute-done.19.refs_11_) | copy-start | bytes 2359300
  80.6 20.0 %collective-permute-start.21 = (bf16[8,8,3072]{2,1,0:T(8,128)(2,1)S(1)}, bf16[8,8,3072]{2,1,0:T(8,128)(2,1)}, u32[]{:S(2)}, u32[]{:S(2)}) collective-permute-start(bf16[8,8,3072]{2,1,0:T(8,128)(2,1)S(1)} %slice.95), channel_id=1, source_target_pairs={{0,192},{64,0},{128,64},{192,128},{1,193},{65,1},{129,65},{193,129... | collective-permute-start | bytes 1179656 | tf_op jit(solution)/shard_map/ppermute | solution.py:36
  91.7 9.3 %collective-permute-start.10 = (bf16[4,8,3072]{2,1,0:T(8,128)(2,1)S(1)}, bf16[4,8,3072]{2,1,0:T(8,128)(2,1)S(1)}, u32[]{:S(2)}, u32[]{:S(2)}) collective-permute-start(bf16[4,8,3072]{2,1,0:T(8,128)(2,1)S(1)} %slice.92), channel_id=1, source_target_pairs={{0,56},{8,0},{16,8},{24,16},{32,24},{40,32},{48,40},{56,48},{1,57}... | collective-permute-start | bytes 589832 | tf_op jit(solution)/shard_map/ppermute | solution.py:36
  96.0 12.0 %collective-permute-start.9 = (bf16[4,8,3072]{2,1,0:T(8,128)(2,1)S(1)}, bf16[4,8,3072]{2,1,0:T(8,128)(2,1)S(1)}, u32[]{:S(2)}, u32[]{:S(2)}) collective-permute-start(bf16[4,8,3072]{2,1,0:T(8,128)(2,1)S(1)} %slice.91), channel_id=1, source_target_pairs={{0,8},{8,16},{16,24},{24,32},{32,40},{40,48},{48,56},{56,0},{1,9},... | collective-permute-start | bytes 589832 | tf_op jit(solution)/shard_map/ppermute | solution.py:36
  101.0 7.0 %copy-start.7 = (bf16[4,8,3072]{2,1,0:T(8,128)(2,1)}, bf16[4,8,3072]{2,1,0:T(8,128)(2,1)S(1)}, u32[]{:S(2)}) copy-start(bf16[4,8,3072]{2,1,0:T(8,128)(2,1)S(1)} %collective-permute-done.10.refs_8_) | copy-start | bytes 589828
  108.0 0.7 copy-start.8
  131.2 68.7 %reduce-scatter.5.cloned.1.call-start = ((), (), s32[]{:S(2)}) async-start(), calls=%async_computation.7 | async-start | bytes 589824 | tf_op jit(solution)/shard_map/reduce_scatter | solution.py:410
  131.3 13.2 %collective-permute-start.22 = (bf16[4,32,2048]{2,1,0:T(8,128)(2,1)}, bf16[4,32,2048]{2,1,0:T(8,128)(2,1)S(1)}, u32[]{:S(2)}, u32[]{:S(2)}) collective-permute-start(bf16[4,32,2048]{2,1,0:T(8,128)(2,1)} %get-tuple-element.37), channel_id=1, source_target_pairs={{0,8},{8,16},{16,24},{24,32},{32,40},{40,48},{48,56},{56,0},{1,9},... | collective-permute-start | bytes 1572872 | tf_op jit(solution)/shard_map/ppermute | solution.py:36
  133.2 29.4 %collective-permute-start.24 = (bf16[4,32,2048]{2,1,0:T(8,128)(2,1)S(1)}, bf16[4,32,2048]{2,1,0:T(8,128)(2,1)S(1)}, u32[]{:S(2)}, u32[]{:S(2)}) collective-permute-start(bf16[4,32,2048]{2,1,0:T(8,128)(2,1)S(1)} %slice_bitcast_fusion), channel_id=1, source_target_pairs={{0,56},{8,0},{16,8},{24,16},{32,24},{40,32},{48,40},{56,48},{1,57}... | collective-permute-start | bytes 1572872 | tf_op jit(solution)/shard_map/ppermute | solution.py:36
  145.7 17.0 %collective-permute-start.23 = (bf16[4,32,2048]{2,1,0:T(8,128)(2,1)S(1)}, bf16[4,32,2048]{2,1,0:T(8,128)(2,1)S(1)}, u32[]{:S(2)}, u32[]{:S(2)}) collective-permute-start(bf16[4,32,2048]{2,1,0:T(8,128)(2,1)S(1)} %fusion.5), channel_id=1, source_target_pairs={{0,8},{8,16},{16,24},{24,32},{32,40},{40,48},{48,56},{56,0},{1,9},... | collective-permute-start | bytes 1572872 | tf_op jit(solution)/shard_map/ppermute | solution.py:36
  166.4 25.0 %collective-permute-start.25 = (bf16[4,32,2048]{2,1,0:T(8,128)(2,1)S(1)}, bf16[4,32,2048]{2,1,0:T(8,128)(2,1)S(1)}, u32[]{:S(2)}, u32[]{:S(2)}) collective-permute-start(bf16[4,32,2048]{2,1,0:T(8,128)(2,1)S(1)} %get-tuple-element.74), channel_id=1, source_target_pairs={{0,8},{8,16},{16,24},{24,32},{32,40},{40,48},{48,56},{56,0},{1,9},... | collective-permute-start | bytes 1572872 | tf_op jit(solution)/shard_map/ppermute | solution.py:36
  167.7 23.6 %collective-permute-start.26 = (bf16[4,32,2048]{2,1,0:T(8,128)(2,1)S(1)}, bf16[4,32,2048]{2,1,0:T(8,128)(2,1)S(1)}, u32[]{:S(2)}, u32[]{:S(2)}) collective-permute-start(bf16[4,32,2048]{2,1,0:T(8,128)(2,1)S(1)} %get-tuple-element.73), channel_id=1, source_target_pairs={{0,56},{8,0},{16,8},{24,16},{32,24},{40,32},{48,40},{56,48},{1,57}... | collective-permute-start | bytes 1572872 | tf_op jit(solution)/shard_map/ppermute | solution.py:36
  201.5 11.9 %collective-permute-start.27 = (bf16[4,32,2048]{2,1,0:T(8,128)(2,1)S(1)}, bf16[4,32,2048]{2,1,0:T(8,128)(2,1)S(1)}, u32[]{:S(2)}, u32[]{:S(2)}) collective-permute-start(bf16[4,32,2048]{2,1,0:T(8,128)(2,1)S(1)} %get-tuple-element.72), channel_id=1, source_target_pairs={{0,8},{8,16},{16,24},{24,32},{32,40},{40,48},{48,56},{56,0},{1,9},... | collective-permute-start | bytes 1572872 | tf_op jit(solution)/shard_map/ppermute | solution.py:36
  202.6 10.8 %collective-permute-start.28 = (bf16[4,32,2048]{2,1,0:T(8,128)(2,1)S(1)}, bf16[4,32,2048]{2,1,0:T(8,128)(2,1)S(1)}, u32[]{:S(2)}, u32[]{:S(2)}) collective-permute-start(bf16[4,32,2048]{2,1,0:T(8,128)(2,1)S(1)} %get-tuple-element.71), channel_id=1, source_target_pairs={{0,56},{8,0},{16,8},{24,16},{32,24},{40,32},{48,40},{56,48},{1,57}... | collective-permute-start | bytes 1572872 | tf_op jit(solution)/shard_map/ppermute | solution.py:36
  204.2 19.5 %copy-start.4 = (bf16[32,1024]{1,0:T(8,128)(2,1)S(1)}, bf16[32,1024]{1,0:T(8,128)(2,1)}, u32[]{:S(2)}) copy-start(bf16[32,1024]{1,0:T(8,128)(2,1)} %reduce-scatter.5.cloned.1.call-done) | copy-start | bytes 196612
  214.7 4.5 %collective-permute-start.29 = (bf16[32,2048]{1,0:T(8,128)(2,1)S(1)}, bf16[32,2048]{1,0:T(8,128)(2,1)S(1)}, u32[]{:S(2)}, u32[]{:S(2)}) collective-permute-start(bf16[32,2048]{1,0:T(8,128)(2,1)S(1)} %get-tuple-element.75), channel_id=1, source_target_pairs={{0,192},{64,0},{128,64},{192,128},{1,193},{65,1},{129,65},{193,129... | collective-permute-start | bytes 393224 | tf_op jit(solution)/shard_map/ppermute | solution.py:36
  217.2 6.4 %collective-permute-start.30 = (bf16[32,2048]{1,0:T(8,128)(2,1)S(1)}, bf16[32,2048]{1,0:T(8,128)(2,1)S(1)}, u32[]{:S(2)}, u32[]{:S(2)}) collective-permute-start(bf16[32,2048]{1,0:T(8,128)(2,1)S(1)} %get-tuple-element.77), channel_id=1, source_target_pairs={{0,64},{64,128},{128,192},{192,0},{1,65},{65,129},{129,193},{193,1... | collective-permute-start | bytes 393224 | tf_op jit(solution)/shard_map/ppermute | solution.py:36
  217.2 6.4 %collective-permute-start.31 = (bf16[32,2048]{1,0:T(8,128)(2,1)S(1)}, bf16[32,2048]{1,0:T(8,128)(2,1)S(1)}, u32[]{:S(2)}, u32[]{:S(2)}) collective-permute-start(bf16[32,2048]{1,0:T(8,128)(2,1)S(1)} %get-tuple-element.76), channel_id=1, source_target_pairs={{0,128},{64,192},{128,0},{192,64},{1,129},{65,193},{129,1},{193,65... | collective-permute-start | bytes 393224 | tf_op jit(solution)/shard_map/ppermute | solution.py:36
  224.5 17.5 %all-to-all-start.3 = ((bf16[8,4,3072]{2,1,0:T(4,128)(2,1)}), bf16[8,4,3072]{2,1,0:T(4,128)(2,1)S(1)}, u32[]{:S(2)}, u32[]{:S(2)}) async-start(bf16[8,4,3072]{2,1,0:T(4,128)(2,1)} %reshape.85), calls=%async_computation.5 | async-start | bytes 393216 | tf_op jit(solution)/shard_map/all_to_all | solution.py:429
Sparse Core Ops, SparseCore 0:
  27.7 103.4 all-gather.2
  133.7 30.9 reduce-scatter.2
  167.4 32.4 reduce-scatter.4
